TPU v7x, 32 devices: a whole 2x2x4 slice. The times are simulated.
32 devices in a mesh: sub: 8 (over z, core), layer: 4 (over y, x).
Axes of the slice: x: 2, y: 2, z: 4, core: 2. Of those that a mesh axis runs over, the one named last changes fastest.
Arguments:
- eigen_vectors: float32 [8, 4, 24, 4096], P('sub', 'layer'), may hold values from -4.1 to 4.1
- row_mass: float32 [8, 4, 4096], P('sub', 'layer'), may hold values from 0.1 to 0.8
- inner_weight: float32 [8, 4, 3, 4096], P('sub', 'layer'), may hold values from 0.05 to 0.4
- face_weight: float32 [8, 4, 2, 128], P('sub', 'layer'), may hold values from 80 to 10240, as said below
- margin_rows: int32 [8, 4, 4, 128], P('sub', 'layer'), may hold values from 0 to 4095, as said below
Outputs:
- applied: float32 [8, 4, 24, 4096], P('sub', 'layer')
- diag_factor: float32 [8, 96, 96], P('sub', 'layer')
- left_factor: float32 [8, 96, 96], P('sub', 'layer')
- right_factor: float32 [8, 96, 96], P('sub', 'layer')
Inputs may be any that keep to these rules, and one draw needn't show every extreme that they name: Row numbers of a subdomain's own rows; a row may appear in several lists or twice in one list. Both sides of an interface list the same row numbers: margin_rows[s, j, 1] equals margin_rows[s-1, j, 0] for s >= 1, and margin_rows[s, j, 3] equals margin_rows[s, j-1, 2] for j >= 1. `face_weight`: index 0 (springs along sub) lies in 1280 to 10240, index 1 (springs along layer) in 2.5 * 32 to 640.
All inputs are finite; a program needn't handle non-finite values.
Results may differ from a plain program's by a relative error of at most 0.0003.
Values sent between devices are 32-bit elements; how exact they have to be, the bound alone decides.
No kernel may reach another device: no remote copies, remote signals or barrier semaphores. Data moves between devices by JAX's collectives and lax.ppermute only.
A program may use at most 128 MiB of HBM per device.

v0:
```python
import jax
import jax.numpy as jnp
from jax import lax
from jax.sharding import PartitionSpec as P

STRIDES = (1, 3, 27)
HIGHEST = lax.Precision.HIGHEST


def from_behind(array, axis, by):
    devices = lax.axis_size(axis)
    pairs = [(i, i + by) for i in range(devices) if 0 <= i + by < devices]
    return lax.ppermute(array, axis, pairs)


def padded(cells, sides, width):
    for axis, dim in sides:
        count = lax.axis_size(axis)
        ends = count - 1
        head = lax.slice_in_dim(cells, 0, width, axis=dim)
        tail = lax.slice_in_dim(cells, cells.shape[dim] - width, cells.shape[dim], axis=dim)
        cells = jnp.concatenate(
            [
                lax.ppermute(tail, axis, [(i, (i + 1) % count) for i in range(ends)]),
                cells,
                lax.ppermute(head, axis, [((i + 1) % count, i) for i in range(ends)]),
            ],
            axis=dim,
        )
    return cells


def device_terms(vectors, masses, interior, row_lists, picked, springs, partners):
    row_count = vectors.shape[-1]
    places = jnp.arange(row_count, dtype=jnp.int32)
    laplace = jnp.zeros_like(vectors)
    for k, t in enumerate(STRIDES):
        edge_weight = jnp.where(places < row_count - t, interior[k], 0.0)
        fluxes = edge_weight * (vectors - jnp.roll(vectors, -t, axis=1))
        laplace = laplace + fluxes - jnp.roll(fluxes, t, axis=1)
    own_part = masses * vectors + laplace
    coupled = jnp.zeros_like(vectors)
    for k in range(4):
        onehot = (row_lists[k][:, None] == places[None, :]).astype(jnp.float32)
        own_part = own_part + jnp.dot(springs[k] * picked[k], onehot, precision=HIGHEST)
        coupled = coupled + jnp.dot(springs[k] * partners[k], onehot, precision=HIGHEST)
    applied = own_part - coupled
    inverse = 1.0 / row_count
    diag_tile = jnp.dot(vectors, own_part.T, precision=HIGHEST) * inverse
    down_tile = -jnp.dot(springs[1] * picked[1], partners[1].T, precision=HIGHEST) * inverse
    up_tile = -jnp.dot(springs[0] * partners[0], picked[0].T, precision=HIGHEST) * inverse
    side_tile = -jnp.dot(springs[3] * picked[3], partners[3].T, precision=HIGHEST) * inverse
    return (applied, jnp.stack([diag_tile, down_tile, up_tile, side_tile]))


def assemble(plane_tiles):
    layers = plane_tiles.shape[0]
    mode_count = plane_tiles.shape[-1]
    size_all = layers * mode_count
    identity = jnp.eye(layers, dtype=jnp.float32)
    subdiag = jnp.eye(layers, k=-1, dtype=jnp.float32)
    diag_block = (
        jnp.einsum("jab,jk->jakb", plane_tiles[:, 0], identity, precision=HIGHEST)
        + jnp.einsum("jab,jk->jakb", plane_tiles[:, 3], subdiag, precision=HIGHEST)
        + jnp.einsum("jba,jk->kajb", plane_tiles[:, 3], subdiag, precision=HIGHEST)
    )
    down_block = jnp.einsum("jab,jk->jakb", plane_tiles[:, 1], identity, precision=HIGHEST)
    up_block = jnp.einsum("jab,jk->jakb", plane_tiles[:, 2], identity, precision=HIGHEST)
    return (
        diag_block.reshape(size_all, size_all),
        down_block.reshape(size_all, size_all),
        up_block.reshape(size_all, size_all),
    )


def eliminate(operands):
    diag_block, down_block, up_block = operands
    lower_factor = jnp.linalg.cholesky(diag_block)
    left_block = lax.linalg.triangular_solve(lower_factor, down_block, left_side=True, lower=True).T
    right_block = lax.linalg.triangular_solve(
        lower_factor, up_block.T, left_side=True, lower=True
    ).T
    left_square = jnp.dot(left_block, left_block.T, precision=HIGHEST)
    right_square = jnp.dot(right_block, right_block.T, precision=HIGHEST)
    cross_term = -jnp.dot(right_block, left_block.T, precision=HIGHEST)
    return (lower_factor, left_block, right_block, left_square, right_square, cross_term)


def skip_plane(operands):
    empty_block = jnp.zeros_like(operands[0])
    return (empty_block, empty_block, empty_block, empty_block, empty_block, empty_block)


def factor_root(diag_block):
    return jnp.linalg.cholesky(diag_block)


def skip_root(diag_block):
    return jnp.zeros_like(diag_block)


def plane_move(square_part, cross_part, offset):
    return from_behind((square_part, cross_part), "sub", offset)


def per_device(eigen_vectors, row_mass, inner_weight, face_weight, margin_rows):
    vectors = eigen_vectors[0, 0]
    row_lists = margin_rows[0, 0]
    face_springs = face_weight[0, 0]
    mode_count = vectors.shape[0]
    subs = lax.axis_size("sub")
    layers = lax.axis_size("layer")
    sub_here = lax.axis_index("sub")
    lay_here = lax.axis_index("layer")
    picked = jnp.stack([jnp.take(vectors, row_lists[k], axis=1) for k in range(4)])
    zero_row = jnp.zeros((1, row_lists.shape[-1]), jnp.float32)
    sub_send = jnp.stack(
        [
            jnp.concatenate([picked[1], zero_row], 0),
            jnp.concatenate([picked[0], face_springs[0:1]], 0),
        ]
    )
    sub_rim = padded(sub_send, (("sub", 0),), 1)
    lay_send = jnp.stack(
        [
            jnp.concatenate([picked[3], zero_row], 0),
            jnp.concatenate([picked[2], face_springs[1:2]], 0),
        ]
    )
    lay_rim = padded(lay_send, (("layer", 0),), 1)
    partners = jnp.stack(
        [
            sub_rim[3, :mode_count],
            sub_rim[0, :mode_count],
            lay_rim[3, :mode_count],
            lay_rim[0, :mode_count],
        ]
    )
    springs = jnp.stack(
        [
            jnp.where(sub_here < subs - 1, face_springs[0], 0.0),
            sub_rim[0, mode_count],
            jnp.where(lay_here < layers - 1, face_springs[1], 0.0),
            lay_rim[0, mode_count],
        ]
    )
    applied, coarse_tiles = device_terms(
        vectors, row_mass[0, 0], inner_weight[0, 0], row_lists, picked, springs, partners
    )
    plane_tiles = lax.all_gather(coarse_tiles[None], "layer", axis=0, tiled=True)
    diag_block, down_block, up_block = assemble(plane_tiles)
    empty_block = jnp.zeros_like(diag_block)
    diag_out = empty_block
    left_out = empty_block
    right_out = empty_block
    row_start = lay_here * mode_count
    for level_index in range(subs.bit_length() - 1):
        distance = 2**level_index
        active = (sub_here + 1) % distance == 0
        retire = jnp.logical_and(active, (sub_here + 1) % (2 * distance) != 0)
        keeper = jnp.logical_and(active, (sub_here + 1) % (2 * distance) == 0)
        results = lax.cond(retire, eliminate, skip_plane, (diag_block, down_block, up_block))
        lower_factor, left_block, right_block, left_square, right_square, cross_term = results
        diag_out = jnp.where(retire, lower_factor, diag_out)
        left_out = jnp.where(retire, left_block, left_out)
        right_out = jnp.where(retire, right_block, right_out)
        from_right = plane_move(left_square, cross_term, -distance)
        from_left = plane_move(right_square, cross_term, distance)
        diag_block = jnp.where(keeper, diag_block - from_right[0] - from_left[0], diag_block)
        up_block = jnp.where(keeper, from_right[1], up_block)
        down_block = jnp.where(keeper, from_left[1], down_block)
    is_root = sub_here == subs - 1
    root_factor = lax.cond(is_root, factor_root, skip_root, diag_block)
    diag_out = jnp.where(is_root, root_factor, diag_out)
    diag_strip = lax.dynamic_slice_in_dim(diag_out, row_start, mode_count, 0)[None]
    left_strip = lax.dynamic_slice_in_dim(left_out, row_start, mode_count, 0)[None]
    right_strip = lax.dynamic_slice_in_dim(right_out, row_start, mode_count, 0)[None]
    return (applied[None, None], diag_strip, left_strip, right_strip)


def solution(mesh):
    in_specs = (
        P("sub", "layer", None, None),
        P("sub", "layer", None),
        P("sub", "layer", None, None),
        P("sub", "layer", None, None),
        P("sub", "layer", None, None),
    )
    out_specs = (
        P("sub", "layer", None, None),
        P("sub", "layer", None),
        P("sub", "layer", None),
        P("sub", "layer", None),
    )
    return jax.shard_map(
        per_device, mesh=mesh, in_specs=in_specs, out_specs=out_specs, check_vma=False
    )
```

profile of v0, /device:TPU:25, one launch (start us, length us, event | category | flops | bytes accessed | tf_op | source)
XLA Modules:
  0.0 134.6 jit_solution(6333313606097919611)
XLA Ops:
  0.6 0.8 compare_and_fusion
  1.5 1.7 %copy.159 = f32[24,4096]{0,1:T(8,128)S(1)} copy(f32[24,4096]{1,0:T(8,128)} %bitcast.198) | data formatting | bytes 786432 | tf_op jit(solution)/shard_map/squeeze | solution.py:107
  3.2 0.6 gather_fusion.3
  4.0 1.3 collective-permute-start.3
  5.3 0.6 gather_fusion.1
  6.0 2.6 %collective-permute-start.2 = (f32[1,25,128]{1,2,0:T(8,128)S(1)}, f32[1,25,128]{1,2,0:T(8,128)S(1)}, u32[]{:S(2)}, u32[]{:S(2)}) collective-permute-start(f32[1,25,128]{1,2,0:T(8,128)S(1)} %pad_bitcast_fusion.1), channel_id=1, source_target_pairs={{4,0},{8,4},{12,8},{16,12},{20,16},{24,20},{28,24},{5,1},{9,5},{13... | collective-permute-start | bytes 38408 | tf_op jit(solution)/shard_map/ppermute | solution.py:26
  8.8 0.6 gather_fusion
  9.6 1.3 collective-permute-start
  11.0 0.6 gather_fusion.2
  11.9 4.3 %collective-permute-start.1 = (f32[1,25,128]{1,2,0:T(8,128)S(1)}, f32[1,25,128]{1,2,0:T(8,128)S(1)}, u32[]{:S(2)}, u32[]{:S(2)}) collective-permute-start(f32[1,25,128]{1,2,0:T(8,128)S(1)} %maximum_bitcast_fusion.1), channel_id=1, source_target_pairs={{0,1},{1,2},{2,3},{4,5},{5,6},{6,7},{8,9},{9,10},{10,11},{12,13},{... | collective-permute-start | bytes 38408 | tf_op jit(solution)/shard_map/ppermute | solution.py:24
  16.2 0.2 slice.170
  16.4 0.2 slice.166
  16.6 0.2 slice.174
  17.3 0.9 convolution_add_fusion.4
  18.2 0.2 slice_reduce_fusion.1
  18.4 0.9 convolution_add_fusion.3
  19.3 0.8 convolution_add_fusion.2
  20.1 0.2 slice_reduce_fusion
  20.3 0.9 convolution_add_fusion.1
  21.2 0.5 fusion.36
  21.7 0.3 fusion.35
  22.0 0.3 fusion.31
  22.3 0.3 fusion.33
  22.7 7.6 %all-gather = f32[16,24,24]{2,1,0:T(8,128)S(1)} all-gather(f32[4,24,24]{2,1,0:T(8,128)S(1)} %copy.169), channel_id=2, replica_groups=mesh['sub'=8,'layer'=4] {'layer'}, dimensions={0}, use_global_device_ids=true | all-gather | bytes 46080 | tf_op jit(solution)/shard_map/all_gather | solution.py:150
  30.3 0.2 multiply_bitcast_fusion.1
  31.5 24.5 %collective-permute-start.7 = (f32[96,96]{0,1:T(8,128)S(1)}, f32[96,96]{0,1:T(8,128)S(1)}, u32[]{:S(2)}, u32[]{:S(2)}) collective-permute-start(f32[96,96]{0,1:T(8,128)S(1)} %get-tuple-element.235), channel_id=1, source_target_pairs={{4,0},{8,4},{12,8},{16,12},{20,16},{24,20},{28,24},{5,1},{9,5},{13... | collective-permute-start | bytes 110600 | tf_op jit(solution)/shard_map/ppermute | solution.py:13
  56.0 1.3 collective-permute-start.6
  57.5 1.3 collective-permute-start.5
  58.8 3.8 %collective-permute-start.4 = (f32[96,96]{0,1:T(8,128)S(1)}, f32[96,96]{0,1:T(8,128)S(1)}, u32[]{:S(2)}, u32[]{:S(2)}) collective-permute-start(f32[96,96]{0,1:T(8,128)S(1)} %copy.175), channel_id=1, source_target_pairs={{4,0},{8,4},{12,8},{16,12},{20,16},{24,20},{28,24},{5,1},{9,5},{13... | collective-permute-start | bytes 110600 | tf_op jit(solution)/shard_map/ppermute | solution.py:13
  62.6 0.8 fusion.27
  63.5 0.8 fusion.29
  64.3 0.8 fusion.28
  65.6 1.3 collective-permute-start.9
  66.9 23.7 %collective-permute-start.8 = (f32[96,96]{0,1:T(8,128)S(1)}, f32[96,96]{0,1:T(8,128)S(1)}, u32[]{:S(2)}, u32[]{:S(2)}) collective-permute-start(f32[96,96]{0,1:T(8,128)S(1)} %copy.181), channel_id=1, source_target_pairs={{8,0},{12,4},{16,8},{20,12},{24,16},{28,20},{9,1},{13,5},{17,9},{2... | collective-permute-start | bytes 110600 | tf_op jit(solution)/shard_map/ppermute | solution.py:13
  90.6 1.6 %fusion.26 = f32[1,1,24,4096]{3,2,1,0:T(8,128)} fusion(f32[24,4096]{1,0:T(8,128)S(1)} %convolution_add_fusion.1, f32[24,4096]{1,0:T(8,128)S(1)} %fusion.27, f32[24,4096]{1,0:T(8,128)S(1)} %fusion.28, f32[24,4096]{1,0:T(8,128)S(1)} %fusion.29, s32[128]{0:T(128)S(1)} %get-tuple-element.277, f32[1,25,128]{1,2,0:T(8,128)S(1)} %collective-permute-done.2, ...), kind=kOutput, calls=%fused_computation.61 | convolution fusion | flops 151915520 | bytes 1979904 | tf_op jit(solution)/shard_map/dot_general | solution.py:46
  92.2 3.4 %collective-permute-start.11 = (f32[96,96]{1,0:T(8,128)S(1)}, f32[96,96]{1,0:T(8,128)S(1)}, u32[]{:S(2)}, u32[]{:S(2)}) collective-permute-start(f32[96,96]{1,0:T(8,128)S(1)} %get-tuple-element.107), channel_id=1, source_target_pairs={{8,0},{12,4},{16,8},{20,12},{24,16},{28,20},{9,1},{13,5},{17,9},{2... | collective-permute-start | bytes 110600 | tf_op jit(solution)/shard_map/ppermute | solution.py:13
  95.5 1.3 collective-permute-start.10
  96.9 3.5 %collective-permute-done.10 = f32[96,96]{1,0:T(8,128)S(1)} collective-permute-done((f32[96,96]{1,0:T(8,128)S(1)}, f32[96,96]{1,0:T(8,128)S(1)}, u32[]{:S(2)}, u32[]{:S(2)}) %collective-permute-start.10) | collective-permute-done | bytes 36896 | tf_op jit(solution)/shard_map/ppermute | solution.py:13
  100.3 0.3 conditional.6
  100.8 1.3 collective-permute-start.13
  102.1 20.4 %collective-permute-start.12 = (f32[96,96]{0,1:T(8,128)S(1)}, f32[96,96]{0,1:T(8,128)S(1)}, u32[]{:S(2)}, u32[]{:S(2)}) collective-permute-start(f32[96,96]{0,1:T(8,128)S(1)} %copy.185), channel_id=1, source_target_pairs={{16,0},{20,4},{24,8},{28,12},{17,1},{21,5},{25,9},{29,13},{18,2},{... | collective-permute-start | bytes 110600 | tf_op jit(solution)/shard_map/ppermute | solution.py:13
  122.5 0.6 fusion.82
  123.1 0.6 fusion.83
  123.7 10.3 %conditional.7 = (f32[96,96]{1,0:T(8,128)S(1)}) conditional(s32[]{:T(128)} %convert_element_type.8, () %tuple.45, (s32[]{:T(128)}, pred[]{:T(512)}, f32[96,96]{0,1:T(8,128)S(1)}, f32[96,96]{0,1:T(8,128)S(1)}, f32[96,96]{0,1:T(8,128)S(1)}) %tuple.52), branch_computations={%region_8.12_spmd, %region_9.13_spmd} | conditional | flops 101473 | bytes 443159 | solution.py:173
  123.9 8.8 %cholesky.107 = f32[96,96]{1,0:T(8,128)S(1)} custom-call(f32[96,96]{1,0:T(8,128)S(1)} %fusion), custom_call_target="Cholesky" | custom-call | tf_op jit(solution)/shard_map/cond/branch_1_fun/jit(cholesky)/cholesky | solution.py:95
  132.7 0.7 compare_reduce_fusion
  133.4 0.6 select_select_fusion
  134.0 0.6 fusion.84
  (94 shorter events, 3.3 us)
Async XLA Ops:
  0.6 8.0 %copy-start.4 = (f32[1,1,2,128]{3,2,1,0:T(2,128)S(1)}, f32[1,1,2,128]{3,2,1,0:T(2,128)}, u32[]{:S(2)}) copy-start(f32[1,1,2,128]{3,2,1,0:T(2,128)} %param.21) | copy-start | bytes 3076
  1.5 14.6 %copy-start.3 = (s32[1,1,4,128]{3,2,1,0:T(4,128)S(1)}, s32[1,1,4,128]{3,2,1,0:T(4,128)}, u32[]{:S(2)}) copy-start(s32[1,1,4,128]{3,2,1,0:T(4,128)} %param.22) | copy-start | bytes 6148
  1.5 14.7 %copy-start = (f32[1,1,24,4096]{3,2,1,0:T(8,128)S(1)}, f32[1,1,24,4096]{3,2,1,0:T(8,128)}, u32[]{:S(2)}) copy-start(f32[1,1,24,4096]{3,2,1,0:T(8,128)} %param.18) | copy-start | bytes 1179652
  3.2 13.5 %copy-start.1 = (f32[1,1,3,4096]{3,1,2,0:T(1,128)S(1)}, f32[1,1,3,4096]{3,1,2,0:T(1,128)}, u32[]{:S(2)}) copy-start(f32[1,1,3,4096]{3,1,2,0:T(1,128)} %param.20) | copy-start | bytes 147460
  4.0 60.4 %collective-permute-start.3 = (f32[1,25,128]{1,2,0:T(8,128)S(1)}, f32[1,25,128]{1,2,0:T(8,128)S(1)}, u32[]{:S(2)}, u32[]{:S(2)}) collective-permute-start(f32[1,25,128]{1,2,0:T(8,128)S(1)} %pad_bitcast_fusion), channel_id=1, source_target_pairs={{1,0},{2,1},{3,2},{5,4},{6,5},{7,6},{9,8},{10,9},{11,10},{13,12},{... | collective-permute-start | bytes 38408 | tf_op jit(solution)/shard_map/ppermute | solution.py:26
  6.0 16.3 %collective-permute-start.2 = (f32[1,25,128]{1,2,0:T(8,128)S(1)}, f32[1,25,128]{1,2,0:T(8,128)S(1)}, u32[]{:S(2)}, u32[]{:S(2)}) collective-permute-start(f32[1,25,128]{1,2,0:T(8,128)S(1)} %pad_bitcast_fusion.1), channel_id=1, source_target_pairs={{4,0},{8,4},{12,8},{16,12},{20,16},{24,20},{28,24},{5,1},{9,5},{13... | collective-permute-start | bytes 38408 | tf_op jit(solution)/shard_map/ppermute | solution.py:26
  9.6 8.6 %collective-permute-start = (f32[1,25,128]{1,2,0:T(8,128)S(1)}, f32[1,25,128]{1,2,0:T(8,128)S(1)}, u32[]{:S(2)}, u32[]{:S(2)}) collective-permute-start(f32[1,25,128]{1,2,0:T(8,128)S(1)} %maximum_bitcast_fusion), channel_id=1, source_target_pairs={{0,4},{4,8},{8,12},{12,16},{16,20},{20,24},{24,28},{1,5},{5,9},{9,... | collective-permute-start | bytes 38408 | tf_op jit(solution)/shard_map/ppermute | solution.py:24
  11.9 8.3 %collective-permute-start.1 = (f32[1,25,128]{1,2,0:T(8,128)S(1)}, f32[1,25,128]{1,2,0:T(8,128)S(1)}, u32[]{:S(2)}, u32[]{:S(2)}) collective-permute-start(f32[1,25,128]{1,2,0:T(8,128)S(1)} %maximum_bitcast_fusion.1), channel_id=1, source_target_pairs={{0,1},{1,2},{2,3},{4,5},{5,6},{6,7},{8,9},{9,10},{10,11},{12,13},{... | collective-permute-start | bytes 38408 | tf_op jit(solution)/shard_map/ppermute | solution.py:24
  16.5 0.7 copy-start.2
  31.5 33.7 %collective-permute-start.7 = (f32[96,96]{0,1:T(8,128)S(1)}, f32[96,96]{0,1:T(8,128)S(1)}, u32[]{:S(2)}, u32[]{:S(2)}) collective-permute-start(f32[96,96]{0,1:T(8,128)S(1)} %get-tuple-element.235), channel_id=1, source_target_pairs={{4,0},{8,4},{12,8},{16,12},{20,16},{24,20},{28,24},{5,1},{9,5},{13... | collective-permute-start | bytes 110600 | tf_op jit(solution)/shard_map/ppermute | solution.py:13
  56.0 9.2 %collective-permute-start.6 = (f32[96,96]{0,1:T(8,128)S(1)}, f32[96,96]{0,1:T(8,128)S(1)}, u32[]{:S(2)}, u32[]{:S(2)}) collective-permute-start(f32[96,96]{0,1:T(8,128)S(1)} %get-tuple-element.235), channel_id=1, source_target_pairs={{0,4},{4,8},{8,12},{12,16},{16,20},{20,24},{24,28},{1,5},{5,9},{9,... | collective-permute-start | bytes 110600 | tf_op jit(solution)/shard_map/ppermute | solution.py:13
  57.5 7.8 %collective-permute-start.5 = (f32[96,96]{0,1:T(8,128)S(1)}, f32[96,96]{0,1:T(8,128)S(1)}, u32[]{:S(2)}, u32[]{:S(2)}) collective-permute-start(f32[96,96]{0,1:T(8,128)S(1)} %copy.176), channel_id=1, source_target_pairs={{0,4},{4,8},{8,12},{12,16},{16,20},{20,24},{24,28},{1,5},{5,9},{9,... | collective-permute-start | bytes 110600 | tf_op jit(solution)/shard_map/ppermute | solution.py:13
  58.8 6.5 %collective-permute-start.4 = (f32[96,96]{0,1:T(8,128)S(1)}, f32[96,96]{0,1:T(8,128)S(1)}, u32[]{:S(2)}, u32[]{:S(2)}) collective-permute-start(f32[96,96]{0,1:T(8,128)S(1)} %copy.175), channel_id=1, source_target_pairs={{4,0},{8,4},{12,8},{16,12},{20,16},{24,20},{28,24},{5,1},{9,5},{13... | collective-permute-start | bytes 110600 | tf_op jit(solution)/shard_map/ppermute | solution.py:13
  65.6 31.2 %collective-permute-start.9 = (f32[96,96]{0,1:T(8,128)S(1)}, f32[96,96]{0,1:T(8,128)S(1)}, u32[]{:S(2)}, u32[]{:S(2)}) collective-permute-start(f32[96,96]{0,1:T(8,128)S(1)} %copy.182), channel_id=1, source_target_pairs={{0,8},{4,12},{8,16},{12,20},{16,24},{20,28},{1,9},{5,13},{9,17},{1... | collective-permute-start | bytes 110600 | tf_op jit(solution)/shard_map/ppermute | solution.py:13
  66.9 30.0 %collective-permute-start.8 = (f32[96,96]{0,1:T(8,128)S(1)}, f32[96,96]{0,1:T(8,128)S(1)}, u32[]{:S(2)}, u32[]{:S(2)}) collective-permute-start(f32[96,96]{0,1:T(8,128)S(1)} %copy.181), channel_id=1, source_target_pairs={{8,0},{12,4},{16,8},{20,12},{24,16},{28,20},{9,1},{13,5},{17,9},{2... | collective-permute-start | bytes 110600 | tf_op jit(solution)/shard_map/ppermute | solution.py:13
  92.2 4.7 %collective-permute-start.11 = (f32[96,96]{1,0:T(8,128)S(1)}, f32[96,96]{1,0:T(8,128)S(1)}, u32[]{:S(2)}, u32[]{:S(2)}) collective-permute-start(f32[96,96]{1,0:T(8,128)S(1)} %get-tuple-element.107), channel_id=1, source_target_pairs={{8,0},{12,4},{16,8},{20,12},{24,16},{28,20},{9,1},{13,5},{17,9},{2... | collective-permute-start | bytes 110600 | tf_op jit(solution)/shard_map/ppermute | solution.py:13
  95.5 4.8 %collective-permute-start.10 = (f32[96,96]{1,0:T(8,128)S(1)}, f32[96,96]{1,0:T(8,128)S(1)}, u32[]{:S(2)}, u32[]{:S(2)}) collective-permute-start(f32[96,96]{1,0:T(8,128)S(1)} %get-tuple-element.107), channel_id=1, source_target_pairs={{0,8},{4,12},{8,16},{12,20},{16,24},{20,28},{1,9},{5,13},{9,17},{1... | collective-permute-start | bytes 110600 | tf_op jit(solution)/shard_map/ppermute | solution.py:13
  100.8 22.9 %collective-permute-start.13 = (f32[96,96]{0,1:T(8,128)S(1)}, f32[96,96]{0,1:T(8,128)S(1)}, u32[]{:S(2)}, u32[]{:S(2)}) collective-permute-start(f32[96,96]{0,1:T(8,128)S(1)} %copy.186), channel_id=1, source_target_pairs={{0,16},{4,20},{8,24},{12,28},{1,17},{5,21},{9,25},{13,29},{2,18},{... | collective-permute-start | bytes 110600 | tf_op jit(solution)/shard_map/ppermute | solution.py:13
  102.1 21.6 %collective-permute-start.12 = (f32[96,96]{0,1:T(8,128)S(1)}, f32[96,96]{0,1:T(8,128)S(1)}, u32[]{:S(2)}, u32[]{:S(2)}) collective-permute-start(f32[96,96]{0,1:T(8,128)S(1)} %copy.185), channel_id=1, source_target_pairs={{16,0},{20,4},{24,8},{28,12},{17,1},{21,5},{25,9},{29,13},{18,2},{... | collective-permute-start | bytes 110600 | tf_op jit(solution)/shard_map/ppermute | solution.py:13
where the time goes:
time: 135 us
  starting transfers between devices  91.7 us (68%)
  other arithmetic  13.9 us (10%)
  matrix products  8.93 us (7%)
  blocking collectives  7.59 us (6%)
  local copies, waits for them, and re-layouts  7.2 us (5%)
  waiting for transfers between devices  3.52 us (3%)
  between operations  1.37 us (1%)
    ppermute x10, starting transfers between devices, from_behind(): return lax.ppermute(array, axis, pairs)  82.3 us
    another operation x3, other arithmetic, factor_root(): return jnp.linalg.cholesky(diag_block)  9.52 us
    all_gather x1, blocking collectives, per_device(): lax.all_gather(coarse_tiles[None], 'layer', axis=0, tiled=True)  7.59 us
    ppermute x2, starting transfers between devices, padded(): lax.ppermute(tail, axis, [(i, (i + 1) % count) for i in range(ends)])  5.56 us
    dot_general x4, matrix products, device_terms(): jnp.dot(springs[k] * partners[k], onehot, precision=HIGHEST)  4.13 us
    ppermute x2, starting transfers between devices, padded(): lax.ppermute(head, axis, [((i + 1) % count, i) for i in range(ends)])  3.87 us
    ppermute x10, waiting for transfers between devices, from_behind(): return lax.ppermute(array, axis, pairs)  3.51 us
    dot_general x4, matrix products, device_terms(): jnp.dot(springs[k] * picked[k], onehot, precision=HIGHEST)  3.46 us
  transfers between devices with their start and end apart: 14, of which 1 were waited for; matrix products, arithmetic and copies ran while one was open for 11% of the time, Pallas kernels for 0%

commit v1 on v0

v1 whole, which is shorter than its diff:
```python
import functools
import jax
import jax.numpy as jnp
from jax import lax
from jax.experimental import pallas as pl
from jax.experimental.pallas import tpu as pltpu
from jax.sharding import PartitionSpec as P

STRIDES = (1, 3, 27)
HIGHEST = lax.Precision.HIGHEST
LANES = 128
ROWS = 8
UNROLLED_LAYERS = 4


def padded(cells, sides, width):
    for axis, dim in sides:
        count = lax.axis_size(axis)
        ends = count - 1
        head = lax.slice_in_dim(cells, 0, width, axis=dim)
        tail = lax.slice_in_dim(cells, cells.shape[dim] - width, cells.shape[dim], axis=dim)
        cells = jnp.concatenate(
            [
                lax.ppermute(tail, axis, [(i, (i + 1) % count) for i in range(ends)]),
                cells,
                lax.ppermute(head, axis, [((i + 1) % count, i) for i in range(ends)]),
            ],
            axis=dim,
        )
    return cells


def device_terms(vectors, masses, interior, row_lists, picked, springs, partners):
    row_count = vectors.shape[-1]
    places = jnp.arange(row_count, dtype=jnp.int32)
    laplace = jnp.zeros_like(vectors)
    for k, t in enumerate(STRIDES):
        edge_weight = jnp.where(places < row_count - t, interior[k], 0.0)
        fluxes = edge_weight * (vectors - jnp.roll(vectors, -t, axis=1))
        laplace = laplace + fluxes - jnp.roll(fluxes, t, axis=1)
    own_part = masses * vectors + laplace
    inverse = 1.0 / row_count
    diag_tile = jnp.dot(vectors, own_part.T, precision=HIGHEST)
    applied = own_part
    for k in range(4):
        onehot = (row_lists[k][:, None] == places[None, :]).astype(jnp.float32)
        diag_tile = diag_tile + jnp.dot(picked[k], (springs[k] * picked[k]).T, precision=HIGHEST)
        applied = applied + jnp.dot(
            springs[k] * (picked[k] - partners[k]), onehot, precision=HIGHEST
        )
    diag_tile = diag_tile * inverse
    down_tile = -jnp.dot(springs[1] * picked[1], partners[1].T, precision=HIGHEST) * inverse
    side_turned = -jnp.dot(partners[3], (springs[3] * picked[3]).T, precision=HIGHEST) * inverse
    tiles = jnp.concatenate([diag_tile, side_turned, down_tile, down_tile.T], axis=1)
    tiles = jnp.pad(tiles, ((0, 0), (0, -tiles.shape[1] % LANES)))
    return applied, tiles


def turned_dot(left, right):
    return lax.dot_general(
        left,
        right,
        (((0,), (0,)), ((), ())),
        precision=HIGHEST,
        preferred_element_type=jnp.float32,
    )


def plain_dot(left, right):
    return lax.dot_general(
        left,
        right,
        (((1,), (0,)), ((), ())),
        precision=HIGHEST,
        preferred_element_type=jnp.float32,
    )


def factor_rows(blocks, tiles_per_part, first_row, turned):
    strip_count = len(blocks[0])
    iota = lax.broadcasted_iota(jnp.int32, (ROWS, LANES), 0)
    lane = lax.broadcasted_iota(jnp.int32, (ROWS, LANES), 1)
    blocks = [[list(strip) for strip in block] for block in blocks]
    for q in range(strip_count):
        for b, block in enumerate(blocks):
            start = q * ROWS
            source = turned(b, block, q)
            columns = [
                [
                    jnp.broadcast_to(source[r][:, start + j : start + j + 1], (ROWS, LANES))
                    for r in range(strip_count - q)
                ]
                for j in range(ROWS)
            ]
            pivots = jnp.zeros((ROWS, LANES), jnp.float32)
            for k in range(ROWS):
                pivot = columns[k][0][k : k + 1, :]
                inverse = 1.0 / pivot
                pivots = jnp.where(iota == k, pivot, pivots)
                below = [jnp.where(iota > k, columns[k][0], 0.0)] + columns[k][1:]
                below = [column * inverse for column in below]
                for j in range(k + 1, ROWS):
                    other = columns[k][0][j : j + 1, :]
                    for r in range(strip_count - q):
                        columns[j][r] = columns[j][r] - below[r] * other
                for t in range(len(block[q])):
                    row = block[q][t][k : k + 1, :]
                    for r in range(strip_count - q):
                        block[q + r][t] = block[q + r][t] - below[r] * row
            scale = lax.rsqrt(pivots)
            for t in range(len(block[q])):
                strip = block[q][t] * scale
                if t < tiles_per_part:
                    keep = lane + t * LANES >= iota + (first_row + start)
                    strip = jnp.where(keep, strip, 0.0)
                block[q][t] = strip
    return blocks


def eliminate_panel(grid_ref, planes, modes, order, part, lanes_used, panel):
    per_part = part // LANES
    first_row = panel * modes
    static = isinstance(panel, int)
    if static:
        rows = pl.ds(first_row, modes)
    else:
        rows = pl.ds(pl.multiple_of(first_row, ROWS), modes)
    blocks = []
    for plane in planes:
        panel_rows = grid_ref[plane, rows, 0:lanes_used]
        blocks.append(
            [
                [
                    panel_rows[q * ROWS : (q + 1) * ROWS, t * LANES : (t + 1) * LANES]
                    for t in range(lanes_used // LANES)
                ]
                for q in range(modes // ROWS)
            ]
        )

    def turned(b, block, q):
        found = []
        for strip in block[q:]:
            if static and first_row // LANES == (first_row + modes - 1) // LANES:
                tile = strip[first_row // LANES]
                offset = first_row % LANES
                found.append(tile if offset == 0 else tile[:, offset : offset + modes])
            else:
                wide = jnp.concatenate(strip[:per_part], axis=1)
                found.append(pltpu.roll(wide, lax.rem(part - first_row, part), 1)[:, :LANES])
        return found

    blocks = factor_rows(blocks, per_part, first_row, turned)
    for plane, block in zip(planes, blocks):
        panel_rows = jnp.concatenate([jnp.concatenate(strip, axis=1) for strip in block], axis=0)
        grid_ref[plane, rows, 0:lanes_used] = panel_rows
        if static:
            below = (panel + 1) * modes
            if below < order:
                columns = panel_rows[:, 0:part].T[below:order]
                update = plain_dot(columns, panel_rows)
                grid_ref[plane, below:order, 0:lanes_used] -= update
        else:
            lane = lax.broadcasted_iota(jnp.int32, (modes, part), 1)
            columns = jnp.where(lane >= first_row + modes, panel_rows[:, 0:part], 0.0)
            update = turned_dot(columns, panel_rows)[0:order]
            grid_ref[plane, :, 0:lanes_used] -= update


def eliminate_planes(grid_ref, planes, modes, order, part, lanes_used):
    layers = order // modes
    if layers <= UNROLLED_LAYERS:
        for panel in range(layers):
            eliminate_panel(grid_ref, planes, modes, order, part, lanes_used, panel)
    else:

        def one_panel(panel, carry):
            eliminate_panel(grid_ref, planes, modes, order, part, lanes_used, panel)
            return carry

        lax.fori_loop(0, layers, one_panel, 0)


def update_partners(grid_ref, plane, distance, part, order, has_left):
    left, right = plane - distance, plane + distance
    both = grid_ref[plane, :, part : 3 * part]
    turned = both.T
    from_right = plain_dot(turned[part : part + order], both)
    grid_ref[right, :, 0:part] -= from_right[:, part : 2 * part]
    grid_ref[right, :, part : 2 * part] = -from_right[:, 0:part]

    def to_left():
        from_left = plain_dot(turned[0:order], both)
        grid_ref[left, :, 0:part] -= from_left[:, 0:part]
        grid_ref[left, :, 2 * part : 3 * part] = -from_left[:, part : 2 * part]

    if isinstance(has_left, bool):
        if has_left:
            to_left()
    else:
        pl.when(has_left)(to_left)


def factor_kernel(place_ref, tiles_ref, diag_ref, left_ref, right_ref, grid_ref, turned_ref):
    subs, layers, modes, _ = tiles_ref.shape
    order = layers * modes
    part = grid_ref.shape[2] // 3
    unrolled = layers <= UNROLLED_LAYERS
    grid_ref[...] = jnp.zeros_like(grid_ref)

    def place_tiles(s, has_left):
        for j in range(layers):
            tile = tiles_ref[s, j]
            rows = slice(j * modes, (j + 1) * modes)
            grid_ref[s, rows, j * modes : (j + 1) * modes] = tile[:, 0:modes]
            if j > 0:
                above = slice((j - 1) * modes, j * modes)
                grid_ref[s, above, j * modes : (j + 1) * modes] = tile[:, modes : 2 * modes]
            lanes = slice(part + j * modes, part + (j + 1) * modes)
            grid_ref[s, rows, lanes] = tile[:, 2 * modes : 3 * modes]
            if has_left:
                lanes = slice(2 * part + j * modes, 2 * part + (j + 1) * modes)
                grid_ref[s - 1, rows, lanes] = tile[:, 3 * modes : 4 * modes]

    place_tiles(0, False)
    if unrolled:
        for s in range(1, subs):
            place_tiles(s, True)
    else:

        def place_one(s, carry):
            place_tiles(s, True)
            return carry

        lax.fori_loop(1, subs, place_one, 0)

    distance = 1
    while distance < subs:
        if unrolled:
            planes = list(range(distance - 1, subs, 2 * distance))
            eliminate_planes(grid_ref, planes, modes, order, part, 3 * part)
            for plane in planes:
                update_partners(grid_ref, plane, distance, part, order, plane >= distance)
        else:

            def one_plane(index, carry, distance=distance):
                plane = distance - 1 + 2 * distance * index
                eliminate_planes(grid_ref, [plane], modes, order, part, 3 * part)
                update_partners(grid_ref, plane, distance, part, order, index > 0)
                return carry

            lax.fori_loop(0, subs // (2 * distance), one_plane, 0)
        distance *= 2
    eliminate_planes(grid_ref, [subs - 1], modes, order, part, part)

    sub_here, lay_here = place_ref[0], place_ref[1]
    strip = pl.ds(pl.multiple_of(lay_here * modes, ROWS), modes)
    for k, out_ref in enumerate((diag_ref, left_ref, right_ref)):
        turned_ref[k] = grid_ref[sub_here, :, k * part : (k + 1) * part].T
        found = turned_ref[k, strip, :]
        out_ref[...] = found if k == 0 else jnp.where(sub_here < subs - 1, found, 0.0)


def factor_planes(place, plane_tiles):
    subs, layers, modes, _ = plane_tiles.shape
    order = layers * modes
    part = -(-order // LANES) * LANES
    strip = jax.ShapeDtypeStruct((modes, order), jnp.float32)
    vmem = pl.BlockSpec(memory_space=pltpu.VMEM)
    return pl.pallas_call(
        factor_kernel,
        out_shape=(strip, strip, strip),
        in_specs=[pl.BlockSpec(memory_space=pltpu.SMEM), vmem],
        out_specs=(vmem, vmem, vmem),
        scratch_shapes=[
            pltpu.VMEM((subs, order, 3 * part), jnp.float32),
            pltpu.VMEM((3, part, order), jnp.float32),
        ],
        compiler_params=pltpu.CompilerParams(vmem_limit_bytes=56 * 1024 * 1024),
        name="factor_planes",
    )(place, plane_tiles)


def per_device(eigen_vectors, row_mass, inner_weight, face_weight, margin_rows):
    vectors = eigen_vectors[0, 0]
    row_lists = margin_rows[0, 0]
    face_springs = face_weight[0, 0]
    mode_count = vectors.shape[0]
    subs = lax.axis_size("sub")
    layers = lax.axis_size("layer")
    sub_here = lax.axis_index("sub")
    lay_here = lax.axis_index("layer")
    picked = jnp.stack([jnp.take(vectors, row_lists[k], axis=1) for k in range(4)])
    zero_row = jnp.zeros((1, row_lists.shape[-1]), jnp.float32)
    sub_send = jnp.stack(
        [
            jnp.concatenate([picked[1], zero_row], 0),
            jnp.concatenate([picked[0], face_springs[0:1]], 0),
        ]
    )
    sub_rim = padded(sub_send, (("sub", 0),), 1)
    lay_send = jnp.stack(
        [
            jnp.concatenate([picked[3], zero_row], 0),
            jnp.concatenate([picked[2], face_springs[1:2]], 0),
        ]
    )
    lay_rim = padded(lay_send, (("layer", 0),), 1)
    partners = jnp.stack(
        [
            sub_rim[3, :mode_count],
            sub_rim[0, :mode_count],
            lay_rim[3, :mode_count],
            lay_rim[0, :mode_count],
        ]
    )
    springs = jnp.stack(
        [
            jnp.where(sub_here < subs - 1, face_springs[0], 0.0),
            sub_rim[0, mode_count],
            jnp.where(lay_here < layers - 1, face_springs[1], 0.0),
            lay_rim[0, mode_count],
        ]
    )
    applied, tiles = device_terms(
        vectors, row_mass[0, 0], inner_weight[0, 0], row_lists, picked, springs, partners
    )
    all_tiles = lax.all_gather(tiles, ("sub", "layer"), axis=0, tiled=False)
    all_tiles = all_tiles.reshape(subs, layers, *tiles.shape)
    place = jnp.stack([sub_here, lay_here]).astype(jnp.int32)
    diag_strip, left_strip, right_strip = factor_planes(place, all_tiles)
    return (applied[None, None], diag_strip[None], left_strip[None], right_strip[None])


def solution(mesh):
    in_specs = (
        P("sub", "layer", None, None),
        P("sub", "layer", None),
        P("sub", "layer", None, None),
        P("sub", "layer", None, None),
        P("sub", "layer", None, None),
    )
    out_specs = (
        P("sub", "layer", None, None),
        P("sub", "layer", None),
        P("sub", "layer", None),
        P("sub", "layer", None),
    )
    return jax.shard_map(
        per_device, mesh=mesh, in_specs=in_specs, out_specs=out_specs, check_vma=False
    )
```

time: 135 us -> 121 us (0.90)
  the two profiles are of different devices: /device:TPU:25 before, /device:TPU:0 now
where the time goes in v1:
time: 121 us
  blocking collectives  77.8 us (64%)
  Pallas kernels  17.8 us (15%)
  starting transfers between devices  9.16 us (8%)
  local copies, waits for them, and re-layouts  6.85 us (6%)
  matrix products  6.69 us (6%)
  other arithmetic  1.31 us (1%)
    all_gather x1, blocking collectives, per_device(): all_tiles = lax.all_gather(tiles, ('sub', 'layer'), axis=0, tiled=False)  77.8 us
    pallas_call x1, Pallas kernels, factor_planes(): pl.pallas_call(factor_kernel, out_shape=(strip, strip, strip), in_specs=[...  17.8 us
    ppermute x2, starting transfers between devices, padded(): lax.ppermute(tail, axis, [(i, (i + 1) % count) for i in range(ends)])  6.59 us
    dot_general x4, matrix products, device_terms(): jnp.dot(springs[k] * (picked[k] - partners[k]), onehot, precision=HIGHEST)  4.2 us
    gather x4, local copies, waits for them, and re-layouts, per_device(): jnp.take(vectors, row_lists[k], axis=1)  2.58 us
    ppermute x2, starting transfers between devices, padded(): lax.ppermute(head, axis, [((i + 1) % count, i) for i in range(ends)])  2.57 us
  transfers between devices with their start and end apart: 4, of which 0 were waited for; matrix products, arithmetic and copies ran while one was open for 8% of the time, Pallas kernels for 15%

profile of v1, /device:TPU:0, one launch (start us, length us, event | category | flops | bytes accessed | tf_op | source)
XLA Modules:
  0.0 120.7 jit_solution(14048318365344625029)
XLA Ops:
  0.7 1.7 %copy.62 = f32[24,4096]{0,1:T(8,128)S(1)} copy(f32[24,4096]{1,0:T(8,128)} %bitcast.123) | data formatting | bytes 786432 | tf_op jit(solution)/shard_map/squeeze | solution.py:285
  2.4 0.1 copy.64
  2.5 0.6 gather_fusion
  3.2 0.1 select_bitcast_fusion.3
  3.3 0.1 maximum_bitcast_fusion
  3.3 2.4 %collective-permute-start.1 = (f32[1,25,128]{1,2,0:T(8,128)S(1)}, f32[1,25,128]{1,2,0:T(8,128)S(1)}, u32[]{:S(2)}, u32[]{:S(2)}) collective-permute-start(f32[1,25,128]{1,2,0:T(8,128)S(1)} %maximum_bitcast_fusion), channel_id=1, source_target_pairs={{0,4},{4,8},{8,12},{12,16},{16,20},{20,24},{24,28},{1,5},{5,9},{9,... | collective-permute-start | bytes 38408 | tf_op jit(solution)/shard_map/ppermute | solution.py:24
  5.7 0.6 gather_fusion.2
  6.4 0.1 copy.67
  6.5 0.1 select_bitcast_fusion.1
  6.6 0.1 maximum_bitcast_fusion.1
  6.7 4.2 %collective-permute-start.3 = (f32[1,25,128]{1,2,0:T(8,128)S(1)}, f32[1,25,128]{1,2,0:T(8,128)S(1)}, u32[]{:S(2)}, u32[]{:S(2)}) collective-permute-start(f32[1,25,128]{1,2,0:T(8,128)S(1)} %maximum_bitcast_fusion.1), channel_id=1, source_target_pairs={{0,1},{1,2},{2,3},{4,5},{5,6},{6,7},{8,9},{9,10},{10,11},{12,13},{... | collective-permute-start | bytes 38408 | tf_op jit(solution)/shard_map/ppermute | solution.py:24
  10.9 0.6 gather_fusion.1
  11.6 0.1 select_bitcast_fusion.2
  11.7 0.6 pad_bitcast_fusion.1
  12.3 1.3 %collective-permute-start = (f32[1,25,128]{1,2,0:T(8,128)}, f32[1,25,128]{1,2,0:T(8,128)S(1)}, u32[]{:S(2)}, u32[]{:S(2)}) collective-permute-start(f32[1,25,128]{1,2,0:T(8,128)} %pad_bitcast_fusion.1), channel_id=1, source_target_pairs={{4,0},{8,4},{12,8},{16,12},{20,16},{24,20},{28,24},{5,1},{9,5},{13... | collective-permute-start | bytes 38408 | tf_op jit(solution)/shard_map/ppermute | solution.py:26
  13.6 0.6 gather_fusion.3
  14.2 0.1 select_bitcast_fusion
  14.4 1.3 %collective-permute-start.2 = (f32[1,25,128]{1,2,0:T(8,128)S(1)}, f32[1,25,128]{1,2,0:T(8,128)S(1)}, u32[]{:S(2)}, u32[]{:S(2)}) collective-permute-start(f32[1,25,128]{1,2,0:T(8,128)S(1)} %pad_bitcast_fusion), channel_id=1, source_target_pairs={{1,0},{2,1},{3,2},{5,4},{6,5},{7,6},{9,8},{10,9},{11,10},{13,12},{... | collective-permute-start | bytes 38408 | tf_op jit(solution)/shard_map/ppermute | solution.py:26
  15.7 0.2 slice_bitcast_fusion.21
  15.8 0.2 slice_bitcast_fusion.23
  16.0 0.2 slice_bitcast_fusion.25
  16.3 0.1 fusion.8
  16.4 0.1 slice_bitcast_fusion.20
  16.5 0.1 slice_bitcast_fusion.14
  16.5 0.1 slice_bitcast_fusion.22
  16.6 0.1 slice_bitcast_fusion.16
  16.7 0.1 slice_bitcast_fusion.24
  16.7 0.1 slice_bitcast_fusion.18
  16.8 0.3 copy-done.1
  17.1 0.8 convolution_bitcast_fusion
  17.9 0.3 convolution_add_fusion.7
  18.2 0.6 pad_add_fusion.place_ref
  18.8 0.2 slice_reduce_fusion.1
  18.9 0.3 convolution_add_fusion.6
  19.2 0.3 convolution_add_fusion.5
  19.5 0.3 fusion.1
  19.8 0.1 copy.78
  19.9 0.2 slice_reduce_fusion
  20.1 0.3 fusion.3
  20.4 0.3 fusion.2
  20.7 0.1 copy.77
  20.8 0.1 select_maximum_fusion
  20.9 0.9 convolution_add_fusion.3
  21.8 0.8 convolution_add_fusion.2
  22.7 77.8 %all-gather = f32[768,128]{1,0:T(8,128)} all-gather(f32[24,128]{1,0:T(8,128)S(1)} %select_maximum_fusion), channel_id=2, replica_groups=mesh['sub'=8,'layer'=4] {'sub','layer'}, dimensions={0}, use_global_device_ids=true | all-gather | bytes 405504 | tf_op jit(solution)/shard_map/all_gather | solution.py:328
  100.5 17.8 %factor_planes.1 = (f32[24,96]{1,0:T(8,128)}, f32[24,96]{1,0:T(8,128)}, f32[24,96]{1,0:T(8,128)}) custom-call(s32[2]{0:T(128)} %pad_add_fusion.place_ref, f32[8,4,24,128]{3,2,1,0:T(8,128)} %bitcast.130), custom_call_target="tpu_custom_call" | custom-call | tf_op jit(solution)/shard_map/factor_planes/pallas_call | solution.py:270
  118.2 0.8 convolution_add_fusion.1
  119.1 1.6 %fusion = f32[1,1,24,4096]{3,2,1,0:T(8,128)} fusion(f32[24,4096]{1,0:T(8,128)S(1)} %convolution_add_fusion.1, s32[128]{0:T(128)S(1)} %get-tuple-element.49, f32[24,128]{0,1:T(8,128)S(1)} %select_bitcast_fusion, f32[1,25,128]{1,2,0:T(8,128)S(1)} %collective-permute-done.3, f32[128]{0:T(128)S(1)} %slice_reduce_fusion), kind=kOutput, calls=%fused_computation.5 | convolution fusion | flops 151623680 | bytes 812544 | tf_op jit(solution)/shard_map/dot_general | solution.py:48
  (27 shorter events, 0.1 us)
Async XLA Ops:
  0.6 1.7 %copy-start.3 = (s32[1,1,4,128]{3,2,1,0:T(4,128)S(1)}, s32[1,1,4,128]{3,2,1,0:T(4,128)}, u32[]{:S(2)}) copy-start(s32[1,1,4,128]{3,2,1,0:T(4,128)} %param.11) | copy-start | bytes 6148
  0.6 1.7 %copy-start.4 = (f32[1,1,2,128]{3,2,1,0:T(2,128)S(1)}, f32[1,1,2,128]{3,2,1,0:T(2,128)}, u32[]{:S(2)}) copy-start(f32[1,1,2,128]{3,2,1,0:T(2,128)} %param.10) | copy-start | bytes 3076
  0.7 15.0 %copy-start = (f32[1,1,24,4096]{3,2,1,0:T(8,128)S(1)}, f32[1,1,24,4096]{3,2,1,0:T(8,128)}, u32[]{:S(2)}) copy-start(f32[1,1,24,4096]{3,2,1,0:T(8,128)} %param.7) | copy-start | bytes 1179652
  3.3 15.4 %collective-permute-start.1 = (f32[1,25,128]{1,2,0:T(8,128)S(1)}, f32[1,25,128]{1,2,0:T(8,128)S(1)}, u32[]{:S(2)}, u32[]{:S(2)}) collective-permute-start(f32[1,25,128]{1,2,0:T(8,128)S(1)} %maximum_bitcast_fusion), channel_id=1, source_target_pairs={{0,4},{4,8},{8,12},{12,16},{16,20},{20,24},{24,28},{1,5},{5,9},{9,... | collective-permute-start | bytes 38408 | tf_op jit(solution)/shard_map/ppermute | solution.py:24
  6.7 13.2 %collective-permute-start.3 = (f32[1,25,128]{1,2,0:T(8,128)S(1)}, f32[1,25,128]{1,2,0:T(8,128)S(1)}, u32[]{:S(2)}, u32[]{:S(2)}) collective-permute-start(f32[1,25,128]{1,2,0:T(8,128)S(1)} %maximum_bitcast_fusion.1), channel_id=1, source_target_pairs={{0,1},{1,2},{2,3},{4,5},{5,6},{6,7},{8,9},{9,10},{10,11},{12,13},{... | collective-permute-start | bytes 38408 | tf_op jit(solution)/shard_map/ppermute | solution.py:24
  11.7 4.6 %copy-start.2 = (f32[1,1,3,4096]{3,1,2,0:T(1,128)S(1)}, f32[1,1,3,4096]{3,1,2,0:T(1,128)}, u32[]{:S(2)}) copy-start(f32[1,1,3,4096]{3,1,2,0:T(1,128)} %param.9) | copy-start | bytes 147460
  12.3 8.6 %collective-permute-start = (f32[1,25,128]{1,2,0:T(8,128)}, f32[1,25,128]{1,2,0:T(8,128)S(1)}, u32[]{:S(2)}, u32[]{:S(2)}) collective-permute-start(f32[1,25,128]{1,2,0:T(8,128)} %pad_bitcast_fusion.1), channel_id=1, source_target_pairs={{4,0},{8,4},{12,8},{16,12},{20,16},{24,20},{28,24},{5,1},{9,5},{13... | collective-permute-start | bytes 38408 | tf_op jit(solution)/shard_map/ppermute | solution.py:26
  14.4 103.9 %collective-permute-start.2 = (f32[1,25,128]{1,2,0:T(8,128)S(1)}, f32[1,25,128]{1,2,0:T(8,128)S(1)}, u32[]{:S(2)}, u32[]{:S(2)}) collective-permute-start(f32[1,25,128]{1,2,0:T(8,128)S(1)} %pad_bitcast_fusion), channel_id=1, source_target_pairs={{1,0},{2,1},{3,2},{5,4},{6,5},{7,6},{9,8},{10,9},{11,10},{13,12},{... | collective-permute-start | bytes 38408 | tf_op jit(solution)/shard_map/ppermute | solution.py:26
  16.4 0.7 copy-start.1

commit v2 on v1

--- a/solution.py
+++ b/solution.py
@@ -325,7 +325,8 @@
     applied, tiles = device_terms(
         vectors, row_mass[0, 0], inner_weight[0, 0], row_lists, picked, springs, partners
     )
-    all_tiles = lax.all_gather(tiles, ("sub", "layer"), axis=0, tiled=False)
+    copies = jnp.broadcast_to(tiles[None], (subs * layers,) + tiles.shape)
+    all_tiles = lax.all_to_all(copies, ("sub", "layer"), split_axis=0, concat_axis=0, tiled=True)
     all_tiles = all_tiles.reshape(subs, layers, *tiles.shape)
     place = jnp.stack([sub_here, lay_here]).astype(jnp.int32)
     diag_strip, left_strip, right_strip = factor_planes(place, all_tiles)

time: 121 us -> 67.1 us (0.55)
  blocking collectives: 77.8 us -> 0 us
  starting transfers between devices: 9.16 us -> 19.2 us
  waiting for transfers between devices: 0.02 us -> 7.43 us
  local copies, waits for them, and re-layouts: 6.85 us -> 11.4 us
  matrix products: 6.69 us -> 8.32 us
    all_gather x1 -> x0, blocking collectives: 77.8 us -> none  [per_device(): all_tiles = lax.all_gather(tiles, ('sub', 'layer'), axis=0, tiled=False)]
    all_to_all x0 -> x1, starting transfers between devices: none -> 10.1 us  [per_device(): lax.all_to_all(copies, ('sub', 'layer'), split_axis=0, concat_axis=0, til...]
    all_to_all x0 -> x1, waiting for transfers between devices: none -> 7.42 us  [per_device(): lax.all_to_all(copies, ('sub', 'layer'), split_axis=0, concat_axis=0, til...]
    concatenate x6, local copies, waits for them, and re-layouts: 0.38 us -> 2.18 us  [device_terms(): laplace = laplace + fluxes - jnp.roll(fluxes, t, axis=1)]
    dot_general x4, matrix products: 4.2 us -> 5.88 us  [device_terms(): jnp.dot(springs[k] * (picked[k] - partners[k]), onehot, precision=HIGHEST)]
  transfers between devices with their start and end apart: 4 -> 5, of which waited for: 0 -> 1; matrix products, arithmetic and copies ran while one was open for 8% -> 26% of each run, Pallas kernels for 15% -> 0%
where the time goes in v2:
time: 67.1 us; the launch traced here: 66.8 us
  starting transfers between devices  19.2 us (29%)
  Pallas kernels  17.8 us (27%)
  local copies, waits for them, and re-layouts  11.4 us (17%)
  matrix products  8.32 us (12%)
  waiting for transfers between devices  7.43 us (11%)
  other arithmetic  1.36 us (2%)
  between operations  1.25 us (2%)
    pallas_call x1, Pallas kernels, factor_planes(): pl.pallas_call(factor_kernel, out_shape=(strip, strip, strip), in_specs=[...  17.8 us
    all_to_all x1, starting transfers between devices, per_device(): lax.all_to_all(copies, ('sub', 'layer'), split_axis=0, concat_axis=0, til...  10.1 us
    all_to_all x1, waiting for transfers between devices, per_device(): lax.all_to_all(copies, ('sub', 'layer'), split_axis=0, concat_axis=0, til...  7.42 us
    ppermute x2, starting transfers between devices, padded(): lax.ppermute(tail, axis, [(i, (i + 1) % count) for i in range(ends)])  6.59 us
    dot_general x4, matrix products, device_terms(): jnp.dot(springs[k] * (picked[k] - partners[k]), onehot, precision=HIGHEST)  5.88 us
    gather x4, local copies, waits for them, and re-layouts, per_device(): jnp.take(vectors, row_lists[k], axis=1)  2.58 us
    ppermute x2, starting transfers between devices, padded(): lax.ppermute(head, axis, [((i + 1) % count, i) for i in range(ends)])  2.56 us
    concatenate x6, local copies, waits for them, and re-layouts, device_terms(): laplace = laplace + fluxes - jnp.roll(fluxes, t, axis=1)  2.18 us
  transfers between devices with their start and end apart: 5, of which 1 were waited for; matrix products, arithmetic and copies ran while one was open for 26% of the time, Pallas kernels for 0%

profile of v2, /device:TPU:0, one launch (start us, length us, event | category | flops | bytes accessed | tf_op | source)
XLA Modules:
  0.0 66.8 jit_solution(15924922111064100878)
XLA Ops:
  0.7 1.7 %copy.62 = f32[24,4096]{0,1:T(8,128)S(1)} copy(f32[24,4096]{1,0:T(8,128)} %bitcast.123) | data formatting | bytes 786432 | tf_op jit(solution)/shard_map/squeeze | solution.py:285
  2.4 0.1 copy.64
  2.5 0.6 gather_fusion
  3.2 0.1 select_bitcast_fusion.3
  3.3 0.1 maximum_bitcast_fusion
  3.4 2.4 %collective-permute-start.1 = (f32[1,25,128]{1,2,0:T(8,128)S(1)}, f32[1,25,128]{1,2,0:T(8,128)S(1)}, u32[]{:S(2)}, u32[]{:S(2)}) collective-permute-start(f32[1,25,128]{1,2,0:T(8,128)S(1)} %maximum_bitcast_fusion), channel_id=1, source_target_pairs={{0,4},{4,8},{8,12},{12,16},{16,20},{20,24},{24,28},{1,5},{5,9},{9,... | collective-permute-start | bytes 38408 | tf_op jit(solution)/shard_map/ppermute | solution.py:24
  5.7 0.6 gather_fusion.2
  6.4 0.1 copy.67
  6.6 0.1 maximum_bitcast_fusion.1
  6.7 4.2 %collective-permute-start.3 = (f32[1,25,128]{1,2,0:T(8,128)S(1)}, f32[1,25,128]{1,2,0:T(8,128)S(1)}, u32[]{:S(2)}, u32[]{:S(2)}) collective-permute-start(f32[1,25,128]{1,2,0:T(8,128)S(1)} %maximum_bitcast_fusion.1), channel_id=1, source_target_pairs={{0,1},{1,2},{2,3},{4,5},{5,6},{6,7},{8,9},{9,10},{10,11},{12,13},{... | collective-permute-start | bytes 38408 | tf_op jit(solution)/shard_map/ppermute | solution.py:24
  10.9 0.6 gather_fusion.1
  11.6 0.1 select_bitcast_fusion.2
  11.7 0.6 pad_bitcast_fusion.1
  12.3 1.3 %collective-permute-start = (f32[1,25,128]{1,2,0:T(8,128)}, f32[1,25,128]{1,2,0:T(8,128)}, u32[]{:S(2)}, u32[]{:S(2)}) collective-permute-start(f32[1,25,128]{1,2,0:T(8,128)} %pad_bitcast_fusion.1), channel_id=1, source_target_pairs={{4,0},{8,4},{12,8},{16,12},{20,16},{24,20},{28,24},{5,1},{9,5},{13... | collective-permute-start | bytes 38408 | tf_op jit(solution)/shard_map/ppermute | solution.py:26
  13.6 0.6 gather_fusion.3
  14.3 0.1 select_bitcast_fusion
  14.4 0.6 pad_bitcast_fusion
  15.0 1.3 %collective-permute-start.2 = (f32[1,25,128]{1,2,0:T(8,128)}, f32[1,25,128]{1,2,0:T(8,128)}, u32[]{:S(2)}, u32[]{:S(2)}) collective-permute-start(f32[1,25,128]{1,2,0:T(8,128)} %pad_bitcast_fusion), channel_id=1, source_target_pairs={{1,0},{2,1},{3,2},{5,4},{6,5},{7,6},{9,8},{10,9},{11,10},{13,12},{... | collective-permute-start | bytes 38408 | tf_op jit(solution)/shard_map/ppermute | solution.py:26
  16.3 0.2 slice_bitcast_fusion.21
  16.5 0.2 slice_bitcast_fusion.23
  16.6 0.2 slice_bitcast_fusion.25
  16.9 0.1 fusion.8
  17.1 0.7 %slice_bitcast_fusion.14 = (f32[1,1,24,27]{3,2,1,0:T(8,128)S(1)}, f32[24,27]{1,0:T(8,128)}) fusion(f32[24,4096]{1,0:T(8,128)S(1)} %get-tuple-element.45), kind=kLoop, calls=%fused_computation.145 | loop fusion | bytes 7776 | tf_op jit(solution)/shard_map/jit(_roll_static)/concatenate | solution.py:40
  17.8 0.7 %slice_bitcast_fusion.16 = (f32[1,1,24,3]{3,2,1,0:T(8,128)S(1)}, f32[24,3]{1,0:T(8,128)}) fusion(f32[24,4096]{1,0:T(8,128)S(1)} %get-tuple-element.44), kind=kLoop, calls=%fused_computation.147 | loop fusion | bytes 864 | tf_op jit(solution)/shard_map/jit(_roll_static)/concatenate | solution.py:40
  18.5 0.7 %slice_bitcast_fusion.18 = (f32[1,1,24,1]{3,2,1,0:T(8,128)S(1)}, f32[24,1]{1,0:T(8,128)}) fusion(f32[24,4096]{1,0:T(8,128)S(1)} %get-tuple-element.43), kind=kLoop, calls=%fused_computation.149 | loop fusion | bytes 288 | tf_op jit(solution)/shard_map/jit(_roll_static)/concatenate | solution.py:40
  19.2 0.6 slice_bitcast_fusion.8
  19.8 0.8 %convolution_bitcast_fusion = f32[24,24]{1,0:T(8,128)S(1)} fusion(f32[1,1,24,4096]{3,2,1,0:T(8,128)S(1)} %copy-done, f32[1,1,24,1]{3,2,1,0:T(8,128)S(1)} %get-tuple-element.41, f32[1,1,24,4095]{3,2,1,0:T(8,128)S(1)} %get-tuple-element.39, f32[1,1,24,4095]{3,2,1,0:T(8,128)S(1)} %get-tuple-element.37, f32[1,1,24,1]{3,2,1,0:T(8,128)S(1)} %get-tuple-element.35, ...), kind=kOutput, calls=%fused_computation.22 | convolution fusion | flops 30179328 | bytes 2820352 | tf_op jit(solution)/shard_map/dot_general | solution.py:43
  20.6 0.3 convolution_add_fusion.7
  20.9 0.6 pad_add_fusion.place_ref
  21.5 0.2 slice_reduce_fusion.1
  21.7 0.3 convolution_add_fusion.6
  22.0 0.3 convolution_add_fusion.5
  22.3 0.3 fusion.1
  22.7 0.2 slice_reduce_fusion
  22.9 0.3 fusion.3
  23.2 0.3 copy-done.4
  23.5 0.3 fusion.2
  23.8 0.1 copy.77
  23.9 0.1 select_maximum_fusion
  23.9 0.8 %broadcast_in_dim.49 = f32[32,24,128]{2,1,0:T(8,128)} broadcast(f32[24,128]{1,0:T(8,128)S(1)} %select_maximum_fusion), dimensions={1,2} | broadcast | bytes 405504 | tf_op jit(solution)/shard_map/broadcast_in_dim | solution.py:328
  24.7 10.1 %all-to-all-start = ((f32[32,24,128]{2,1,0:T(8,128)}), f32[32,24,128]{2,1,0:T(8,128)S(1)}, u32[]{:S(2)}, u32[]{:S(2)}) async-start(f32[32,24,128]{2,1,0:T(8,128)} %broadcast_in_dim.49), calls=%async_computation | async-start | bytes 786432 | tf_op jit(solution)/shard_map/all_to_all | solution.py:329
  34.9 1.8 %convolution_add_fusion.3 = f32[24,4096]{1,0:T(8,128)S(1)} fusion(s32[128]{0:T(128)} %get-tuple-element.51, f32[24,4096]{1,0:T(8,128)S(1)} %get-tuple-element.45, f32[24,4096]{1,0:T(8,128)S(1)} %get-tuple-element.44, f32[24,4096]{1,0:T(8,128)S(1)} %get-tuple-element.43, f32[24,4095]{1,0:T(8,128)S(1)} %get-tuple-element.38, f32[24,1]{1,0:T(8,128)} %get-tuple-element.36, ...), kind=kOutput, calls=%fused_computation.8 | convolution fusion | flops 152606720 | bytes 3188224 | tf_op jit(solution)/shard_map/dot_general | solution.py:48
  36.6 0.8 %convolution_add_fusion.2 = f32[24,4096]{1,0:T(8,128)S(1)} fusion(f32[24,4096]{1,0:T(8,128)S(1)} %convolution_add_fusion.3, s32[128]{0:T(128)S(1)} %copy-done.14, f32[24,128]{0,1:T(8,128)S(1)} %select_bitcast_fusion.2, f32[1,25,128]{1,2,0:T(8,128)S(1)} %collective-permute-done.1, f32[128]{0:T(128)S(1)} %copy-done.7), kind=kOutput, calls=%fused_computation.7 | convolution fusion | flops 151623680 | bytes 812544 | tf_op jit(solution)/shard_map/dot_general | solution.py:48
  37.5 1.7 %convolution_add_fusion.1 = f32[24,4096]{1,0:T(8,128)S(1)} fusion(f32[24,4096]{1,0:T(8,128)S(1)} %convolution_add_fusion.2, s32[128]{0:T(128)S(1)} %copy-done.13, f32[24,128]{0,1:T(8,128)S(1)} %select_bitcast_fusion.1, f32[1,25,128]{1,2,0:T(8,128)} %collective-permute-done.2, f32[128]{0:T(128)S(1)} %copy-done.10), kind=kOutput, calls=%fused_computation.6 | convolution fusion | flops 151623680 | bytes 812544 | tf_op jit(solution)/shard_map/dot_general | solution.py:48
  39.2 1.6 %fusion = f32[1,1,24,4096]{3,2,1,0:T(8,128)} fusion(f32[24,4096]{1,0:T(8,128)S(1)} %convolution_add_fusion.1, s32[128]{0:T(128)S(1)} %copy-done.12, f32[24,128]{0,1:T(8,128)S(1)} %select_bitcast_fusion, f32[1,25,128]{1,2,0:T(8,128)S(1)} %collective-permute-done.3, f32[128]{0:T(128)S(1)} %copy-done.5), kind=kOutput, calls=%fused_computation.5 | convolution fusion | flops 151623680 | bytes 812544 | tf_op jit(solution)/shard_map/dot_general | solution.py:48
  40.8 7.4 %all-to-all-done = f32[32,24,128]{2,1,0:T(8,128)S(1)} async-done(((f32[32,24,128]{2,1,0:T(8,128)}), f32[32,24,128]{2,1,0:T(8,128)S(1)}, u32[]{:S(2)}, u32[]{:S(2)}) %all-to-all-start) | async-done | bytes 393248 | tf_op jit(solution)/shard_map/all_to_all | solution.py:329
  48.2 0.7 %copy-done.1 = f32[32,24,128]{2,1,0:T(8,128)} copy-done((f32[32,24,128]{2,1,0:T(8,128)}, f32[32,24,128]{2,1,0:T(8,128)S(1)}, u32[]{:S(2)}) %copy-start.1) | copy-done | bytes 393240
  49.0 17.8 %factor_planes.1 = (f32[24,96]{1,0:T(8,128)}, f32[24,96]{1,0:T(8,128)}, f32[24,96]{1,0:T(8,128)}) custom-call(s32[2]{0:T(128)} %pad_add_fusion.place_ref, f32[8,4,24,128]{3,2,1,0:T(8,128)} %bitcast.130), custom_call_target="tpu_custom_call" | custom-call | tf_op jit(solution)/shard_map/factor_planes/pallas_call | solution.py:270
  (51 shorter events, 0.5 us)
Async XLA Ops:
  0.6 1.7 %copy-start.8 = (s32[1,1,4,128]{3,2,1,0:T(4,128)S(1)}, s32[1,1,4,128]{3,2,1,0:T(4,128)}, u32[]{:S(2)}) copy-start(s32[1,1,4,128]{3,2,1,0:T(4,128)} %param.11) | copy-start | bytes 6148
  0.6 1.7 %copy-start.15 = (f32[1,1,2,128]{3,2,1,0:T(2,128)S(1)}, f32[1,1,2,128]{3,2,1,0:T(2,128)}, u32[]{:S(2)}) copy-start(f32[1,1,2,128]{3,2,1,0:T(2,128)} %param.10) | copy-start | bytes 3076
  0.7 15.6 %copy-start = (f32[1,1,24,4096]{3,2,1,0:T(8,128)S(1)}, f32[1,1,24,4096]{3,2,1,0:T(8,128)}, u32[]{:S(2)}) copy-start(f32[1,1,24,4096]{3,2,1,0:T(8,128)} %param.7) | copy-start | bytes 1179652
  2.4 18.2 %copy-start.11 = (f32[128]{0:T(128)}, f32[128]{0:T(128)S(1)}, u32[]{:S(2)}) copy-start(f32[128]{0:T(128)S(1)} %get-tuple-element.62) | copy-start | bytes 1540
  2.4 19.6 %copy-start.9 = (f32[128]{0:T(128)}, f32[128]{0:T(128)S(1)}, u32[]{:S(2)}) copy-start(f32[128]{0:T(128)S(1)} %get-tuple-element.61) | copy-start | bytes 1540
  3.4 18.2 %collective-permute-start.1 = (f32[1,25,128]{1,2,0:T(8,128)S(1)}, f32[1,25,128]{1,2,0:T(8,128)S(1)}, u32[]{:S(2)}, u32[]{:S(2)}) collective-permute-start(f32[1,25,128]{1,2,0:T(8,128)S(1)} %maximum_bitcast_fusion), channel_id=1, source_target_pairs={{0,4},{4,8},{8,12},{12,16},{16,20},{20,24},{24,28},{1,5},{5,9},{9,... | collective-permute-start | bytes 38408 | tf_op jit(solution)/shard_map/ppermute | solution.py:24
  6.7 16.0 %collective-permute-start.3 = (f32[1,25,128]{1,2,0:T(8,128)S(1)}, f32[1,25,128]{1,2,0:T(8,128)S(1)}, u32[]{:S(2)}, u32[]{:S(2)}) collective-permute-start(f32[1,25,128]{1,2,0:T(8,128)S(1)} %maximum_bitcast_fusion.1), channel_id=1, source_target_pairs={{0,1},{1,2},{2,3},{4,5},{5,6},{6,7},{8,9},{9,10},{10,11},{12,13},{... | collective-permute-start | bytes 38408 | tf_op jit(solution)/shard_map/ppermute | solution.py:24
  11.7 5.2 %copy-start.3 = (f32[1,1,3,4096]{3,1,2,0:T(1,128)S(1)}, f32[1,1,3,4096]{3,1,2,0:T(1,128)}, u32[]{:S(2)}) copy-start(f32[1,1,3,4096]{3,1,2,0:T(1,128)} %param.9) | copy-start | bytes 147460
  12.3 22.5 %collective-permute-start = (f32[1,25,128]{1,2,0:T(8,128)}, f32[1,25,128]{1,2,0:T(8,128)}, u32[]{:S(2)}, u32[]{:S(2)}) collective-permute-start(f32[1,25,128]{1,2,0:T(8,128)} %pad_bitcast_fusion.1), channel_id=1, source_target_pairs={{4,0},{8,4},{12,8},{16,12},{20,16},{24,20},{28,24},{5,1},{9,5},{13... | collective-permute-start | bytes 38408 | tf_op jit(solution)/shard_map/ppermute | solution.py:26
  15.0 22.5 %collective-permute-start.2 = (f32[1,25,128]{1,2,0:T(8,128)}, f32[1,25,128]{1,2,0:T(8,128)}, u32[]{:S(2)}, u32[]{:S(2)}) collective-permute-start(f32[1,25,128]{1,2,0:T(8,128)} %pad_bitcast_fusion), channel_id=1, source_target_pairs={{1,0},{2,1},{3,2},{5,4},{6,5},{7,6},{9,8},{10,9},{11,10},{13,12},{... | collective-permute-start | bytes 38408 | tf_op jit(solution)/shard_map/ppermute | solution.py:26
  17.0 2.8 %copy-start.2 = (f32[1,1,4096]{2,1,0:T(1,128)S(1)}, f32[1,1,4096]{2,1,0:T(1,128)}, u32[]{:S(2)}) copy-start(f32[1,1,4096]{2,1,0:T(1,128)} %param.8) | copy-start | bytes 49156
  21.7 0.6 copy-start.6
  22.9 0.6 copy-start.4
  24.7 23.5 %all-to-all-start = ((f32[32,24,128]{2,1,0:T(8,128)}), f32[32,24,128]{2,1,0:T(8,128)S(1)}, u32[]{:S(2)}, u32[]{:S(2)}) async-start(f32[32,24,128]{2,1,0:T(8,128)} %broadcast_in_dim.49), calls=%async_computation | async-start | bytes 786432 | tf_op jit(solution)/shard_map/all_to_all | solution.py:329
  34.8 1.8 %copy-start.7 = (f32[128]{0:T(128)S(1)}, f32[128]{0:T(128)}, u32[]{:S(2)}) copy-start(f32[128]{0:T(128)} %copy-done.6) | copy-start | bytes 1540
  34.8 1.8 %copy-start.14 = (s32[128]{0:T(128)S(1)}, s32[128]{0:T(128)}, u32[]{:S(2)}) copy-start(s32[128]{0:T(128)} %get-tuple-element.50) | copy-start | bytes 1540
  34.8 2.7 %copy-start.10 = (f32[128]{0:T(128)S(1)}, f32[128]{0:T(128)}, u32[]{:S(2)}) copy-start(f32[128]{0:T(128)} %copy-done.9) | copy-start | bytes 1540
  34.8 2.7 %copy-start.13 = (s32[128]{0:T(128)S(1)}, s32[128]{0:T(128)}, u32[]{:S(2)}) copy-start(s32[128]{0:T(128)} %get-tuple-element.52) | copy-start | bytes 1540
  34.8 4.4 %copy-start.5 = (f32[128]{0:T(128)S(1)}, f32[128]{0:T(128)}, u32[]{:S(2)}) copy-start(f32[128]{0:T(128)} %copy-done.4) | copy-start | bytes 1540
  34.9 4.4 %copy-start.12 = (s32[128]{0:T(128)S(1)}, s32[128]{0:T(128)}, u32[]{:S(2)}) copy-start(s32[128]{0:T(128)} %get-tuple-element.49) | copy-start | bytes 1540
  48.2 0.7 %copy-start.1 = (f32[32,24,128]{2,1,0:T(8,128)}, f32[32,24,128]{2,1,0:T(8,128)S(1)}, u32[]{:S(2)}) copy-start(f32[32,24,128]{2,1,0:T(8,128)S(1)} %all-to-all-done) | copy-start | bytes 1179652

commit v3 on v1

--- a/solution.py
+++ b/solution.py
@@ -11,49 +11,6 @@
 LANES = 128
 ROWS = 8
 UNROLLED_LAYERS = 4
-
-
-def padded(cells, sides, width):
-    for axis, dim in sides:
-        count = lax.axis_size(axis)
-        ends = count - 1
-        head = lax.slice_in_dim(cells, 0, width, axis=dim)
-        tail = lax.slice_in_dim(cells, cells.shape[dim] - width, cells.shape[dim], axis=dim)
-        cells = jnp.concatenate(
-            [
-                lax.ppermute(tail, axis, [(i, (i + 1) % count) for i in range(ends)]),
-                cells,
-                lax.ppermute(head, axis, [((i + 1) % count, i) for i in range(ends)]),
-            ],
-            axis=dim,
-        )
-    return cells
-
-
-def device_terms(vectors, masses, interior, row_lists, picked, springs, partners):
-    row_count = vectors.shape[-1]
-    places = jnp.arange(row_count, dtype=jnp.int32)
-    laplace = jnp.zeros_like(vectors)
-    for k, t in enumerate(STRIDES):
-        edge_weight = jnp.where(places < row_count - t, interior[k], 0.0)
-        fluxes = edge_weight * (vectors - jnp.roll(vectors, -t, axis=1))
-        laplace = laplace + fluxes - jnp.roll(fluxes, t, axis=1)
-    own_part = masses * vectors + laplace
-    inverse = 1.0 / row_count
-    diag_tile = jnp.dot(vectors, own_part.T, precision=HIGHEST)
-    applied = own_part
-    for k in range(4):
-        onehot = (row_lists[k][:, None] == places[None, :]).astype(jnp.float32)
-        diag_tile = diag_tile + jnp.dot(picked[k], (springs[k] * picked[k]).T, precision=HIGHEST)
-        applied = applied + jnp.dot(
-            springs[k] * (picked[k] - partners[k]), onehot, precision=HIGHEST
-        )
-    diag_tile = diag_tile * inverse
-    down_tile = -jnp.dot(springs[1] * picked[1], partners[1].T, precision=HIGHEST) * inverse
-    side_turned = -jnp.dot(partners[3], (springs[3] * picked[3]).T, precision=HIGHEST) * inverse
-    tiles = jnp.concatenate([diag_tile, side_turned, down_tile, down_tile.T], axis=1)
-    tiles = jnp.pad(tiles, ((0, 0), (0, -tiles.shape[1] % LANES)))
-    return applied, tiles
 
 
 def turned_dot(left, right):
@@ -201,26 +158,47 @@
         pl.when(has_left)(to_left)
 
 
+def unpack_tile(packed, modes):
+    half = 3 * modes // 2
+    upper = packed[:, 0 : 3 * modes]
+    lower = jnp.concatenate(
+        [packed[0:ROWS, 3 * modes : 3 * modes + half], packed[ROWS:, 3 * modes : 3 * modes + half]],
+        axis=1,
+    )
+    return jnp.concatenate([upper, lower], axis=0)
+
+
+def pack_tile(tile):
+    modes = tile.shape[0]
+    half = 3 * modes // 2
+    top = modes - ROWS
+    upper = tile[0:top]
+    lower = jnp.concatenate([tile[top:, 0:half], tile[top:, half:]], axis=0)
+    spare = jnp.zeros((top, LANES - 3 * modes - half), jnp.float32)
+    return jnp.concatenate([upper, lower, spare], axis=1)
+
+
 def factor_kernel(place_ref, tiles_ref, diag_ref, left_ref, right_ref, grid_ref, turned_ref):
-    subs, layers, modes, _ = tiles_ref.shape
-    order = layers * modes
+    layers, subs, _, _ = tiles_ref.shape
+    modes, order = diag_ref.shape
     part = grid_ref.shape[2] // 3
     unrolled = layers <= UNROLLED_LAYERS
     grid_ref[...] = jnp.zeros_like(grid_ref)
 
     def place_tiles(s, has_left):
         for j in range(layers):
-            tile = tiles_ref[s, j]
+            tile = unpack_tile(tiles_ref[j, s], modes)
             rows = slice(j * modes, (j + 1) * modes)
             grid_ref[s, rows, j * modes : (j + 1) * modes] = tile[:, 0:modes]
             if j > 0:
                 above = slice((j - 1) * modes, j * modes)
                 grid_ref[s, above, j * modes : (j + 1) * modes] = tile[:, modes : 2 * modes]
-            lanes = slice(part + j * modes, part + (j + 1) * modes)
-            grid_ref[s, rows, lanes] = tile[:, 2 * modes : 3 * modes]
             if has_left:
+                down_turned = tile[:, 2 * modes : 3 * modes]
+                lanes = slice(part + j * modes, part + (j + 1) * modes)
+                grid_ref[s, rows, lanes] = down_turned.T
                 lanes = slice(2 * part + j * modes, 2 * part + (j + 1) * modes)
-                grid_ref[s - 1, rows, lanes] = tile[:, 3 * modes : 4 * modes]
+                grid_ref[s - 1, rows, lanes] = down_turned
 
     place_tiles(0, False)
     if unrolled:
@@ -261,74 +239,200 @@
         out_ref[...] = found if k == 0 else jnp.where(sub_here < subs - 1, found, 0.0)
 
 
-def factor_planes(place, plane_tiles):
-    subs, layers, modes, _ = plane_tiles.shape
+VMEM_BLOCK = pl.BlockSpec(memory_space=pltpu.VMEM)
+SMEM_BLOCK = pl.BlockSpec(memory_space=pltpu.SMEM)
+PARAMS = pltpu.CompilerParams(vmem_limit_bytes=56 * 1024 * 1024)
+
+
+def factor_planes(place, plane_tiles, modes):
+    layers, subs, _, _ = plane_tiles.shape
     order = layers * modes
     part = -(-order // LANES) * LANES
     strip = jax.ShapeDtypeStruct((modes, order), jnp.float32)
-    vmem = pl.BlockSpec(memory_space=pltpu.VMEM)
     return pl.pallas_call(
         factor_kernel,
         out_shape=(strip, strip, strip),
-        in_specs=[pl.BlockSpec(memory_space=pltpu.SMEM), vmem],
-        out_specs=(vmem, vmem, vmem),
+        in_specs=[SMEM_BLOCK, VMEM_BLOCK],
+        out_specs=(VMEM_BLOCK, VMEM_BLOCK, VMEM_BLOCK),
         scratch_shapes=[
             pltpu.VMEM((subs, order, 3 * part), jnp.float32),
             pltpu.VMEM((3, part, order), jnp.float32),
         ],
-        compiler_params=pltpu.CompilerParams(vmem_limit_bytes=56 * 1024 * 1024),
+        compiler_params=PARAMS,
         name="factor_planes",
     )(place, plane_tiles)
+
+
+def across_dot(left, right):
+    return lax.dot_general(
+        left,
+        right,
+        (((1,), (1,)), ((), ())),
+        precision=HIGHEST,
+        preferred_element_type=jnp.float32,
+    )
+
+
+def pick_kernel(place_ref, vectors_ref, lists_ref, face_ref, picked_ref, sub_ref, layer_ref):
+    lay_here, layers = place_ref[1], layer_ref.shape[0]
+    modes, row_count = vectors_ref.shape
+    layer_ref[...] = jnp.zeros_like(layer_ref)
+    sub_ref[...] = jnp.zeros_like(sub_ref)
+    for k in range(4):
+        rows = jnp.broadcast_to(lists_ref[k : k + 1, :], (ROWS, LANES))
+        tile_of, lane_of = rows // LANES, rows % LANES
+        found = [jnp.zeros((ROWS, LANES), jnp.float32) for _ in range(modes // ROWS)]
+        for c in range(row_count // LANES):
+            here = tile_of == c
+            for r in range(modes // ROWS):
+                tile = vectors_ref[r * ROWS : (r + 1) * ROWS, c * LANES : (c + 1) * LANES]
+                moved = jnp.take_along_axis(tile, lane_of, axis=1, mode="promise_in_bounds")
+                found[r] = jnp.where(here, moved, found[r])
+        picked_ref[k] = jnp.concatenate(found, axis=0)
+    sub_ref[0:modes] = picked_ref[0]
+    sub_ref[modes : modes + 1] = face_ref[0:1]
+
+    @pl.when(lay_here < layers - 1)
+    def _():
+        layer_ref[lay_here + 1, 0:modes] = picked_ref[2]
+        layer_ref[lay_here + 1, modes : modes + 1] = face_ref[1:2]
+
+    @pl.when(lay_here > 0)
+    def _():
+        layer_ref[lay_here - 1, 0:modes] = picked_ref[3]
+
+
+def own_kernel(place_ref, vectors_ref, mass_ref, inner_ref, face_ref, picked_ref, base_ref, own_ref, *, subs, layers):
+    vectors = vectors_ref[...]
+    row_count = vectors.shape[1]
+    places = lax.broadcasted_iota(jnp.int32, (1, row_count), 1)
+    base = mass_ref[...] * vectors
+    for k, t in enumerate(STRIDES):
+        edge_weight = jnp.where(places < row_count - t, inner_ref[k : k + 1, :], 0.0)
+        fluxes = edge_weight * (vectors - pltpu.roll(vectors, row_count - t, 1))
+        base = base + fluxes - pltpu.roll(fluxes, t, 1)
+    base_ref[...] = base
+    own = across_dot(vectors, base)
+    for k, has_next in ((0, place_ref[0] < subs - 1), (2, place_ref[1] < layers - 1)):
+        springs = jnp.where(has_next, face_ref[k // 2 : k // 2 + 1, :], 0.0)
+        own = own + across_dot(picked_ref[k], springs * picked_ref[k])
+    own_ref[...] = own
+
+
+def partner_from(layer_ref, position, exists):
+    clamped = jnp.clip(position, 0, layer_ref.shape[0] - 1)
+    return jnp.where(exists, layer_ref[clamped], 0.0)
+
+
+def tile_kernel(place_ref, own_ref, picked_ref, sub_ref, layer_ref, copies_ref, *, row_count):
+    modes = own_ref.shape[0]
+    lay_here = place_ref[1]
+    inverse = 1.0 / row_count
+    before = partner_from(layer_ref, lay_here - 1, lay_here > 0)
+    pairs = []
+    for mine, theirs in ((picked_ref[1], sub_ref[...]), (picked_ref[3], before)):
+        sprung = theirs[modes : modes + 1] * mine
+        stacked = jnp.concatenate([mine, theirs[0:modes]], axis=0)
+        pairs.append(across_dot(stacked, sprung))
+    down, side = pairs
+    diag_tile = (own_ref[...] + down[0:modes] + side[0:modes]) * inverse
+    side_turned = -side[modes:] * inverse
+    down_turned = -down[modes:] * inverse
+    packed = pack_tile(jnp.concatenate([diag_tile, side_turned, down_turned], axis=1))
+    for s in range(copies_ref.shape[0]):
+        copies_ref[s] = packed
+
+
+def scatter_kernel(place_ref, base_ref, lists_ref, face_ref, picked_ref, sub_ref, next_ref, layer_ref, applied_ref, *, subs):
+    modes, row_count = base_ref.shape
+    sub_here, lay_here = place_ref[0], place_ref[1]
+    layers = layer_ref.shape[0]
+    width = 2 * LANES
+    after = partner_from(layer_ref, lay_here + 1, lay_here < layers - 1)
+    before = partner_from(layer_ref, lay_here - 1, lay_here > 0)
+    springs = [
+        jnp.where(sub_here < subs - 1, face_ref[0:1, :], 0.0),
+        sub_ref[modes : modes + 1, :],
+        jnp.where(lay_here < layers - 1, face_ref[1:2, :], 0.0),
+        before[modes : modes + 1],
+    ]
+    partners = [next_ref[...], sub_ref[0:modes, :], after[0:modes], before[0:modes]]
+    pulls = jnp.concatenate(
+        [springs[k] * (picked_ref[k] - partners[k]) for k in range(4)], axis=1
+    )
+    rows = jnp.concatenate([lists_ref[k : k + 1, :] for k in range(4)], axis=1)
+    block_of, lane_of = rows // width, rows % width
+    lanes = lax.broadcasted_iota(jnp.int32, (width, rows.shape[1]), 0)
+    onehot = jnp.where(lanes == lane_of, 1.0, 0.0).astype(jnp.bfloat16)
+    total = None
+    rest = pulls
+    for _ in range(3):
+        piece = rest.astype(jnp.bfloat16).astype(jnp.float32)
+        rest = rest - piece
+        spread = jnp.concatenate(
+            [jnp.where(block_of == h, piece, 0.0) for h in range(row_count // width)], axis=0
+        ).astype(jnp.bfloat16)
+        moved = lax.dot_general(
+            spread, onehot, (((1,), (1,)), ((), ())), preferred_element_type=jnp.float32
+        )
+        total = moved if total is None else total + moved
+    for h in range(row_count // width):
+        lanes = slice(h * width, (h + 1) * width)
+        applied_ref[:, lanes] = base_ref[:, lanes] + total[h * modes : (h + 1) * modes]
+
+
+def local_call(body, outputs, operands, name):
+    shapes = tuple(jax.ShapeDtypeStruct(shape, jnp.float32) for shape in outputs)
+    return pl.pallas_call(
+        body,
+        out_shape=shapes,
+        in_specs=[SMEM_BLOCK] + [VMEM_BLOCK] * (len(operands) - 1),
+        out_specs=tuple(VMEM_BLOCK for _ in shapes),
+        compiler_params=PARAMS,
+        name=name,
+    )(*operands)
 
 
 def per_device(eigen_vectors, row_mass, inner_weight, face_weight, margin_rows):
     vectors = eigen_vectors[0, 0]
     row_lists = margin_rows[0, 0]
     face_springs = face_weight[0, 0]
-    mode_count = vectors.shape[0]
+    modes, row_count = vectors.shape
+    width = row_lists.shape[-1]
     subs = lax.axis_size("sub")
     layers = lax.axis_size("layer")
-    sub_here = lax.axis_index("sub")
-    lay_here = lax.axis_index("layer")
-    picked = jnp.stack([jnp.take(vectors, row_lists[k], axis=1) for k in range(4)])
-    zero_row = jnp.zeros((1, row_lists.shape[-1]), jnp.float32)
-    sub_send = jnp.stack(
-        [
-            jnp.concatenate([picked[1], zero_row], 0),
-            jnp.concatenate([picked[0], face_springs[0:1]], 0),
-        ]
-    )
-    sub_rim = padded(sub_send, (("sub", 0),), 1)
-    lay_send = jnp.stack(
-        [
-            jnp.concatenate([picked[3], zero_row], 0),
-            jnp.concatenate([picked[2], face_springs[1:2]], 0),
-        ]
-    )
-    lay_rim = padded(lay_send, (("layer", 0),), 1)
-    partners = jnp.stack(
-        [
-            sub_rim[3, :mode_count],
-            sub_rim[0, :mode_count],
-            lay_rim[3, :mode_count],
-            lay_rim[0, :mode_count],
-        ]
-    )
-    springs = jnp.stack(
-        [
-            jnp.where(sub_here < subs - 1, face_springs[0], 0.0),
-            sub_rim[0, mode_count],
-            jnp.where(lay_here < layers - 1, face_springs[1], 0.0),
-            lay_rim[0, mode_count],
-        ]
-    )
-    applied, tiles = device_terms(
-        vectors, row_mass[0, 0], inner_weight[0, 0], row_lists, picked, springs, partners
-    )
-    all_tiles = lax.all_gather(tiles, ("sub", "layer"), axis=0, tiled=False)
-    all_tiles = all_tiles.reshape(subs, layers, *tiles.shape)
-    place = jnp.stack([sub_here, lay_here]).astype(jnp.int32)
-    diag_strip, left_strip, right_strip = factor_planes(place, all_tiles)
+    place = jnp.stack([lax.axis_index("sub"), lax.axis_index("layer")]).astype(jnp.int32)
+    picked, sub_send, layer_send = local_call(
+        pick_kernel,
+        [(4, modes, width), (modes + ROWS, width), (layers, modes + ROWS, width)],
+        (place, vectors, row_lists, face_springs),
+        "pick_rows",
+    )
+    layer_rim = lax.all_to_all(layer_send, "layer", split_axis=0, concat_axis=0, tiled=True)
+    sub_rim = lax.ppermute(sub_send, "sub", [(i, i + 1) for i in range(subs - 1)])
+    next_rim = lax.ppermute(picked[1], "sub", [(i + 1, i) for i in range(subs - 1)])
+    base, own = local_call(
+        functools.partial(own_kernel, subs=subs, layers=layers),
+        [(modes, row_count), (modes, modes)],
+        (place, vectors, row_mass[0], inner_weight[0, 0], face_springs, picked),
+        "own_rows",
+    )
+    (copies,) = local_call(
+        functools.partial(tile_kernel, row_count=row_count),
+        [(subs, modes - ROWS, LANES)],
+        (place, own, picked, sub_rim, layer_rim),
+        "coarse_tiles",
+    )
+    column = lax.all_to_all(copies, "sub", split_axis=0, concat_axis=0, tiled=True)
+    columns = jnp.broadcast_to(column[None], (layers,) + column.shape)
+    plane_tiles = lax.all_to_all(columns, "layer", split_axis=0, concat_axis=0, tiled=True)
+    (applied,) = local_call(
+        functools.partial(scatter_kernel, subs=subs),
+        [(modes, row_count)],
+        (place, base, row_lists, face_springs, picked, sub_rim, next_rim, layer_rim),
+        "spread_rows",
+    )
+    diag_strip, left_strip, right_strip = factor_planes(place, plane_tiles, modes)
     return (applied[None, None], diag_strip[None], left_strip[None], right_strip[None])
 
 

time: 121 us -> 61 us (0.50)
  the two profiles are of different devices: /device:TPU:0 before, /device:TPU:1 now
where the time goes in v3:
time: 61 us; the launch traced here: 60.3 us
  Pallas kernels  28.3 us (46%)
  starting transfers between devices  15.4 us (25%)
  blocking collectives  9.05 us (15%)
  local copies, waits for them, and re-layouts  4.02 us (7%)
  waiting for transfers between devices  2.27 us (4%)
  between operations  0.68 us (1%)
  other arithmetic  0.66 us (1%)
    pallas_call x1, Pallas kernels, factor_planes(): pl.pallas_call(factor_kernel, out_shape=(strip, strip, strip), in_specs=[...  19 us
    pallas_call x4, Pallas kernels, local_call(): pl.pallas_call(body, out_shape=shapes, in_specs=[SMEM_BLOCK] + [VMEM_BLOC...  9.29 us
    all_to_all x1, blocking collectives, per_device(): lax.all_to_all(copies, 'sub', split_axis=0, concat_axis=0, tiled=True)  9.05 us
    all_to_all x1, starting transfers between devices, per_device(): lax.all_to_all(layer_send, 'layer', split_axis=0, concat_axis=0, tiled=True)  4.4 us
    ppermute x1, starting transfers between devices, per_device(): lax.ppermute(sub_send, 'sub', [(i, i + 1) for i in range(subs - 1)])  4.03 us
    all_to_all x1, starting transfers between devices, per_device(): lax.all_to_all(columns, 'layer', split_axis=0, concat_axis=0, tiled=True)  3.91 us
    ppermute x1, starting transfers between devices, per_device(): lax.ppermute(picked[1], 'sub', [(i + 1, i) for i in range(subs - 1)])  3.02 us
    unnamed x13, local copies, waits for them, and re-layouts  2.59 us
  transfers between devices with their start and end apart: 4, of which 1 were waited for; matrix products, arithmetic and copies ran while one was open for 2% of the time, Pallas kernels for 9%

profile of v3, /device:TPU:1, one launch (start us, length us, event | category | flops | bytes accessed | tf_op | source)
XLA Modules:
  0.0 60.3 jit_solution(1320250575846088146)
XLA Ops:
  0.6 0.7 %pad_add_fusion.place_ref = s32[2]{0:T(128)} fusion(s32[1]{0:T(128)} %bitcast.1, s32[1]{0:T(128)} %bitcast), kind=kLoop, calls=%fused_computation.2 | loop fusion | flops 2 | bytes 16 | tf_op jit(solution)/shard_map/stack | solution.py:404
  1.3 2.2 %pick_rows.1 = (f32[4,24,128]{2,1,0:T(8,128)}, f32[32,128]{1,0:T(8,128)}, f32[4,32,128]{2,1,0:T(8,128)}) custom-call(s32[2]{0:T(128)} %pad_add_fusion.place_ref, f32[24,4096]{1,0:T(8,128)} %bitcast.15, s32[4,128]{1,0:T(4,128)} %bitcast.23, f32[2,128]{1,0:T(2,128)} %bitcast.20), custom_call_target="tpu_custom_call" | custom-call | tf_op jit(solution)/shard_map/pick_rows/pallas_call | solution.py:386
  3.5 0.0 copy-start.5
  3.5 0.0 copy-start.3
  3.5 4.4 %all-to-all-start = ((f32[4,32,128]{2,1,0:T(8,128)}), f32[4,32,128]{2,1,0:T(8,128)S(1)}, u32[]{:S(2)}, u32[]{:S(2)}) async-start(f32[4,32,128]{2,1,0:T(8,128)} %get-tuple-element.15), calls=%async_computation | async-start | bytes 131072 | tf_op jit(solution)/shard_map/all_to_all | solution.py:411
  7.9 0.0 copy-done.5
  7.9 4.0 %collective-permute-start = (f32[32,128]{1,0:T(8,128)S(1)}, f32[32,128]{1,0:T(8,128)S(1)}, u32[]{:S(2)}, u32[]{:S(2)}) collective-permute-start(f32[32,128]{1,0:T(8,128)S(1)} %copy-done.5), channel_id=1, source_target_pairs={{0,4},{4,8},{8,12},{12,16},{16,20},{20,24},{24,28},{1,5},{5,9},{9,... | collective-permute-start | bytes 49160 | tf_op jit(solution)/shard_map/ppermute | solution.py:412
  11.9 0.0 copy-done.3
  11.9 0.7 %copy.11 = f32[1,1,3,4096]{3,2,1,0:T(4,128)} copy(f32[1,1,3,4096]{3,1,2,0:T(1,128)S(1)} %copy-done.3) | data formatting | bytes 98304
  12.6 2.8 %own_rows.1 = (f32[24,4096]{1,0:T(8,128)}, f32[24,24]{1,0:T(8,128)}) custom-call(s32[2]{0:T(128)} %pad_add_fusion.place_ref, f32[24,4096]{1,0:T(8,128)} %bitcast.16, f32[1,4096]{1,0:T(1,128)} %bitcast.19, f32[3,4096]{1,0:T(4,128)} %bitcast.18, f32[2,128]{1,0:T(2,128)} %bitcast.21, f32[4,24,128]{2,1,0:T(8,128)} %get-tuple-element.12.picked_ref), custom_call_target="tpu_custom_call" | custom-call | tf_op jit(solution)/shard_map/own_rows/pallas_call | solution.py:386
  15.4 0.0 collective-permute-done.sub_ref
  15.4 0.0 copy-start.2
  15.4 0.0 all-to-all-done.layer_ref
  15.4 0.0 copy-start.1
  15.4 0.6 copy-done.2
  16.0 0.0 copy-done.1
  16.0 1.9 %coarse_tiles.1 = f32[8,16,128]{2,1,0:T(8,128)} custom-call(s32[2]{0:T(128)} %pad_add_fusion.place_ref, f32[24,24]{1,0:T(8,128)} %get-tuple-element.16.own_ref, f32[4,24,128]{2,1,0:T(8,128)} %get-tuple-element.12.picked_ref, f32[32,128]{1,0:T(8,128)} %copy-done.2, f32[4,32,128]{2,1,0:T(8,128)} %copy-done.1), custom_call_target="tpu_custom_call" | custom-call | tf_op jit(solution)/shard_map/coarse_tiles/pallas_call | solution.py:386
  18.0 9.0 %all_to_all.15 = f32[8,16,128]{2,1,0:T(8,128)S(1)} all-to-all(f32[8,16,128]{2,1,0:T(8,128)} %coarse_tiles.1), channel_id=1, replica_groups=mesh['sub'=8,'layer'=4] {'sub'}, dimensions={0} | all-to-all | bytes 131072 | tf_op jit(solution)/shard_map/all_to_all | solution.py:426
  27.0 0.7 %broadcast_in_dim.19 = f32[4,8,16,128]{3,2,1,0:T(8,128)} broadcast(f32[8,16,128]{2,1,0:T(8,128)S(1)} %all_to_all.15), dimensions={1,2,3} | broadcast | bytes 327680 | tf_op jit(solution)/shard_map/broadcast_in_dim | solution.py:427
  27.7 3.9 %all-to-all-start.2 = ((f32[4,8,16,128]{3,2,1,0:T(8,128)}), f32[4,8,16,128]{3,2,1,0:T(8,128)S(1)}, u32[]{:S(2)}, u32[]{:S(2)}) async-start(f32[4,8,16,128]{3,2,1,0:T(8,128)} %broadcast_in_dim.19), calls=%async_computation.2 | async-start | bytes 524288 | tf_op jit(solution)/shard_map/all_to_all | solution.py:428
  31.7 0.7 %slice_bitcast_fusion = f32[24,128]{1,0:T(8,128)S(1)} fusion(f32[4,24,128]{2,1,0:T(8,128)} %get-tuple-element.12.picked_ref), kind=kLoop, calls=%fused_computation.1 | loop fusion | bytes 24576 | tf_op jit(solution)/shard_map/squeeze | solution.py:413
  32.4 3.0 %collective-permute-start.1 = (f32[24,128]{1,0:T(8,128)S(1)}, f32[24,128]{1,0:T(8,128)S(1)}, u32[]{:S(2)}, u32[]{:S(2)}) collective-permute-start(f32[24,128]{1,0:T(8,128)S(1)} %slice_bitcast_fusion), channel_id=1, source_target_pairs={{4,0},{8,4},{12,8},{16,12},{20,16},{24,20},{28,24},{5,1},{9,5},{13... | collective-permute-start | bytes 36872 | tf_op jit(solution)/shard_map/ppermute | solution.py:413
  35.4 2.3 %collective-permute-done.1.next_ref = f32[24,128]{1,0:T(8,128)S(1)} collective-permute-done((f32[24,128]{1,0:T(8,128)S(1)}, f32[24,128]{1,0:T(8,128)S(1)}, u32[]{:S(2)}, u32[]{:S(2)}) %collective-permute-start.1) | collective-permute-done | bytes 12320 | tf_op jit(solution)/shard_map/ppermute | solution.py:413
  37.7 0.0 copy-start.4
  37.7 0.6 copy-done.4
  38.3 2.4 %spread_rows.1 = f32[24,4096]{1,0:T(8,128)} custom-call(s32[2]{0:T(128)} %pad_add_fusion.place_ref, f32[24,4096]{1,0:T(8,128)} %get-tuple-element.13.base_ref, s32[4,128]{1,0:T(4,128)} %bitcast.24, f32[2,128]{1,0:T(2,128)} %bitcast.22, f32[4,24,128]{2,1,0:T(8,128)} %get-tuple-element.12.picked_ref, f32[32,128]{1,0:T(8,128)} %copy-done.2, ...), custom_call_target="tpu_custom_call" | custom-call | tf_op jit(solution)/shard_map/spread_rows/pallas_call | solution.py:386
  40.6 0.0 all-to-all-done.2.tiles_ref
  40.6 0.0 copy-start
  40.6 0.7 %copy-done = f32[4,8,16,128]{3,2,1,0:T(8,128)} copy-done((f32[4,8,16,128]{3,2,1,0:T(8,128)}, f32[4,8,16,128]{3,2,1,0:T(8,128)S(1)}, u32[]{:S(2)}) %copy-start) | copy-done | bytes 262168
  41.4 19.0 %factor_planes.1 = (f32[24,96]{1,0:T(8,128)}, f32[24,96]{1,0:T(8,128)}, f32[24,96]{1,0:T(8,128)}) custom-call(s32[2]{0:T(128)} %pad_add_fusion.place_ref, f32[4,8,16,128]{3,2,1,0:T(8,128)} %copy-done), custom_call_target="tpu_custom_call" | custom-call | tf_op jit(solution)/shard_map/factor_planes/pallas_call | solution.py:252
Async XLA Ops:
  3.5 4.4 %copy-start.5 = (f32[32,128]{1,0:T(8,128)S(1)}, f32[32,128]{1,0:T(8,128)}, u32[]{:S(2)}) copy-start(f32[32,128]{1,0:T(8,128)} %get-tuple-element.14) | copy-start | bytes 49156
  3.5 8.5 %copy-start.3 = (f32[1,1,3,4096]{3,1,2,0:T(1,128)S(1)}, f32[1,1,3,4096]{3,1,2,0:T(1,128)}, u32[]{:S(2)}) copy-start(f32[1,1,3,4096]{3,1,2,0:T(1,128)} %param.7) | copy-start | bytes 147460
  3.5 11.9 %all-to-all-start = ((f32[4,32,128]{2,1,0:T(8,128)}), f32[4,32,128]{2,1,0:T(8,128)S(1)}, u32[]{:S(2)}, u32[]{:S(2)}) async-start(f32[4,32,128]{2,1,0:T(8,128)} %get-tuple-element.15), calls=%async_computation | async-start | bytes 131072 | tf_op jit(solution)/shard_map/all_to_all | solution.py:411
  7.9 7.5 %collective-permute-start = (f32[32,128]{1,0:T(8,128)S(1)}, f32[32,128]{1,0:T(8,128)S(1)}, u32[]{:S(2)}, u32[]{:S(2)}) collective-permute-start(f32[32,128]{1,0:T(8,128)S(1)} %copy-done.5), channel_id=1, source_target_pairs={{0,4},{4,8},{8,12},{12,16},{16,20},{20,24},{24,28},{1,5},{5,9},{9,... | collective-permute-start | bytes 49160 | tf_op jit(solution)/shard_map/ppermute | solution.py:412
  15.4 0.6 %copy-start.2 = (f32[32,128]{1,0:T(8,128)}, f32[32,128]{1,0:T(8,128)S(1)}, u32[]{:S(2)}) copy-start(f32[32,128]{1,0:T(8,128)S(1)} %collective-permute-done.sub_ref) | copy-start | bytes 49156
  15.4 0.6 %copy-start.1 = (f32[4,32,128]{2,1,0:T(8,128)}, f32[4,32,128]{2,1,0:T(8,128)S(1)}, u32[]{:S(2)}) copy-start(f32[4,32,128]{2,1,0:T(8,128)S(1)} %all-to-all-done.layer_ref) | copy-start | bytes 196612
  27.7 12.9 %all-to-all-start.2 = ((f32[4,8,16,128]{3,2,1,0:T(8,128)}), f32[4,8,16,128]{3,2,1,0:T(8,128)S(1)}, u32[]{:S(2)}, u32[]{:S(2)}) async-start(f32[4,8,16,128]{3,2,1,0:T(8,128)} %broadcast_in_dim.19), calls=%async_computation.2 | async-start | bytes 524288 | tf_op jit(solution)/shard_map/all_to_all | solution.py:428
  32.4 5.3 %collective-permute-start.1 = (f32[24,128]{1,0:T(8,128)S(1)}, f32[24,128]{1,0:T(8,128)S(1)}, u32[]{:S(2)}, u32[]{:S(2)}) collective-permute-start(f32[24,128]{1,0:T(8,128)S(1)} %slice_bitcast_fusion), channel_id=1, source_target_pairs={{4,0},{8,4},{12,8},{16,12},{20,16},{24,20},{28,24},{5,1},{9,5},{13... | collective-permute-start | bytes 36872 | tf_op jit(solution)/shard_map/ppermute | solution.py:413
  37.7 0.6 copy-start.4
  40.6 0.7 %copy-start = (f32[4,8,16,128]{3,2,1,0:T(8,128)}, f32[4,8,16,128]{3,2,1,0:T(8,128)S(1)}, u32[]{:S(2)}) copy-start(f32[4,8,16,128]{3,2,1,0:T(8,128)S(1)} %all-to-all-done.2.tiles_ref) | copy-start | bytes 786436

commit v4 on v3

--- a/solution.py
+++ b/solution.py
@@ -1,4 +1,5 @@
 import functools
+import math
 import jax
 import jax.numpy as jnp
 from jax import lax
@@ -178,16 +179,17 @@
     return jnp.concatenate([upper, lower, spare], axis=1)
 
 
-def factor_kernel(place_ref, tiles_ref, diag_ref, left_ref, right_ref, grid_ref, turned_ref):
-    layers, subs, _, _ = tiles_ref.shape
+def factor_kernel(tiles_ref, after_ref, diag_ref, left_ref, right_ref, grid_ref, turned_ref):
+    subs, layers, _, _ = tiles_ref.shape
     modes, order = diag_ref.shape
     part = grid_ref.shape[2] // 3
     unrolled = layers <= UNROLLED_LAYERS
+    del after_ref
     grid_ref[...] = jnp.zeros_like(grid_ref)
 
     def place_tiles(s, has_left):
         for j in range(layers):
-            tile = unpack_tile(tiles_ref[j, s], modes)
+            tile = unpack_tile(tiles_ref[s, j], modes)
             rows = slice(j * modes, (j + 1) * modes)
             grid_ref[s, rows, j * modes : (j + 1) * modes] = tile[:, 0:modes]
             if j > 0:
@@ -231,7 +233,7 @@
         distance *= 2
     eliminate_planes(grid_ref, [subs - 1], modes, order, part, part)
 
-    sub_here, lay_here = place_ref[0], place_ref[1]
+    sub_here, lay_here = lax.axis_index("sub"), lax.axis_index("layer")
     strip = pl.ds(pl.multiple_of(lay_here * modes, ROWS), modes)
     for k, out_ref in enumerate((diag_ref, left_ref, right_ref)):
         turned_ref[k] = grid_ref[sub_here, :, k * part : (k + 1) * part].T
@@ -240,27 +242,29 @@
 
 
 VMEM_BLOCK = pl.BlockSpec(memory_space=pltpu.VMEM)
-SMEM_BLOCK = pl.BlockSpec(memory_space=pltpu.SMEM)
-PARAMS = pltpu.CompilerParams(vmem_limit_bytes=56 * 1024 * 1024)
-
-
-def factor_planes(place, plane_tiles, modes):
-    layers, subs, _, _ = plane_tiles.shape
+SPARE_BYTES = 4 * 1024 * 1024
+
+
+def kernel_params(shapes):
+    held = sum(4 * math.prod(shape) for shape in shapes)
+    return pltpu.CompilerParams(vmem_limit_bytes=min(2 * held + SPARE_BYTES, 60 * 1024 * 1024))
+
+
+def factor_planes(plane_tiles, modes, after):
+    subs, layers, _, _ = plane_tiles.shape
     order = layers * modes
     part = -(-order // LANES) * LANES
     strip = jax.ShapeDtypeStruct((modes, order), jnp.float32)
+    scratch = ((subs, order, 3 * part), (3, part, order))
     return pl.pallas_call(
         factor_kernel,
         out_shape=(strip, strip, strip),
-        in_specs=[SMEM_BLOCK, VMEM_BLOCK],
+        in_specs=[VMEM_BLOCK, pl.BlockSpec(memory_space=pl.ANY)],
         out_specs=(VMEM_BLOCK, VMEM_BLOCK, VMEM_BLOCK),
-        scratch_shapes=[
-            pltpu.VMEM((subs, order, 3 * part), jnp.float32),
-            pltpu.VMEM((3, part, order), jnp.float32),
-        ],
-        compiler_params=PARAMS,
+        scratch_shapes=[pltpu.VMEM(shape, jnp.float32) for shape in scratch],
+        compiler_params=kernel_params((plane_tiles.shape,) + scratch),
         name="factor_planes",
-    )(place, plane_tiles)
+    )(plane_tiles, after)
 
 
 def across_dot(left, right):
@@ -273,11 +277,8 @@
     )
 
 
-def pick_kernel(place_ref, vectors_ref, lists_ref, face_ref, picked_ref, sub_ref, layer_ref):
-    lay_here, layers = place_ref[1], layer_ref.shape[0]
+def pick_kernel(vectors_ref, lists_ref, face_ref, picked_ref, sub_ref, layer_ref):
     modes, row_count = vectors_ref.shape
-    layer_ref[...] = jnp.zeros_like(layer_ref)
-    sub_ref[...] = jnp.zeros_like(sub_ref)
     for k in range(4):
         rows = jnp.broadcast_to(lists_ref[k : k + 1, :], (ROWS, LANES))
         tile_of, lane_of = rows // LANES, rows % LANES
@@ -289,50 +290,40 @@
                 moved = jnp.take_along_axis(tile, lane_of, axis=1, mode="promise_in_bounds")
                 found[r] = jnp.where(here, moved, found[r])
         picked_ref[k] = jnp.concatenate(found, axis=0)
-    sub_ref[0:modes] = picked_ref[0]
-    sub_ref[modes : modes + 1] = face_ref[0:1]
-
-    @pl.when(lay_here < layers - 1)
-    def _():
-        layer_ref[lay_here + 1, 0:modes] = picked_ref[2]
-        layer_ref[lay_here + 1, modes : modes + 1] = face_ref[1:2]
-
-    @pl.when(lay_here > 0)
-    def _():
-        layer_ref[lay_here - 1, 0:modes] = picked_ref[3]
-
-
-def own_kernel(place_ref, vectors_ref, mass_ref, inner_ref, face_ref, picked_ref, base_ref, own_ref, *, subs, layers):
+    for k, send_ref in ((0, sub_ref), (2, layer_ref)):
+        send_ref[0:modes] = picked_ref[k]
+        send_ref[modes:] = jnp.broadcast_to(face_ref[k // 2 : k // 2 + 1, :], (ROWS, LANES))
+
+
+def own_kernel(
+    vectors_ref, mass_ref, inner_ref, face_ref, picked_ref, base_ref, own_ref, *, subs, layers
+):
     vectors = vectors_ref[...]
     row_count = vectors.shape[1]
     places = lax.broadcasted_iota(jnp.int32, (1, row_count), 1)
     base = mass_ref[...] * vectors
     for k, t in enumerate(STRIDES):
-        edge_weight = jnp.where(places < row_count - t, inner_ref[k : k + 1, :], 0.0)
+        edge_weight = jnp.where(places < row_count - t, inner_ref[k], 0.0)
         fluxes = edge_weight * (vectors - pltpu.roll(vectors, row_count - t, 1))
         base = base + fluxes - pltpu.roll(fluxes, t, 1)
     base_ref[...] = base
     own = across_dot(vectors, base)
-    for k, has_next in ((0, place_ref[0] < subs - 1), (2, place_ref[1] < layers - 1)):
-        springs = jnp.where(has_next, face_ref[k // 2 : k // 2 + 1, :], 0.0)
+    for k, axis, ends in ((0, "sub", subs - 1), (2, "layer", layers - 1)):
+        springs = jnp.where(lax.axis_index(axis) < ends, face_ref[k // 2 : k // 2 + 1, :], 0.0)
         own = own + across_dot(picked_ref[k], springs * picked_ref[k])
     own_ref[...] = own
 
 
-def partner_from(layer_ref, position, exists):
-    clamped = jnp.clip(position, 0, layer_ref.shape[0] - 1)
-    return jnp.where(exists, layer_ref[clamped], 0.0)
-
-
-def tile_kernel(place_ref, own_ref, picked_ref, sub_ref, layer_ref, copies_ref, *, row_count):
+def tile_kernel(
+    own_ref, picked_ref, sub_ref, layer_ref, copies_ref, sub_send_ref, layer_send_ref, *, row_count
+):
     modes = own_ref.shape[0]
-    lay_here = place_ref[1]
     inverse = 1.0 / row_count
-    before = partner_from(layer_ref, lay_here - 1, lay_here > 0)
     pairs = []
-    for mine, theirs in ((picked_ref[1], sub_ref[...]), (picked_ref[3], before)):
-        sprung = theirs[modes : modes + 1] * mine
-        stacked = jnp.concatenate([mine, theirs[0:modes]], axis=0)
+    for k, theirs_ref in ((1, sub_ref), (3, layer_ref)):
+        mine = picked_ref[k]
+        sprung = theirs_ref[modes : modes + 1] * mine
+        stacked = jnp.concatenate([mine, theirs_ref[0:modes]], axis=0)
         pairs.append(across_dot(stacked, sprung))
     down, side = pairs
     diag_tile = (own_ref[...] + down[0:modes] + side[0:modes]) * inverse
@@ -341,22 +332,28 @@
     packed = pack_tile(jnp.concatenate([diag_tile, side_turned, down_turned], axis=1))
     for s in range(copies_ref.shape[0]):
         copies_ref[s] = packed
-
-
-def scatter_kernel(place_ref, base_ref, lists_ref, face_ref, picked_ref, sub_ref, next_ref, layer_ref, applied_ref, *, subs):
+    sub_send_ref[...] = picked_ref[1]
+    layer_send_ref[...] = picked_ref[3]
+
+
+def scatter_kernel(
+    base_ref, lists_ref, face_ref, picked_ref, before_sub_ref, after_sub_ref,
+    before_layer_ref, after_layer_ref, applied_ref, *, subs, layers
+):
     modes, row_count = base_ref.shape
-    sub_here, lay_here = place_ref[0], place_ref[1]
-    layers = layer_ref.shape[0]
     width = 2 * LANES
-    after = partner_from(layer_ref, lay_here + 1, lay_here < layers - 1)
-    before = partner_from(layer_ref, lay_here - 1, lay_here > 0)
     springs = [
-        jnp.where(sub_here < subs - 1, face_ref[0:1, :], 0.0),
-        sub_ref[modes : modes + 1, :],
-        jnp.where(lay_here < layers - 1, face_ref[1:2, :], 0.0),
-        before[modes : modes + 1],
+        jnp.where(lax.axis_index("sub") < subs - 1, face_ref[0:1, :], 0.0),
+        before_sub_ref[modes : modes + 1, :],
+        jnp.where(lax.axis_index("layer") < layers - 1, face_ref[1:2, :], 0.0),
+        before_layer_ref[modes : modes + 1, :],
     ]
-    partners = [next_ref[...], sub_ref[0:modes, :], after[0:modes], before[0:modes]]
+    partners = [
+        after_sub_ref[...],
+        before_sub_ref[0:modes, :],
+        after_layer_ref[...],
+        before_layer_ref[0:modes, :],
+    ]
     pulls = jnp.concatenate(
         [springs[k] * (picked_ref[k] - partners[k]) for k in range(4)], axis=1
     )
@@ -386,9 +383,9 @@
     return pl.pallas_call(
         body,
         out_shape=shapes,
-        in_specs=[SMEM_BLOCK] + [VMEM_BLOCK] * (len(operands) - 1),
+        in_specs=[VMEM_BLOCK] * len(operands),
         out_specs=tuple(VMEM_BLOCK for _ in shapes),
-        compiler_params=PARAMS,
+        compiler_params=kernel_params([x.shape for x in operands] + list(outputs)),
         name=name,
     )(*operands)
 
@@ -401,38 +398,42 @@
     width = row_lists.shape[-1]
     subs = lax.axis_size("sub")
     layers = lax.axis_size("layer")
-    place = jnp.stack([lax.axis_index("sub"), lax.axis_index("layer")]).astype(jnp.int32)
+    up_sub = [(i, i + 1) for i in range(subs - 1)]
+    up_layer = [(i, i + 1) for i in range(layers - 1)]
+    down_sub = [(i + 1, i) for i in range(subs - 1)]
+    down_layer = [(i + 1, i) for i in range(layers - 1)]
     picked, sub_send, layer_send = local_call(
         pick_kernel,
-        [(4, modes, width), (modes + ROWS, width), (layers, modes + ROWS, width)],
-        (place, vectors, row_lists, face_springs),
+        [(4, modes, width), (modes + ROWS, width), (modes + ROWS, width)],
+        (vectors, row_lists, face_springs),
         "pick_rows",
     )
-    layer_rim = lax.all_to_all(layer_send, "layer", split_axis=0, concat_axis=0, tiled=True)
-    sub_rim = lax.ppermute(sub_send, "sub", [(i, i + 1) for i in range(subs - 1)])
-    next_rim = lax.ppermute(picked[1], "sub", [(i + 1, i) for i in range(subs - 1)])
+    before_sub = lax.ppermute(sub_send, "sub", up_sub)
+    before_layer = lax.ppermute(layer_send, "layer", up_layer)
     base, own = local_call(
         functools.partial(own_kernel, subs=subs, layers=layers),
         [(modes, row_count), (modes, modes)],
-        (place, vectors, row_mass[0], inner_weight[0, 0], face_springs, picked),
+        (vectors, row_mass[0], inner_weight[0].reshape(-1, 1, row_count), face_springs, picked),
         "own_rows",
     )
-    (copies,) = local_call(
+    copies, sub_send, layer_send = local_call(
         functools.partial(tile_kernel, row_count=row_count),
-        [(subs, modes - ROWS, LANES)],
-        (place, own, picked, sub_rim, layer_rim),
+        [(subs * layers, modes - ROWS, LANES), (modes, width), (modes, width)],
+        (own, picked, before_sub, before_layer),
         "coarse_tiles",
     )
-    column = lax.all_to_all(copies, "sub", split_axis=0, concat_axis=0, tiled=True)
-    columns = jnp.broadcast_to(column[None], (layers,) + column.shape)
-    plane_tiles = lax.all_to_all(columns, "layer", split_axis=0, concat_axis=0, tiled=True)
+    tiles = lax.all_to_all(copies, ("sub", "layer"), split_axis=0, concat_axis=0, tiled=True)
+    after_sub = lax.ppermute(sub_send, "sub", down_sub)
+    after_layer = lax.ppermute(layer_send, "layer", down_layer)
     (applied,) = local_call(
-        functools.partial(scatter_kernel, subs=subs),
+        functools.partial(scatter_kernel, subs=subs, layers=layers),
         [(modes, row_count)],
-        (place, base, row_lists, face_springs, picked, sub_rim, next_rim, layer_rim),
+        (base, row_lists, face_springs, picked, before_sub, after_sub, before_layer, after_layer),
         "spread_rows",
     )
-    diag_strip, left_strip, right_strip = factor_planes(place, plane_tiles, modes)
+    diag_strip, left_strip, right_strip = factor_planes(
+        tiles.reshape(subs, layers, *tiles.shape[1:]), modes, applied
+    )
     return (applied[None, None], diag_strip[None], left_strip[None], right_strip[None])
 
 

time: 61 us -> 49.2 us (0.81)
  the two profiles are of different devices: /device:TPU:1 before, /device:TPU:0 now
where the time goes in v4:
time: 49.2 us; the launch traced here: 48.7 us
  Pallas kernels  22.1 us (45%)
  starting transfers between devices  14.7 us (30%)
  waiting for transfers between devices  7.05 us (14%)
  local copies, waits for them, and re-layouts  4.18 us (8%)
  between operations  0.73 us (1%)
    pallas_call x1, Pallas kernels, factor_planes(): pl.pallas_call(factor_kernel, out_shape=(strip, strip, strip), in_specs=[...  18 us
    all_to_all x1, starting transfers between devices, per_device(): lax.all_to_all(copies, ('sub', 'layer'), split_axis=0, concat_axis=0, til...  5.55 us
    ppermute x1, starting transfers between devices, per_device(): before_layer = lax.ppermute(layer_send, 'layer', up_layer)  4.23 us
    unnamed x14, local copies, waits for them, and re-layouts  4.18 us
    pallas_call x4, Pallas kernels, local_call(): pl.pallas_call(body, out_shape=shapes, in_specs=[VMEM_BLOCK] * len(operan...  4.05 us
    ppermute x1, waiting for transfers between devices, per_device(): after_layer = lax.ppermute(layer_send, 'layer', down_layer)  3.82 us
    all_to_all x1, waiting for transfers between devices, per_device(): lax.all_to_all(copies, ('sub', 'layer'), split_axis=0, concat_axis=0, til...  2.75 us
    ppermute x1, starting transfers between devices, per_device(): before_sub = lax.ppermute(sub_send, 'sub', up_sub)  2.36 us
  transfers between devices with their start and end apart: 5, of which 3 were waited for; matrix products, arithmetic and copies ran while one was open for 0% of the time, Pallas kernels for 5%

profile of v4, /device:TPU:0, one launch (start us, length us, event | category | flops | bytes accessed | tf_op | source)
XLA Modules:
  0.0 48.7 jit_solution(16497859034270600079)
XLA Ops:
  0.6 0.0 copy-start.6
  0.6 0.0 copy-start.5
  0.7 0.7 %copy-done.6 = s32[1,1,4,128]{3,2,1,0:T(4,128)S(1)} copy-done((s32[1,1,4,128]{3,2,1,0:T(4,128)S(1)}, s32[1,1,4,128]{3,2,1,0:T(4,128)}, u32[]{:S(2)}) %copy-start.6) | copy-done | bytes 2072
  1.3 0.0 copy-done.5
  1.3 0.0 copy-start.1
  1.3 1.0 %copy-done.1 = f32[1,1,24,4096]{3,2,1,0:T(8,128)S(1)} copy-done((f32[1,1,24,4096]{3,2,1,0:T(8,128)S(1)}, f32[1,1,24,4096]{3,2,1,0:T(8,128)}, u32[]{:S(2)}) %copy-start.1) | copy-done | bytes 393240
  2.3 0.0 copy-start.2
  2.3 0.5 %pick_rows.1 = (f32[4,24,128]{2,1,0:T(8,128)S(1)}, f32[32,128]{1,0:T(8,128)S(1)}, f32[32,128]{1,0:T(8,128)S(1)}) custom-call(f32[24,4096]{1,0:T(8,128)S(1)} %bitcast.11, s32[4,128]{1,0:T(4,128)S(1)} %bitcast.19, f32[2,128]{1,0:T(2,128)S(1)} %bitcast.16), custom_call_target="tpu_custom_call" | custom-call | tf_op jit(solution)/shard_map/pick_rows/pallas_call | solution.py:383
  2.8 2.4 %collective-permute-start = (f32[32,128]{1,0:T(8,128)S(1)}, f32[32,128]{1,0:T(8,128)S(1)}, u32[]{:S(2)}, u32[]{:S(2)}) collective-permute-start(f32[32,128]{1,0:T(8,128)S(1)} %get-tuple-element.17), channel_id=1, source_target_pairs={{0,4},{4,8},{8,12},{12,16},{16,20},{20,24},{24,28},{1,5},{5,9},{9,... | collective-permute-start | bytes 49160 | tf_op jit(solution)/shard_map/ppermute | solution.py:411
  5.2 4.2 %collective-permute-start.1 = (f32[32,128]{1,0:T(8,128)S(1)}, f32[32,128]{1,0:T(8,128)S(1)}, u32[]{:S(2)}, u32[]{:S(2)}) collective-permute-start(f32[32,128]{1,0:T(8,128)S(1)} %get-tuple-element.19), channel_id=1, source_target_pairs={{0,1},{1,2},{2,3},{4,5},{5,6},{6,7},{8,9},{9,10},{10,11},{12,13},{... | collective-permute-start | bytes 49160 | tf_op jit(solution)/shard_map/ppermute | solution.py:412
  9.4 0.0 copy-done.2
  9.4 0.0 copy-start.3
  9.4 0.8 %copy-done.3 = f32[1,1,3,4096]{3,1,2,0:T(1,128)S(1)} copy-done((f32[1,1,3,4096]{3,1,2,0:T(1,128)S(1)}, f32[1,1,3,4096]{3,1,2,0:T(1,128)}, u32[]{:S(2)}) %copy-start.3) | copy-done | bytes 49176
  10.2 0.0 copy-start.4
  10.2 0.7 %copy-done.4 = f32[1,1,4096]{2,1,0:T(1,128)S(1)} copy-done((f32[1,1,4096]{2,1,0:T(1,128)S(1)}, f32[1,1,4096]{2,1,0:T(1,128)}, u32[]{:S(2)}) %copy-start.4) | copy-done | bytes 16408
  10.9 1.2 %own_rows.1 = (f32[24,4096]{1,0:T(8,128)S(1)}, f32[24,24]{1,0:T(8,128)S(1)}) custom-call(f32[24,4096]{1,0:T(8,128)S(1)} %bitcast.12, f32[1,4096]{1,0:T(1,128)S(1)} %bitcast.15, f32[3,1,4096]{2,1,0:T(1,128)S(1)} %bitcast.14, f32[2,128]{1,0:T(2,128)S(1)} %bitcast.17, f32[4,24,128]{2,1,0:T(8,128)S(1)} %get-tuple-element.15.picked_ref), custom_call_target="tpu_custom_call" | custom-call | tf_op jit(solution)/shard_map/own_rows/pallas_call | solution.py:383
  12.1 0.0 collective-permute-done.sub_ref.before_sub_ref
  12.1 0.0 collective-permute-done.1.layer_ref.before_layer_ref
  12.1 1.1 %coarse_tiles.1 = (f32[32,16,128]{2,1,0:T(8,128)}, f32[24,128]{1,0:T(8,128)S(1)}, f32[24,128]{1,0:T(8,128)S(1)}) custom-call(f32[24,24]{1,0:T(8,128)S(1)} %get-tuple-element.18.own_ref, f32[4,24,128]{2,1,0:T(8,128)S(1)} %get-tuple-element.15.picked_ref, f32[32,128]{1,0:T(8,128)S(1)} %collective-permute-done.sub_ref.before_sub_ref, ...), custom_call_target="tpu_custom_call" | custom-call | tf_op jit(solution)/shard_map/coarse_tiles/pallas_call | solution.py:383
  13.2 5.5 %all-to-all-start = ((f32[32,16,128]{2,1,0:T(8,128)}), f32[32,16,128]{2,1,0:T(8,128)S(1)}, u32[]{:S(2)}, u32[]{:S(2)}) async-start(f32[32,16,128]{2,1,0:T(8,128)} %get-tuple-element.22), calls=%async_computation | async-start | bytes 524288 | tf_op jit(solution)/shard_map/all_to_all | solution.py:425
  18.8 1.3 %collective-permute-start.2 = (f32[24,128]{1,0:T(8,128)S(1)}, f32[24,128]{1,0:T(8,128)S(1)}, u32[]{:S(2)}, u32[]{:S(2)}) collective-permute-start(f32[24,128]{1,0:T(8,128)S(1)} %get-tuple-element.20), channel_id=1, source_target_pairs={{4,0},{8,4},{12,8},{16,12},{20,16},{24,20},{28,24},{5,1},{9,5},{13... | collective-permute-start | bytes 36872 | tf_op jit(solution)/shard_map/ppermute | solution.py:426
  20.1 1.3 %collective-permute-start.3 = (f32[24,128]{1,0:T(8,128)S(1)}, f32[24,128]{1,0:T(8,128)S(1)}, u32[]{:S(2)}, u32[]{:S(2)}) collective-permute-start(f32[24,128]{1,0:T(8,128)S(1)} %get-tuple-element.21), channel_id=1, source_target_pairs={{1,0},{2,1},{3,2},{5,4},{6,5},{7,6},{9,8},{10,9},{11,10},{13,12},{... | collective-permute-start | bytes 36872 | tf_op jit(solution)/shard_map/ppermute | solution.py:427
  21.4 0.5 collective-permute-done.2.after_sub_ref
  21.9 3.8 %collective-permute-done.3.after_layer_ref = f32[24,128]{1,0:T(8,128)S(1)} collective-permute-done((f32[24,128]{1,0:T(8,128)S(1)}, f32[24,128]{1,0:T(8,128)S(1)}, u32[]{:S(2)}, u32[]{:S(2)}) %collective-permute-start.3) | collective-permute-done | bytes 12320 | tf_op jit(solution)/shard_map/ppermute | solution.py:427
  25.7 1.3 %spread_rows.1.after_ref = f32[24,4096]{1,0:T(8,128)} custom-call(f32[24,4096]{1,0:T(8,128)S(1)} %get-tuple-element.16.base_ref, s32[4,128]{1,0:T(4,128)S(1)} %bitcast.20, f32[2,128]{1,0:T(2,128)S(1)} %bitcast.18, f32[4,24,128]{2,1,0:T(8,128)S(1)} %get-tuple-element.15.picked_ref, f32[32,128]{1,0:T(8,128)S(1)} %collective-permute-done.sub_ref.before_sub_ref, ...), custom_call_target="tpu_custom_call" | custom-call | tf_op jit(solution)/shard_map/spread_rows/pallas_call | solution.py:383
  27.0 2.7 %all-to-all-done = f32[32,16,128]{2,1,0:T(8,128)S(1)} async-done(((f32[32,16,128]{2,1,0:T(8,128)}), f32[32,16,128]{2,1,0:T(8,128)S(1)}, u32[]{:S(2)}, u32[]{:S(2)}) %all-to-all-start) | async-done | bytes 262176 | tf_op jit(solution)/shard_map/all_to_all | solution.py:425
  29.7 0.0 copy-start
  29.7 1.0 %copy-done = f32[24,4096]{1,0:T(8,128)S(1)} copy-done((f32[24,4096]{1,0:T(8,128)S(1)}, f32[24,4096]{1,0:T(8,128)}, u32[]{:S(2)}) %copy-start) | copy-done | bytes 393240
  30.7 18.0 %factor_planes.1 = (f32[24,96]{1,0:T(8,128)}, f32[24,96]{1,0:T(8,128)}, f32[24,96]{1,0:T(8,128)}) custom-call(f32[8,4,16,128]{3,2,1,0:T(8,128)S(1)} %bitcast.13, f32[24,4096]{1,0:T(8,128)S(1)} %copy-done), custom_call_target="tpu_custom_call" | custom-call | tf_op jit(solution)/shard_map/factor_planes/pallas_call | solution.py:259
Async XLA Ops:
  0.6 0.7 %copy-start.6 = (s32[1,1,4,128]{3,2,1,0:T(4,128)S(1)}, s32[1,1,4,128]{3,2,1,0:T(4,128)}, u32[]{:S(2)}) copy-start(s32[1,1,4,128]{3,2,1,0:T(4,128)} %param.9) | copy-start | bytes 6148
  0.6 0.7 %copy-start.5 = (f32[1,1,2,128]{3,2,1,0:T(2,128)S(1)}, f32[1,1,2,128]{3,2,1,0:T(2,128)}, u32[]{:S(2)}) copy-start(f32[1,1,2,128]{3,2,1,0:T(2,128)} %param.8) | copy-start | bytes 3076
  1.3 1.0 %copy-start.1 = (f32[1,1,24,4096]{3,2,1,0:T(8,128)S(1)}, f32[1,1,24,4096]{3,2,1,0:T(8,128)}, u32[]{:S(2)}) copy-start(f32[1,1,24,4096]{3,2,1,0:T(8,128)} %param.5) | copy-start | bytes 1179652
  2.3 7.1 %copy-start.2 = (f32[1,1,24,4096]{3,2,1,0:T(8,128)S(1)}, f32[1,1,24,4096]{3,2,1,0:T(8,128)}, u32[]{:S(2)}) copy-start(f32[1,1,24,4096]{3,2,1,0:T(8,128)} %param.5) | copy-start | bytes 1179652
  2.8 9.3 %collective-permute-start = (f32[32,128]{1,0:T(8,128)S(1)}, f32[32,128]{1,0:T(8,128)S(1)}, u32[]{:S(2)}, u32[]{:S(2)}) collective-permute-start(f32[32,128]{1,0:T(8,128)S(1)} %get-tuple-element.17), channel_id=1, source_target_pairs={{0,4},{4,8},{8,12},{12,16},{16,20},{20,24},{24,28},{1,5},{5,9},{9,... | collective-permute-start | bytes 49160 | tf_op jit(solution)/shard_map/ppermute | solution.py:411
  5.2 6.9 %collective-permute-start.1 = (f32[32,128]{1,0:T(8,128)S(1)}, f32[32,128]{1,0:T(8,128)S(1)}, u32[]{:S(2)}, u32[]{:S(2)}) collective-permute-start(f32[32,128]{1,0:T(8,128)S(1)} %get-tuple-element.19), channel_id=1, source_target_pairs={{0,1},{1,2},{2,3},{4,5},{5,6},{6,7},{8,9},{9,10},{10,11},{12,13},{... | collective-permute-start | bytes 49160 | tf_op jit(solution)/shard_map/ppermute | solution.py:412
  9.4 0.8 %copy-start.3 = (f32[1,1,3,4096]{3,1,2,0:T(1,128)S(1)}, f32[1,1,3,4096]{3,1,2,0:T(1,128)}, u32[]{:S(2)}) copy-start(f32[1,1,3,4096]{3,1,2,0:T(1,128)} %param.7) | copy-start | bytes 147460
  10.2 0.7 %copy-start.4 = (f32[1,1,4096]{2,1,0:T(1,128)S(1)}, f32[1,1,4096]{2,1,0:T(1,128)}, u32[]{:S(2)}) copy-start(f32[1,1,4096]{2,1,0:T(1,128)} %param.6) | copy-start | bytes 49156
  13.2 16.5 %all-to-all-start = ((f32[32,16,128]{2,1,0:T(8,128)}), f32[32,16,128]{2,1,0:T(8,128)S(1)}, u32[]{:S(2)}, u32[]{:S(2)}) async-start(f32[32,16,128]{2,1,0:T(8,128)} %get-tuple-element.22), calls=%async_computation | async-start | bytes 524288 | tf_op jit(solution)/shard_map/all_to_all | solution.py:425
  18.8 3.1 %collective-permute-start.2 = (f32[24,128]{1,0:T(8,128)S(1)}, f32[24,128]{1,0:T(8,128)S(1)}, u32[]{:S(2)}, u32[]{:S(2)}) collective-permute-start(f32[24,128]{1,0:T(8,128)S(1)} %get-tuple-element.20), channel_id=1, source_target_pairs={{4,0},{8,4},{12,8},{16,12},{20,16},{24,20},{28,24},{5,1},{9,5},{13... | collective-permute-start | bytes 36872 | tf_op jit(solution)/shard_map/ppermute | solution.py:426
  20.1 5.6 %collective-permute-start.3 = (f32[24,128]{1,0:T(8,128)S(1)}, f32[24,128]{1,0:T(8,128)S(1)}, u32[]{:S(2)}, u32[]{:S(2)}) collective-permute-start(f32[24,128]{1,0:T(8,128)S(1)} %get-tuple-element.21), channel_id=1, source_target_pairs={{1,0},{2,1},{3,2},{5,4},{6,5},{7,6},{9,8},{10,9},{11,10},{13,12},{... | collective-permute-start | bytes 36872 | tf_op jit(solution)/shard_map/ppermute | solution.py:427
  29.7 1.0 %copy-start = (f32[24,4096]{1,0:T(8,128)S(1)}, f32[24,4096]{1,0:T(8,128)}, u32[]{:S(2)}) copy-start(f32[24,4096]{1,0:T(8,128)} %spread_rows.1.after_ref) | copy-start | bytes 1179652

commit v5 on v4

--- a/solution.py
+++ b/solution.py
@@ -32,6 +32,10 @@
         precision=HIGHEST,
         preferred_element_type=jnp.float32,
     )
+
+
+def spread_row(strip, k):
+    return jnp.broadcast_to(strip[k : k + 1, :], strip.shape)
 
 
 def factor_rows(blocks, tiles_per_part, first_row, turned):
@@ -51,20 +55,31 @@
                 for j in range(ROWS)
             ]
             pivots = jnp.zeros((ROWS, LANES), jnp.float32)
-            for k in range(ROWS):
-                pivot = columns[k][0][k : k + 1, :]
-                inverse = 1.0 / pivot
-                pivots = jnp.where(iota == k, pivot, pivots)
-                below = [jnp.where(iota > k, columns[k][0], 0.0)] + columns[k][1:]
-                below = [column * inverse for column in below]
-                for j in range(k + 1, ROWS):
-                    other = columns[k][0][j : j + 1, :]
+            for k in range(0, ROWS, 2):
+                first, second = columns[k], columns[k + 1]
+                corner, joint = spread_row(first[0], k), spread_row(first[0], k + 1)
+                other_corner = spread_row(second[0], k + 1)
+                minor = corner * other_corner - joint * joint
+                inverse = pl.reciprocal(corner, approx=True)
+                other_inverse = corner * pl.reciprocal(minor, approx=True)
+                pivots = jnp.where(iota == k, corner, pivots)
+                pivots = jnp.where(iota == k + 1, minor * inverse, pivots)
+                below = [column * inverse for column in first]
+                second = [second[r] - below[r] * joint for r in range(len(second))]
+                other_below = [column * other_inverse for column in second]
+                below[0] = jnp.where(iota > k, below[0], 0.0)
+                other_below[0] = jnp.where(iota > k + 1, other_below[0], 0.0)
+                for j in range(k + 2, ROWS):
+                    head, other_head = spread_row(first[0], j), spread_row(second[0], j)
                     for r in range(strip_count - q):
-                        columns[j][r] = columns[j][r] - below[r] * other
+                        columns[j][r] = columns[j][r] - below[r] * head - other_below[r] * other_head
                 for t in range(len(block[q])):
-                    row = block[q][t][k : k + 1, :]
+                    row = spread_row(block[q][t], k)
                     for r in range(strip_count - q):
                         block[q + r][t] = block[q + r][t] - below[r] * row
+                    row = spread_row(block[q][t], k + 1)
+                    for r in range(strip_count - q):
+                        block[q + r][t] = block[q + r][t] - other_below[r] * row
             scale = lax.rsqrt(pivots)
             for t in range(len(block[q])):
                 strip = block[q][t] * scale
@@ -75,7 +90,7 @@
     return blocks
 
 
-def eliminate_panel(grid_ref, planes, modes, order, part, lanes_used, panel):
+def eliminate_panel(grid_ref, planes, modes, order, part, lanes_used, panel, banded):
     per_part = part // LANES
     first_row = panel * modes
     static = isinstance(panel, int)
@@ -114,10 +129,11 @@
         grid_ref[plane, rows, 0:lanes_used] = panel_rows
         if static:
             below = (panel + 1) * modes
+            end = min(below + modes, order) if banded else order
             if below < order:
-                columns = panel_rows[:, 0:part].T[below:order]
+                columns = panel_rows[:, 0:part].T[below:end]
                 update = plain_dot(columns, panel_rows)
-                grid_ref[plane, below:order, 0:lanes_used] -= update
+                grid_ref[plane, below:end, 0:lanes_used] -= update
         else:
             lane = lax.broadcasted_iota(jnp.int32, (modes, part), 1)
             columns = jnp.where(lane >= first_row + modes, panel_rows[:, 0:part], 0.0)
@@ -125,15 +141,15 @@
             grid_ref[plane, :, 0:lanes_used] -= update
 
 
-def eliminate_planes(grid_ref, planes, modes, order, part, lanes_used):
+def eliminate_planes(grid_ref, planes, modes, order, part, lanes_used, banded=False):
     layers = order // modes
     if layers <= UNROLLED_LAYERS:
         for panel in range(layers):
-            eliminate_panel(grid_ref, planes, modes, order, part, lanes_used, panel)
+            eliminate_panel(grid_ref, planes, modes, order, part, lanes_used, panel, banded)
     else:
 
         def one_panel(panel, carry):
-            eliminate_panel(grid_ref, planes, modes, order, part, lanes_used, panel)
+            eliminate_panel(grid_ref, planes, modes, order, part, lanes_used, panel, banded)
             return carry
 
         lax.fori_loop(0, layers, one_panel, 0)
@@ -218,7 +234,7 @@
     while distance < subs:
         if unrolled:
             planes = list(range(distance - 1, subs, 2 * distance))
-            eliminate_planes(grid_ref, planes, modes, order, part, 3 * part)
+            eliminate_planes(grid_ref, planes, modes, order, part, 3 * part, distance == 1)
             for plane in planes:
                 update_partners(grid_ref, plane, distance, part, order, plane >= distance)
         else:
@@ -259,7 +275,7 @@
     return pl.pallas_call(
         factor_kernel,
         out_shape=(strip, strip, strip),
-        in_specs=[VMEM_BLOCK, pl.BlockSpec(memory_space=pl.ANY)],
+        in_specs=[VMEM_BLOCK, VMEM_BLOCK],
         out_specs=(VMEM_BLOCK, VMEM_BLOCK, VMEM_BLOCK),
         scratch_shapes=[pltpu.VMEM(shape, jnp.float32) for shape in scratch],
         compiler_params=kernel_params((plane_tiles.shape,) + scratch),
@@ -277,19 +293,39 @@
     )
 
 
-def pick_kernel(vectors_ref, lists_ref, face_ref, picked_ref, sub_ref, layer_ref):
+def pick_kernel(
+    vectors_in, lists_in, face_in, mass_in, inner_in,
+    vectors_ref, lists_ref, face_ref, mass_ref, inner_ref, picked_ref, sub_ref, layer_ref, sems
+):
     modes, row_count = vectors_ref.shape
+    strips = modes // ROWS
+    pairs = [(lists_in, lists_ref)]
+    pairs += [
+        (vectors_in.at[pl.ds(r * ROWS, ROWS)], vectors_ref.at[pl.ds(r * ROWS, ROWS)])
+        for r in range(strips)
+    ]
+    pairs += [(face_in, face_ref), (mass_in, mass_ref), (inner_in, inner_ref)]
+    copies = [pltpu.make_async_copy(a, b, sems.at[i]) for i, (a, b) in enumerate(pairs)]
+    for copy in copies:
+        copy.start()
+    copies[0].wait()
+    lists = []
     for k in range(4):
         rows = jnp.broadcast_to(lists_ref[k : k + 1, :], (ROWS, LANES))
-        tile_of, lane_of = rows // LANES, rows % LANES
-        found = [jnp.zeros((ROWS, LANES), jnp.float32) for _ in range(modes // ROWS)]
+        lists.append((rows // LANES, rows % LANES))
+    for r in range(strips):
+        copies[1 + r].wait()
+        strip = slice(r * ROWS, (r + 1) * ROWS)
+        found = [jnp.zeros((ROWS, LANES), jnp.float32) for _ in range(4)]
         for c in range(row_count // LANES):
-            here = tile_of == c
-            for r in range(modes // ROWS):
-                tile = vectors_ref[r * ROWS : (r + 1) * ROWS, c * LANES : (c + 1) * LANES]
+            tile = vectors_ref[strip, c * LANES : (c + 1) * LANES]
+            for k, (tile_of, lane_of) in enumerate(lists):
                 moved = jnp.take_along_axis(tile, lane_of, axis=1, mode="promise_in_bounds")
-                found[r] = jnp.where(here, moved, found[r])
-        picked_ref[k] = jnp.concatenate(found, axis=0)
+                found[k] = jnp.where(tile_of == c, moved, found[k])
+        for k in range(4):
+            picked_ref[k, strip] = found[k]
+    for copy in copies[1 + strips :]:
+        copy.wait()
     for k, send_ref in ((0, sub_ref), (2, layer_ref)):
         send_ref[0:modes] = picked_ref[k]
         send_ref[modes:] = jnp.broadcast_to(face_ref[k // 2 : k // 2 + 1, :], (ROWS, LANES))
@@ -338,7 +374,7 @@
 
 def scatter_kernel(
     base_ref, lists_ref, face_ref, picked_ref, before_sub_ref, after_sub_ref,
-    before_layer_ref, after_layer_ref, applied_ref, *, subs, layers
+    before_layer_ref, after_layer_ref, applied_ref, token_ref, *, subs, layers
 ):
     modes, row_count = base_ref.shape
     width = 2 * LANES
@@ -376,6 +412,7 @@
     for h in range(row_count // width):
         lanes = slice(h * width, (h + 1) * width)
         applied_ref[:, lanes] = base_ref[:, lanes] + total[h * modes : (h + 1) * modes]
+    token_ref[...] = jnp.zeros_like(token_ref)
 
 
 def local_call(body, outputs, operands, name):
@@ -402,18 +439,25 @@
     up_layer = [(i, i + 1) for i in range(layers - 1)]
     down_sub = [(i + 1, i) for i in range(subs - 1)]
     down_layer = [(i + 1, i) for i in range(layers - 1)]
-    picked, sub_send, layer_send = local_call(
+    taken = (vectors, row_lists, face_springs, row_mass[0], inner_weight[0].reshape(-1, 1, row_count))
+    held = [(x.shape, x.dtype) for x in taken]
+    made = [(4, modes, width), (modes + ROWS, width), (modes + ROWS, width)]
+    held += [(shape, jnp.float32) for shape in made]
+    vectors, row_lists, face_springs, masses, interior, picked, sub_send, layer_send = pl.pallas_call(
         pick_kernel,
-        [(4, modes, width), (modes + ROWS, width), (modes + ROWS, width)],
-        (vectors, row_lists, face_springs),
-        "pick_rows",
-    )
+        out_shape=tuple(jax.ShapeDtypeStruct(*pair) for pair in held),
+        in_specs=[pl.BlockSpec(memory_space=pltpu.HBM)] * len(taken),
+        out_specs=(VMEM_BLOCK,) * len(held),
+        scratch_shapes=[pltpu.SemaphoreType.DMA((len(taken) + modes // ROWS - 1,))],
+        compiler_params=kernel_params([shape for shape, _ in held]),
+        name="pick_rows",
+    )(*(pltpu.with_memory_space_constraint(x, pltpu.HBM) for x in taken))
     before_sub = lax.ppermute(sub_send, "sub", up_sub)
     before_layer = lax.ppermute(layer_send, "layer", up_layer)
     base, own = local_call(
         functools.partial(own_kernel, subs=subs, layers=layers),
         [(modes, row_count), (modes, modes)],
-        (vectors, row_mass[0], inner_weight[0].reshape(-1, 1, row_count), face_springs, picked),
+        (vectors, masses, interior, face_springs, picked),
         "own_rows",
     )
     copies, sub_send, layer_send = local_call(
@@ -425,14 +469,14 @@
     tiles = lax.all_to_all(copies, ("sub", "layer"), split_axis=0, concat_axis=0, tiled=True)
     after_sub = lax.ppermute(sub_send, "sub", down_sub)
     after_layer = lax.ppermute(layer_send, "layer", down_layer)
-    (applied,) = local_call(
+    applied, token = local_call(
         functools.partial(scatter_kernel, subs=subs, layers=layers),
-        [(modes, row_count)],
+        [(modes, row_count), (ROWS, LANES)],
         (base, row_lists, face_springs, picked, before_sub, after_sub, before_layer, after_layer),
         "spread_rows",
     )
     diag_strip, left_strip, right_strip = factor_planes(
-        tiles.reshape(subs, layers, *tiles.shape[1:]), modes, applied
+        tiles.reshape(subs, layers, *tiles.shape[1:]), modes, token
     )
     return (applied[None, None], diag_strip[None], left_strip[None], right_strip[None])
 

time: 49.2 us -> 47.2 us (0.959)
  local copies, waits for them, and re-layouts: 4.18 us -> 0 us
  starting transfers between devices: 14.7 us -> 16 us
  Pallas kernels: 22.1 us -> 23 us
    unnamed x14 -> x0, local copies, waits for them, and re-layouts: 4.18 us -> none
    pallas_call x0 -> x1, Pallas kernels: none -> 2.26 us  [per_device(): pl.pallas_call(pick_kernel, out_shape=tuple((jax.ShapeDtypeStruct(*pair)...]
    all_to_all x1, starting transfers between devices: 5.55 us -> 6.83 us  [per_device(): lax.all_to_all(copies, ('sub', 'layer'), split_axis=0, concat_axis=0, til...]
    pallas_call x1, Pallas kernels: 18 us -> 17.1 us  [factor_planes(): pl.pallas_call(factor_kernel, out_shape=(strip, strip, strip), in_specs=[...]
    pallas_call x4 -> x3, Pallas kernels: 4.05 us -> 3.58 us  [local_call(): pl.pallas_call(body, out_shape=shapes, in_specs=[VMEM_BLOCK] * len(operan...]
  transfers between devices with their start and end apart: 5 -> 5, of which waited for: 3 -> 4; matrix products, arithmetic and copies ran while one was open for 0% -> 0% of each run, Pallas kernels for 5% -> 5%
where the time goes in v5:
time: 47.2 us; the launch traced here: 46.9 us
  Pallas kernels  23 us (49%)
  starting transfers between devices  16 us (34%)
  waiting for transfers between devices  7.3 us (15%)
  between operations  0.68 us (1%)
    pallas_call x1, Pallas kernels, factor_planes(): pl.pallas_call(factor_kernel, out_shape=(strip, strip, strip), in_specs=[...  17.1 us
    all_to_all x1, starting transfers between devices, per_device(): lax.all_to_all(copies, ('sub', 'layer'), split_axis=0, concat_axis=0, til...  6.83 us
    ppermute x1, starting transfers between devices, per_device(): before_layer = lax.ppermute(layer_send, 'layer', up_layer)  4.23 us
    ppermute x1, waiting for transfers between devices, per_device(): after_layer = lax.ppermute(layer_send, 'layer', down_layer)  3.82 us
    pallas_call x3, Pallas kernels, local_call(): pl.pallas_call(body, out_shape=shapes, in_specs=[VMEM_BLOCK] * len(operan...  3.58 us
    all_to_all x1, waiting for transfers between devices, per_device(): lax.all_to_all(copies, ('sub', 'layer'), split_axis=0, concat_axis=0, til...  2.75 us
    ppermute x1, starting transfers between devices, per_device(): before_sub = lax.ppermute(sub_send, 'sub', up_sub)  2.36 us
    pallas_call x1, Pallas kernels, per_device(): pl.pallas_call(pick_kernel, out_shape=tuple((jax.ShapeDtypeStruct(*pair)...  2.26 us
  transfers between devices with their start and end apart: 5, of which 4 were waited for; matrix products, arithmetic and copies ran while one was open for 0% of the time, Pallas kernels for 5%

profile of v5, /device:TPU:0, one launch (start us, length us, event | category | flops | bytes accessed | tf_op | source)
XLA Modules:
  0.0 46.9 jit_solution(11596777544209207508)
XLA Ops:
  0.6 2.3 %pick_rows.1 = (f32[24,4096]{1,0:T(8,128)S(1)}, s32[4,128]{1,0:T(4,128)S(1)}, f32[2,128]{1,0:T(2,128)S(1)}, f32[1,4096]{1,0:T(1,128)S(1)}, f32[3,1,4096]{2,1,0:T...) custom-call(f32[24,4096]{1,0:T(8,128)} %bitcast.11, s32[4,128]{1,0:T(4,128)} %bitcast.14, ...), custom_call_target="tpu_custom_call" | custom-call | tf_op jit(solution)/shard_map/pick_rows/pallas_call | solution.py:446
  2.9 2.4 %collective-permute-start = (f32[32,128]{1,0:T(8,128)S(1)}, f32[32,128]{1,0:T(8,128)S(1)}, u32[]{:S(2)}, u32[]{:S(2)}) collective-permute-start(f32[32,128]{1,0:T(8,128)S(1)} %get-tuple-element.29), channel_id=1, source_target_pairs={{0,4},{4,8},{8,12},{12,16},{16,20},{20,24},{24,28},{1,5},{5,9},{9,... | collective-permute-start | bytes 49160 | tf_op jit(solution)/shard_map/ppermute | solution.py:455
  5.3 4.2 %collective-permute-start.1 = (f32[32,128]{1,0:T(8,128)S(1)}, f32[32,128]{1,0:T(8,128)S(1)}, u32[]{:S(2)}, u32[]{:S(2)}) collective-permute-start(f32[32,128]{1,0:T(8,128)S(1)} %get-tuple-element.31), channel_id=1, source_target_pairs={{0,1},{1,2},{2,3},{4,5},{5,6},{6,7},{8,9},{9,10},{10,11},{12,13},{... | collective-permute-start | bytes 49160 | tf_op jit(solution)/shard_map/ppermute | solution.py:456
  9.5 1.2 %own_rows.1 = (f32[24,4096]{1,0:T(8,128)S(1)}, f32[24,24]{1,0:T(8,128)S(1)}) custom-call(f32[24,4096]{1,0:T(8,128)S(1)} %get-tuple-element.22.vectors_ref, f32[1,4096]{1,0:T(1,128)S(1)} %get-tuple-element.23.mass_ref, f32[3,1,4096]{2,1,0:T(1,128)S(1)} %get-tuple-element.24.inner_ref, f32[2,128]{1,0:T(2,128)S(1)} %get-tuple-element.25.face_ref, ...), custom_call_target="tpu_custom_call" | custom-call | tf_op jit(solution)/shard_map/own_rows/pallas_call | solution.py:420
  10.7 0.0 collective-permute-done.sub_ref.before_sub_ref
  10.7 0.3 collective-permute-done.1.layer_ref.before_layer_ref
  10.9 1.1 %coarse_tiles.1 = (f32[32,16,128]{2,1,0:T(8,128)}, f32[24,128]{1,0:T(8,128)S(1)}, f32[24,128]{1,0:T(8,128)S(1)}) custom-call(f32[24,24]{1,0:T(8,128)S(1)} %get-tuple-element.30.own_ref, f32[4,24,128]{2,1,0:T(8,128)S(1)} %get-tuple-element.26.picked_ref, f32[32,128]{1,0:T(8,128)S(1)} %collective-permute-done.sub_ref.before_sub_ref, ...), custom_call_target="tpu_custom_call" | custom-call | tf_op jit(solution)/shard_map/coarse_tiles/pallas_call | solution.py:420
  12.0 6.8 %all-to-all-start = ((f32[32,16,128]{2,1,0:T(8,128)}), f32[32,16,128]{2,1,0:T(8,128)S(1)}, u32[]{:S(2)}, u32[]{:S(2)}) async-start(f32[32,16,128]{2,1,0:T(8,128)} %get-tuple-element.35), calls=%async_computation | async-start | bytes 524288 | tf_op jit(solution)/shard_map/all_to_all | solution.py:469
  18.9 1.3 %collective-permute-start.2 = (f32[24,128]{1,0:T(8,128)S(1)}, f32[24,128]{1,0:T(8,128)S(1)}, u32[]{:S(2)}, u32[]{:S(2)}) collective-permute-start(f32[24,128]{1,0:T(8,128)S(1)} %get-tuple-element.32), channel_id=1, source_target_pairs={{4,0},{8,4},{12,8},{16,12},{20,16},{24,20},{28,24},{5,1},{9,5},{13... | collective-permute-start | bytes 36872 | tf_op jit(solution)/shard_map/ppermute | solution.py:470
  20.2 1.3 %collective-permute-start.3 = (f32[24,128]{1,0:T(8,128)S(1)}, f32[24,128]{1,0:T(8,128)S(1)}, u32[]{:S(2)}, u32[]{:S(2)}) collective-permute-start(f32[24,128]{1,0:T(8,128)S(1)} %get-tuple-element.33), channel_id=1, source_target_pairs={{1,0},{2,1},{3,2},{5,4},{6,5},{7,6},{9,8},{10,9},{11,10},{13,12},{... | collective-permute-start | bytes 36872 | tf_op jit(solution)/shard_map/ppermute | solution.py:471
  21.5 0.5 %collective-permute-done.2.after_sub_ref = f32[24,128]{1,0:T(8,128)S(1)} collective-permute-done((f32[24,128]{1,0:T(8,128)S(1)}, f32[24,128]{1,0:T(8,128)S(1)}, u32[]{:S(2)}, u32[]{:S(2)}) %collective-permute-start.2) | collective-permute-done | bytes 12320 | tf_op jit(solution)/shard_map/ppermute | solution.py:470
  21.9 3.8 %collective-permute-done.3.after_layer_ref = f32[24,128]{1,0:T(8,128)S(1)} collective-permute-done((f32[24,128]{1,0:T(8,128)S(1)}, f32[24,128]{1,0:T(8,128)S(1)}, u32[]{:S(2)}, u32[]{:S(2)}) %collective-permute-start.3) | collective-permute-done | bytes 12320 | tf_op jit(solution)/shard_map/ppermute | solution.py:471
  25.8 1.3 %spread_rows.1 = (f32[24,4096]{1,0:T(8,128)}, f32[8,128]{1,0:T(8,128)S(1)}) custom-call(f32[24,4096]{1,0:T(8,128)S(1)} %get-tuple-element.27.base_ref, s32[4,128]{1,0:T(4,128)S(1)} %get-tuple-element.28.lists_ref, f32[2,128]{1,0:T(2,128)S(1)} %get-tuple-element.25.face_ref, f32[4,24,128]{2,1,0:T(8,128)S(1)} %get-tuple-element.26.picked_ref, ...), custom_call_target="tpu_custom_call" | custom-call | tf_op jit(solution)/shard_map/spread_rows/pallas_call | solution.py:420
  27.1 2.7 %all-to-all-done = f32[32,16,128]{2,1,0:T(8,128)S(1)} async-done(((f32[32,16,128]{2,1,0:T(8,128)}), f32[32,16,128]{2,1,0:T(8,128)S(1)}, u32[]{:S(2)}, u32[]{:S(2)}) %all-to-all-start) | async-done | bytes 262176 | tf_op jit(solution)/shard_map/all_to_all | solution.py:469
  29.8 17.1 %factor_planes.1 = (f32[24,96]{1,0:T(8,128)}, f32[24,96]{1,0:T(8,128)}, f32[24,96]{1,0:T(8,128)}) custom-call(f32[8,4,16,128]{3,2,1,0:T(8,128)S(1)} %bitcast.10, f32[8,128]{1,0:T(8,128)S(1)} %get-tuple-element.36.after_ref), custom_call_target="tpu_custom_call" | custom-call | tf_op jit(solution)/shard_map/factor_planes/pallas_call | solution.py:275
Async XLA Ops:
  2.9 7.8 %collective-permute-start = (f32[32,128]{1,0:T(8,128)S(1)}, f32[32,128]{1,0:T(8,128)S(1)}, u32[]{:S(2)}, u32[]{:S(2)}) collective-permute-start(f32[32,128]{1,0:T(8,128)S(1)} %get-tuple-element.29), channel_id=1, source_target_pairs={{0,4},{4,8},{8,12},{12,16},{16,20},{20,24},{24,28},{1,5},{5,9},{9,... | collective-permute-start | bytes 49160 | tf_op jit(solution)/shard_map/ppermute | solution.py:455
  5.3 5.7 %collective-permute-start.1 = (f32[32,128]{1,0:T(8,128)S(1)}, f32[32,128]{1,0:T(8,128)S(1)}, u32[]{:S(2)}, u32[]{:S(2)}) collective-permute-start(f32[32,128]{1,0:T(8,128)S(1)} %get-tuple-element.31), channel_id=1, source_target_pairs={{0,1},{1,2},{2,3},{4,5},{5,6},{6,7},{8,9},{9,10},{10,11},{12,13},{... | collective-permute-start | bytes 49160 | tf_op jit(solution)/shard_map/ppermute | solution.py:456
  12.0 17.8 %all-to-all-start = ((f32[32,16,128]{2,1,0:T(8,128)}), f32[32,16,128]{2,1,0:T(8,128)S(1)}, u32[]{:S(2)}, u32[]{:S(2)}) async-start(f32[32,16,128]{2,1,0:T(8,128)} %get-tuple-element.35), calls=%async_computation | async-start | bytes 524288 | tf_op jit(solution)/shard_map/all_to_all | solution.py:469
  18.9 3.1 %collective-permute-start.2 = (f32[24,128]{1,0:T(8,128)S(1)}, f32[24,128]{1,0:T(8,128)S(1)}, u32[]{:S(2)}, u32[]{:S(2)}) collective-permute-start(f32[24,128]{1,0:T(8,128)S(1)} %get-tuple-element.32), channel_id=1, source_target_pairs={{4,0},{8,4},{12,8},{16,12},{20,16},{24,20},{28,24},{5,1},{9,5},{13... | collective-permute-start | bytes 36872 | tf_op jit(solution)/shard_map/ppermute | solution.py:470
  20.2 5.6 %collective-permute-start.3 = (f32[24,128]{1,0:T(8,128)S(1)}, f32[24,128]{1,0:T(8,128)S(1)}, u32[]{:S(2)}, u32[]{:S(2)}) collective-permute-start(f32[24,128]{1,0:T(8,128)S(1)} %get-tuple-element.33), channel_id=1, source_target_pairs={{1,0},{2,1},{3,2},{5,4},{6,5},{7,6},{9,8},{10,9},{11,10},{13,12},{... | collective-permute-start | bytes 36872 | tf_op jit(solution)/shard_map/ppermute | solution.py:471

commit v6 on v5

--- a/solution.py
+++ b/solution.py
@@ -144,8 +144,9 @@
 def eliminate_planes(grid_ref, planes, modes, order, part, lanes_used, banded=False):
     layers = order // modes
     if layers <= UNROLLED_LAYERS:
-        for panel in range(layers):
-            eliminate_panel(grid_ref, planes, modes, order, part, lanes_used, panel, banded)
+        height = modes if banded else modes * max(1, layers // len(planes))
+        for panel in range(order // height):
+            eliminate_panel(grid_ref, planes, height, order, part, lanes_used, panel, banded)
     else:
 
         def one_panel(panel, carry):
@@ -206,17 +207,18 @@
     def place_tiles(s, has_left):
         for j in range(layers):
             tile = unpack_tile(tiles_ref[s, j], modes)
+            turned = tile.T
             rows = slice(j * modes, (j + 1) * modes)
             grid_ref[s, rows, j * modes : (j + 1) * modes] = tile[:, 0:modes]
             if j > 0:
                 above = slice((j - 1) * modes, j * modes)
                 grid_ref[s, above, j * modes : (j + 1) * modes] = tile[:, modes : 2 * modes]
+                grid_ref[s, rows, (j - 1) * modes : j * modes] = turned[modes : 2 * modes]
             if has_left:
-                down_turned = tile[:, 2 * modes : 3 * modes]
                 lanes = slice(part + j * modes, part + (j + 1) * modes)
-                grid_ref[s, rows, lanes] = down_turned.T
+                grid_ref[s, rows, lanes] = turned[2 * modes : 3 * modes]
                 lanes = slice(2 * part + j * modes, 2 * part + (j + 1) * modes)
-                grid_ref[s - 1, rows, lanes] = down_turned
+                grid_ref[s - 1, rows, lanes] = tile[:, 2 * modes : 3 * modes]
 
     place_tiles(0, False)
     if unrolled:

time: 47.2 us -> 48.2 us (1.021)
  Pallas kernels: 23 us -> 23.9 us
    pallas_call x1, Pallas kernels: 17.1 us -> 18.1 us  [factor_planes(): pl.pallas_call(factor_kernel, out_shape=(strip, strip, strip), in_specs=[...]
where the time goes in v6:
time: 48.2 us; the launch traced here: 47.9 us
  Pallas kernels  23.9 us (50%)
  starting transfers between devices  16 us (33%)
  waiting for transfers between devices  7.3 us (15%)
  between operations  0.68 us (1%)
    pallas_call x1, Pallas kernels, factor_planes(): pl.pallas_call(factor_kernel, out_shape=(strip, strip, strip), in_specs=[...  18.1 us
    all_to_all x1, starting transfers between devices, per_device(): lax.all_to_all(copies, ('sub', 'layer'), split_axis=0, concat_axis=0, til...  6.83 us
    ppermute x1, starting transfers between devices, per_device(): before_layer = lax.ppermute(layer_send, 'layer', up_layer)  4.23 us
    ppermute x1, waiting for transfers between devices, per_device(): after_layer = lax.ppermute(layer_send, 'layer', down_layer)  3.82 us
    pallas_call x3, Pallas kernels, local_call(): pl.pallas_call(body, out_shape=shapes, in_specs=[VMEM_BLOCK] * len(operan...  3.58 us
    all_to_all x1, waiting for transfers between devices, per_device(): lax.all_to_all(copies, ('sub', 'layer'), split_axis=0, concat_axis=0, til...  2.75 us
    ppermute x1, starting transfers between devices, per_device(): before_sub = lax.ppermute(sub_send, 'sub', up_sub)  2.36 us
    pallas_call x1, Pallas kernels, per_device(): pl.pallas_call(pick_kernel, out_shape=tuple((jax.ShapeDtypeStruct(*pair)...  2.26 us
  transfers between devices with their start and end apart: 5, of which 4 were waited for; matrix products, arithmetic and copies ran while one was open for 0% of the time, Pallas kernels for 5%

profile of v6, /device:TPU:0, one launch (start us, length us, event | category | flops | bytes accessed | tf_op | source)
XLA Modules:
  0.0 47.9 jit_solution(9065489998907323835)
XLA Ops:
  0.6 2.3 %pick_rows.1 = (f32[24,4096]{1,0:T(8,128)S(1)}, s32[4,128]{1,0:T(4,128)S(1)}, f32[2,128]{1,0:T(2,128)S(1)}, f32[1,4096]{1,0:T(1,128)S(1)}, f32[3,1,4096]{2,1,0:T...) custom-call(f32[24,4096]{1,0:T(8,128)} %bitcast.11, s32[4,128]{1,0:T(4,128)} %bitcast.14, ...), custom_call_target="tpu_custom_call" | custom-call | tf_op jit(solution)/shard_map/pick_rows/pallas_call | solution.py:448
  2.9 2.4 %collective-permute-start = (f32[32,128]{1,0:T(8,128)S(1)}, f32[32,128]{1,0:T(8,128)S(1)}, u32[]{:S(2)}, u32[]{:S(2)}) collective-permute-start(f32[32,128]{1,0:T(8,128)S(1)} %get-tuple-element.29), channel_id=1, source_target_pairs={{0,4},{4,8},{8,12},{12,16},{16,20},{20,24},{24,28},{1,5},{5,9},{9,... | collective-permute-start | bytes 49160 | tf_op jit(solution)/shard_map/ppermute | solution.py:457
  5.3 4.2 %collective-permute-start.1 = (f32[32,128]{1,0:T(8,128)S(1)}, f32[32,128]{1,0:T(8,128)S(1)}, u32[]{:S(2)}, u32[]{:S(2)}) collective-permute-start(f32[32,128]{1,0:T(8,128)S(1)} %get-tuple-element.31), channel_id=1, source_target_pairs={{0,1},{1,2},{2,3},{4,5},{5,6},{6,7},{8,9},{9,10},{10,11},{12,13},{... | collective-permute-start | bytes 49160 | tf_op jit(solution)/shard_map/ppermute | solution.py:458
  9.5 1.2 %own_rows.1 = (f32[24,4096]{1,0:T(8,128)S(1)}, f32[24,24]{1,0:T(8,128)S(1)}) custom-call(f32[24,4096]{1,0:T(8,128)S(1)} %get-tuple-element.22.vectors_ref, f32[1,4096]{1,0:T(1,128)S(1)} %get-tuple-element.23.mass_ref, f32[3,1,4096]{2,1,0:T(1,128)S(1)} %get-tuple-element.24.inner_ref, f32[2,128]{1,0:T(2,128)S(1)} %get-tuple-element.25.face_ref, ...), custom_call_target="tpu_custom_call" | custom-call | tf_op jit(solution)/shard_map/own_rows/pallas_call | solution.py:422
  10.7 0.0 collective-permute-done.sub_ref.before_sub_ref
  10.7 0.3 collective-permute-done.1.layer_ref.before_layer_ref
  10.9 1.1 %coarse_tiles.1 = (f32[32,16,128]{2,1,0:T(8,128)}, f32[24,128]{1,0:T(8,128)S(1)}, f32[24,128]{1,0:T(8,128)S(1)}) custom-call(f32[24,24]{1,0:T(8,128)S(1)} %get-tuple-element.30.own_ref, f32[4,24,128]{2,1,0:T(8,128)S(1)} %get-tuple-element.26.picked_ref, f32[32,128]{1,0:T(8,128)S(1)} %collective-permute-done.sub_ref.before_sub_ref, ...), custom_call_target="tpu_custom_call" | custom-call | tf_op jit(solution)/shard_map/coarse_tiles/pallas_call | solution.py:422
  12.0 6.8 %all-to-all-start = ((f32[32,16,128]{2,1,0:T(8,128)}), f32[32,16,128]{2,1,0:T(8,128)S(1)}, u32[]{:S(2)}, u32[]{:S(2)}) async-start(f32[32,16,128]{2,1,0:T(8,128)} %get-tuple-element.35), calls=%async_computation | async-start | bytes 524288 | tf_op jit(solution)/shard_map/all_to_all | solution.py:471
  18.9 1.3 %collective-permute-start.2 = (f32[24,128]{1,0:T(8,128)S(1)}, f32[24,128]{1,0:T(8,128)S(1)}, u32[]{:S(2)}, u32[]{:S(2)}) collective-permute-start(f32[24,128]{1,0:T(8,128)S(1)} %get-tuple-element.32), channel_id=1, source_target_pairs={{4,0},{8,4},{12,8},{16,12},{20,16},{24,20},{28,24},{5,1},{9,5},{13... | collective-permute-start | bytes 36872 | tf_op jit(solution)/shard_map/ppermute | solution.py:472
  20.2 1.3 %collective-permute-start.3 = (f32[24,128]{1,0:T(8,128)S(1)}, f32[24,128]{1,0:T(8,128)S(1)}, u32[]{:S(2)}, u32[]{:S(2)}) collective-permute-start(f32[24,128]{1,0:T(8,128)S(1)} %get-tuple-element.33), channel_id=1, source_target_pairs={{1,0},{2,1},{3,2},{5,4},{6,5},{7,6},{9,8},{10,9},{11,10},{13,12},{... | collective-permute-start | bytes 36872 | tf_op jit(solution)/shard_map/ppermute | solution.py:473
  21.5 0.5 collective-permute-done.2.after_sub_ref
  21.9 3.8 %collective-permute-done.3.after_layer_ref = f32[24,128]{1,0:T(8,128)S(1)} collective-permute-done((f32[24,128]{1,0:T(8,128)S(1)}, f32[24,128]{1,0:T(8,128)S(1)}, u32[]{:S(2)}, u32[]{:S(2)}) %collective-permute-start.3) | collective-permute-done | bytes 12320 | tf_op jit(solution)/shard_map/ppermute | solution.py:473
  25.8 1.3 %spread_rows.1 = (f32[24,4096]{1,0:T(8,128)}, f32[8,128]{1,0:T(8,128)S(1)}) custom-call(f32[24,4096]{1,0:T(8,128)S(1)} %get-tuple-element.27.base_ref, s32[4,128]{1,0:T(4,128)S(1)} %get-tuple-element.28.lists_ref, f32[2,128]{1,0:T(2,128)S(1)} %get-tuple-element.25.face_ref, f32[4,24,128]{2,1,0:T(8,128)S(1)} %get-tuple-element.26.picked_ref, ...), custom_call_target="tpu_custom_call" | custom-call | tf_op jit(solution)/shard_map/spread_rows/pallas_call | solution.py:422
  27.1 2.7 %all-to-all-done = f32[32,16,128]{2,1,0:T(8,128)S(1)} async-done(((f32[32,16,128]{2,1,0:T(8,128)}), f32[32,16,128]{2,1,0:T(8,128)S(1)}, u32[]{:S(2)}, u32[]{:S(2)}) %all-to-all-start) | async-done | bytes 262176 | tf_op jit(solution)/shard_map/all_to_all | solution.py:471
  29.8 18.1 %factor_planes.1 = (f32[24,96]{1,0:T(8,128)}, f32[24,96]{1,0:T(8,128)}, f32[24,96]{1,0:T(8,128)}) custom-call(f32[8,4,16,128]{3,2,1,0:T(8,128)S(1)} %bitcast.10, f32[8,128]{1,0:T(8,128)S(1)} %get-tuple-element.36.after_ref), custom_call_target="tpu_custom_call" | custom-call | tf_op jit(solution)/shard_map/factor_planes/pallas_call | solution.py:277
Async XLA Ops:
  2.9 7.8 %collective-permute-start = (f32[32,128]{1,0:T(8,128)S(1)}, f32[32,128]{1,0:T(8,128)S(1)}, u32[]{:S(2)}, u32[]{:S(2)}) collective-permute-start(f32[32,128]{1,0:T(8,128)S(1)} %get-tuple-element.29), channel_id=1, source_target_pairs={{0,4},{4,8},{8,12},{12,16},{16,20},{20,24},{24,28},{1,5},{5,9},{9,... | collective-permute-start | bytes 49160 | tf_op jit(solution)/shard_map/ppermute | solution.py:457
  5.3 5.7 %collective-permute-start.1 = (f32[32,128]{1,0:T(8,128)S(1)}, f32[32,128]{1,0:T(8,128)S(1)}, u32[]{:S(2)}, u32[]{:S(2)}) collective-permute-start(f32[32,128]{1,0:T(8,128)S(1)} %get-tuple-element.31), channel_id=1, source_target_pairs={{0,1},{1,2},{2,3},{4,5},{5,6},{6,7},{8,9},{9,10},{10,11},{12,13},{... | collective-permute-start | bytes 49160 | tf_op jit(solution)/shard_map/ppermute | solution.py:458
  12.0 17.8 %all-to-all-start = ((f32[32,16,128]{2,1,0:T(8,128)}), f32[32,16,128]{2,1,0:T(8,128)S(1)}, u32[]{:S(2)}, u32[]{:S(2)}) async-start(f32[32,16,128]{2,1,0:T(8,128)} %get-tuple-element.35), calls=%async_computation | async-start | bytes 524288 | tf_op jit(solution)/shard_map/all_to_all | solution.py:471
  18.9 3.1 %collective-permute-start.2 = (f32[24,128]{1,0:T(8,128)S(1)}, f32[24,128]{1,0:T(8,128)S(1)}, u32[]{:S(2)}, u32[]{:S(2)}) collective-permute-start(f32[24,128]{1,0:T(8,128)S(1)} %get-tuple-element.32), channel_id=1, source_target_pairs={{4,0},{8,4},{12,8},{16,12},{20,16},{24,20},{28,24},{5,1},{9,5},{13... | collective-permute-start | bytes 36872 | tf_op jit(solution)/shard_map/ppermute | solution.py:472
  20.2 5.6 %collective-permute-start.3 = (f32[24,128]{1,0:T(8,128)S(1)}, f32[24,128]{1,0:T(8,128)S(1)}, u32[]{:S(2)}, u32[]{:S(2)}) collective-permute-start(f32[24,128]{1,0:T(8,128)S(1)} %get-tuple-element.33), channel_id=1, source_target_pairs={{1,0},{2,1},{3,2},{5,4},{6,5},{7,6},{9,8},{10,9},{11,10},{13,12},{... | collective-permute-start | bytes 36872 | tf_op jit(solution)/shard_map/ppermute | solution.py:473

commit v7 on v6

--- a/solution.py
+++ b/solution.py
@@ -38,49 +38,59 @@
     return jnp.broadcast_to(strip[k : k + 1, :], strip.shape)
 
 
+def eliminate_pair(block, columns, pivots, iota, q, k):
+    first, second = columns[k], columns[k + 1]
+    corner, joint = spread_row(first[0], k), spread_row(first[0], k + 1)
+    other_corner = spread_row(second[0], k + 1)
+    minor = corner * other_corner - joint * joint
+    inverse = pl.reciprocal(corner, approx=True)
+    other_inverse = corner * pl.reciprocal(minor, approx=True)
+    below = [column * inverse for column in first]
+    second = [column - below[r] * joint for r, column in enumerate(second)]
+    other_below = [column * other_inverse for column in second]
+    below[0] = jnp.where(iota > k, below[0], 0.0)
+    other_below[0] = jnp.where(iota > k + 1, other_below[0], 0.0)
+    for j in range(k + 2, ROWS):
+        head, other_head = spread_row(first[0], j), spread_row(second[0], j)
+        columns[j] = [
+            column - below[r] * head - other_below[r] * other_head
+            for r, column in enumerate(columns[j])
+        ]
+    for t in range(len(block[q])):
+        row = spread_row(block[q][t], k)
+        for r, lower in enumerate(below):
+            block[q + r][t] = block[q + r][t] - lower * row
+        row = spread_row(block[q][t], k + 1)
+        for r, lower in enumerate(other_below):
+            block[q + r][t] = block[q + r][t] - lower * row
+    return jnp.where(iota == k, corner, jnp.where(iota == k + 1, minor * inverse, pivots))
+
+
 def factor_rows(blocks, tiles_per_part, first_row, turned):
     strip_count = len(blocks[0])
     iota = lax.broadcasted_iota(jnp.int32, (ROWS, LANES), 0)
     lane = lax.broadcasted_iota(jnp.int32, (ROWS, LANES), 1)
     blocks = [[list(strip) for strip in block] for block in blocks]
     for q in range(strip_count):
+        start = q * ROWS
+        held = []
         for b, block in enumerate(blocks):
-            start = q * ROWS
             source = turned(b, block, q)
-            columns = [
+            held.append(
                 [
-                    jnp.broadcast_to(source[r][:, start + j : start + j + 1], (ROWS, LANES))
-                    for r in range(strip_count - q)
+                    [
+                        jnp.broadcast_to(strip[:, start + j : start + j + 1], (ROWS, LANES))
+                        for strip in source
+                    ]
+                    for j in range(ROWS)
                 ]
-                for j in range(ROWS)
-            ]
-            pivots = jnp.zeros((ROWS, LANES), jnp.float32)
-            for k in range(0, ROWS, 2):
-                first, second = columns[k], columns[k + 1]
-                corner, joint = spread_row(first[0], k), spread_row(first[0], k + 1)
-                other_corner = spread_row(second[0], k + 1)
-                minor = corner * other_corner - joint * joint
-                inverse = pl.reciprocal(corner, approx=True)
-                other_inverse = corner * pl.reciprocal(minor, approx=True)
-                pivots = jnp.where(iota == k, corner, pivots)
-                pivots = jnp.where(iota == k + 1, minor * inverse, pivots)
-                below = [column * inverse for column in first]
-                second = [second[r] - below[r] * joint for r in range(len(second))]
-                other_below = [column * other_inverse for column in second]
-                below[0] = jnp.where(iota > k, below[0], 0.0)
-                other_below[0] = jnp.where(iota > k + 1, other_below[0], 0.0)
-                for j in range(k + 2, ROWS):
-                    head, other_head = spread_row(first[0], j), spread_row(second[0], j)
-                    for r in range(strip_count - q):
-                        columns[j][r] = columns[j][r] - below[r] * head - other_below[r] * other_head
-                for t in range(len(block[q])):
-                    row = spread_row(block[q][t], k)
-                    for r in range(strip_count - q):
-                        block[q + r][t] = block[q + r][t] - below[r] * row
-                    row = spread_row(block[q][t], k + 1)
-                    for r in range(strip_count - q):
-                        block[q + r][t] = block[q + r][t] - other_below[r] * row
-            scale = lax.rsqrt(pivots)
+            )
+        pivots = [jnp.zeros((ROWS, LANES), jnp.float32) for _ in blocks]
+        for k in range(0, ROWS, 2):
+            for b, block in enumerate(blocks):
+                pivots[b] = eliminate_pair(block, held[b], pivots[b], iota, q, k)
+        for b, block in enumerate(blocks):
+            scale = lax.rsqrt(pivots[b])
             for t in range(len(block[q])):
                 strip = block[q][t] * scale
                 if t < tiles_per_part:
@@ -144,9 +154,8 @@
 def eliminate_planes(grid_ref, planes, modes, order, part, lanes_used, banded=False):
     layers = order // modes
     if layers <= UNROLLED_LAYERS:
-        height = modes if banded else modes * max(1, layers // len(planes))
-        for panel in range(order // height):
-            eliminate_panel(grid_ref, planes, height, order, part, lanes_used, panel, banded)
+        for panel in range(layers):
+            eliminate_panel(grid_ref, planes, modes, order, part, lanes_used, panel, banded)
     else:
 
         def one_panel(panel, carry):
@@ -213,7 +222,6 @@
             if j > 0:
                 above = slice((j - 1) * modes, j * modes)
                 grid_ref[s, above, j * modes : (j + 1) * modes] = tile[:, modes : 2 * modes]
-                grid_ref[s, rows, (j - 1) * modes : j * modes] = turned[modes : 2 * modes]
             if has_left:
                 lanes = slice(part + j * modes, part + (j + 1) * modes)
                 grid_ref[s, rows, lanes] = turned[2 * modes : 3 * modes]

time: 48.2 us -> 46.9 us (0.973)
  Pallas kernels: 23.9 us -> 22.6 us
    pallas_call x1, Pallas kernels: 18.1 us -> 16.8 us  [factor_planes(): pl.pallas_call(factor_kernel, out_shape=(strip, strip, strip), in_specs=[...]
where the time goes in v7:
time: 46.9 us; the launch traced here: 46.6 us
  Pallas kernels  22.6 us (48%)
  starting transfers between devices  16 us (34%)
  waiting for transfers between devices  7.3 us (16%)
  between operations  0.68 us (1%)
    pallas_call x1, Pallas kernels, factor_planes(): pl.pallas_call(factor_kernel, out_shape=(strip, strip, strip), in_specs=[...  16.8 us
    all_to_all x1, starting transfers between devices, per_device(): lax.all_to_all(copies, ('sub', 'layer'), split_axis=0, concat_axis=0, til...  6.83 us
    ppermute x1, starting transfers between devices, per_device(): before_layer = lax.ppermute(layer_send, 'layer', up_layer)  4.23 us
    ppermute x1, waiting for transfers between devices, per_device(): after_layer = lax.ppermute(layer_send, 'layer', down_layer)  3.82 us
    pallas_call x3, Pallas kernels, local_call(): pl.pallas_call(body, out_shape=shapes, in_specs=[VMEM_BLOCK] * len(operan...  3.58 us
    all_to_all x1, waiting for transfers between devices, per_device(): lax.all_to_all(copies, ('sub', 'layer'), split_axis=0, concat_axis=0, til...  2.75 us
    ppermute x1, starting transfers between devices, per_device(): before_sub = lax.ppermute(sub_send, 'sub', up_sub)  2.36 us
    pallas_call x1, Pallas kernels, per_device(): pl.pallas_call(pick_kernel, out_shape=tuple((jax.ShapeDtypeStruct(*pair)...  2.26 us
  transfers between devices with their start and end apart: 5, of which 4 were waited for; matrix products, arithmetic and copies ran while one was open for 0% of the time, Pallas kernels for 5%

profile of v7, /device:TPU:0, one launch (start us, length us, event | category | flops | bytes accessed | tf_op | source)
XLA Modules:
  0.0 46.6 jit_solution(3640843505129926503)
XLA Ops:
  0.6 2.3 %pick_rows.1 = (f32[24,4096]{1,0:T(8,128)S(1)}, s32[4,128]{1,0:T(4,128)S(1)}, f32[2,128]{1,0:T(2,128)S(1)}, f32[1,4096]{1,0:T(1,128)S(1)}, f32[3,1,4096]{2,1,0:T...) custom-call(f32[24,4096]{1,0:T(8,128)} %bitcast.11, s32[4,128]{1,0:T(4,128)} %bitcast.14, ...), custom_call_target="tpu_custom_call" | custom-call | tf_op jit(solution)/shard_map/pick_rows/pallas_call | solution.py:456
  2.9 2.4 %collective-permute-start = (f32[32,128]{1,0:T(8,128)S(1)}, f32[32,128]{1,0:T(8,128)S(1)}, u32[]{:S(2)}, u32[]{:S(2)}) collective-permute-start(f32[32,128]{1,0:T(8,128)S(1)} %get-tuple-element.29), channel_id=1, source_target_pairs={{0,4},{4,8},{8,12},{12,16},{16,20},{20,24},{24,28},{1,5},{5,9},{9,... | collective-permute-start | bytes 49160 | tf_op jit(solution)/shard_map/ppermute | solution.py:465
  5.3 4.2 %collective-permute-start.1 = (f32[32,128]{1,0:T(8,128)S(1)}, f32[32,128]{1,0:T(8,128)S(1)}, u32[]{:S(2)}, u32[]{:S(2)}) collective-permute-start(f32[32,128]{1,0:T(8,128)S(1)} %get-tuple-element.31), channel_id=1, source_target_pairs={{0,1},{1,2},{2,3},{4,5},{5,6},{6,7},{8,9},{9,10},{10,11},{12,13},{... | collective-permute-start | bytes 49160 | tf_op jit(solution)/shard_map/ppermute | solution.py:466
  9.5 1.2 %own_rows.1 = (f32[24,4096]{1,0:T(8,128)S(1)}, f32[24,24]{1,0:T(8,128)S(1)}) custom-call(f32[24,4096]{1,0:T(8,128)S(1)} %get-tuple-element.22.vectors_ref, f32[1,4096]{1,0:T(1,128)S(1)} %get-tuple-element.23.mass_ref, f32[3,1,4096]{2,1,0:T(1,128)S(1)} %get-tuple-element.24.inner_ref, f32[2,128]{1,0:T(2,128)S(1)} %get-tuple-element.25.face_ref, ...), custom_call_target="tpu_custom_call" | custom-call | tf_op jit(solution)/shard_map/own_rows/pallas_call | solution.py:430
  10.7 0.0 collective-permute-done.sub_ref.before_sub_ref
  10.7 0.3 collective-permute-done.1.layer_ref.before_layer_ref
  10.9 1.1 %coarse_tiles.1 = (f32[32,16,128]{2,1,0:T(8,128)}, f32[24,128]{1,0:T(8,128)S(1)}, f32[24,128]{1,0:T(8,128)S(1)}) custom-call(f32[24,24]{1,0:T(8,128)S(1)} %get-tuple-element.30.own_ref, f32[4,24,128]{2,1,0:T(8,128)S(1)} %get-tuple-element.26.picked_ref, f32[32,128]{1,0:T(8,128)S(1)} %collective-permute-done.sub_ref.before_sub_ref, ...), custom_call_target="tpu_custom_call" | custom-call | tf_op jit(solution)/shard_map/coarse_tiles/pallas_call | solution.py:430
  12.0 6.8 %all-to-all-start = ((f32[32,16,128]{2,1,0:T(8,128)}), f32[32,16,128]{2,1,0:T(8,128)S(1)}, u32[]{:S(2)}, u32[]{:S(2)}) async-start(f32[32,16,128]{2,1,0:T(8,128)} %get-tuple-element.35), calls=%async_computation | async-start | bytes 524288 | tf_op jit(solution)/shard_map/all_to_all | solution.py:479
  18.9 1.3 %collective-permute-start.2 = (f32[24,128]{1,0:T(8,128)S(1)}, f32[24,128]{1,0:T(8,128)S(1)}, u32[]{:S(2)}, u32[]{:S(2)}) collective-permute-start(f32[24,128]{1,0:T(8,128)S(1)} %get-tuple-element.32), channel_id=1, source_target_pairs={{4,0},{8,4},{12,8},{16,12},{20,16},{24,20},{28,24},{5,1},{9,5},{13... | collective-permute-start | bytes 36872 | tf_op jit(solution)/shard_map/ppermute | solution.py:480
  20.2 1.3 %collective-permute-start.3 = (f32[24,128]{1,0:T(8,128)S(1)}, f32[24,128]{1,0:T(8,128)S(1)}, u32[]{:S(2)}, u32[]{:S(2)}) collective-permute-start(f32[24,128]{1,0:T(8,128)S(1)} %get-tuple-element.33), channel_id=1, source_target_pairs={{1,0},{2,1},{3,2},{5,4},{6,5},{7,6},{9,8},{10,9},{11,10},{13,12},{... | collective-permute-start | bytes 36872 | tf_op jit(solution)/shard_map/ppermute | solution.py:481
  21.5 0.5 %collective-permute-done.2.after_sub_ref = f32[24,128]{1,0:T(8,128)S(1)} collective-permute-done((f32[24,128]{1,0:T(8,128)S(1)}, f32[24,128]{1,0:T(8,128)S(1)}, u32[]{:S(2)}, u32[]{:S(2)}) %collective-permute-start.2) | collective-permute-done | bytes 12320 | tf_op jit(solution)/shard_map/ppermute | solution.py:480
  21.9 3.8 %collective-permute-done.3.after_layer_ref = f32[24,128]{1,0:T(8,128)S(1)} collective-permute-done((f32[24,128]{1,0:T(8,128)S(1)}, f32[24,128]{1,0:T(8,128)S(1)}, u32[]{:S(2)}, u32[]{:S(2)}) %collective-permute-start.3) | collective-permute-done | bytes 12320 | tf_op jit(solution)/shard_map/ppermute | solution.py:481
  25.8 1.3 %spread_rows.1 = (f32[24,4096]{1,0:T(8,128)}, f32[8,128]{1,0:T(8,128)S(1)}) custom-call(f32[24,4096]{1,0:T(8,128)S(1)} %get-tuple-element.27.base_ref, s32[4,128]{1,0:T(4,128)S(1)} %get-tuple-element.28.lists_ref, f32[2,128]{1,0:T(2,128)S(1)} %get-tuple-element.25.face_ref, f32[4,24,128]{2,1,0:T(8,128)S(1)} %get-tuple-element.26.picked_ref, ...), custom_call_target="tpu_custom_call" | custom-call | tf_op jit(solution)/shard_map/spread_rows/pallas_call | solution.py:430
  27.1 2.7 %all-to-all-done = f32[32,16,128]{2,1,0:T(8,128)S(1)} async-done(((f32[32,16,128]{2,1,0:T(8,128)}), f32[32,16,128]{2,1,0:T(8,128)S(1)}, u32[]{:S(2)}, u32[]{:S(2)}) %all-to-all-start) | async-done | bytes 262176 | tf_op jit(solution)/shard_map/all_to_all | solution.py:479
  29.8 16.8 %factor_planes.1 = (f32[24,96]{1,0:T(8,128)}, f32[24,96]{1,0:T(8,128)}, f32[24,96]{1,0:T(8,128)}) custom-call(f32[8,4,16,128]{3,2,1,0:T(8,128)S(1)} %bitcast.10, f32[8,128]{1,0:T(8,128)S(1)} %get-tuple-element.36.after_ref), custom_call_target="tpu_custom_call" | custom-call | tf_op jit(solution)/shard_map/factor_planes/pallas_call | solution.py:285
Async XLA Ops:
  2.9 7.8 %collective-permute-start = (f32[32,128]{1,0:T(8,128)S(1)}, f32[32,128]{1,0:T(8,128)S(1)}, u32[]{:S(2)}, u32[]{:S(2)}) collective-permute-start(f32[32,128]{1,0:T(8,128)S(1)} %get-tuple-element.29), channel_id=1, source_target_pairs={{0,4},{4,8},{8,12},{12,16},{16,20},{20,24},{24,28},{1,5},{5,9},{9,... | collective-permute-start | bytes 49160 | tf_op jit(solution)/shard_map/ppermute | solution.py:465
  5.3 5.7 %collective-permute-start.1 = (f32[32,128]{1,0:T(8,128)S(1)}, f32[32,128]{1,0:T(8,128)S(1)}, u32[]{:S(2)}, u32[]{:S(2)}) collective-permute-start(f32[32,128]{1,0:T(8,128)S(1)} %get-tuple-element.31), channel_id=1, source_target_pairs={{0,1},{1,2},{2,3},{4,5},{5,6},{6,7},{8,9},{9,10},{10,11},{12,13},{... | collective-permute-start | bytes 49160 | tf_op jit(solution)/shard_map/ppermute | solution.py:466
  12.0 17.8 %all-to-all-start = ((f32[32,16,128]{2,1,0:T(8,128)}), f32[32,16,128]{2,1,0:T(8,128)S(1)}, u32[]{:S(2)}, u32[]{:S(2)}) async-start(f32[32,16,128]{2,1,0:T(8,128)} %get-tuple-element.35), calls=%async_computation | async-start | bytes 524288 | tf_op jit(solution)/shard_map/all_to_all | solution.py:479
  18.9 3.1 %collective-permute-start.2 = (f32[24,128]{1,0:T(8,128)S(1)}, f32[24,128]{1,0:T(8,128)S(1)}, u32[]{:S(2)}, u32[]{:S(2)}) collective-permute-start(f32[24,128]{1,0:T(8,128)S(1)} %get-tuple-element.32), channel_id=1, source_target_pairs={{4,0},{8,4},{12,8},{16,12},{20,16},{24,20},{28,24},{5,1},{9,5},{13... | collective-permute-start | bytes 36872 | tf_op jit(solution)/shard_map/ppermute | solution.py:480
  20.2 5.6 %collective-permute-start.3 = (f32[24,128]{1,0:T(8,128)S(1)}, f32[24,128]{1,0:T(8,128)S(1)}, u32[]{:S(2)}, u32[]{:S(2)}) collective-permute-start(f32[24,128]{1,0:T(8,128)S(1)} %get-tuple-element.33), channel_id=1, source_target_pairs={{1,0},{2,1},{3,2},{5,4},{6,5},{7,6},{9,8},{10,9},{11,10},{13,12},{... | collective-permute-start | bytes 36872 | tf_op jit(solution)/shard_map/ppermute | solution.py:481

commit v8 on v7

--- a/solution.py
+++ b/solution.py
@@ -11,17 +11,8 @@
 HIGHEST = lax.Precision.HIGHEST
 LANES = 128
 ROWS = 8
-UNROLLED_LAYERS = 4
-
-
-def turned_dot(left, right):
-    return lax.dot_general(
-        left,
-        right,
-        (((0,), (0,)), ((), ())),
-        precision=HIGHEST,
-        preferred_element_type=jnp.float32,
-    )
+PLANES_AT_ONCE = 4
+BLOCKS_AT_ONCE = 3
 
 
 def plain_dot(left, right):
@@ -66,25 +57,23 @@
     return jnp.where(iota == k, corner, jnp.where(iota == k + 1, minor * inverse, pivots))
 
 
-def factor_rows(blocks, tiles_per_part, first_row, turned):
+def factor_rows(blocks, tiles_per_part, columns_left):
     strip_count = len(blocks[0])
     iota = lax.broadcasted_iota(jnp.int32, (ROWS, LANES), 0)
     lane = lax.broadcasted_iota(jnp.int32, (ROWS, LANES), 1)
     blocks = [[list(strip) for strip in block] for block in blocks]
     for q in range(strip_count):
         start = q * ROWS
-        held = []
-        for b, block in enumerate(blocks):
-            source = turned(b, block, q)
-            held.append(
+        held = [
+            [
                 [
-                    [
-                        jnp.broadcast_to(strip[:, start + j : start + j + 1], (ROWS, LANES))
-                        for strip in source
-                    ]
-                    for j in range(ROWS)
+                    jnp.broadcast_to(strip[0][:, start + j : start + j + 1], (ROWS, LANES))
+                    for strip in block[q:]
                 ]
-            )
+                for j in range(ROWS)
+            ]
+            for block in blocks
+        ]
         pivots = [jnp.zeros((ROWS, LANES), jnp.float32) for _ in blocks]
         for k in range(0, ROWS, 2):
             for b, block in enumerate(blocks):
@@ -94,95 +83,87 @@
             for t in range(len(block[q])):
                 strip = block[q][t] * scale
                 if t < tiles_per_part:
-                    keep = lane + t * LANES >= iota + (first_row + start)
+                    place = lane + t * LANES
+                    keep = (place >= iota + start) & (place < columns_left)
                     strip = jnp.where(keep, strip, 0.0)
                 block[q][t] = strip
     return blocks
 
 
-def eliminate_panel(grid_ref, planes, modes, order, part, lanes_used, panel, banded):
-    per_part = part // LANES
-    first_row = panel * modes
-    static = isinstance(panel, int)
-    if static:
-        rows = pl.ds(first_row, modes)
-    else:
-        rows = pl.ds(pl.multiple_of(first_row, ROWS), modes)
+def eliminate_panel(grid_ref, turned_ref, planes, modes, order, part, panel, banded):
+    first_row = pl.multiple_of(panel * modes, ROWS)
+    rows = pl.ds(first_row, modes)
+    reach = modes if banded else min(order - modes, BLOCKS_AT_ONCE * modes)
+    chunks = 1
+    if not banded and reach < order - modes:
+        chunks = lax.div(order - first_row - modes + reach - 1, reach)
     blocks = []
     for plane in planes:
-        panel_rows = grid_ref[plane, rows, 0:lanes_used]
+        panel_rows = grid_ref[plane, rows, :]
         blocks.append(
             [
                 [
                     panel_rows[q * ROWS : (q + 1) * ROWS, t * LANES : (t + 1) * LANES]
-                    for t in range(lanes_used // LANES)
+                    for t in range(3 * part // LANES)
                 ]
                 for q in range(modes // ROWS)
             ]
         )
-
-    def turned(b, block, q):
-        found = []
-        for strip in block[q:]:
-            if static and first_row // LANES == (first_row + modes - 1) // LANES:
-                tile = strip[first_row // LANES]
-                offset = first_row % LANES
-                found.append(tile if offset == 0 else tile[:, offset : offset + modes])
-            else:
-                wide = jnp.concatenate(strip[:per_part], axis=1)
-                found.append(pltpu.roll(wide, lax.rem(part - first_row, part), 1)[:, :LANES])
-        return found
-
-    blocks = factor_rows(blocks, per_part, first_row, turned)
+    blocks = factor_rows(blocks, part // LANES, order - first_row)
     for plane, block in zip(planes, blocks):
         panel_rows = jnp.concatenate([jnp.concatenate(strip, axis=1) for strip in block], axis=0)
-        grid_ref[plane, rows, 0:lanes_used] = panel_rows
-        if static:
-            below = (panel + 1) * modes
-            end = min(below + modes, order) if banded else order
-            if below < order:
-                columns = panel_rows[:, 0:part].T[below:end]
-                update = plain_dot(columns, panel_rows)
-                grid_ref[plane, below:end, 0:lanes_used] -= update
+        grid_ref[plane, rows, :] = panel_rows
+        own = panel_rows[:, 0:part]
+        if banded:
+            panel_rows = jnp.concatenate(
+                [pltpu.roll(own, part - modes, 1), panel_rows[:, part:]], axis=1
+            )
+
+        def update_rows(first, columns, plane=plane, panel_rows=panel_rows):
+            below = pl.ds(pl.multiple_of(first_row + first, ROWS), reach)
+            rest = grid_ref[plane, below, :] - plain_dot(columns, panel_rows)
+            if banded:
+                grid_ref[plane, below, :] = rest
+            else:
+                grid_ref[plane, below, 0:part] = pltpu.roll(rest[:, 0:part], part - modes, 1)
+                grid_ref[plane, below, part:] = rest[:, part:]
+
+        if isinstance(chunks, int):
+            update_rows(modes, own.T[modes : modes + reach])
         else:
-            lane = lax.broadcasted_iota(jnp.int32, (modes, part), 1)
-            columns = jnp.where(lane >= first_row + modes, panel_rows[:, 0:part], 0.0)
-            update = turned_dot(columns, panel_rows)[0:order]
-            grid_ref[plane, :, 0:lanes_used] -= update
-
-
-def eliminate_planes(grid_ref, planes, modes, order, part, lanes_used, banded=False):
-    layers = order // modes
-    if layers <= UNROLLED_LAYERS:
-        for panel in range(layers):
-            eliminate_panel(grid_ref, planes, modes, order, part, lanes_used, panel, banded)
-    else:
-
-        def one_panel(panel, carry):
-            eliminate_panel(grid_ref, planes, modes, order, part, lanes_used, panel, banded)
-            return carry
-
-        lax.fori_loop(0, layers, one_panel, 0)
+            turned_ref[0, :, 0:modes] = own.T
+
+            def one_chunk(chunk, carry):
+                first = pl.multiple_of(modes + chunk * reach, ROWS)
+                update_rows(first, turned_ref[0, pl.ds(first, reach), 0:modes])
+                return carry
+
+            lax.fori_loop(0, chunks, one_chunk, 0)
+
+
+def eliminate_planes(grid_ref, turned_ref, planes, modes, order, part, banded=False):
+    def one_panel(panel, carry):
+        eliminate_panel(grid_ref, turned_ref, planes, modes, order, part, panel, banded)
+        return carry
+
+    lax.fori_loop(0, order // modes, one_panel, 0)
 
 
 def update_partners(grid_ref, plane, distance, part, order, has_left):
     left, right = plane - distance, plane + distance
-    both = grid_ref[plane, :, part : 3 * part]
+    both = grid_ref[plane, 0:order, part : 3 * part]
     turned = both.T
     from_right = plain_dot(turned[part : part + order], both)
-    grid_ref[right, :, 0:part] -= from_right[:, part : 2 * part]
-    grid_ref[right, :, part : 2 * part] = -from_right[:, 0:part]
-
-    def to_left():
+    grid_ref[right, 0:order, 0:part] -= from_right[:, part : 2 * part]
+    grid_ref[right, 0:order, part : 2 * part] = -from_right[:, 0:part]
+    if has_left is False:
+        return
+
+    @pl.when(has_left)
+    def _():
         from_left = plain_dot(turned[0:order], both)
-        grid_ref[left, :, 0:part] -= from_left[:, 0:part]
-        grid_ref[left, :, 2 * part : 3 * part] = -from_left[:, part : 2 * part]
-
-    if isinstance(has_left, bool):
-        if has_left:
-            to_left()
-    else:
-        pl.when(has_left)(to_left)
+        grid_ref[left, 0:order, 0:part] -= from_left[:, 0:part]
+        grid_ref[left, 0:order, 2 * part : 3 * part] = -from_left[:, part : 2 * part]
 
 
 def unpack_tile(packed, modes):
@@ -209,60 +190,70 @@
     subs, layers, _, _ = tiles_ref.shape
     modes, order = diag_ref.shape
     part = grid_ref.shape[2] // 3
-    unrolled = layers <= UNROLLED_LAYERS
     del after_ref
-    grid_ref[...] = jnp.zeros_like(grid_ref)
-
-    def place_tiles(s, has_left):
+
+    def place_plane(s, banded):
+        grid_ref[s] = jnp.zeros(grid_ref.shape[1:], jnp.float32)
+        before = jnp.maximum(s - 1, 0)
         for j in range(layers):
             tile = unpack_tile(tiles_ref[s, j], modes)
             turned = tile.T
             rows = slice(j * modes, (j + 1) * modes)
-            grid_ref[s, rows, j * modes : (j + 1) * modes] = tile[:, 0:modes]
+            first = 0 if banded else j * modes
+            grid_ref[s, rows, first : first + modes] = tile[:, 0:modes]
             if j > 0:
                 above = slice((j - 1) * modes, j * modes)
-                grid_ref[s, above, j * modes : (j + 1) * modes] = tile[:, modes : 2 * modes]
-            if has_left:
-                lanes = slice(part + j * modes, part + (j + 1) * modes)
-                grid_ref[s, rows, lanes] = turned[2 * modes : 3 * modes]
-                lanes = slice(2 * part + j * modes, 2 * part + (j + 1) * modes)
-                grid_ref[s - 1, rows, lanes] = tile[:, 2 * modes : 3 * modes]
-
-    place_tiles(0, False)
-    if unrolled:
-        for s in range(1, subs):
-            place_tiles(s, True)
-    else:
-
-        def place_one(s, carry):
-            place_tiles(s, True)
+                first = modes if banded else j * modes
+                grid_ref[s, above, first : first + modes] = tile[:, modes : 2 * modes]
+            lanes = slice(part + j * modes, part + (j + 1) * modes)
+            grid_ref[s, rows, lanes] = turned[2 * modes : 3 * modes]
+            lanes = slice(2 * part + j * modes, 2 * part + (j + 1) * modes)
+            grid_ref[before, rows, lanes] = tile[:, 2 * modes : 3 * modes]
+
+    def place_pair(i, carry):
+        place_plane(2 * i, True)
+        place_plane(2 * i + 1, False)
+        return carry
+
+    lax.fori_loop(0, subs // 2, place_pair, 0)
+
+    distance = 1
+    while distance < subs // 2:
+        count = subs // (2 * distance)
+        planes = [distance - 1 + 2 * distance * i for i in range(count)]
+        taken = min(count, PLANES_AT_ONCE)
+        for first in range(0, count, taken):
+            some = planes[first : first + taken]
+            eliminate_planes(grid_ref, turned_ref, some, modes, order, part, distance == 1)
+
+        def one_plane(index, carry, distance=distance):
+            plane = distance - 1 + 2 * distance * index
+            update_partners(grid_ref, plane, distance, part, order, index > 0)
             return carry
 
-        lax.fori_loop(1, subs, place_one, 0)
-
-    distance = 1
-    while distance < subs:
-        if unrolled:
-            planes = list(range(distance - 1, subs, 2 * distance))
-            eliminate_planes(grid_ref, planes, modes, order, part, 3 * part, distance == 1)
-            for plane in planes:
-                update_partners(grid_ref, plane, distance, part, order, plane >= distance)
-        else:
-
-            def one_plane(index, carry, distance=distance):
-                plane = distance - 1 + 2 * distance * index
-                eliminate_planes(grid_ref, [plane], modes, order, part, 3 * part)
-                update_partners(grid_ref, plane, distance, part, order, index > 0)
-                return carry
-
-            lax.fori_loop(0, subs // (2 * distance), one_plane, 0)
+        lax.fori_loop(0, count, one_plane, 0)
         distance *= 2
-    eliminate_planes(grid_ref, [subs - 1], modes, order, part, part)
+
+    def last_planes(index, carry):
+        plane = distance - 1 + distance * index
+        eliminate_planes(grid_ref, turned_ref, [plane], modes, order, part)
+
+        @pl.when(index == 0)
+        def _():
+            update_partners(grid_ref, plane, distance, part, order, False)
+
+        return carry
+
+    lax.fori_loop(0, 2, last_planes, 0)
 
     sub_here, lay_here = lax.axis_index("sub"), lax.axis_index("layer")
     strip = pl.ds(pl.multiple_of(lay_here * modes, ROWS), modes)
+    for j in range(layers):
+        rows = slice(j * modes, (j + 1) * modes)
+        own = grid_ref[sub_here, rows, 0:part]
+        grid_ref[sub_here, rows, 0:part] = pltpu.roll(own, j * modes, 1) if j else own
     for k, out_ref in enumerate((diag_ref, left_ref, right_ref)):
-        turned_ref[k] = grid_ref[sub_here, :, k * part : (k + 1) * part].T
+        turned_ref[k] = grid_ref[sub_here, 0:order, k * part : (k + 1) * part].T
         found = turned_ref[k, strip, :]
         out_ref[...] = found if k == 0 else jnp.where(sub_here < subs - 1, found, 0.0)
 
@@ -281,7 +272,8 @@
     order = layers * modes
     part = -(-order // LANES) * LANES
     strip = jax.ShapeDtypeStruct((modes, order), jnp.float32)
-    scratch = ((subs, order, 3 * part), (3, part, order))
+    spare = modes * min(layers - 1, BLOCKS_AT_ONCE)
+    scratch = ((subs, order + spare, 3 * part), (3, part, order))
     return pl.pallas_call(
         factor_kernel,
         out_shape=(strip, strip, strip),

time: 46.9 us -> 52.5 us (1.12)
  Pallas kernels: 22.6 us -> 28.2 us
    pallas_call x1, Pallas kernels: 16.8 us -> 22.4 us  [factor_planes(): pl.pallas_call(factor_kernel, out_shape=(strip, strip, strip), in_specs=[...]
where the time goes in v8:
time: 52.5 us; the launch traced here: 52.2 us
  Pallas kernels  28.2 us (54%)
  starting transfers between devices  16 us (30%)
  waiting for transfers between devices  7.3 us (14%)
  between operations  0.68 us (1%)
    pallas_call x1, Pallas kernels, factor_planes(): pl.pallas_call(factor_kernel, out_shape=(strip, strip, strip), in_specs=[...  22.4 us
    all_to_all x1, starting transfers between devices, per_device(): lax.all_to_all(copies, ('sub', 'layer'), split_axis=0, concat_axis=0, til...  6.83 us
    ppermute x1, starting transfers between devices, per_device(): before_layer = lax.ppermute(layer_send, 'layer', up_layer)  4.23 us
    ppermute x1, waiting for transfers between devices, per_device(): after_layer = lax.ppermute(layer_send, 'layer', down_layer)  3.82 us
    pallas_call x3, Pallas kernels, local_call(): pl.pallas_call(body, out_shape=shapes, in_specs=[VMEM_BLOCK] * len(operan...  3.58 us
    all_to_all x1, waiting for transfers between devices, per_device(): lax.all_to_all(copies, ('sub', 'layer'), split_axis=0, concat_axis=0, til...  2.75 us
    ppermute x1, starting transfers between devices, per_device(): before_sub = lax.ppermute(sub_send, 'sub', up_sub)  2.36 us
    pallas_call x1, Pallas kernels, per_device(): pl.pallas_call(pick_kernel, out_shape=tuple((jax.ShapeDtypeStruct(*pair)...  2.26 us
  transfers between devices with their start and end apart: 5, of which 4 were waited for; matrix products, arithmetic and copies ran while one was open for 0% of the time, Pallas kernels for 5%

profile of v8, /device:TPU:0, one launch (start us, length us, event | category | flops | bytes accessed | tf_op | source)
XLA Modules:
  0.0 52.2 jit_solution(6514361461320577892)
XLA Ops:
  0.6 2.3 %pick_rows.1 = (f32[24,4096]{1,0:T(8,128)S(1)}, s32[4,128]{1,0:T(4,128)S(1)}, f32[2,128]{1,0:T(2,128)S(1)}, f32[1,4096]{1,0:T(1,128)S(1)}, f32[3,1,4096]{2,1,0:T...) custom-call(f32[24,4096]{1,0:T(8,128)} %bitcast.11, s32[4,128]{1,0:T(4,128)} %bitcast.14, ...), custom_call_target="tpu_custom_call" | custom-call | tf_op jit(solution)/shard_map/pick_rows/pallas_call | solution.py:448
  2.9 2.4 %collective-permute-start = (f32[32,128]{1,0:T(8,128)S(1)}, f32[32,128]{1,0:T(8,128)S(1)}, u32[]{:S(2)}, u32[]{:S(2)}) collective-permute-start(f32[32,128]{1,0:T(8,128)S(1)} %get-tuple-element.29), channel_id=1, source_target_pairs={{0,4},{4,8},{8,12},{12,16},{16,20},{20,24},{24,28},{1,5},{5,9},{9,... | collective-permute-start | bytes 49160 | tf_op jit(solution)/shard_map/ppermute | solution.py:457
  5.3 4.2 %collective-permute-start.1 = (f32[32,128]{1,0:T(8,128)S(1)}, f32[32,128]{1,0:T(8,128)S(1)}, u32[]{:S(2)}, u32[]{:S(2)}) collective-permute-start(f32[32,128]{1,0:T(8,128)S(1)} %get-tuple-element.31), channel_id=1, source_target_pairs={{0,1},{1,2},{2,3},{4,5},{5,6},{6,7},{8,9},{9,10},{10,11},{12,13},{... | collective-permute-start | bytes 49160 | tf_op jit(solution)/shard_map/ppermute | solution.py:458
  9.5 1.2 %own_rows.1 = (f32[24,4096]{1,0:T(8,128)S(1)}, f32[24,24]{1,0:T(8,128)S(1)}) custom-call(f32[24,4096]{1,0:T(8,128)S(1)} %get-tuple-element.22.vectors_ref, f32[1,4096]{1,0:T(1,128)S(1)} %get-tuple-element.23.mass_ref, f32[3,1,4096]{2,1,0:T(1,128)S(1)} %get-tuple-element.24.inner_ref, f32[2,128]{1,0:T(2,128)S(1)} %get-tuple-element.25.face_ref, ...), custom_call_target="tpu_custom_call" | custom-call | tf_op jit(solution)/shard_map/own_rows/pallas_call | solution.py:422
  10.7 0.0 collective-permute-done.sub_ref.before_sub_ref
  10.7 0.3 collective-permute-done.1.layer_ref.before_layer_ref
  10.9 1.1 %coarse_tiles.1 = (f32[32,16,128]{2,1,0:T(8,128)}, f32[24,128]{1,0:T(8,128)S(1)}, f32[24,128]{1,0:T(8,128)S(1)}) custom-call(f32[24,24]{1,0:T(8,128)S(1)} %get-tuple-element.30.own_ref, f32[4,24,128]{2,1,0:T(8,128)S(1)} %get-tuple-element.26.picked_ref, f32[32,128]{1,0:T(8,128)S(1)} %collective-permute-done.sub_ref.before_sub_ref, ...), custom_call_target="tpu_custom_call" | custom-call | tf_op jit(solution)/shard_map/coarse_tiles/pallas_call | solution.py:422
  12.0 6.8 %all-to-all-start = ((f32[32,16,128]{2,1,0:T(8,128)}), f32[32,16,128]{2,1,0:T(8,128)S(1)}, u32[]{:S(2)}, u32[]{:S(2)}) async-start(f32[32,16,128]{2,1,0:T(8,128)} %get-tuple-element.35), calls=%async_computation | async-start | bytes 524288 | tf_op jit(solution)/shard_map/all_to_all | solution.py:471
  18.9 1.3 %collective-permute-start.2 = (f32[24,128]{1,0:T(8,128)S(1)}, f32[24,128]{1,0:T(8,128)S(1)}, u32[]{:S(2)}, u32[]{:S(2)}) collective-permute-start(f32[24,128]{1,0:T(8,128)S(1)} %get-tuple-element.32), channel_id=1, source_target_pairs={{4,0},{8,4},{12,8},{16,12},{20,16},{24,20},{28,24},{5,1},{9,5},{13... | collective-permute-start | bytes 36872 | tf_op jit(solution)/shard_map/ppermute | solution.py:472
  20.2 1.3 %collective-permute-start.3 = (f32[24,128]{1,0:T(8,128)S(1)}, f32[24,128]{1,0:T(8,128)S(1)}, u32[]{:S(2)}, u32[]{:S(2)}) collective-permute-start(f32[24,128]{1,0:T(8,128)S(1)} %get-tuple-element.33), channel_id=1, source_target_pairs={{1,0},{2,1},{3,2},{5,4},{6,5},{7,6},{9,8},{10,9},{11,10},{13,12},{... | collective-permute-start | bytes 36872 | tf_op jit(solution)/shard_map/ppermute | solution.py:473
  21.5 0.5 collective-permute-done.2.after_sub_ref
  21.9 3.8 %collective-permute-done.3.after_layer_ref = f32[24,128]{1,0:T(8,128)S(1)} collective-permute-done((f32[24,128]{1,0:T(8,128)S(1)}, f32[24,128]{1,0:T(8,128)S(1)}, u32[]{:S(2)}, u32[]{:S(2)}) %collective-permute-start.3) | collective-permute-done | bytes 12320 | tf_op jit(solution)/shard_map/ppermute | solution.py:473
  25.8 1.3 %spread_rows.1 = (f32[24,4096]{1,0:T(8,128)}, f32[8,128]{1,0:T(8,128)S(1)}) custom-call(f32[24,4096]{1,0:T(8,128)S(1)} %get-tuple-element.27.base_ref, s32[4,128]{1,0:T(4,128)S(1)} %get-tuple-element.28.lists_ref, f32[2,128]{1,0:T(2,128)S(1)} %get-tuple-element.25.face_ref, f32[4,24,128]{2,1,0:T(8,128)S(1)} %get-tuple-element.26.picked_ref, ...), custom_call_target="tpu_custom_call" | custom-call | tf_op jit(solution)/shard_map/spread_rows/pallas_call | solution.py:422
  27.1 2.7 %all-to-all-done = f32[32,16,128]{2,1,0:T(8,128)S(1)} async-done(((f32[32,16,128]{2,1,0:T(8,128)}), f32[32,16,128]{2,1,0:T(8,128)S(1)}, u32[]{:S(2)}, u32[]{:S(2)}) %all-to-all-start) | async-done | bytes 262176 | tf_op jit(solution)/shard_map/all_to_all | solution.py:471
  29.8 22.4 %factor_planes.1 = (f32[24,96]{1,0:T(8,128)}, f32[24,96]{1,0:T(8,128)}, f32[24,96]{1,0:T(8,128)}) custom-call(f32[8,4,16,128]{3,2,1,0:T(8,128)S(1)} %bitcast.10, f32[8,128]{1,0:T(8,128)S(1)} %get-tuple-element.36.after_ref), custom_call_target="tpu_custom_call" | custom-call | tf_op jit(solution)/shard_map/factor_planes/pallas_call | solution.py:277
Async XLA Ops:
  2.9 7.8 %collective-permute-start = (f32[32,128]{1,0:T(8,128)S(1)}, f32[32,128]{1,0:T(8,128)S(1)}, u32[]{:S(2)}, u32[]{:S(2)}) collective-permute-start(f32[32,128]{1,0:T(8,128)S(1)} %get-tuple-element.29), channel_id=1, source_target_pairs={{0,4},{4,8},{8,12},{12,16},{16,20},{20,24},{24,28},{1,5},{5,9},{9,... | collective-permute-start | bytes 49160 | tf_op jit(solution)/shard_map/ppermute | solution.py:457
  5.3 5.7 %collective-permute-start.1 = (f32[32,128]{1,0:T(8,128)S(1)}, f32[32,128]{1,0:T(8,128)S(1)}, u32[]{:S(2)}, u32[]{:S(2)}) collective-permute-start(f32[32,128]{1,0:T(8,128)S(1)} %get-tuple-element.31), channel_id=1, source_target_pairs={{0,1},{1,2},{2,3},{4,5},{5,6},{6,7},{8,9},{9,10},{10,11},{12,13},{... | collective-permute-start | bytes 49160 | tf_op jit(solution)/shard_map/ppermute | solution.py:458
  12.0 17.8 %all-to-all-start = ((f32[32,16,128]{2,1,0:T(8,128)}), f32[32,16,128]{2,1,0:T(8,128)S(1)}, u32[]{:S(2)}, u32[]{:S(2)}) async-start(f32[32,16,128]{2,1,0:T(8,128)} %get-tuple-element.35), calls=%async_computation | async-start | bytes 524288 | tf_op jit(solution)/shard_map/all_to_all | solution.py:471
  18.9 3.1 %collective-permute-start.2 = (f32[24,128]{1,0:T(8,128)S(1)}, f32[24,128]{1,0:T(8,128)S(1)}, u32[]{:S(2)}, u32[]{:S(2)}) collective-permute-start(f32[24,128]{1,0:T(8,128)S(1)} %get-tuple-element.32), channel_id=1, source_target_pairs={{4,0},{8,4},{12,8},{16,12},{20,16},{24,20},{28,24},{5,1},{9,5},{13... | collective-permute-start | bytes 36872 | tf_op jit(solution)/shard_map/ppermute | solution.py:472
  20.2 5.6 %collective-permute-start.3 = (f32[24,128]{1,0:T(8,128)S(1)}, f32[24,128]{1,0:T(8,128)S(1)}, u32[]{:S(2)}, u32[]{:S(2)}) collective-permute-start(f32[24,128]{1,0:T(8,128)S(1)} %get-tuple-element.33), channel_id=1, source_target_pairs={{1,0},{2,1},{3,2},{5,4},{6,5},{7,6},{9,8},{10,9},{11,10},{13,12},{... | collective-permute-start | bytes 36872 | tf_op jit(solution)/shard_map/ppermute | solution.py:473

commit v9 on v7

--- a/solution.py
+++ b/solution.py
@@ -22,6 +22,42 @@
         precision=HIGHEST,
         preferred_element_type=jnp.float32,
     )
+
+
+PRODUCTS = ((0, 0), (1, 0), (2, 0), (0, 1), (1, 1), (0, 2))
+
+
+def pieces_of(values):
+    first = values.astype(jnp.bfloat16).astype(jnp.float32)
+    rest = values - first
+    second = rest.astype(jnp.bfloat16).astype(jnp.float32)
+    return first, second, rest - second
+
+
+def single_dot(left, right):
+    return lax.dot_general(
+        left, right, (((1,), (0,)), ((), ())), preferred_element_type=jnp.float32
+    )
+
+
+def narrow_product(panel_rows, part, below, end):
+    modes = panel_rows.shape[0]
+    first, second, third = pieces_of(panel_rows)
+    stacked = jnp.concatenate([x[:, 0:part] for x in (first, second, third)], axis=0)
+    turned = stacked.T[below:end]
+    lane = lax.broadcasted_iota(jnp.int32, (end - below, LANES), 1)
+    wide = jnp.concatenate(
+        [turned, jnp.zeros((end - below, LANES - 3 * modes), jnp.float32)], axis=1
+    )
+    again = pltpu.roll(wide, 3 * modes, 1)
+    left = jnp.where(lane < 3 * modes, wide, jnp.where(lane < 5 * modes, again, 0.0))
+    last = jnp.where(lane < modes, wide, 0.0)
+    depth = LANES + 2 * LANES // 8
+    columns = jnp.concatenate([left, last], axis=1)[:, 0:depth]
+    gap = jnp.zeros((LANES - 5 * modes, panel_rows.shape[1]), jnp.float32)
+    tail = jnp.zeros((depth - LANES - modes, panel_rows.shape[1]), jnp.float32)
+    rows = jnp.concatenate([first] * 3 + [second] * 2 + [gap, third, tail], axis=0)
+    return single_dot(columns.astype(jnp.bfloat16), rows.astype(jnp.bfloat16))
 
 
 def plain_dot(left, right):
@@ -141,8 +177,7 @@
             below = (panel + 1) * modes
             end = min(below + modes, order) if banded else order
             if below < order:
-                columns = panel_rows[:, 0:part].T[below:end]
-                update = plain_dot(columns, panel_rows)
+                update = narrow_product(panel_rows, part, below, end)
                 grid_ref[plane, below:end, 0:lanes_used] -= update
         else:
             lane = lax.broadcasted_iota(jnp.int32, (modes, part), 1)
@@ -168,13 +203,23 @@
 def update_partners(grid_ref, plane, distance, part, order, has_left):
     left, right = plane - distance, plane + distance
     both = grid_ref[plane, :, part : 3 * part]
-    turned = both.T
-    from_right = plain_dot(turned[part : part + order], both)
+    if part > order:
+        spare = jnp.zeros((part - order, 2 * part), jnp.float32)
+        both = jnp.concatenate([both, spare], axis=0)
+    turned = [piece.astype(jnp.bfloat16) for piece in pieces_of(both.T)]
+    held = [piece.astype(jnp.bfloat16) for piece in pieces_of(both)]
+    held = jnp.concatenate([held[right] for _, right in PRODUCTS], axis=0)
+
+    def product(rows):
+        columns = jnp.concatenate([turned[left][rows] for left, _ in PRODUCTS], axis=1)
+        return single_dot(columns, held)
+
+    from_right = product(slice(part, part + order))
     grid_ref[right, :, 0:part] -= from_right[:, part : 2 * part]
     grid_ref[right, :, part : 2 * part] = -from_right[:, 0:part]
 
     def to_left():
-        from_left = plain_dot(turned[0:order], both)
+        from_left = product(slice(0, order))
         grid_ref[left, :, 0:part] -= from_left[:, 0:part]
         grid_ref[left, :, 2 * part : 3 * part] = -from_left[:, part : 2 * part]
 

time: 46.9 us -> 46.5 us (level)
  no operation moved by 1% of the time
where the time goes in v9:
time: 46.5 us; the launch traced here: 46.2 us
  Pallas kernels  22.2 us (48%)
  starting transfers between devices  16 us (34%)
  waiting for transfers between devices  7.3 us (16%)
  between operations  0.68 us (1%)
    pallas_call x1, Pallas kernels, factor_planes(): pl.pallas_call(factor_kernel, out_shape=(strip, strip, strip), in_specs=[...  16.4 us
    all_to_all x1, starting transfers between devices, per_device(): lax.all_to_all(copies, ('sub', 'layer'), split_axis=0, concat_axis=0, til...  6.83 us
    ppermute x1, starting transfers between devices, per_device(): before_layer = lax.ppermute(layer_send, 'layer', up_layer)  4.23 us
    ppermute x1, waiting for transfers between devices, per_device(): after_layer = lax.ppermute(layer_send, 'layer', down_layer)  3.82 us
    pallas_call x3, Pallas kernels, local_call(): pl.pallas_call(body, out_shape=shapes, in_specs=[VMEM_BLOCK] * len(operan...  3.58 us
    all_to_all x1, waiting for transfers between devices, per_device(): lax.all_to_all(copies, ('sub', 'layer'), split_axis=0, concat_axis=0, til...  2.75 us
    ppermute x1, starting transfers between devices, per_device(): before_sub = lax.ppermute(sub_send, 'sub', up_sub)  2.36 us
    pallas_call x1, Pallas kernels, per_device(): pl.pallas_call(pick_kernel, out_shape=tuple((jax.ShapeDtypeStruct(*pair)...  2.26 us
  transfers between devices with their start and end apart: 5, of which 4 were waited for; matrix products, arithmetic and copies ran while one was open for 0% of the time, Pallas kernels for 5%

profile of v9, /device:TPU:0, one launch (start us, length us, event | category | flops | bytes accessed | tf_op | source)
XLA Modules:
  0.0 46.2 jit_solution(13393741264576376139)
XLA Ops:
  0.6 2.3 %pick_rows.1 = (f32[24,4096]{1,0:T(8,128)S(1)}, s32[4,128]{1,0:T(4,128)S(1)}, f32[2,128]{1,0:T(2,128)S(1)}, f32[1,4096]{1,0:T(1,128)S(1)}, f32[3,1,4096]{2,1,0:T...) custom-call(f32[24,4096]{1,0:T(8,128)} %bitcast.11, s32[4,128]{1,0:T(4,128)} %bitcast.14, ...), custom_call_target="tpu_custom_call" | custom-call | tf_op jit(solution)/shard_map/pick_rows/pallas_call | solution.py:501
  2.9 2.4 %collective-permute-start = (f32[32,128]{1,0:T(8,128)S(1)}, f32[32,128]{1,0:T(8,128)S(1)}, u32[]{:S(2)}, u32[]{:S(2)}) collective-permute-start(f32[32,128]{1,0:T(8,128)S(1)} %get-tuple-element.29), channel_id=1, source_target_pairs={{0,4},{4,8},{8,12},{12,16},{16,20},{20,24},{24,28},{1,5},{5,9},{9,... | collective-permute-start | bytes 49160 | tf_op jit(solution)/shard_map/ppermute | solution.py:510
  5.3 4.2 %collective-permute-start.1 = (f32[32,128]{1,0:T(8,128)S(1)}, f32[32,128]{1,0:T(8,128)S(1)}, u32[]{:S(2)}, u32[]{:S(2)}) collective-permute-start(f32[32,128]{1,0:T(8,128)S(1)} %get-tuple-element.31), channel_id=1, source_target_pairs={{0,1},{1,2},{2,3},{4,5},{5,6},{6,7},{8,9},{9,10},{10,11},{12,13},{... | collective-permute-start | bytes 49160 | tf_op jit(solution)/shard_map/ppermute | solution.py:511
  9.5 1.2 %own_rows.1 = (f32[24,4096]{1,0:T(8,128)S(1)}, f32[24,24]{1,0:T(8,128)S(1)}) custom-call(f32[24,4096]{1,0:T(8,128)S(1)} %get-tuple-element.22.vectors_ref, f32[1,4096]{1,0:T(1,128)S(1)} %get-tuple-element.23.mass_ref, f32[3,1,4096]{2,1,0:T(1,128)S(1)} %get-tuple-element.24.inner_ref, f32[2,128]{1,0:T(2,128)S(1)} %get-tuple-element.25.face_ref, ...), custom_call_target="tpu_custom_call" | custom-call | tf_op jit(solution)/shard_map/own_rows/pallas_call | solution.py:475
  10.7 0.0 collective-permute-done.sub_ref.before_sub_ref
  10.7 0.3 collective-permute-done.1.layer_ref.before_layer_ref
  10.9 1.1 %coarse_tiles.1 = (f32[32,16,128]{2,1,0:T(8,128)}, f32[24,128]{1,0:T(8,128)S(1)}, f32[24,128]{1,0:T(8,128)S(1)}) custom-call(f32[24,24]{1,0:T(8,128)S(1)} %get-tuple-element.30.own_ref, f32[4,24,128]{2,1,0:T(8,128)S(1)} %get-tuple-element.26.picked_ref, f32[32,128]{1,0:T(8,128)S(1)} %collective-permute-done.sub_ref.before_sub_ref, ...), custom_call_target="tpu_custom_call" | custom-call | tf_op jit(solution)/shard_map/coarse_tiles/pallas_call | solution.py:475
  12.0 6.8 %all-to-all-start = ((f32[32,16,128]{2,1,0:T(8,128)}), f32[32,16,128]{2,1,0:T(8,128)S(1)}, u32[]{:S(2)}, u32[]{:S(2)}) async-start(f32[32,16,128]{2,1,0:T(8,128)} %get-tuple-element.35), calls=%async_computation | async-start | bytes 524288 | tf_op jit(solution)/shard_map/all_to_all | solution.py:524
  18.9 1.3 %collective-permute-start.2 = (f32[24,128]{1,0:T(8,128)S(1)}, f32[24,128]{1,0:T(8,128)S(1)}, u32[]{:S(2)}, u32[]{:S(2)}) collective-permute-start(f32[24,128]{1,0:T(8,128)S(1)} %get-tuple-element.32), channel_id=1, source_target_pairs={{4,0},{8,4},{12,8},{16,12},{20,16},{24,20},{28,24},{5,1},{9,5},{13... | collective-permute-start | bytes 36872 | tf_op jit(solution)/shard_map/ppermute | solution.py:525
  20.2 1.3 %collective-permute-start.3 = (f32[24,128]{1,0:T(8,128)S(1)}, f32[24,128]{1,0:T(8,128)S(1)}, u32[]{:S(2)}, u32[]{:S(2)}) collective-permute-start(f32[24,128]{1,0:T(8,128)S(1)} %get-tuple-element.33), channel_id=1, source_target_pairs={{1,0},{2,1},{3,2},{5,4},{6,5},{7,6},{9,8},{10,9},{11,10},{13,12},{... | collective-permute-start | bytes 36872 | tf_op jit(solution)/shard_map/ppermute | solution.py:526
  21.5 0.5 %collective-permute-done.2.after_sub_ref = f32[24,128]{1,0:T(8,128)S(1)} collective-permute-done((f32[24,128]{1,0:T(8,128)S(1)}, f32[24,128]{1,0:T(8,128)S(1)}, u32[]{:S(2)}, u32[]{:S(2)}) %collective-permute-start.2) | collective-permute-done | bytes 12320 | tf_op jit(solution)/shard_map/ppermute | solution.py:525
  21.9 3.8 %collective-permute-done.3.after_layer_ref = f32[24,128]{1,0:T(8,128)S(1)} collective-permute-done((f32[24,128]{1,0:T(8,128)S(1)}, f32[24,128]{1,0:T(8,128)S(1)}, u32[]{:S(2)}, u32[]{:S(2)}) %collective-permute-start.3) | collective-permute-done | bytes 12320 | tf_op jit(solution)/shard_map/ppermute | solution.py:526
  25.8 1.3 %spread_rows.1 = (f32[24,4096]{1,0:T(8,128)}, f32[8,128]{1,0:T(8,128)S(1)}) custom-call(f32[24,4096]{1,0:T(8,128)S(1)} %get-tuple-element.27.base_ref, s32[4,128]{1,0:T(4,128)S(1)} %get-tuple-element.28.lists_ref, f32[2,128]{1,0:T(2,128)S(1)} %get-tuple-element.25.face_ref, f32[4,24,128]{2,1,0:T(8,128)S(1)} %get-tuple-element.26.picked_ref, ...), custom_call_target="tpu_custom_call" | custom-call | tf_op jit(solution)/shard_map/spread_rows/pallas_call | solution.py:475
  27.1 2.7 %all-to-all-done = f32[32,16,128]{2,1,0:T(8,128)S(1)} async-done(((f32[32,16,128]{2,1,0:T(8,128)}), f32[32,16,128]{2,1,0:T(8,128)S(1)}, u32[]{:S(2)}, u32[]{:S(2)}) %all-to-all-start) | async-done | bytes 262176 | tf_op jit(solution)/shard_map/all_to_all | solution.py:524
  29.8 16.4 %factor_planes.1 = (f32[24,96]{1,0:T(8,128)}, f32[24,96]{1,0:T(8,128)}, f32[24,96]{1,0:T(8,128)}) custom-call(f32[8,4,16,128]{3,2,1,0:T(8,128)S(1)} %bitcast.10, f32[8,128]{1,0:T(8,128)S(1)} %get-tuple-element.36.after_ref), custom_call_target="tpu_custom_call" | custom-call | tf_op jit(solution)/shard_map/factor_planes/pallas_call | solution.py:330
Async XLA Ops:
  2.9 7.8 %collective-permute-start = (f32[32,128]{1,0:T(8,128)S(1)}, f32[32,128]{1,0:T(8,128)S(1)}, u32[]{:S(2)}, u32[]{:S(2)}) collective-permute-start(f32[32,128]{1,0:T(8,128)S(1)} %get-tuple-element.29), channel_id=1, source_target_pairs={{0,4},{4,8},{8,12},{12,16},{16,20},{20,24},{24,28},{1,5},{5,9},{9,... | collective-permute-start | bytes 49160 | tf_op jit(solution)/shard_map/ppermute | solution.py:510
  5.3 5.7 %collective-permute-start.1 = (f32[32,128]{1,0:T(8,128)S(1)}, f32[32,128]{1,0:T(8,128)S(1)}, u32[]{:S(2)}, u32[]{:S(2)}) collective-permute-start(f32[32,128]{1,0:T(8,128)S(1)} %get-tuple-element.31), channel_id=1, source_target_pairs={{0,1},{1,2},{2,3},{4,5},{5,6},{6,7},{8,9},{9,10},{10,11},{12,13},{... | collective-permute-start | bytes 49160 | tf_op jit(solution)/shard_map/ppermute | solution.py:511
  12.0 17.8 %all-to-all-start = ((f32[32,16,128]{2,1,0:T(8,128)}), f32[32,16,128]{2,1,0:T(8,128)S(1)}, u32[]{:S(2)}, u32[]{:S(2)}) async-start(f32[32,16,128]{2,1,0:T(8,128)} %get-tuple-element.35), calls=%async_computation | async-start | bytes 524288 | tf_op jit(solution)/shard_map/all_to_all | solution.py:524
  18.9 3.1 %collective-permute-start.2 = (f32[24,128]{1,0:T(8,128)S(1)}, f32[24,128]{1,0:T(8,128)S(1)}, u32[]{:S(2)}, u32[]{:S(2)}) collective-permute-start(f32[24,128]{1,0:T(8,128)S(1)} %get-tuple-element.32), channel_id=1, source_target_pairs={{4,0},{8,4},{12,8},{16,12},{20,16},{24,20},{28,24},{5,1},{9,5},{13... | collective-permute-start | bytes 36872 | tf_op jit(solution)/shard_map/ppermute | solution.py:525
  20.2 5.6 %collective-permute-start.3 = (f32[24,128]{1,0:T(8,128)S(1)}, f32[24,128]{1,0:T(8,128)S(1)}, u32[]{:S(2)}, u32[]{:S(2)}) collective-permute-start(f32[24,128]{1,0:T(8,128)S(1)} %get-tuple-element.33), channel_id=1, source_target_pairs={{1,0},{2,1},{3,2},{5,4},{6,5},{7,6},{9,8},{10,9},{11,10},{13,12},{... | collective-permute-start | bytes 36872 | tf_op jit(solution)/shard_map/ppermute | solution.py:526

commit v10 on v9

--- a/solution.py
+++ b/solution.py
@@ -12,6 +12,8 @@
 LANES = 128
 ROWS = 8
 UNROLLED_LAYERS = 4
+PLANES_AT_ONCE = 2
+CUTS = 4
 
 
 def turned_dot(left, right):
@@ -75,7 +77,8 @@
 
 
 def eliminate_pair(block, columns, pivots, iota, q, k):
-    first, second = columns[k], columns[k + 1]
+    start = q * ROWS
+    first, second = columns[start + k], columns[start + k + 1]
     corner, joint = spread_row(first[0], k), spread_row(first[0], k + 1)
     other_corner = spread_row(second[0], k + 1)
     minor = corner * other_corner - joint * joint
@@ -86,10 +89,12 @@
     other_below = [column * other_inverse for column in second]
     below[0] = jnp.where(iota > k, below[0], 0.0)
     other_below[0] = jnp.where(iota > k + 1, other_below[0], 0.0)
-    for j in range(k + 2, ROWS):
-        head, other_head = spread_row(first[0], j), spread_row(second[0], j)
+    for j in range(start + k + 2, len(columns)):
+        strip = j // ROWS - q
+        head = spread_row(first[strip], j % ROWS)
+        other_head = spread_row(second[strip], j % ROWS)
         columns[j] = [
-            column - below[r] * head - other_below[r] * other_head
+            column - below[strip + r] * head - other_below[strip + r] * other_head
             for r, column in enumerate(columns[j])
         ]
     for t in range(len(block[q])):
@@ -107,20 +112,20 @@
     iota = lax.broadcasted_iota(jnp.int32, (ROWS, LANES), 0)
     lane = lax.broadcasted_iota(jnp.int32, (ROWS, LANES), 1)
     blocks = [[list(strip) for strip in block] for block in blocks]
+    at_once = len(blocks) <= PLANES_AT_ONCE
+    held = [[] for _ in blocks]
     for q in range(strip_count):
         start = q * ROWS
-        held = []
-        for b, block in enumerate(blocks):
-            source = turned(b, block, q)
-            held.append(
-                [
-                    [
-                        jnp.broadcast_to(strip[:, start + j : start + j + 1], (ROWS, LANES))
-                        for strip in source
-                    ]
-                    for j in range(ROWS)
-                ]
-            )
+        if q == 0 or not at_once:
+            for b, block in enumerate(blocks):
+                source = turned(b, block, q)
+                for j in range(start, strip_count * ROWS if at_once else start + ROWS):
+                    held[b].append(
+                        [
+                            jnp.broadcast_to(strip[:, j : j + 1], (ROWS, LANES))
+                            for strip in source[j // ROWS - q :]
+                        ]
+                    )
         pivots = [jnp.zeros((ROWS, LANES), jnp.float32) for _ in blocks]
         for k in range(0, ROWS, 2):
             for b, block in enumerate(blocks):
@@ -256,31 +261,37 @@
     part = grid_ref.shape[2] // 3
     unrolled = layers <= UNROLLED_LAYERS
     del after_ref
-    grid_ref[...] = jnp.zeros_like(grid_ref)
-
-    def place_tiles(s, has_left):
-        for j in range(layers):
-            tile = unpack_tile(tiles_ref[s, j], modes)
-            turned = tile.T
+    lane = lax.broadcasted_iota(jnp.int32, (modes, part), 1)
+    inside = [(lane >= j * modes) & (lane < (j + 1) * modes) for j in range(layers)]
+
+    def place_tiles(s, before):
+        tiles = [unpack_tile(tiles_ref[s, j], modes) for j in range(layers)]
+        stacked = tiles
+        if part > order:
+            stacked = tiles + [jnp.zeros((part - order, tiles[0].shape[1]), jnp.float32)]
+        turned = jnp.concatenate(stacked, axis=0).T
+        for j, tile in enumerate(tiles):
             rows = slice(j * modes, (j + 1) * modes)
-            grid_ref[s, rows, j * modes : (j + 1) * modes] = tile[:, 0:modes]
-            if j > 0:
-                above = slice((j - 1) * modes, j * modes)
-                grid_ref[s, above, j * modes : (j + 1) * modes] = tile[:, modes : 2 * modes]
-            if has_left:
-                lanes = slice(part + j * modes, part + (j + 1) * modes)
-                grid_ref[s, rows, lanes] = turned[2 * modes : 3 * modes]
-                lanes = slice(2 * part + j * modes, 2 * part + (j + 1) * modes)
-                grid_ref[s - 1, rows, lanes] = tile[:, 2 * modes : 3 * modes]
-
-    place_tiles(0, False)
+            own = jnp.where(inside[j], turned[0:modes], 0.0)
+            if j + 1 < layers:
+                own = jnp.where(inside[j + 1], turned[modes : 2 * modes], own)
+            grid_ref[s, rows, 0:part] = own
+            spare = jnp.zeros((modes, part - 3 * modes), jnp.float32)
+            wide = jnp.concatenate([tile, spare], axis=1)
+            shift = (j - 2) * modes % part
+            down = pltpu.roll(wide, shift, 1) if shift else wide
+            grid_ref[s, rows, part : 2 * part] = jnp.where(inside[j], down, 0.0)
+            down = jnp.where(inside[j], turned[2 * modes : 3 * modes], 0.0)
+            grid_ref[before, rows, 2 * part : 3 * part] = down
+
+    place_tiles(0, subs - 1)
     if unrolled:
         for s in range(1, subs):
-            place_tiles(s, True)
+            place_tiles(s, s - 1)
     else:
 
         def place_one(s, carry):
-            place_tiles(s, True)
+            place_tiles(s, s - 1)
             return carry
 
         lax.fori_loop(1, subs, place_one, 0)
@@ -355,10 +366,11 @@
     modes, row_count = vectors_ref.shape
     strips = modes // ROWS
     pairs = [(lists_in, lists_ref)]
-    pairs += [
-        (vectors_in.at[pl.ds(r * ROWS, ROWS)], vectors_ref.at[pl.ds(r * ROWS, ROWS)])
-        for r in range(strips)
-    ]
+    cut = row_count // CUTS
+    for r in range(strips):
+        for c in range(CUTS):
+            piece = (pl.ds(r * ROWS, ROWS), pl.ds(c * cut, cut))
+            pairs.append((vectors_in.at[piece], vectors_ref.at[piece]))
     pairs += [(face_in, face_ref), (mass_in, mass_ref), (inner_in, inner_ref)]
     copies = [pltpu.make_async_copy(a, b, sems.at[i]) for i, (a, b) in enumerate(pairs)]
     for copy in copies:
@@ -369,7 +381,8 @@
         rows = jnp.broadcast_to(lists_ref[k : k + 1, :], (ROWS, LANES))
         lists.append((rows // LANES, rows % LANES))
     for r in range(strips):
-        copies[1 + r].wait()
+        for c in range(CUTS):
+            copies[1 + r * CUTS + c].wait()
         strip = slice(r * ROWS, (r + 1) * ROWS)
         found = [jnp.zeros((ROWS, LANES), jnp.float32) for _ in range(4)]
         for c in range(row_count // LANES):
@@ -379,7 +392,7 @@
                 found[k] = jnp.where(tile_of == c, moved, found[k])
         for k in range(4):
             picked_ref[k, strip] = found[k]
-    for copy in copies[1 + strips :]:
+    for copy in copies[1 + strips * CUTS :]:
         copy.wait()
     for k, send_ref in ((0, sub_ref), (2, layer_ref)):
         send_ref[0:modes] = picked_ref[k]
@@ -415,12 +428,12 @@
         mine = picked_ref[k]
         sprung = theirs_ref[modes : modes + 1] * mine
         stacked = jnp.concatenate([mine, theirs_ref[0:modes]], axis=0)
-        pairs.append(across_dot(stacked, sprung))
+        pairs.append(across_dot(sprung, stacked))
     down, side = pairs
-    diag_tile = (own_ref[...] + down[0:modes] + side[0:modes]) * inverse
-    side_turned = -side[modes:] * inverse
-    down_turned = -down[modes:] * inverse
-    packed = pack_tile(jnp.concatenate([diag_tile, side_turned, down_turned], axis=1))
+    diag_tile = (own_ref[...] + down[:, 0:modes] + side[:, 0:modes]) * inverse
+    side_tile = -side[:, modes:] * inverse
+    down_tile = -down[:, modes:] * inverse
+    packed = pack_tile(jnp.concatenate([diag_tile, side_tile, down_tile], axis=1))
     for s in range(copies_ref.shape[0]):
         copies_ref[s] = packed
     sub_send_ref[...] = picked_ref[1]
@@ -503,7 +516,7 @@
         out_shape=tuple(jax.ShapeDtypeStruct(*pair) for pair in held),
         in_specs=[pl.BlockSpec(memory_space=pltpu.HBM)] * len(taken),
         out_specs=(VMEM_BLOCK,) * len(held),
-        scratch_shapes=[pltpu.SemaphoreType.DMA((len(taken) + modes // ROWS - 1,))],
+        scratch_shapes=[pltpu.SemaphoreType.DMA((len(taken) + CUTS * modes // ROWS - 1,))],
         compiler_params=kernel_params([shape for shape, _ in held]),
         name="pick_rows",
     )(*(pltpu.with_memory_space_constraint(x, pltpu.HBM) for x in taken))

time: 46.5 us -> 44.1 us (0.948)
  Pallas kernels: 22.2 us -> 19.9 us
    pallas_call x1, Pallas kernels: 16.4 us -> 14 us  [factor_planes(): pl.pallas_call(factor_kernel, out_shape=(strip, strip, strip), in_specs=[...]
  transfers between devices with their start and end apart: 5 -> 5, of which waited for: 4 -> 4; matrix products, arithmetic and copies ran while one was open for 0% -> 0% of each run, Pallas kernels for 5% -> 6%
where the time goes in v10:
time: 44.1 us; the launch traced here: 43.8 us
  Pallas kernels  19.9 us (45%)
  starting transfers between devices  16 us (36%)
  waiting for transfers between devices  7.3 us (17%)
  between operations  0.68 us (2%)
    pallas_call x1, Pallas kernels, factor_planes(): pl.pallas_call(factor_kernel, out_shape=(strip, strip, strip), in_specs=[...  14 us
    all_to_all x1, starting transfers between devices, per_device(): lax.all_to_all(copies, ('sub', 'layer'), split_axis=0, concat_axis=0, til...  6.83 us
    ppermute x1, starting transfers between devices, per_device(): before_layer = lax.ppermute(layer_send, 'layer', up_layer)  4.23 us
    ppermute x1, waiting for transfers between devices, per_device(): after_layer = lax.ppermute(layer_send, 'layer', down_layer)  3.82 us
    pallas_call x3, Pallas kernels, local_call(): pl.pallas_call(body, out_shape=shapes, in_specs=[VMEM_BLOCK] * len(operan...  3.59 us
    all_to_all x1, waiting for transfers between devices, per_device(): lax.all_to_all(copies, ('sub', 'layer'), split_axis=0, concat_axis=0, til...  2.75 us
    ppermute x1, starting transfers between devices, per_device(): before_sub = lax.ppermute(sub_send, 'sub', up_sub)  2.36 us
    pallas_call x1, Pallas kernels, per_device(): pl.pallas_call(pick_kernel, out_shape=tuple((jax.ShapeDtypeStruct(*pair)...  2.25 us
  transfers between devices with their start and end apart: 5, of which 4 were waited for; matrix products, arithmetic and copies ran while one was open for 0% of the time, Pallas kernels for 6%

profile of v10, /device:TPU:0, one launch (start us, length us, event | category | flops | bytes accessed | tf_op | source)
XLA Modules:
  0.0 43.8 jit_solution(12883562589653685192)
XLA Ops:
  0.6 2.2 %pick_rows.1 = (f32[24,4096]{1,0:T(8,128)S(1)}, s32[4,128]{1,0:T(4,128)S(1)}, f32[2,128]{1,0:T(2,128)S(1)}, f32[1,4096]{1,0:T(1,128)S(1)}, f32[3,1,4096]{2,1,0:T...) custom-call(f32[24,4096]{1,0:T(8,128)} %bitcast.11, s32[4,128]{1,0:T(4,128)} %bitcast.14, ...), custom_call_target="tpu_custom_call" | custom-call | tf_op jit(solution)/shard_map/pick_rows/pallas_call | solution.py:514
  2.9 2.4 %collective-permute-start = (f32[32,128]{1,0:T(8,128)S(1)}, f32[32,128]{1,0:T(8,128)S(1)}, u32[]{:S(2)}, u32[]{:S(2)}) collective-permute-start(f32[32,128]{1,0:T(8,128)S(1)} %get-tuple-element.29), channel_id=1, source_target_pairs={{0,4},{4,8},{8,12},{12,16},{16,20},{20,24},{24,28},{1,5},{5,9},{9,... | collective-permute-start | bytes 49160 | tf_op jit(solution)/shard_map/ppermute | solution.py:523
  5.3 4.2 %collective-permute-start.1 = (f32[32,128]{1,0:T(8,128)S(1)}, f32[32,128]{1,0:T(8,128)S(1)}, u32[]{:S(2)}, u32[]{:S(2)}) collective-permute-start(f32[32,128]{1,0:T(8,128)S(1)} %get-tuple-element.31), channel_id=1, source_target_pairs={{0,1},{1,2},{2,3},{4,5},{5,6},{6,7},{8,9},{9,10},{10,11},{12,13},{... | collective-permute-start | bytes 49160 | tf_op jit(solution)/shard_map/ppermute | solution.py:524
  9.5 1.2 %own_rows.1 = (f32[24,4096]{1,0:T(8,128)S(1)}, f32[24,24]{1,0:T(8,128)S(1)}) custom-call(f32[24,4096]{1,0:T(8,128)S(1)} %get-tuple-element.22.vectors_ref, f32[1,4096]{1,0:T(1,128)S(1)} %get-tuple-element.23.mass_ref, f32[3,1,4096]{2,1,0:T(1,128)S(1)} %get-tuple-element.24.inner_ref, f32[2,128]{1,0:T(2,128)S(1)} %get-tuple-element.25.face_ref, ...), custom_call_target="tpu_custom_call" | custom-call | tf_op jit(solution)/shard_map/own_rows/pallas_call | solution.py:488
  10.6 0.0 collective-permute-done.sub_ref.before_sub_ref
  10.6 0.3 collective-permute-done.1.layer_ref.before_layer_ref
  10.9 1.1 %coarse_tiles.1 = (f32[32,16,128]{2,1,0:T(8,128)}, f32[24,128]{1,0:T(8,128)S(1)}, f32[24,128]{1,0:T(8,128)S(1)}) custom-call(f32[24,24]{1,0:T(8,128)S(1)} %get-tuple-element.30.own_ref, f32[4,24,128]{2,1,0:T(8,128)S(1)} %get-tuple-element.26.picked_ref, f32[32,128]{1,0:T(8,128)S(1)} %collective-permute-done.sub_ref.before_sub_ref, ...), custom_call_target="tpu_custom_call" | custom-call | tf_op jit(solution)/shard_map/coarse_tiles/pallas_call | solution.py:488
  12.0 6.8 %all-to-all-start = ((f32[32,16,128]{2,1,0:T(8,128)}), f32[32,16,128]{2,1,0:T(8,128)S(1)}, u32[]{:S(2)}, u32[]{:S(2)}) async-start(f32[32,16,128]{2,1,0:T(8,128)} %get-tuple-element.35), calls=%async_computation | async-start | bytes 524288 | tf_op jit(solution)/shard_map/all_to_all | solution.py:537
  18.9 1.3 %collective-permute-start.2 = (f32[24,128]{1,0:T(8,128)S(1)}, f32[24,128]{1,0:T(8,128)S(1)}, u32[]{:S(2)}, u32[]{:S(2)}) collective-permute-start(f32[24,128]{1,0:T(8,128)S(1)} %get-tuple-element.32), channel_id=1, source_target_pairs={{4,0},{8,4},{12,8},{16,12},{20,16},{24,20},{28,24},{5,1},{9,5},{13... | collective-permute-start | bytes 36872 | tf_op jit(solution)/shard_map/ppermute | solution.py:538
  20.2 1.3 %collective-permute-start.3 = (f32[24,128]{1,0:T(8,128)S(1)}, f32[24,128]{1,0:T(8,128)S(1)}, u32[]{:S(2)}, u32[]{:S(2)}) collective-permute-start(f32[24,128]{1,0:T(8,128)S(1)} %get-tuple-element.33), channel_id=1, source_target_pairs={{1,0},{2,1},{3,2},{5,4},{6,5},{7,6},{9,8},{10,9},{11,10},{13,12},{... | collective-permute-start | bytes 36872 | tf_op jit(solution)/shard_map/ppermute | solution.py:539
  21.5 0.5 %collective-permute-done.2.after_sub_ref = f32[24,128]{1,0:T(8,128)S(1)} collective-permute-done((f32[24,128]{1,0:T(8,128)S(1)}, f32[24,128]{1,0:T(8,128)S(1)}, u32[]{:S(2)}, u32[]{:S(2)}) %collective-permute-start.2) | collective-permute-done | bytes 12320 | tf_op jit(solution)/shard_map/ppermute | solution.py:538
  21.9 3.8 %collective-permute-done.3.after_layer_ref = f32[24,128]{1,0:T(8,128)S(1)} collective-permute-done((f32[24,128]{1,0:T(8,128)S(1)}, f32[24,128]{1,0:T(8,128)S(1)}, u32[]{:S(2)}, u32[]{:S(2)}) %collective-permute-start.3) | collective-permute-done | bytes 12320 | tf_op jit(solution)/shard_map/ppermute | solution.py:539
  25.8 1.3 %spread_rows.1 = (f32[24,4096]{1,0:T(8,128)}, f32[8,128]{1,0:T(8,128)S(1)}) custom-call(f32[24,4096]{1,0:T(8,128)S(1)} %get-tuple-element.27.base_ref, s32[4,128]{1,0:T(4,128)S(1)} %get-tuple-element.28.lists_ref, f32[2,128]{1,0:T(2,128)S(1)} %get-tuple-element.25.face_ref, f32[4,24,128]{2,1,0:T(8,128)S(1)} %get-tuple-element.26.picked_ref, ...), custom_call_target="tpu_custom_call" | custom-call | tf_op jit(solution)/shard_map/spread_rows/pallas_call | solution.py:488
  27.1 2.7 %all-to-all-done = f32[32,16,128]{2,1,0:T(8,128)S(1)} async-done(((f32[32,16,128]{2,1,0:T(8,128)}), f32[32,16,128]{2,1,0:T(8,128)S(1)}, u32[]{:S(2)}, u32[]{:S(2)}) %all-to-all-start) | async-done | bytes 262176 | tf_op jit(solution)/shard_map/all_to_all | solution.py:537
  29.8 14.0 %factor_planes.1 = (f32[24,96]{1,0:T(8,128)}, f32[24,96]{1,0:T(8,128)}, f32[24,96]{1,0:T(8,128)}) custom-call(f32[8,4,16,128]{3,2,1,0:T(8,128)S(1)} %bitcast.10, f32[8,128]{1,0:T(8,128)S(1)} %get-tuple-element.36.after_ref), custom_call_target="tpu_custom_call" | custom-call | tf_op jit(solution)/shard_map/factor_planes/pallas_call | solution.py:341
Async XLA Ops:
  2.9 7.8 %collective-permute-start = (f32[32,128]{1,0:T(8,128)S(1)}, f32[32,128]{1,0:T(8,128)S(1)}, u32[]{:S(2)}, u32[]{:S(2)}) collective-permute-start(f32[32,128]{1,0:T(8,128)S(1)} %get-tuple-element.29), channel_id=1, source_target_pairs={{0,4},{4,8},{8,12},{12,16},{16,20},{20,24},{24,28},{1,5},{5,9},{9,... | collective-permute-start | bytes 49160 | tf_op jit(solution)/shard_map/ppermute | solution.py:523
  5.3 5.7 %collective-permute-start.1 = (f32[32,128]{1,0:T(8,128)S(1)}, f32[32,128]{1,0:T(8,128)S(1)}, u32[]{:S(2)}, u32[]{:S(2)}) collective-permute-start(f32[32,128]{1,0:T(8,128)S(1)} %get-tuple-element.31), channel_id=1, source_target_pairs={{0,1},{1,2},{2,3},{4,5},{5,6},{6,7},{8,9},{9,10},{10,11},{12,13},{... | collective-permute-start | bytes 49160 | tf_op jit(solution)/shard_map/ppermute | solution.py:524
  12.0 17.8 %all-to-all-start = ((f32[32,16,128]{2,1,0:T(8,128)}), f32[32,16,128]{2,1,0:T(8,128)S(1)}, u32[]{:S(2)}, u32[]{:S(2)}) async-start(f32[32,16,128]{2,1,0:T(8,128)} %get-tuple-element.35), calls=%async_computation | async-start | bytes 524288 | tf_op jit(solution)/shard_map/all_to_all | solution.py:537
  18.9 3.1 %collective-permute-start.2 = (f32[24,128]{1,0:T(8,128)S(1)}, f32[24,128]{1,0:T(8,128)S(1)}, u32[]{:S(2)}, u32[]{:S(2)}) collective-permute-start(f32[24,128]{1,0:T(8,128)S(1)} %get-tuple-element.32), channel_id=1, source_target_pairs={{4,0},{8,4},{12,8},{16,12},{20,16},{24,20},{28,24},{5,1},{9,5},{13... | collective-permute-start | bytes 36872 | tf_op jit(solution)/shard_map/ppermute | solution.py:538
  20.2 5.6 %collective-permute-start.3 = (f32[24,128]{1,0:T(8,128)S(1)}, f32[24,128]{1,0:T(8,128)S(1)}, u32[]{:S(2)}, u32[]{:S(2)}) collective-permute-start(f32[24,128]{1,0:T(8,128)S(1)} %get-tuple-element.33), channel_id=1, source_target_pairs={{1,0},{2,1},{3,2},{5,4},{6,5},{7,6},{9,8},{10,9},{11,10},{13,12},{... | collective-permute-start | bytes 36872 | tf_op jit(solution)/shard_map/ppermute | solution.py:539

commit v11 on v10

--- a/solution.py
+++ b/solution.py
@@ -13,7 +13,7 @@
 ROWS = 8
 UNROLLED_LAYERS = 4
 PLANES_AT_ONCE = 2
-CUTS = 4
+NARROW_DEPTH = LANES + LANES // 4
 
 
 def turned_dot(left, right):
@@ -42,24 +42,23 @@
     )
 
 
-def narrow_product(panel_rows, part, below, end):
-    modes = panel_rows.shape[0]
-    first, second, third = pieces_of(panel_rows)
-    stacked = jnp.concatenate([x[:, 0:part] for x in (first, second, third)], axis=0)
-    turned = stacked.T[below:end]
-    lane = lax.broadcasted_iota(jnp.int32, (end - below, LANES), 1)
-    wide = jnp.concatenate(
-        [turned, jnp.zeros((end - below, LANES - 3 * modes), jnp.float32)], axis=1
-    )
+def narrow_columns(turned, modes):
+    height = turned.shape[0]
+    lane = lax.broadcasted_iota(jnp.int32, (height, LANES), 1)
+    wide = jnp.concatenate([turned, jnp.zeros((height, LANES - 3 * modes), jnp.float32)], axis=1)
     again = pltpu.roll(wide, 3 * modes, 1)
     left = jnp.where(lane < 3 * modes, wide, jnp.where(lane < 5 * modes, again, 0.0))
     last = jnp.where(lane < modes, wide, 0.0)
-    depth = LANES + 2 * LANES // 8
-    columns = jnp.concatenate([left, last], axis=1)[:, 0:depth]
-    gap = jnp.zeros((LANES - 5 * modes, panel_rows.shape[1]), jnp.float32)
-    tail = jnp.zeros((depth - LANES - modes, panel_rows.shape[1]), jnp.float32)
+    return jnp.concatenate([left, last], axis=1)[:, 0:NARROW_DEPTH].astype(jnp.bfloat16)
+
+
+def narrow_rows(pieces):
+    first, second, third = pieces
+    modes, width = first.shape
+    gap = jnp.zeros((LANES - 5 * modes, width), jnp.float32)
+    tail = jnp.zeros((NARROW_DEPTH - LANES - modes, width), jnp.float32)
     rows = jnp.concatenate([first] * 3 + [second] * 2 + [gap, third, tail], axis=0)
-    return single_dot(columns.astype(jnp.bfloat16), rows.astype(jnp.bfloat16))
+    return rows.astype(jnp.bfloat16)
 
 
 def plain_dot(left, right):
@@ -141,7 +140,7 @@
     return blocks
 
 
-def eliminate_panel(grid_ref, planes, modes, order, part, lanes_used, panel, banded):
+def eliminate_panel(grid_ref, planes, modes, order, part, lanes_used, panel, banded, distance):
     per_part = part // LANES
     first_row = panel * modes
     static = isinstance(panel, int)
@@ -181,9 +180,14 @@
         if static:
             below = (panel + 1) * modes
             end = min(below + modes, order) if banded else order
+            pieces = pieces_of(panel_rows)
+            right = narrow_rows(pieces)
+            stacked = jnp.concatenate(pieces, axis=0)
             if below < order:
-                update = narrow_product(panel_rows, part, below, end)
-                grid_ref[plane, below:end, 0:lanes_used] -= update
+                columns = narrow_columns(stacked[:, 0:part].T[below:end], modes)
+                grid_ref[plane, below:end, 0:lanes_used] -= single_dot(columns, right)
+            if distance:
+                share_panel(grid_ref, plane, distance, stacked, right, modes, order, part, panel)
         else:
             lane = lax.broadcasted_iota(jnp.int32, (modes, part), 1)
             columns = jnp.where(lane >= first_row + modes, panel_rows[:, 0:part], 0.0)
@@ -191,18 +195,41 @@
             grid_ref[plane, :, 0:lanes_used] -= update
 
 
-def eliminate_planes(grid_ref, planes, modes, order, part, lanes_used, banded=False):
+def eliminate_planes(
+    grid_ref, planes, modes, order, part, lanes_used, banded=False, distance=0
+):
     layers = order // modes
     if layers <= UNROLLED_LAYERS:
         for panel in range(layers):
-            eliminate_panel(grid_ref, planes, modes, order, part, lanes_used, panel, banded)
+            eliminate_panel(
+                grid_ref, planes, modes, order, part, lanes_used, panel, banded, distance
+            )
     else:
 
         def one_panel(panel, carry):
-            eliminate_panel(grid_ref, planes, modes, order, part, lanes_used, panel, banded)
+            eliminate_panel(grid_ref, planes, modes, order, part, lanes_used, panel, banded, 0)
             return carry
 
         lax.fori_loop(0, layers, one_panel, 0)
+
+
+def share_panel(grid_ref, plane, distance, stacked, right, modes, order, part, panel):
+    left_plane, right_plane = plane - distance, plane + distance
+    turned = stacked[:, part : 3 * part].T
+    both = right[:, part : 3 * part]
+
+    def add(row_lanes, other, square, cross):
+        found = single_dot(narrow_columns(turned[row_lanes : row_lanes + order], modes), both)
+        grid_ref[other, :, 0:part] -= found[:, square : square + part]
+        crossed = found[:, part - square : 2 * part - square]
+        if panel == 0:
+            grid_ref[other, :, cross : cross + part] = -crossed
+        else:
+            grid_ref[other, :, cross : cross + part] -= crossed
+
+    add(part, right_plane, part, part)
+    if left_plane >= 0:
+        add(0, left_plane, 0, 2 * part)
 
 
 def update_partners(grid_ref, plane, distance, part, order, has_left):
@@ -300,8 +327,11 @@
     while distance < subs:
         if unrolled:
             planes = list(range(distance - 1, subs, 2 * distance))
-            eliminate_planes(grid_ref, planes, modes, order, part, 3 * part, distance == 1)
-            for plane in planes:
+            share = distance if len(planes) <= PLANES_AT_ONCE else 0
+            eliminate_planes(
+                grid_ref, planes, modes, order, part, 3 * part, distance == 1, share
+            )
+            for plane in planes if not share else []:
                 update_partners(grid_ref, plane, distance, part, order, plane >= distance)
         else:
 
@@ -324,6 +354,7 @@
 
 
 VMEM_BLOCK = pl.BlockSpec(memory_space=pltpu.VMEM)
+HBM_BLOCK = pl.BlockSpec(memory_space=pltpu.HBM)
 SPARE_BYTES = 4 * 1024 * 1024
 
 
@@ -359,51 +390,59 @@
     )
 
 
+def pick_lists(vectors_ref, lists_ref, chosen, strip):
+    lists = []
+    for k in chosen:
+        rows = jnp.broadcast_to(lists_ref[k : k + 1, :], (ROWS, LANES))
+        lists.append((rows // LANES, rows % LANES))
+    found = [jnp.zeros((ROWS, LANES), jnp.float32) for _ in lists]
+    for c in range(vectors_ref.shape[1] // LANES):
+        tile = vectors_ref[strip, c * LANES : (c + 1) * LANES]
+        for i, (tile_of, lane_of) in enumerate(lists):
+            moved = jnp.take_along_axis(tile, lane_of, axis=1, mode="promise_in_bounds")
+            found[i] = jnp.where(tile_of == c, moved, found[i])
+    return found
+
+
 def pick_kernel(
-    vectors_in, lists_in, face_in, mass_in, inner_in,
-    vectors_ref, lists_ref, face_ref, mass_ref, inner_ref, picked_ref, sub_ref, layer_ref, sems
+    vectors_in, lists_in, face_in, vectors_ref, lists_ref, face_ref, sub_ref, layer_ref, sems
 ):
-    modes, row_count = vectors_ref.shape
-    strips = modes // ROWS
+    modes = vectors_ref.shape[0]
+    strips = [slice(first, first + ROWS) for first in range(0, modes, ROWS)]
     pairs = [(lists_in, lists_ref)]
-    cut = row_count // CUTS
-    for r in range(strips):
-        for c in range(CUTS):
-            piece = (pl.ds(r * ROWS, ROWS), pl.ds(c * cut, cut))
-            pairs.append((vectors_in.at[piece], vectors_ref.at[piece]))
-    pairs += [(face_in, face_ref), (mass_in, mass_ref), (inner_in, inner_ref)]
+    pairs += [(vectors_in.at[pl.ds(s.start, ROWS)], vectors_ref.at[pl.ds(s.start, ROWS)]) for s in strips]
+    pairs += [(face_in, face_ref)]
     copies = [pltpu.make_async_copy(a, b, sems.at[i]) for i, (a, b) in enumerate(pairs)]
     for copy in copies:
         copy.start()
     copies[0].wait()
-    lists = []
-    for k in range(4):
-        rows = jnp.broadcast_to(lists_ref[k : k + 1, :], (ROWS, LANES))
-        lists.append((rows // LANES, rows % LANES))
-    for r in range(strips):
-        for c in range(CUTS):
-            copies[1 + r * CUTS + c].wait()
-        strip = slice(r * ROWS, (r + 1) * ROWS)
-        found = [jnp.zeros((ROWS, LANES), jnp.float32) for _ in range(4)]
-        for c in range(row_count // LANES):
-            tile = vectors_ref[strip, c * LANES : (c + 1) * LANES]
-            for k, (tile_of, lane_of) in enumerate(lists):
-                moved = jnp.take_along_axis(tile, lane_of, axis=1, mode="promise_in_bounds")
-                found[k] = jnp.where(tile_of == c, moved, found[k])
-        for k in range(4):
-            picked_ref[k, strip] = found[k]
-    for copy in copies[1 + strips * CUTS :]:
+    copies[-1].wait()
+    for k, send_ref in ((0, sub_ref), (2, layer_ref)):
+        send_ref[modes:] = jnp.broadcast_to(face_ref[k // 2 : k // 2 + 1, :], (ROWS, LANES))
+    for copy, strip in zip(copies[1:], strips):
         copy.wait()
-    for k, send_ref in ((0, sub_ref), (2, layer_ref)):
-        send_ref[0:modes] = picked_ref[k]
-        send_ref[modes:] = jnp.broadcast_to(face_ref[k // 2 : k // 2 + 1, :], (ROWS, LANES))
+        sub_ref[strip], layer_ref[strip] = pick_lists(vectors_ref, lists_ref, (0, 2), strip)
 
 
 def own_kernel(
-    vectors_ref, mass_ref, inner_ref, face_ref, picked_ref, base_ref, own_ref, *, subs, layers
+    mass_in, inner_in, vectors_ref, lists_ref, face_ref, sub_ref, layer_ref,
+    base_ref, own_ref, before_sub_ref, before_layer_ref, mass_ref, inner_ref, sems, *, subs, layers
 ):
+    copies = [
+        pltpu.make_async_copy(mass_in, mass_ref, sems.at[0]),
+        pltpu.make_async_copy(inner_in, inner_ref, sems.at[1]),
+    ]
+    for copy in copies:
+        copy.start()
     vectors = vectors_ref[...]
-    row_count = vectors.shape[1]
+    modes, row_count = vectors.shape
+    for first in range(0, modes, ROWS):
+        strip = slice(first, first + ROWS)
+        before_sub_ref[strip], before_layer_ref[strip] = pick_lists(
+            vectors_ref, lists_ref, (1, 3), strip
+        )
+    for copy in copies:
+        copy.wait()
     places = lax.broadcasted_iota(jnp.int32, (1, row_count), 1)
     base = mass_ref[...] * vectors
     for k, t in enumerate(STRIDES):
@@ -412,20 +451,21 @@
         base = base + fluxes - pltpu.roll(fluxes, t, 1)
     base_ref[...] = base
     own = across_dot(vectors, base)
-    for k, axis, ends in ((0, "sub", subs - 1), (2, "layer", layers - 1)):
-        springs = jnp.where(lax.axis_index(axis) < ends, face_ref[k // 2 : k // 2 + 1, :], 0.0)
-        own = own + across_dot(picked_ref[k], springs * picked_ref[k])
+    for k, axis, ends, send_ref in ((0, "sub", subs - 1, sub_ref), (1, "layer", layers - 1, layer_ref)):
+        springs = jnp.where(lax.axis_index(axis) < ends, face_ref[k : k + 1, :], 0.0)
+        picked = send_ref[0:modes]
+        own = own + across_dot(picked, springs * picked)
     own_ref[...] = own
 
 
 def tile_kernel(
-    own_ref, picked_ref, sub_ref, layer_ref, copies_ref, sub_send_ref, layer_send_ref, *, row_count
+    own_ref, mine_sub_ref, mine_layer_ref, sub_ref, layer_ref, copies_ref, layer_send_ref, *, row_count
 ):
     modes = own_ref.shape[0]
     inverse = 1.0 / row_count
     pairs = []
-    for k, theirs_ref in ((1, sub_ref), (3, layer_ref)):
-        mine = picked_ref[k]
+    for mine_ref, theirs_ref in ((mine_sub_ref, sub_ref), (mine_layer_ref, layer_ref)):
+        mine = mine_ref[...]
         sprung = theirs_ref[modes : modes + 1] * mine
         stacked = jnp.concatenate([mine, theirs_ref[0:modes]], axis=0)
         pairs.append(across_dot(sprung, stacked))
@@ -436,12 +476,11 @@
     packed = pack_tile(jnp.concatenate([diag_tile, side_tile, down_tile], axis=1))
     for s in range(copies_ref.shape[0]):
         copies_ref[s] = packed
-    sub_send_ref[...] = picked_ref[1]
-    layer_send_ref[...] = picked_ref[3]
+    layer_send_ref[...] = mine_layer_ref[...]
 
 
 def scatter_kernel(
-    base_ref, lists_ref, face_ref, picked_ref, before_sub_ref, after_sub_ref,
+    base_ref, lists_ref, face_ref, up_sub_ref, down_sub_ref, up_layer_ref, down_layer_ref, before_sub_ref, after_sub_ref,
     before_layer_ref, after_layer_ref, applied_ref, token_ref, *, subs, layers
 ):
     modes, row_count = base_ref.shape
@@ -458,9 +497,8 @@
         after_layer_ref[...],
         before_layer_ref[0:modes, :],
     ]
-    pulls = jnp.concatenate(
-        [springs[k] * (picked_ref[k] - partners[k]) for k in range(4)], axis=1
-    )
+    picked = [up_sub_ref[0:modes], down_sub_ref[...], up_layer_ref[0:modes], down_layer_ref[...]]
+    pulls = jnp.concatenate([springs[k] * (picked[k] - partners[k]) for k in range(4)], axis=1)
     rows = jnp.concatenate([lists_ref[k : k + 1, :] for k in range(4)], axis=1)
     block_of, lane_of = rows // width, rows % width
     lanes = lax.broadcasted_iota(jnp.int32, (width, rows.shape[1]), 0)
@@ -507,40 +545,55 @@
     up_layer = [(i, i + 1) for i in range(layers - 1)]
     down_sub = [(i + 1, i) for i in range(subs - 1)]
     down_layer = [(i + 1, i) for i in range(layers - 1)]
-    taken = (vectors, row_lists, face_springs, row_mass[0], inner_weight[0].reshape(-1, 1, row_count))
-    held = [(x.shape, x.dtype) for x in taken]
-    made = [(4, modes, width), (modes + ROWS, width), (modes + ROWS, width)]
-    held += [(shape, jnp.float32) for shape in made]
-    vectors, row_lists, face_springs, masses, interior, picked, sub_send, layer_send = pl.pallas_call(
+    def pinned(*arrays):
+        return [pltpu.with_memory_space_constraint(x, pltpu.HBM) for x in arrays]
+
+    def shaped(*shapes):
+        return tuple(jax.ShapeDtypeStruct(shape, jnp.float32) for shape in shapes)
+
+    taken = (vectors, row_lists, face_springs)
+    held = tuple(jax.ShapeDtypeStruct(x.shape, x.dtype) for x in taken)
+    held += shaped((modes + ROWS, width), (modes + ROWS, width))
+    vectors, row_lists, face_springs, sub_send, layer_send = pl.pallas_call(
         pick_kernel,
-        out_shape=tuple(jax.ShapeDtypeStruct(*pair) for pair in held),
-        in_specs=[pl.BlockSpec(memory_space=pltpu.HBM)] * len(taken),
+        out_shape=held,
+        in_specs=[HBM_BLOCK] * len(taken),
         out_specs=(VMEM_BLOCK,) * len(held),
-        scratch_shapes=[pltpu.SemaphoreType.DMA((len(taken) + CUTS * modes // ROWS - 1,))],
-        compiler_params=kernel_params([shape for shape, _ in held]),
+        scratch_shapes=[pltpu.SemaphoreType.DMA((2 + modes // ROWS,))],
+        compiler_params=kernel_params([x.shape for x in held]),
         name="pick_rows",
-    )(*(pltpu.with_memory_space_constraint(x, pltpu.HBM) for x in taken))
+    )(*pinned(*taken))
     before_sub = lax.ppermute(sub_send, "sub", up_sub)
     before_layer = lax.ppermute(layer_send, "layer", up_layer)
-    base, own = local_call(
+    masses, interior = row_mass[0], inner_weight[0].reshape(-1, 1, row_count)
+    made = shaped((modes, row_count), (modes, modes), (modes, width), (modes, width))
+    base, own, picked_sub, picked_layer = pl.pallas_call(
         functools.partial(own_kernel, subs=subs, layers=layers),
-        [(modes, row_count), (modes, modes)],
-        (vectors, masses, interior, face_springs, picked),
-        "own_rows",
-    )
-    copies, sub_send, layer_send = local_call(
+        out_shape=made,
+        in_specs=[HBM_BLOCK] * 2 + [VMEM_BLOCK] * len(held),
+        out_specs=(VMEM_BLOCK,) * len(made),
+        scratch_shapes=[
+            pltpu.VMEM(masses.shape, jnp.float32),
+            pltpu.VMEM(interior.shape, jnp.float32),
+            pltpu.SemaphoreType.DMA((2,)),
+        ],
+        compiler_params=kernel_params([x.shape for x in held + made]),
+        name="own_rows",
+    )(*pinned(masses, interior), vectors, row_lists, face_springs, sub_send, layer_send)
+    after_sub = lax.ppermute(picked_sub, "sub", down_sub)
+    copies, after_send = local_call(
         functools.partial(tile_kernel, row_count=row_count),
-        [(subs * layers, modes - ROWS, LANES), (modes, width), (modes, width)],
-        (own, picked, before_sub, before_layer),
+        [(subs * layers, modes - ROWS, LANES), (modes, width)],
+        (own, picked_sub, picked_layer, before_sub, before_layer),
         "coarse_tiles",
     )
     tiles = lax.all_to_all(copies, ("sub", "layer"), split_axis=0, concat_axis=0, tiled=True)
-    after_sub = lax.ppermute(sub_send, "sub", down_sub)
-    after_layer = lax.ppermute(layer_send, "layer", down_layer)
+    after_layer = lax.ppermute(after_send, "layer", down_layer)
     applied, token = local_call(
         functools.partial(scatter_kernel, subs=subs, layers=layers),
         [(modes, row_count), (ROWS, LANES)],
-        (base, row_lists, face_springs, picked, before_sub, after_sub, before_layer, after_layer),
+        (base, row_lists, face_springs, sub_send, picked_sub, layer_send, picked_layer)
+        + (before_sub, after_sub, before_layer, after_layer),
         "spread_rows",
     )
     diag_strip, left_strip, right_strip = factor_planes(

time: 44.1 us -> 43.9 us (level)
  starting transfers between devices: 16 us -> 15.4 us
    pallas_call x1 -> x2, Pallas kernels: 2.25 us -> 3.42 us  [the longest x1 2 us: per_device(): pl.pallas_call(functools.partial(own_kernel, subs=subs, layers=layers), o...]
    pallas_call x3 -> x2, Pallas kernels: 3.59 us -> 2.44 us  [local_call(): pl.pallas_call(body, out_shape=shapes, in_specs=[VMEM_BLOCK] * len(operan...]
    all_to_all x1, starting transfers between devices: 6.83 us -> 6.23 us  [per_device(): lax.all_to_all(copies, ('sub', 'layer'), split_axis=0, concat_axis=0, til...]
    pallas_call x1, Pallas kernels: 14 us -> 14.5 us  [factor_planes(): pl.pallas_call(factor_kernel, out_shape=(strip, strip, strip), in_specs=[...]
  transfers between devices with their start and end apart: 5 -> 5, of which waited for: 4 -> 3; matrix products, arithmetic and copies ran while one was open for 0% -> 0% of each run, Pallas kernels for 6% -> 8%
where the time goes in v11:
time: 43.9 us; the launch traced here: 43.5 us
  Pallas kernels  20.3 us (46%)
  starting transfers between devices  15.4 us (35%)
  waiting for transfers between devices  7.04 us (16%)
  between operations  0.7 us (2%)
    pallas_call x1, Pallas kernels, factor_planes(): pl.pallas_call(factor_kernel, out_shape=(strip, strip, strip), in_specs=[...  14.5 us
    all_to_all x1, starting transfers between devices, per_device(): lax.all_to_all(copies, ('sub', 'layer'), split_axis=0, concat_axis=0, til...  6.23 us
    ppermute x1, starting transfers between devices, per_device(): before_layer = lax.ppermute(layer_send, 'layer', up_layer)  4.23 us
    ppermute x1, waiting for transfers between devices, per_device(): after_layer = lax.ppermute(after_send, 'layer', down_layer)  3.82 us
    all_to_all x1, waiting for transfers between devices, per_device(): lax.all_to_all(copies, ('sub', 'layer'), split_axis=0, concat_axis=0, til...  2.75 us
    pallas_call x2, Pallas kernels, local_call(): pl.pallas_call(body, out_shape=shapes, in_specs=[VMEM_BLOCK] * len(operan...  2.44 us
    ppermute x1, starting transfers between devices, per_device(): before_sub = lax.ppermute(sub_send, 'sub', up_sub)  2.36 us
    pallas_call x1, Pallas kernels, per_device(): pl.pallas_call(functools.partial(own_kernel, subs=subs, layers=layers), o...  2 us
  transfers between devices with their start and end apart: 5, of which 3 were waited for; matrix products, arithmetic and copies ran while one was open for 0% of the time, Pallas kernels for 8%

profile of v11, /device:TPU:0, one launch (start us, length us, event | category | flops | bytes accessed | tf_op | source)
XLA Modules:
  0.0 43.5 jit_solution(7903126764148738239)
XLA Ops:
  0.6 1.4 %pick_rows.1 = (f32[24,4096]{1,0:T(8,128)S(1)}, s32[4,128]{1,0:T(4,128)S(1)}, f32[2,128]{1,0:T(2,128)S(1)}, f32[32,128]{1,0:T(8,128)S(1)}, f32[32,128]{1,0:T(8,128)S(1)}) custom-call(f32[24,4096]{1,0:T(8,128)} %bitcast.11, s32[4,128]{1,0:T(4,128)} %bitcast.14, f32[2,128]{1,0:T(2,128)} %bitcast.15), custom_call_target="tpu_custom_call" | custom-call | tf_op jit(solution)/shard_map/pick_rows/pallas_call | solution.py:557
  2.1 2.4 %collective-permute-start = (f32[32,128]{1,0:T(8,128)S(1)}, f32[32,128]{1,0:T(8,128)S(1)}, u32[]{:S(2)}, u32[]{:S(2)}) collective-permute-start(f32[32,128]{1,0:T(8,128)S(1)} %get-tuple-element.23.sub_ref.up_sub_ref), channel_id=1, source_target_pairs={{0,4},{4,8},{8,12},{12,16},{16,20},{20,24},{24,28},{1,5},{5,9},{9,... | collective-permute-start | bytes 49160 | tf_op jit(solution)/shard_map/ppermute | solution.py:566
  4.4 4.2 %collective-permute-start.2 = (f32[32,128]{1,0:T(8,128)S(1)}, f32[32,128]{1,0:T(8,128)S(1)}, u32[]{:S(2)}, u32[]{:S(2)}) collective-permute-start(f32[32,128]{1,0:T(8,128)S(1)} %get-tuple-element.24.layer_ref.up_layer_ref), channel_id=1, source_target_pairs={{0,1},{1,2},{2,3},{4,5},{5,6},{6,7},{8,9},{9,10},{10,11},{12,13},{... | collective-permute-start | bytes 49160 | tf_op jit(solution)/shard_map/ppermute | solution.py:567
  8.7 2.0 %own_rows.1 = (f32[24,4096]{1,0:T(8,128)S(1)}, f32[24,24]{1,0:T(8,128)S(1)}, f32[24,128]{1,0:T(8,128)S(1)}, f32[24,128]{1,0:T(8,128)S(1)}) custom-call(f32[1,4096]{1,0:T(1,128)} %bitcast.13, f32[3,1,4096]{2,1,0:T(1,128)} %bitcast.12, f32[24,4096]{1,0:T(8,128)S(1)} %get-tuple-element.20.vectors_ref, s32[4,128]{1,0:T(4,128)S(1)} %get-tuple-element.21.lists_ref, ...), custom_call_target="tpu_custom_call" | custom-call | tf_op jit(solution)/shard_map/own_rows/pallas_call | solution.py:570
  10.7 0.0 collective-permute-done.sub_ref.before_sub_ref
  10.7 0.0 collective-permute-done.2.layer_ref.before_layer_ref
  10.7 1.1 %coarse_tiles.1 = (f32[32,16,128]{2,1,0:T(8,128)}, f32[24,128]{1,0:T(8,128)S(1)}) custom-call(f32[24,24]{1,0:T(8,128)S(1)} %get-tuple-element.28.own_ref, f32[24,128]{1,0:T(8,128)S(1)} %get-tuple-element.26.mine_sub_ref.down_sub_ref, f32[24,128]{1,0:T(8,128)S(1)} %get-tuple-element.27.mine_layer_ref.down_layer_ref, ...), custom_call_target="tpu_custom_call" | custom-call | tf_op jit(solution)/shard_map/coarse_tiles/pallas_call | solution.py:526
  11.8 6.2 %all-to-all-start = ((f32[32,16,128]{2,1,0:T(8,128)}), f32[32,16,128]{2,1,0:T(8,128)S(1)}, u32[]{:S(2)}, u32[]{:S(2)}) async-start(f32[32,16,128]{2,1,0:T(8,128)} %get-tuple-element.31), calls=%async_computation | async-start | bytes 524288 | tf_op jit(solution)/shard_map/all_to_all | solution.py:590
  18.0 1.3 %collective-permute-start.1 = (f32[24,128]{1,0:T(8,128)S(1)}, f32[24,128]{1,0:T(8,128)S(1)}, u32[]{:S(2)}, u32[]{:S(2)}) collective-permute-start(f32[24,128]{1,0:T(8,128)S(1)} %get-tuple-element.26.mine_sub_ref.down_sub_ref), channel_id=1, source_target_pairs={{4,0},{8,4},{12,8},{16,12},{20,16},{24,20},{28,24},{5,1},{9,5},{13... | collective-permute-start | bytes 36872 | tf_op jit(solution)/shard_map/ppermute | solution.py:583
  19.3 1.3 %collective-permute-start.3 = (f32[24,128]{1,0:T(8,128)S(1)}, f32[24,128]{1,0:T(8,128)S(1)}, u32[]{:S(2)}, u32[]{:S(2)}) collective-permute-start(f32[24,128]{1,0:T(8,128)S(1)} %get-tuple-element.29), channel_id=1, source_target_pairs={{1,0},{2,1},{3,2},{5,4},{6,5},{7,6},{9,8},{10,9},{11,10},{13,12},{... | collective-permute-start | bytes 36872 | tf_op jit(solution)/shard_map/ppermute | solution.py:591
  20.6 0.5 %collective-permute-done.1.after_sub_ref = f32[24,128]{1,0:T(8,128)S(1)} collective-permute-done((f32[24,128]{1,0:T(8,128)S(1)}, f32[24,128]{1,0:T(8,128)S(1)}, u32[]{:S(2)}, u32[]{:S(2)}) %collective-permute-start.1) | collective-permute-done | bytes 12320 | tf_op jit(solution)/shard_map/ppermute | solution.py:583
  21.1 3.8 %collective-permute-done.3.after_layer_ref = f32[24,128]{1,0:T(8,128)S(1)} collective-permute-done((f32[24,128]{1,0:T(8,128)S(1)}, f32[24,128]{1,0:T(8,128)S(1)}, u32[]{:S(2)}, u32[]{:S(2)}) %collective-permute-start.3) | collective-permute-done | bytes 12320 | tf_op jit(solution)/shard_map/ppermute | solution.py:591
  24.9 1.3 %spread_rows.1 = (f32[24,4096]{1,0:T(8,128)}, f32[8,128]{1,0:T(8,128)S(1)}) custom-call(f32[24,4096]{1,0:T(8,128)S(1)} %get-tuple-element.25.base_ref, s32[4,128]{1,0:T(4,128)S(1)} %get-tuple-element.21.lists_ref, f32[2,128]{1,0:T(2,128)S(1)} %get-tuple-element.22.face_ref, f32[32,128]{1,0:T(8,128)S(1)} %get-tuple-element.23.sub_ref.up_sub_ref, ...), custom_call_target="tpu_custom_call" | custom-call | tf_op jit(solution)/shard_map/spread_rows/pallas_call | solution.py:526
  26.2 2.7 %all-to-all-done = f32[32,16,128]{2,1,0:T(8,128)S(1)} async-done(((f32[32,16,128]{2,1,0:T(8,128)}), f32[32,16,128]{2,1,0:T(8,128)S(1)}, u32[]{:S(2)}, u32[]{:S(2)}) %all-to-all-start) | async-done | bytes 262176 | tf_op jit(solution)/shard_map/all_to_all | solution.py:590
  29.0 14.5 %factor_planes.1 = (f32[24,96]{1,0:T(8,128)}, f32[24,96]{1,0:T(8,128)}, f32[24,96]{1,0:T(8,128)}) custom-call(f32[8,4,16,128]{3,2,1,0:T(8,128)S(1)} %bitcast.10, f32[8,128]{1,0:T(8,128)S(1)} %get-tuple-element.32.after_ref), custom_call_target="tpu_custom_call" | custom-call | tf_op jit(solution)/shard_map/factor_planes/pallas_call | solution.py:372
Async XLA Ops:
  2.1 8.6 %collective-permute-start = (f32[32,128]{1,0:T(8,128)S(1)}, f32[32,128]{1,0:T(8,128)S(1)}, u32[]{:S(2)}, u32[]{:S(2)}) collective-permute-start(f32[32,128]{1,0:T(8,128)S(1)} %get-tuple-element.23.sub_ref.up_sub_ref), channel_id=1, source_target_pairs={{0,4},{4,8},{8,12},{12,16},{16,20},{20,24},{24,28},{1,5},{5,9},{9,... | collective-permute-start | bytes 49160 | tf_op jit(solution)/shard_map/ppermute | solution.py:566
  4.4 6.3 %collective-permute-start.2 = (f32[32,128]{1,0:T(8,128)S(1)}, f32[32,128]{1,0:T(8,128)S(1)}, u32[]{:S(2)}, u32[]{:S(2)}) collective-permute-start(f32[32,128]{1,0:T(8,128)S(1)} %get-tuple-element.24.layer_ref.up_layer_ref), channel_id=1, source_target_pairs={{0,1},{1,2},{2,3},{4,5},{5,6},{6,7},{8,9},{9,10},{10,11},{12,13},{... | collective-permute-start | bytes 49160 | tf_op jit(solution)/shard_map/ppermute | solution.py:567
  11.8 17.2 %all-to-all-start = ((f32[32,16,128]{2,1,0:T(8,128)}), f32[32,16,128]{2,1,0:T(8,128)S(1)}, u32[]{:S(2)}, u32[]{:S(2)}) async-start(f32[32,16,128]{2,1,0:T(8,128)} %get-tuple-element.31), calls=%async_computation | async-start | bytes 524288 | tf_op jit(solution)/shard_map/all_to_all | solution.py:590
  18.0 3.1 %collective-permute-start.1 = (f32[24,128]{1,0:T(8,128)S(1)}, f32[24,128]{1,0:T(8,128)S(1)}, u32[]{:S(2)}, u32[]{:S(2)}) collective-permute-start(f32[24,128]{1,0:T(8,128)S(1)} %get-tuple-element.26.mine_sub_ref.down_sub_ref), channel_id=1, source_target_pairs={{4,0},{8,4},{12,8},{16,12},{20,16},{24,20},{28,24},{5,1},{9,5},{13... | collective-permute-start | bytes 36872 | tf_op jit(solution)/shard_map/ppermute | solution.py:583
  19.3 5.6 %collective-permute-start.3 = (f32[24,128]{1,0:T(8,128)S(1)}, f32[24,128]{1,0:T(8,128)S(1)}, u32[]{:S(2)}, u32[]{:S(2)}) collective-permute-start(f32[24,128]{1,0:T(8,128)S(1)} %get-tuple-element.29), channel_id=1, source_target_pairs={{1,0},{2,1},{3,2},{5,4},{6,5},{7,6},{9,8},{10,9},{11,10},{13,12},{... | collective-permute-start | bytes 36872 | tf_op jit(solution)/shard_map/ppermute | solution.py:591

commit v12 on v11

--- a/solution.py
+++ b/solution.py
@@ -140,7 +140,7 @@
     return blocks
 
 
-def eliminate_panel(grid_ref, planes, modes, order, part, lanes_used, panel, banded, distance):
+def eliminate_panel(grid_ref, planes, modes, order, part, lanes_used, panel, banded):
     per_part = part // LANES
     first_row = panel * modes
     static = isinstance(panel, int)
@@ -186,8 +186,6 @@
             if below < order:
                 columns = narrow_columns(stacked[:, 0:part].T[below:end], modes)
                 grid_ref[plane, below:end, 0:lanes_used] -= single_dot(columns, right)
-            if distance:
-                share_panel(grid_ref, plane, distance, stacked, right, modes, order, part, panel)
         else:
             lane = lax.broadcasted_iota(jnp.int32, (modes, part), 1)
             columns = jnp.where(lane >= first_row + modes, panel_rows[:, 0:part], 0.0)
@@ -195,41 +193,18 @@
             grid_ref[plane, :, 0:lanes_used] -= update
 
 
-def eliminate_planes(
-    grid_ref, planes, modes, order, part, lanes_used, banded=False, distance=0
-):
+def eliminate_planes(grid_ref, planes, modes, order, part, lanes_used, banded=False):
     layers = order // modes
     if layers <= UNROLLED_LAYERS:
         for panel in range(layers):
-            eliminate_panel(
-                grid_ref, planes, modes, order, part, lanes_used, panel, banded, distance
-            )
+            eliminate_panel(grid_ref, planes, modes, order, part, lanes_used, panel, banded)
     else:
 
         def one_panel(panel, carry):
-            eliminate_panel(grid_ref, planes, modes, order, part, lanes_used, panel, banded, 0)
+            eliminate_panel(grid_ref, planes, modes, order, part, lanes_used, panel, banded)
             return carry
 
         lax.fori_loop(0, layers, one_panel, 0)
-
-
-def share_panel(grid_ref, plane, distance, stacked, right, modes, order, part, panel):
-    left_plane, right_plane = plane - distance, plane + distance
-    turned = stacked[:, part : 3 * part].T
-    both = right[:, part : 3 * part]
-
-    def add(row_lanes, other, square, cross):
-        found = single_dot(narrow_columns(turned[row_lanes : row_lanes + order], modes), both)
-        grid_ref[other, :, 0:part] -= found[:, square : square + part]
-        crossed = found[:, part - square : 2 * part - square]
-        if panel == 0:
-            grid_ref[other, :, cross : cross + part] = -crossed
-        else:
-            grid_ref[other, :, cross : cross + part] -= crossed
-
-    add(part, right_plane, part, part)
-    if left_plane >= 0:
-        add(0, left_plane, 0, 2 * part)
 
 
 def update_partners(grid_ref, plane, distance, part, order, has_left):
@@ -327,11 +302,8 @@
     while distance < subs:
         if unrolled:
             planes = list(range(distance - 1, subs, 2 * distance))
-            share = distance if len(planes) <= PLANES_AT_ONCE else 0
-            eliminate_planes(
-                grid_ref, planes, modes, order, part, 3 * part, distance == 1, share
-            )
-            for plane in planes if not share else []:
+            eliminate_planes(grid_ref, planes, modes, order, part, 3 * part, distance == 1)
+            for plane in planes:
                 update_partners(grid_ref, plane, distance, part, order, plane >= distance)
         else:
 
@@ -381,13 +353,27 @@
 
 
 def across_dot(left, right):
-    return lax.dot_general(
-        left,
-        right,
+    rows, columns = left.shape[0], right.shape[0]
+
+    def stacked(values):
+        short = -3 * values.shape[0] % (2 * ROWS)
+        spare = [jnp.zeros((short, values.shape[1]), jnp.float32)] if short else []
+        return jnp.concatenate(list(pieces_of(values)) + spare, axis=0).astype(jnp.bfloat16)
+
+    found = lax.dot_general(
+        stacked(left),
+        stacked(right),
         (((1,), (1,)), ((), ())),
-        precision=HIGHEST,
         preferred_element_type=jnp.float32,
     )
+    total = None
+    for b in (2, 1, 0):
+        column = found[:, b * columns : (b + 1) * columns]
+        for a in (2, 1, 0):
+            if (a, b) in PRODUCTS:
+                block = column[a * rows : (a + 1) * rows]
+                total = block if total is None else total + block
+    return total
 
 
 def pick_lists(vectors_ref, lists_ref, chosen, strip):
@@ -405,7 +391,7 @@
 
 
 def pick_kernel(
-    vectors_in, lists_in, face_in, vectors_ref, lists_ref, face_ref, sub_ref, layer_ref, sems
+    vectors_in, lists_in, face_in, vectors_ref, lists_ref, face_ref, layer_ref, sub_ref, sems
 ):
     modes = vectors_ref.shape[0]
     strips = [slice(first, first + ROWS) for first in range(0, modes, ROWS)]
@@ -459,7 +445,7 @@
 
 
 def tile_kernel(
-    own_ref, mine_sub_ref, mine_layer_ref, sub_ref, layer_ref, copies_ref, layer_send_ref, *, row_count
+    own_ref, mine_layer_ref, mine_sub_ref, layer_ref, sub_ref, copies_ref, layer_send_ref, *, row_count
 ):
     modes = own_ref.shape[0]
     inverse = 1.0 / row_count
@@ -554,7 +540,7 @@
     taken = (vectors, row_lists, face_springs)
     held = tuple(jax.ShapeDtypeStruct(x.shape, x.dtype) for x in taken)
     held += shaped((modes + ROWS, width), (modes + ROWS, width))
-    vectors, row_lists, face_springs, sub_send, layer_send = pl.pallas_call(
+    vectors, row_lists, face_springs, layer_send, sub_send = pl.pallas_call(
         pick_kernel,
         out_shape=held,
         in_specs=[HBM_BLOCK] * len(taken),
@@ -563,8 +549,8 @@
         compiler_params=kernel_params([x.shape for x in held]),
         name="pick_rows",
     )(*pinned(*taken))
+    before_layer = lax.ppermute(layer_send, "layer", up_layer)
     before_sub = lax.ppermute(sub_send, "sub", up_sub)
-    before_layer = lax.ppermute(layer_send, "layer", up_layer)
     masses, interior = row_mass[0], inner_weight[0].reshape(-1, 1, row_count)
     made = shaped((modes, row_count), (modes, modes), (modes, width), (modes, width))
     base, own, picked_sub, picked_layer = pl.pallas_call(
@@ -584,7 +570,7 @@
     copies, after_send = local_call(
         functools.partial(tile_kernel, row_count=row_count),
         [(subs * layers, modes - ROWS, LANES), (modes, width)],
-        (own, picked_sub, picked_layer, before_sub, before_layer),
+        (own, picked_layer, picked_sub, before_layer, before_sub),
         "coarse_tiles",
     )
     tiles = lax.all_to_all(copies, ("sub", "layer"), split_axis=0, concat_axis=0, tiled=True)

time: 43.9 us -> 43.5 us (level)
    pallas_call x1, Pallas kernels: 14.5 us -> 14 us  [factor_planes(): pl.pallas_call(factor_kernel, out_shape=(strip, strip, strip), in_specs=[...]
where the time goes in v12:
time: 43.5 us; the launch traced here: 43.1 us
  Pallas kernels  19.9 us (46%)
  starting transfers between devices  15.4 us (35%)
  waiting for transfers between devices  7.04 us (16%)
  between operations  0.7 us (2%)
    pallas_call x1, Pallas kernels, factor_planes(): pl.pallas_call(factor_kernel, out_shape=(strip, strip, strip), in_specs=[...  14 us
    all_to_all x1, starting transfers between devices, per_device(): lax.all_to_all(copies, ('sub', 'layer'), split_axis=0, concat_axis=0, til...  6.26 us
    ppermute x1, starting transfers between devices, per_device(): before_layer = lax.ppermute(layer_send, 'layer', up_layer)  4.23 us
    ppermute x1, waiting for transfers between devices, per_device(): after_layer = lax.ppermute(after_send, 'layer', down_layer)  3.82 us
    all_to_all x1, waiting for transfers between devices, per_device(): lax.all_to_all(copies, ('sub', 'layer'), split_axis=0, concat_axis=0, til...  2.75 us
    pallas_call x2, Pallas kernels, local_call(): pl.pallas_call(body, out_shape=shapes, in_specs=[VMEM_BLOCK] * len(operan...  2.49 us
    ppermute x1, starting transfers between devices, per_device(): before_sub = lax.ppermute(sub_send, 'sub', up_sub)  2.36 us
    pallas_call x1, Pallas kernels, per_device(): pl.pallas_call(functools.partial(own_kernel, subs=subs, layers=layers), o...  1.96 us
  transfers between devices with their start and end apart: 5, of which 3 were waited for; matrix products, arithmetic and copies ran while one was open for 0% of the time, Pallas kernels for 8%

profile of v12, /device:TPU:0, one launch (start us, length us, event | category | flops | bytes accessed | tf_op | source)
XLA Modules:
  0.0 43.1 jit_solution(15953547084337134208)
XLA Ops:
  0.6 1.4 %pick_rows.1 = (f32[24,4096]{1,0:T(8,128)S(1)}, s32[4,128]{1,0:T(4,128)S(1)}, f32[2,128]{1,0:T(2,128)S(1)}, f32[32,128]{1,0:T(8,128)S(1)}, f32[32,128]{1,0:T(8,128)S(1)}) custom-call(f32[24,4096]{1,0:T(8,128)} %bitcast.11, s32[4,128]{1,0:T(4,128)} %bitcast.14, f32[2,128]{1,0:T(2,128)} %bitcast.15), custom_call_target="tpu_custom_call" | custom-call | tf_op jit(solution)/shard_map/pick_rows/pallas_call | solution.py:543
  2.1 2.4 %collective-permute-start = (f32[32,128]{1,0:T(8,128)S(1)}, f32[32,128]{1,0:T(8,128)S(1)}, u32[]{:S(2)}, u32[]{:S(2)}) collective-permute-start(f32[32,128]{1,0:T(8,128)S(1)} %get-tuple-element.23.sub_ref.up_sub_ref), channel_id=1, source_target_pairs={{0,4},{4,8},{8,12},{12,16},{16,20},{20,24},{24,28},{1,5},{5,9},{9,... | collective-permute-start | bytes 49160 | tf_op jit(solution)/shard_map/ppermute | solution.py:553
  4.4 4.2 %collective-permute-start.2 = (f32[32,128]{1,0:T(8,128)S(1)}, f32[32,128]{1,0:T(8,128)S(1)}, u32[]{:S(2)}, u32[]{:S(2)}) collective-permute-start(f32[32,128]{1,0:T(8,128)S(1)} %get-tuple-element.24.layer_ref.up_layer_ref), channel_id=1, source_target_pairs={{0,1},{1,2},{2,3},{4,5},{5,6},{6,7},{8,9},{9,10},{10,11},{12,13},{... | collective-permute-start | bytes 49160 | tf_op jit(solution)/shard_map/ppermute | solution.py:552
  8.7 2.0 %own_rows.1 = (f32[24,4096]{1,0:T(8,128)S(1)}, f32[24,24]{1,0:T(8,128)S(1)}, f32[24,128]{1,0:T(8,128)S(1)}, f32[24,128]{1,0:T(8,128)S(1)}) custom-call(f32[1,4096]{1,0:T(1,128)} %bitcast.13, f32[3,1,4096]{2,1,0:T(1,128)} %bitcast.12, f32[24,4096]{1,0:T(8,128)S(1)} %get-tuple-element.20.vectors_ref, s32[4,128]{1,0:T(4,128)S(1)} %get-tuple-element.21.lists_ref, ...), custom_call_target="tpu_custom_call" | custom-call | tf_op jit(solution)/shard_map/own_rows/pallas_call | solution.py:556
  10.6 0.0 collective-permute-done.sub_ref.before_sub_ref
  10.6 0.0 collective-permute-done.2.layer_ref.before_layer_ref
  10.6 1.2 %coarse_tiles.1 = (f32[32,16,128]{2,1,0:T(8,128)}, f32[24,128]{1,0:T(8,128)S(1)}) custom-call(f32[24,24]{1,0:T(8,128)S(1)} %get-tuple-element.28.own_ref, f32[24,128]{1,0:T(8,128)S(1)} %get-tuple-element.27.mine_layer_ref.down_layer_ref, f32[24,128]{1,0:T(8,128)S(1)} %get-tuple-element.26.mine_sub_ref.down_sub_ref, ...), custom_call_target="tpu_custom_call" | custom-call | tf_op jit(solution)/shard_map/coarse_tiles/pallas_call | solution.py:512
  11.8 6.3 %all-to-all-start = ((f32[32,16,128]{2,1,0:T(8,128)}), f32[32,16,128]{2,1,0:T(8,128)S(1)}, u32[]{:S(2)}, u32[]{:S(2)}) async-start(f32[32,16,128]{2,1,0:T(8,128)} %get-tuple-element.31), calls=%async_computation | async-start | bytes 524288 | tf_op jit(solution)/shard_map/all_to_all | solution.py:576
  18.1 1.3 %collective-permute-start.1 = (f32[24,128]{1,0:T(8,128)S(1)}, f32[24,128]{1,0:T(8,128)S(1)}, u32[]{:S(2)}, u32[]{:S(2)}) collective-permute-start(f32[24,128]{1,0:T(8,128)S(1)} %get-tuple-element.26.mine_sub_ref.down_sub_ref), channel_id=1, source_target_pairs={{4,0},{8,4},{12,8},{16,12},{20,16},{24,20},{28,24},{5,1},{9,5},{13... | collective-permute-start | bytes 36872 | tf_op jit(solution)/shard_map/ppermute | solution.py:569
  19.4 1.3 %collective-permute-start.3 = (f32[24,128]{1,0:T(8,128)S(1)}, f32[24,128]{1,0:T(8,128)S(1)}, u32[]{:S(2)}, u32[]{:S(2)}) collective-permute-start(f32[24,128]{1,0:T(8,128)S(1)} %get-tuple-element.29), channel_id=1, source_target_pairs={{1,0},{2,1},{3,2},{5,4},{6,5},{7,6},{9,8},{10,9},{11,10},{13,12},{... | collective-permute-start | bytes 36872 | tf_op jit(solution)/shard_map/ppermute | solution.py:577
  20.7 0.5 %collective-permute-done.1.after_sub_ref = f32[24,128]{1,0:T(8,128)S(1)} collective-permute-done((f32[24,128]{1,0:T(8,128)S(1)}, f32[24,128]{1,0:T(8,128)S(1)}, u32[]{:S(2)}, u32[]{:S(2)}) %collective-permute-start.1) | collective-permute-done | bytes 12320 | tf_op jit(solution)/shard_map/ppermute | solution.py:569
  21.2 3.8 %collective-permute-done.3.after_layer_ref = f32[24,128]{1,0:T(8,128)S(1)} collective-permute-done((f32[24,128]{1,0:T(8,128)S(1)}, f32[24,128]{1,0:T(8,128)S(1)}, u32[]{:S(2)}, u32[]{:S(2)}) %collective-permute-start.3) | collective-permute-done | bytes 12320 | tf_op jit(solution)/shard_map/ppermute | solution.py:577
  25.0 1.3 %spread_rows.1 = (f32[24,4096]{1,0:T(8,128)}, f32[8,128]{1,0:T(8,128)S(1)}) custom-call(f32[24,4096]{1,0:T(8,128)S(1)} %get-tuple-element.25.base_ref, s32[4,128]{1,0:T(4,128)S(1)} %get-tuple-element.21.lists_ref, f32[2,128]{1,0:T(2,128)S(1)} %get-tuple-element.22.face_ref, f32[32,128]{1,0:T(8,128)S(1)} %get-tuple-element.23.sub_ref.up_sub_ref, ...), custom_call_target="tpu_custom_call" | custom-call | tf_op jit(solution)/shard_map/spread_rows/pallas_call | solution.py:512
  26.3 2.7 %all-to-all-done = f32[32,16,128]{2,1,0:T(8,128)S(1)} async-done(((f32[32,16,128]{2,1,0:T(8,128)}), f32[32,16,128]{2,1,0:T(8,128)S(1)}, u32[]{:S(2)}, u32[]{:S(2)}) %all-to-all-start) | async-done | bytes 262176 | tf_op jit(solution)/shard_map/all_to_all | solution.py:576
  29.0 14.0 %factor_planes.1 = (f32[24,96]{1,0:T(8,128)}, f32[24,96]{1,0:T(8,128)}, f32[24,96]{1,0:T(8,128)}) custom-call(f32[8,4,16,128]{3,2,1,0:T(8,128)S(1)} %bitcast.10, f32[8,128]{1,0:T(8,128)S(1)} %get-tuple-element.32.after_ref), custom_call_target="tpu_custom_call" | custom-call | tf_op jit(solution)/shard_map/factor_planes/pallas_call | solution.py:344
Async XLA Ops:
  2.1 8.6 %collective-permute-start = (f32[32,128]{1,0:T(8,128)S(1)}, f32[32,128]{1,0:T(8,128)S(1)}, u32[]{:S(2)}, u32[]{:S(2)}) collective-permute-start(f32[32,128]{1,0:T(8,128)S(1)} %get-tuple-element.23.sub_ref.up_sub_ref), channel_id=1, source_target_pairs={{0,4},{4,8},{8,12},{12,16},{16,20},{20,24},{24,28},{1,5},{5,9},{9,... | collective-permute-start | bytes 49160 | tf_op jit(solution)/shard_map/ppermute | solution.py:553
  4.4 6.2 %collective-permute-start.2 = (f32[32,128]{1,0:T(8,128)S(1)}, f32[32,128]{1,0:T(8,128)S(1)}, u32[]{:S(2)}, u32[]{:S(2)}) collective-permute-start(f32[32,128]{1,0:T(8,128)S(1)} %get-tuple-element.24.layer_ref.up_layer_ref), channel_id=1, source_target_pairs={{0,1},{1,2},{2,3},{4,5},{5,6},{6,7},{8,9},{9,10},{10,11},{12,13},{... | collective-permute-start | bytes 49160 | tf_op jit(solution)/shard_map/ppermute | solution.py:552
  11.8 17.2 %all-to-all-start = ((f32[32,16,128]{2,1,0:T(8,128)}), f32[32,16,128]{2,1,0:T(8,128)S(1)}, u32[]{:S(2)}, u32[]{:S(2)}) async-start(f32[32,16,128]{2,1,0:T(8,128)} %get-tuple-element.31), calls=%async_computation | async-start | bytes 524288 | tf_op jit(solution)/shard_map/all_to_all | solution.py:576
  18.1 3.1 %collective-permute-start.1 = (f32[24,128]{1,0:T(8,128)S(1)}, f32[24,128]{1,0:T(8,128)S(1)}, u32[]{:S(2)}, u32[]{:S(2)}) collective-permute-start(f32[24,128]{1,0:T(8,128)S(1)} %get-tuple-element.26.mine_sub_ref.down_sub_ref), channel_id=1, source_target_pairs={{4,0},{8,4},{12,8},{16,12},{20,16},{24,20},{28,24},{5,1},{9,5},{13... | collective-permute-start | bytes 36872 | tf_op jit(solution)/shard_map/ppermute | solution.py:569
  19.4 5.6 %collective-permute-start.3 = (f32[24,128]{1,0:T(8,128)S(1)}, f32[24,128]{1,0:T(8,128)S(1)}, u32[]{:S(2)}, u32[]{:S(2)}) collective-permute-start(f32[24,128]{1,0:T(8,128)S(1)} %get-tuple-element.29), channel_id=1, source_target_pairs={{1,0},{2,1},{3,2},{5,4},{6,5},{7,6},{9,8},{10,9},{11,10},{13,12},{... | collective-permute-start | bytes 36872 | tf_op jit(solution)/shard_map/ppermute | solution.py:577

commit v13 on v12

--- a/solution.py
+++ b/solution.py
@@ -298,8 +298,9 @@
 
         lax.fori_loop(1, subs, place_one, 0)
 
-    distance = 1
-    while distance < subs:
+    sub_here, lay_here = lax.axis_index("sub"), lax.axis_index("layer")
+
+    def one_level(distance):
         if unrolled:
             planes = list(range(distance - 1, subs, 2 * distance))
             eliminate_planes(grid_ref, planes, modes, order, part, 3 * part, distance == 1)
@@ -307,17 +308,24 @@
                 update_partners(grid_ref, plane, distance, part, order, plane >= distance)
         else:
 
-            def one_plane(index, carry, distance=distance):
+            def one_plane(index, carry):
                 plane = distance - 1 + 2 * distance * index
                 eliminate_planes(grid_ref, [plane], modes, order, part, 3 * part)
                 update_partners(grid_ref, plane, distance, part, order, index > 0)
                 return carry
 
             lax.fori_loop(0, subs // (2 * distance), one_plane, 0)
+
+    one_level(1)
+    distance = 2
+    while distance < subs:
+        pl.when(lax.rem(sub_here + 1, distance) == 0)(functools.partial(one_level, distance))
         distance *= 2
-    eliminate_planes(grid_ref, [subs - 1], modes, order, part, part)
-
-    sub_here, lay_here = lax.axis_index("sub"), lax.axis_index("layer")
+
+    @pl.when(sub_here == subs - 1)
+    def _():
+        eliminate_planes(grid_ref, [subs - 1], modes, order, part, part)
+
     strip = pl.ds(pl.multiple_of(lay_here * modes, ROWS), modes)
     for k, out_ref in enumerate((diag_ref, left_ref, right_ref)):
         turned_ref[k] = grid_ref[sub_here, :, k * part : (k + 1) * part].T

time: 43.5 us -> 41.4 us (0.952)
  the two profiles are of different devices: /device:TPU:0 before, /device:TPU:27 now
where the time goes in v13:
time: 41.4 us; the launch traced here: 40.9 us
  Pallas kernels  20.9 us (50%)
  starting transfers between devices  16.2 us (39%)
  waiting for transfers between devices  3.17 us (8%)
  between operations  0.71 us (2%)
    pallas_call x1, Pallas kernels, factor_planes(): pl.pallas_call(factor_kernel, out_shape=(strip, strip, strip), in_specs=[...  15 us
    all_to_all x1, starting transfers between devices, per_device(): lax.all_to_all(copies, ('sub', 'layer'), split_axis=0, concat_axis=0, til...  7.31 us
    ppermute x1, waiting for transfers between devices, per_device(): after_layer = lax.ppermute(after_send, 'layer', down_layer)  3.16 us
    ppermute x1, starting transfers between devices, per_device(): before_layer = lax.ppermute(layer_send, 'layer', up_layer)  3.12 us
    pallas_call x2, Pallas kernels, local_call(): pl.pallas_call(body, out_shape=shapes, in_specs=[VMEM_BLOCK] * len(operan...  2.49 us
    ppermute x1, starting transfers between devices, per_device(): after_sub = lax.ppermute(picked_sub, 'sub', down_sub)  2.27 us
    ppermute x1, starting transfers between devices, per_device(): after_layer = lax.ppermute(after_send, 'layer', down_layer)  2.17 us
    pallas_call x1, Pallas kernels, per_device(): pl.pallas_call(functools.partial(own_kernel, subs=subs, layers=layers), o...  1.97 us
  transfers between devices with their start and end apart: 5, of which 1 were waited for; matrix products, arithmetic and copies ran while one was open for 0% of the time, Pallas kernels for 8%

profile of v13, /device:TPU:27, one launch (start us, length us, event | category | flops | bytes accessed | tf_op | source)
XLA Modules:
  0.0 40.9 jit_solution(8178997583200896895)
XLA Ops:
  0.6 1.4 %pick_rows.1 = (f32[24,4096]{1,0:T(8,128)S(1)}, s32[4,128]{1,0:T(4,128)S(1)}, f32[2,128]{1,0:T(2,128)S(1)}, f32[32,128]{1,0:T(8,128)S(1)}, f32[32,128]{1,0:T(8,128)S(1)}) custom-call(f32[24,4096]{1,0:T(8,128)} %bitcast.11, s32[4,128]{1,0:T(4,128)} %bitcast.14, f32[2,128]{1,0:T(2,128)} %bitcast.15), custom_call_target="tpu_custom_call" | custom-call | tf_op jit(solution)/shard_map/pick_rows/pallas_call | solution.py:551
  2.1 1.3 %collective-permute-start = (f32[32,128]{1,0:T(8,128)S(1)}, f32[32,128]{1,0:T(8,128)S(1)}, u32[]{:S(2)}, u32[]{:S(2)}) collective-permute-start(f32[32,128]{1,0:T(8,128)S(1)} %get-tuple-element.23.sub_ref.up_sub_ref), channel_id=1, source_target_pairs={{0,4},{4,8},{8,12},{12,16},{16,20},{20,24},{24,28},{1,5},{5,9},{9,... | collective-permute-start | bytes 49160 | tf_op jit(solution)/shard_map/ppermute | solution.py:561
  3.4 3.1 %collective-permute-start.2 = (f32[32,128]{1,0:T(8,128)S(1)}, f32[32,128]{1,0:T(8,128)S(1)}, u32[]{:S(2)}, u32[]{:S(2)}) collective-permute-start(f32[32,128]{1,0:T(8,128)S(1)} %get-tuple-element.24.layer_ref.up_layer_ref), channel_id=1, source_target_pairs={{0,1},{1,2},{2,3},{4,5},{5,6},{6,7},{8,9},{9,10},{10,11},{12,13},{... | collective-permute-start | bytes 49160 | tf_op jit(solution)/shard_map/ppermute | solution.py:560
  6.5 2.0 %own_rows.1 = (f32[24,4096]{1,0:T(8,128)S(1)}, f32[24,24]{1,0:T(8,128)S(1)}, f32[24,128]{1,0:T(8,128)S(1)}, f32[24,128]{1,0:T(8,128)S(1)}) custom-call(f32[1,4096]{1,0:T(1,128)} %bitcast.13, f32[3,1,4096]{2,1,0:T(1,128)} %bitcast.12, f32[24,4096]{1,0:T(8,128)S(1)} %get-tuple-element.20.vectors_ref, s32[4,128]{1,0:T(4,128)S(1)} %get-tuple-element.21.lists_ref, ...), custom_call_target="tpu_custom_call" | custom-call | tf_op jit(solution)/shard_map/own_rows/pallas_call | solution.py:564
  8.5 0.0 collective-permute-done.sub_ref.before_sub_ref
  8.5 0.0 collective-permute-done.2.layer_ref.before_layer_ref
  8.5 1.2 %coarse_tiles.1 = (f32[32,16,128]{2,1,0:T(8,128)}, f32[24,128]{1,0:T(8,128)S(1)}) custom-call(f32[24,24]{1,0:T(8,128)S(1)} %get-tuple-element.28.own_ref, f32[24,128]{1,0:T(8,128)S(1)} %get-tuple-element.27.mine_layer_ref.down_layer_ref, f32[24,128]{1,0:T(8,128)S(1)} %get-tuple-element.26.mine_sub_ref.down_sub_ref, ...), custom_call_target="tpu_custom_call" | custom-call | tf_op jit(solution)/shard_map/coarse_tiles/pallas_call | solution.py:520
  9.7 7.3 %all-to-all-start = ((f32[32,16,128]{2,1,0:T(8,128)}), f32[32,16,128]{2,1,0:T(8,128)S(1)}, u32[]{:S(2)}, u32[]{:S(2)}) async-start(f32[32,16,128]{2,1,0:T(8,128)} %get-tuple-element.31), calls=%async_computation | async-start | bytes 524288 | tf_op jit(solution)/shard_map/all_to_all | solution.py:584
  17.0 2.3 %collective-permute-start.1 = (f32[24,128]{1,0:T(8,128)S(1)}, f32[24,128]{1,0:T(8,128)S(1)}, u32[]{:S(2)}, u32[]{:S(2)}) collective-permute-start(f32[24,128]{1,0:T(8,128)S(1)} %get-tuple-element.26.mine_sub_ref.down_sub_ref), channel_id=1, source_target_pairs={{4,0},{8,4},{12,8},{16,12},{20,16},{24,20},{28,24},{5,1},{9,5},{13... | collective-permute-start | bytes 36872 | tf_op jit(solution)/shard_map/ppermute | solution.py:577
  19.2 2.2 %collective-permute-start.3 = (f32[24,128]{1,0:T(8,128)S(1)}, f32[24,128]{1,0:T(8,128)S(1)}, u32[]{:S(2)}, u32[]{:S(2)}) collective-permute-start(f32[24,128]{1,0:T(8,128)S(1)} %get-tuple-element.29), channel_id=1, source_target_pairs={{1,0},{2,1},{3,2},{5,4},{6,5},{7,6},{9,8},{10,9},{11,10},{13,12},{... | collective-permute-start | bytes 36872 | tf_op jit(solution)/shard_map/ppermute | solution.py:585
  21.4 0.0 collective-permute-done.1.after_sub_ref
  21.4 3.2 %collective-permute-done.3.after_layer_ref = f32[24,128]{1,0:T(8,128)S(1)} collective-permute-done((f32[24,128]{1,0:T(8,128)S(1)}, f32[24,128]{1,0:T(8,128)S(1)}, u32[]{:S(2)}, u32[]{:S(2)}) %collective-permute-start.3) | collective-permute-done | bytes 12320 | tf_op jit(solution)/shard_map/ppermute | solution.py:585
  24.6 1.3 %spread_rows.1 = (f32[24,4096]{1,0:T(8,128)}, f32[8,128]{1,0:T(8,128)S(1)}) custom-call(f32[24,4096]{1,0:T(8,128)S(1)} %get-tuple-element.25.base_ref, s32[4,128]{1,0:T(4,128)S(1)} %get-tuple-element.21.lists_ref, f32[2,128]{1,0:T(2,128)S(1)} %get-tuple-element.22.face_ref, f32[32,128]{1,0:T(8,128)S(1)} %get-tuple-element.23.sub_ref.up_sub_ref, ...), custom_call_target="tpu_custom_call" | custom-call | tf_op jit(solution)/shard_map/spread_rows/pallas_call | solution.py:520
  25.9 0.0 all-to-all-done
  25.9 15.0 %factor_planes.1 = (f32[24,96]{1,0:T(8,128)}, f32[24,96]{1,0:T(8,128)}, f32[24,96]{1,0:T(8,128)}) custom-call(f32[8,4,16,128]{3,2,1,0:T(8,128)S(1)} %bitcast.10, f32[8,128]{1,0:T(8,128)S(1)} %get-tuple-element.32.after_ref), custom_call_target="tpu_custom_call" | custom-call | tf_op jit(solution)/shard_map/factor_planes/pallas_call | solution.py:352
Async XLA Ops:
  2.1 6.4 %collective-permute-start = (f32[32,128]{1,0:T(8,128)S(1)}, f32[32,128]{1,0:T(8,128)S(1)}, u32[]{:S(2)}, u32[]{:S(2)}) collective-permute-start(f32[32,128]{1,0:T(8,128)S(1)} %get-tuple-element.23.sub_ref.up_sub_ref), channel_id=1, source_target_pairs={{0,4},{4,8},{8,12},{12,16},{16,20},{20,24},{24,28},{1,5},{5,9},{9,... | collective-permute-start | bytes 49160 | tf_op jit(solution)/shard_map/ppermute | solution.py:561
  3.4 5.1 %collective-permute-start.2 = (f32[32,128]{1,0:T(8,128)S(1)}, f32[32,128]{1,0:T(8,128)S(1)}, u32[]{:S(2)}, u32[]{:S(2)}) collective-permute-start(f32[32,128]{1,0:T(8,128)S(1)} %get-tuple-element.24.layer_ref.up_layer_ref), channel_id=1, source_target_pairs={{0,1},{1,2},{2,3},{4,5},{5,6},{6,7},{8,9},{9,10},{10,11},{12,13},{... | collective-permute-start | bytes 49160 | tf_op jit(solution)/shard_map/ppermute | solution.py:560
  9.7 16.3 %all-to-all-start = ((f32[32,16,128]{2,1,0:T(8,128)}), f32[32,16,128]{2,1,0:T(8,128)S(1)}, u32[]{:S(2)}, u32[]{:S(2)}) async-start(f32[32,16,128]{2,1,0:T(8,128)} %get-tuple-element.31), calls=%async_computation | async-start | bytes 524288 | tf_op jit(solution)/shard_map/all_to_all | solution.py:584
  17.0 4.5 %collective-permute-start.1 = (f32[24,128]{1,0:T(8,128)S(1)}, f32[24,128]{1,0:T(8,128)S(1)}, u32[]{:S(2)}, u32[]{:S(2)}) collective-permute-start(f32[24,128]{1,0:T(8,128)S(1)} %get-tuple-element.26.mine_sub_ref.down_sub_ref), channel_id=1, source_target_pairs={{4,0},{8,4},{12,8},{16,12},{20,16},{24,20},{28,24},{5,1},{9,5},{13... | collective-permute-start | bytes 36872 | tf_op jit(solution)/shard_map/ppermute | solution.py:577
  19.2 5.3 %collective-permute-start.3 = (f32[24,128]{1,0:T(8,128)S(1)}, f32[24,128]{1,0:T(8,128)S(1)}, u32[]{:S(2)}, u32[]{:S(2)}) collective-permute-start(f32[24,128]{1,0:T(8,128)S(1)} %get-tuple-element.29), channel_id=1, source_target_pairs={{1,0},{2,1},{3,2},{5,4},{6,5},{7,6},{9,8},{10,9},{11,10},{13,12},{... | collective-permute-start | bytes 36872 | tf_op jit(solution)/shard_map/ppermute | solution.py:585

commit v14 on v13

--- a/solution.py
+++ b/solution.py
@@ -317,7 +317,9 @@
             lax.fori_loop(0, subs // (2 * distance), one_plane, 0)
 
     one_level(1)
-    distance = 2
+    if subs > 2:
+        one_level(2)
+    distance = 4
     while distance < subs:
         pl.when(lax.rem(sub_here + 1, distance) == 0)(functools.partial(one_level, distance))
         distance *= 2
@@ -336,6 +338,7 @@
 VMEM_BLOCK = pl.BlockSpec(memory_space=pltpu.VMEM)
 HBM_BLOCK = pl.BlockSpec(memory_space=pltpu.HBM)
 SPARE_BYTES = 4 * 1024 * 1024
+WORK = 8 * 1024 * 1024
 
 
 def kernel_params(shapes):
@@ -398,49 +401,59 @@
     return found
 
 
+def mode_strips(modes):
+    return [slice(first, first + ROWS) for first in range(0, modes, ROWS)]
+
+
 def pick_kernel(
-    vectors_in, lists_in, face_in, vectors_ref, lists_ref, face_ref, layer_ref, sub_ref, sems
+    vectors_in, lists_in, face_in, mass_in, inner_in,
+    vectors_ref, lists_ref, face_ref, mass_ref, inner_ref, layer_ref, sub_ref, sems
 ):
-    modes = vectors_ref.shape[0]
-    strips = [slice(first, first + ROWS) for first in range(0, modes, ROWS)]
+    strips = mode_strips(vectors_ref.shape[0])
     pairs = [(lists_in, lists_ref)]
-    pairs += [(vectors_in.at[pl.ds(s.start, ROWS)], vectors_ref.at[pl.ds(s.start, ROWS)]) for s in strips]
-    pairs += [(face_in, face_ref)]
+    for strip in strips:
+        rows = pl.ds(strip.start, ROWS)
+        pairs.append((vectors_in.at[rows], vectors_ref.at[rows]))
+    pairs += [(face_in, face_ref), (mass_in, mass_ref), (inner_in, inner_ref)]
     copies = [pltpu.make_async_copy(a, b, sems.at[i]) for i, (a, b) in enumerate(pairs)]
     for copy in copies:
         copy.start()
     copies[0].wait()
-    copies[-1].wait()
-    for k, send_ref in ((0, sub_ref), (2, layer_ref)):
-        send_ref[modes:] = jnp.broadcast_to(face_ref[k // 2 : k // 2 + 1, :], (ROWS, LANES))
+    copies[1 + len(strips)].wait()
+    for k, send_ref in ((1, layer_ref), (0, sub_ref)):
+        send_ref[vectors_ref.shape[0] :] = jnp.broadcast_to(face_ref[k : k + 1, :], (ROWS, LANES))
     for copy, strip in zip(copies[1:], strips):
         copy.wait()
-        sub_ref[strip], layer_ref[strip] = pick_lists(vectors_ref, lists_ref, (0, 2), strip)
+        layer_ref[strip], sub_ref[strip] = pick_lists(vectors_ref, lists_ref, (2, 0), strip)
+    for copy in copies[2 + len(strips) :]:
+        copy.wait()
+
+
+def spread_weights(weights_ref, first, count, height):
+    rows = [
+        jnp.broadcast_to(weights_ref[first + c : first + c + 1, :], (ROWS, LANES))
+        for c in range(count)
+    ]
+    wide = jnp.concatenate(rows, axis=1)
+    return jnp.concatenate([wide] * (height // ROWS), axis=0)
 
 
 def own_kernel(
-    mass_in, inner_in, vectors_ref, lists_ref, face_ref, sub_ref, layer_ref,
-    base_ref, own_ref, before_sub_ref, before_layer_ref, mass_ref, inner_ref, sems, *, subs, layers
+    vectors_ref, lists_ref, face_ref, mass_ref, inner_ref, layer_ref, sub_ref, theirs_ref,
+    base_ref, own_ref, side_ref, before_sub_ref, before_layer_ref, *, subs, layers
 ):
-    copies = [
-        pltpu.make_async_copy(mass_in, mass_ref, sems.at[0]),
-        pltpu.make_async_copy(inner_in, inner_ref, sems.at[1]),
-    ]
-    for copy in copies:
-        copy.start()
     vectors = vectors_ref[...]
     modes, row_count = vectors.shape
-    for first in range(0, modes, ROWS):
-        strip = slice(first, first + ROWS)
+    tiles = row_count // LANES
+    for strip in mode_strips(modes):
         before_sub_ref[strip], before_layer_ref[strip] = pick_lists(
             vectors_ref, lists_ref, (1, 3), strip
         )
-    for copy in copies:
-        copy.wait()
-    places = lax.broadcasted_iota(jnp.int32, (1, row_count), 1)
-    base = mass_ref[...] * vectors
+    places = lax.broadcasted_iota(jnp.int32, (modes, row_count), 1)
+    base = spread_weights(mass_ref, 0, tiles, modes) * vectors
     for k, t in enumerate(STRIDES):
-        edge_weight = jnp.where(places < row_count - t, inner_ref[k], 0.0)
+        edge_weight = spread_weights(inner_ref, k * tiles, tiles, modes)
+        edge_weight = jnp.where(places < row_count - t, edge_weight, 0.0)
         fluxes = edge_weight * (vectors - pltpu.roll(vectors, row_count - t, 1))
         base = base + fluxes - pltpu.roll(fluxes, t, 1)
     base_ref[...] = base
@@ -449,23 +462,23 @@
         springs = jnp.where(lax.axis_index(axis) < ends, face_ref[k : k + 1, :], 0.0)
         picked = send_ref[0:modes]
         own = own + across_dot(picked, springs * picked)
-    own_ref[...] = own
+    mine, theirs = before_layer_ref[...], theirs_ref[0:modes]
+    sprung = theirs_ref[modes : modes + 1] * mine
+    side = across_dot(sprung, jnp.concatenate([mine, theirs], axis=0))
+    own_ref[...] = own + side[:, 0:modes]
+    side_ref[...] = -side[:, modes:] * (1.0 / row_count)
 
 
 def tile_kernel(
-    own_ref, mine_layer_ref, mine_sub_ref, layer_ref, sub_ref, copies_ref, layer_send_ref, *, row_count
+    own_ref, side_ref, mine_sub_ref, mine_layer_ref, sub_ref, copies_ref, layer_send_ref, *, row_count
 ):
     modes = own_ref.shape[0]
     inverse = 1.0 / row_count
-    pairs = []
-    for mine_ref, theirs_ref in ((mine_sub_ref, sub_ref), (mine_layer_ref, layer_ref)):
-        mine = mine_ref[...]
-        sprung = theirs_ref[modes : modes + 1] * mine
-        stacked = jnp.concatenate([mine, theirs_ref[0:modes]], axis=0)
-        pairs.append(across_dot(sprung, stacked))
-    down, side = pairs
-    diag_tile = (own_ref[...] + down[:, 0:modes] + side[:, 0:modes]) * inverse
-    side_tile = -side[:, modes:] * inverse
+    mine, theirs = mine_sub_ref[...], sub_ref[0:modes]
+    sprung = sub_ref[modes : modes + 1] * mine
+    down = across_dot(sprung, jnp.concatenate([mine, theirs], axis=0))
+    diag_tile = (own_ref[...] + down[:, 0:modes]) * inverse
+    side_tile = side_ref[...]
     down_tile = -down[:, modes:] * inverse
     packed = pack_tile(jnp.concatenate([diag_tile, side_tile, down_tile], axis=1))
     for s in range(copies_ref.shape[0]):
@@ -515,7 +528,7 @@
     token_ref[...] = jnp.zeros_like(token_ref)
 
 
-def local_call(body, outputs, operands, name):
+def local_call(body, outputs, operands, name, work=0):
     shapes = tuple(jax.ShapeDtypeStruct(shape, jnp.float32) for shape in outputs)
     return pl.pallas_call(
         body,
@@ -523,6 +536,7 @@
         in_specs=[VMEM_BLOCK] * len(operands),
         out_specs=tuple(VMEM_BLOCK for _ in shapes),
         compiler_params=kernel_params([x.shape for x in operands] + list(outputs)),
+        cost_estimate=pl.CostEstimate(flops=work, bytes_accessed=work, transcendentals=0),
         name=name,
     )(*operands)
 
@@ -545,40 +559,34 @@
     def shaped(*shapes):
         return tuple(jax.ShapeDtypeStruct(shape, jnp.float32) for shape in shapes)
 
-    taken = (vectors, row_lists, face_springs)
+    masses = row_mass.reshape(row_count // LANES, LANES)
+    interior = inner_weight.reshape(-1, LANES)
+    taken = (vectors, row_lists, face_springs, masses, interior)
     held = tuple(jax.ShapeDtypeStruct(x.shape, x.dtype) for x in taken)
     held += shaped((modes + ROWS, width), (modes + ROWS, width))
-    vectors, row_lists, face_springs, layer_send, sub_send = pl.pallas_call(
+    vectors, row_lists, face_springs, masses, interior, layer_send, sub_send = pl.pallas_call(
         pick_kernel,
         out_shape=held,
         in_specs=[HBM_BLOCK] * len(taken),
         out_specs=(VMEM_BLOCK,) * len(held),
-        scratch_shapes=[pltpu.SemaphoreType.DMA((2 + modes // ROWS,))],
+        scratch_shapes=[pltpu.SemaphoreType.DMA((4 + modes // ROWS,))],
         compiler_params=kernel_params([x.shape for x in held]),
         name="pick_rows",
     )(*pinned(*taken))
     before_layer = lax.ppermute(layer_send, "layer", up_layer)
     before_sub = lax.ppermute(sub_send, "sub", up_sub)
-    masses, interior = row_mass[0], inner_weight[0].reshape(-1, 1, row_count)
-    made = shaped((modes, row_count), (modes, modes), (modes, width), (modes, width))
-    base, own, picked_sub, picked_layer = pl.pallas_call(
+    base, own, side, picked_sub, picked_layer = local_call(
         functools.partial(own_kernel, subs=subs, layers=layers),
-        out_shape=made,
-        in_specs=[HBM_BLOCK] * 2 + [VMEM_BLOCK] * len(held),
-        out_specs=(VMEM_BLOCK,) * len(made),
-        scratch_shapes=[
-            pltpu.VMEM(masses.shape, jnp.float32),
-            pltpu.VMEM(interior.shape, jnp.float32),
-            pltpu.SemaphoreType.DMA((2,)),
-        ],
-        compiler_params=kernel_params([x.shape for x in held + made]),
-        name="own_rows",
-    )(*pinned(masses, interior), vectors, row_lists, face_springs, sub_send, layer_send)
+        [(modes, row_count), (modes, modes), (modes, modes), (modes, width), (modes, width)],
+        (vectors, row_lists, face_springs, masses, interior, layer_send, sub_send, before_layer),
+        "own_rows",
+        WORK,
+    )
     after_sub = lax.ppermute(picked_sub, "sub", down_sub)
     copies, after_send = local_call(
         functools.partial(tile_kernel, row_count=row_count),
         [(subs * layers, modes - ROWS, LANES), (modes, width)],
-        (own, picked_layer, picked_sub, before_layer, before_sub),
+        (own, side, picked_sub, picked_layer, before_sub),
         "coarse_tiles",
     )
     tiles = lax.all_to_all(copies, ("sub", "layer"), split_axis=0, concat_axis=0, tiled=True)
@@ -589,6 +597,7 @@
         (base, row_lists, face_springs, sub_send, picked_sub, layer_send, picked_layer)
         + (before_sub, after_sub, before_layer, after_layer),
         "spread_rows",
+        WORK,
     )
     diag_strip, left_strip, right_strip = factor_planes(
         tiles.reshape(subs, layers, *tiles.shape[1:]), modes, token

time: 41.4 us -> 40.3 us (0.973)
  Pallas kernels: 20.9 us -> 19.5 us
  waiting for transfers between devices: 3.17 us -> 3.92 us
    pallas_call x1 -> x0, Pallas kernels: 1.97 us -> none  [per_device(): pl.pallas_call(functools.partial(own_kernel, subs=subs, layers=layers), o...]
    pallas_call x2 -> x3, Pallas kernels: 2.49 us -> 3.95 us  [local_call(): pl.pallas_call(body, out_shape=shapes, in_specs=[VMEM_BLOCK] * len(operan...]
    pallas_call x1, Pallas kernels: 15 us -> 14.1 us  [factor_planes(): pl.pallas_call(factor_kernel, out_shape=(strip, strip, strip), in_specs=[...]
    ppermute x1, waiting for transfers between devices: 0.01 us -> 0.7 us  [per_device(): before_sub = lax.ppermute(sub_send, 'sub', up_sub)]
  transfers between devices with their start and end apart: 5 -> 5, of which waited for: 1 -> 3; matrix products, arithmetic and copies ran while one was open for 0% -> 0% of each run, Pallas kernels for 8% -> 7%
where the time goes in v14:
time: 40.3 us; the launch traced here: 40 us
  Pallas kernels  19.5 us (48%)
  starting transfers between devices  15.9 us (39%)
  waiting for transfers between devices  3.92 us (10%)
  between operations  0.69 us (2%)
    pallas_call x1, Pallas kernels, factor_planes(): pl.pallas_call(factor_kernel, out_shape=(strip, strip, strip), in_specs=[...  14.1 us
    all_to_all x1, starting transfers between devices, per_device(): lax.all_to_all(copies, ('sub', 'layer'), split_axis=0, concat_axis=0, til...  7.05 us
    pallas_call x3, Pallas kernels, local_call(): pl.pallas_call(body, out_shape=shapes, in_specs=[VMEM_BLOCK] * len(operan...  3.95 us
    ppermute x1, waiting for transfers between devices, per_device(): after_layer = lax.ppermute(after_send, 'layer', down_layer)  3.16 us
    ppermute x1, starting transfers between devices, per_device(): before_layer = lax.ppermute(layer_send, 'layer', up_layer)  3.12 us
    ppermute x1, starting transfers between devices, per_device(): after_sub = lax.ppermute(picked_sub, 'sub', down_sub)  2.27 us
    ppermute x1, starting transfers between devices, per_device(): after_layer = lax.ppermute(after_send, 'layer', down_layer)  2.17 us
    pallas_call x1, Pallas kernels, per_device(): pl.pallas_call(pick_kernel, out_shape=held, in_specs=[HBM_BLOCK] * len(ta...  1.44 us
  transfers between devices with their start and end apart: 5, of which 3 were waited for; matrix products, arithmetic and copies ran while one was open for 0% of the time, Pallas kernels for 7%

profile of v14, /device:TPU:27, one launch (start us, length us, event | category | flops | bytes accessed | tf_op | source)
XLA Modules:
  0.0 40.0 jit_solution(2167679474150642697)
XLA Ops:
  0.6 1.4 %pick_rows.1 = (f32[24,4096]{1,0:T(8,128)S(1)}, s32[4,128]{1,0:T(4,128)S(1)}, f32[2,128]{1,0:T(2,128)S(1)}, f32[32,128]{1,0:T(8,128)S(1)}, f32[96,128]{1,0:T(8,1...) custom-call(f32[24,4096]{1,0:T(8,128)} %bitcast.11, s32[4,128]{1,0:T(4,128)} %bitcast.14, f32[2,128]{1,0:T(2,128)} %bitcast.15, ...), custom_call_target="tpu_custom_call" | custom-call | tf_op jit(solution)/shard_map/pick_rows/pallas_call | solution.py:567
  2.1 3.1 %collective-permute-start = (f32[32,128]{1,0:T(8,128)S(1)}, f32[32,128]{1,0:T(8,128)S(1)}, u32[]{:S(2)}, u32[]{:S(2)}) collective-permute-start(f32[32,128]{1,0:T(8,128)S(1)} %get-tuple-element.28.layer_ref.up_layer_ref), channel_id=1, source_target_pairs={{0,1},{1,2},{2,3},{4,5},{5,6},{6,7},{8,9},{9,10},{10,11},{12,13},{... | collective-permute-start | bytes 49160 | tf_op jit(solution)/shard_map/ppermute | solution.py:576
  5.2 1.3 %collective-permute-start.1 = (f32[32,128]{1,0:T(8,128)S(1)}, f32[32,128]{1,0:T(8,128)S(1)}, u32[]{:S(2)}, u32[]{:S(2)}) collective-permute-start(f32[32,128]{1,0:T(8,128)S(1)} %get-tuple-element.29.sub_ref.up_sub_ref), channel_id=1, source_target_pairs={{0,4},{4,8},{8,12},{12,16},{16,20},{20,24},{24,28},{1,5},{5,9},{9,... | collective-permute-start | bytes 49160 | tf_op jit(solution)/shard_map/ppermute | solution.py:577
  6.5 0.1 collective-permute-done.theirs_ref.before_layer_ref
  6.6 1.5 %own_rows.1 = (f32[24,4096]{1,0:T(8,128)S(1)}, f32[24,24]{1,0:T(8,128)S(1)}, f32[24,24]{1,0:T(8,128)S(1)}, f32[24,128]{1,0:T(8,128)S(1)}, f32[24,128]{1,0:T(8,128)S(1)}) custom-call(f32[24,4096]{1,0:T(8,128)S(1)} %get-tuple-element.23.vectors_ref, s32[4,128]{1,0:T(4,128)S(1)} %get-tuple-element.24.lists_ref, f32[2,128]{1,0:T(2,128)S(1)} %get-tuple-element.25.face_ref, ...), custom_call_target="tpu_custom_call" | custom-call | flops 8388608 | bytes 8388608 | tf_op jit(solution)/shard_map/own_rows/pallas_call | solution.py:533
  8.0 0.7 %collective-permute-done.1.sub_ref.before_sub_ref = f32[32,128]{1,0:T(8,128)S(1)} collective-permute-done((f32[32,128]{1,0:T(8,128)S(1)}, f32[32,128]{1,0:T(8,128)S(1)}, u32[]{:S(2)}, u32[]{:S(2)}) %collective-permute-start.1) | collective-permute-done | bytes 16416 | tf_op jit(solution)/shard_map/ppermute | solution.py:577
  8.7 1.2 %coarse_tiles.1 = (f32[32,16,128]{2,1,0:T(8,128)}, f32[24,128]{1,0:T(8,128)S(1)}) custom-call(f32[24,24]{1,0:T(8,128)S(1)} %get-tuple-element.33.own_ref, f32[24,24]{1,0:T(8,128)S(1)} %get-tuple-element.34.side_ref, f32[24,128]{1,0:T(8,128)S(1)} %get-tuple-element.31.mine_sub_ref.down_sub_ref, f32[24,128]{1,0:T(8,128)S(1)} %get-tuple-element.32.mine_layer_ref.down_layer_ref, ...), custom_call_target="tpu_custom_call" | custom-call | tf_op jit(solution)/shard_map/coarse_tiles/pallas_call | solution.py:533
  9.9 7.0 %all-to-all-start = ((f32[32,16,128]{2,1,0:T(8,128)}), f32[32,16,128]{2,1,0:T(8,128)S(1)}, u32[]{:S(2)}, u32[]{:S(2)}) async-start(f32[32,16,128]{2,1,0:T(8,128)} %get-tuple-element.37), calls=%async_computation | async-start | bytes 524288 | tf_op jit(solution)/shard_map/all_to_all | solution.py:592
  17.0 2.3 %collective-permute-start.2 = (f32[24,128]{1,0:T(8,128)S(1)}, f32[24,128]{1,0:T(8,128)S(1)}, u32[]{:S(2)}, u32[]{:S(2)}) collective-permute-start(f32[24,128]{1,0:T(8,128)S(1)} %get-tuple-element.31.mine_sub_ref.down_sub_ref), channel_id=1, source_target_pairs={{4,0},{8,4},{12,8},{16,12},{20,16},{24,20},{28,24},{5,1},{9,5},{13... | collective-permute-start | bytes 36872 | tf_op jit(solution)/shard_map/ppermute | solution.py:585
  19.2 2.2 %collective-permute-start.3 = (f32[24,128]{1,0:T(8,128)S(1)}, f32[24,128]{1,0:T(8,128)S(1)}, u32[]{:S(2)}, u32[]{:S(2)}) collective-permute-start(f32[24,128]{1,0:T(8,128)S(1)} %get-tuple-element.35), channel_id=1, source_target_pairs={{1,0},{2,1},{3,2},{5,4},{6,5},{7,6},{9,8},{10,9},{11,10},{13,12},{... | collective-permute-start | bytes 36872 | tf_op jit(solution)/shard_map/ppermute | solution.py:593
  21.4 0.0 collective-permute-done.2.after_sub_ref
  21.4 3.2 %collective-permute-done.3.after_layer_ref = f32[24,128]{1,0:T(8,128)S(1)} collective-permute-done((f32[24,128]{1,0:T(8,128)S(1)}, f32[24,128]{1,0:T(8,128)S(1)}, u32[]{:S(2)}, u32[]{:S(2)}) %collective-permute-start.3) | collective-permute-done | bytes 12320 | tf_op jit(solution)/shard_map/ppermute | solution.py:593
  24.6 1.3 %spread_rows.1 = (f32[24,4096]{1,0:T(8,128)}, f32[8,128]{1,0:T(8,128)S(1)}) custom-call(f32[24,4096]{1,0:T(8,128)S(1)} %get-tuple-element.30.base_ref, s32[4,128]{1,0:T(4,128)S(1)} %get-tuple-element.24.lists_ref, f32[2,128]{1,0:T(2,128)S(1)} %get-tuple-element.25.face_ref, f32[32,128]{1,0:T(8,128)S(1)} %get-tuple-element.29.sub_ref.up_sub_ref, ...), custom_call_target="tpu_custom_call" | custom-call | flops 8388608 | bytes 8388608 | tf_op jit(solution)/shard_map/spread_rows/pallas_call | solution.py:533
  25.9 0.0 all-to-all-done
  25.9 14.1 %factor_planes.1 = (f32[24,96]{1,0:T(8,128)}, f32[24,96]{1,0:T(8,128)}, f32[24,96]{1,0:T(8,128)}) custom-call(f32[8,4,16,128]{3,2,1,0:T(8,128)S(1)} %bitcast.10, f32[8,128]{1,0:T(8,128)S(1)} %get-tuple-element.38.after_ref), custom_call_target="tpu_custom_call" | custom-call | tf_op jit(solution)/shard_map/factor_planes/pallas_call | solution.py:355
Async XLA Ops:
  2.1 4.5 %collective-permute-start = (f32[32,128]{1,0:T(8,128)S(1)}, f32[32,128]{1,0:T(8,128)S(1)}, u32[]{:S(2)}, u32[]{:S(2)}) collective-permute-start(f32[32,128]{1,0:T(8,128)S(1)} %get-tuple-element.28.layer_ref.up_layer_ref), channel_id=1, source_target_pairs={{0,1},{1,2},{2,3},{4,5},{5,6},{6,7},{8,9},{9,10},{10,11},{12,13},{... | collective-permute-start | bytes 49160 | tf_op jit(solution)/shard_map/ppermute | solution.py:576
  5.2 3.5 %collective-permute-start.1 = (f32[32,128]{1,0:T(8,128)S(1)}, f32[32,128]{1,0:T(8,128)S(1)}, u32[]{:S(2)}, u32[]{:S(2)}) collective-permute-start(f32[32,128]{1,0:T(8,128)S(1)} %get-tuple-element.29.sub_ref.up_sub_ref), channel_id=1, source_target_pairs={{0,4},{4,8},{8,12},{12,16},{16,20},{20,24},{24,28},{1,5},{5,9},{9,... | collective-permute-start | bytes 49160 | tf_op jit(solution)/shard_map/ppermute | solution.py:577
  9.9 16.0 %all-to-all-start = ((f32[32,16,128]{2,1,0:T(8,128)}), f32[32,16,128]{2,1,0:T(8,128)S(1)}, u32[]{:S(2)}, u32[]{:S(2)}) async-start(f32[32,16,128]{2,1,0:T(8,128)} %get-tuple-element.37), calls=%async_computation | async-start | bytes 524288 | tf_op jit(solution)/shard_map/all_to_all | solution.py:592
  17.0 4.5 %collective-permute-start.2 = (f32[24,128]{1,0:T(8,128)S(1)}, f32[24,128]{1,0:T(8,128)S(1)}, u32[]{:S(2)}, u32[]{:S(2)}) collective-permute-start(f32[24,128]{1,0:T(8,128)S(1)} %get-tuple-element.31.mine_sub_ref.down_sub_ref), channel_id=1, source_target_pairs={{4,0},{8,4},{12,8},{16,12},{20,16},{24,20},{28,24},{5,1},{9,5},{13... | collective-permute-start | bytes 36872 | tf_op jit(solution)/shard_map/ppermute | solution.py:585
  19.2 5.3 %collective-permute-start.3 = (f32[24,128]{1,0:T(8,128)S(1)}, f32[24,128]{1,0:T(8,128)S(1)}, u32[]{:S(2)}, u32[]{:S(2)}) collective-permute-start(f32[24,128]{1,0:T(8,128)S(1)} %get-tuple-element.35), channel_id=1, source_target_pairs={{1,0},{2,1},{3,2},{5,4},{6,5},{7,6},{9,8},{10,9},{11,10},{13,12},{... | collective-permute-start | bytes 36872 | tf_op jit(solution)/shard_map/ppermute | solution.py:593

commit v15 on v14

--- a/solution.py
+++ b/solution.py
@@ -12,7 +12,7 @@
 LANES = 128
 ROWS = 8
 UNROLLED_LAYERS = 4
-PLANES_AT_ONCE = 2
+PLANES_AT_ONCE = 4
 NARROW_DEPTH = LANES + LANES // 4
 
 
@@ -470,7 +470,7 @@
 
 
 def tile_kernel(
-    own_ref, side_ref, mine_sub_ref, mine_layer_ref, sub_ref, copies_ref, layer_send_ref, *, row_count
+    own_ref, side_ref, mine_sub_ref, sub_ref, copies_ref, sub_send_ref, *, row_count
 ):
     modes = own_ref.shape[0]
     inverse = 1.0 / row_count
@@ -483,7 +483,7 @@
     packed = pack_tile(jnp.concatenate([diag_tile, side_tile, down_tile], axis=1))
     for s in range(copies_ref.shape[0]):
         copies_ref[s] = packed
-    layer_send_ref[...] = mine_layer_ref[...]
+    sub_send_ref[...] = mine_sub_ref[...]
 
 
 def scatter_kernel(
@@ -582,15 +582,15 @@
         "own_rows",
         WORK,
     )
-    after_sub = lax.ppermute(picked_sub, "sub", down_sub)
+    after_layer = lax.ppermute(picked_layer, "layer", down_layer)
     copies, after_send = local_call(
         functools.partial(tile_kernel, row_count=row_count),
         [(subs * layers, modes - ROWS, LANES), (modes, width)],
-        (own, side, picked_sub, picked_layer, before_sub),
+        (own, side, picked_sub, before_sub),
         "coarse_tiles",
     )
     tiles = lax.all_to_all(copies, ("sub", "layer"), split_axis=0, concat_axis=0, tiled=True)
-    after_layer = lax.ppermute(after_send, "layer", down_layer)
+    after_sub = lax.ppermute(after_send, "sub", down_sub)
     applied, token = local_call(
         functools.partial(scatter_kernel, subs=subs, layers=layers),
         [(modes, row_count), (ROWS, LANES)],

time: 40.3 us -> 41.2 us (1.022)
  the two profiles are of different devices: /device:TPU:27 before, /device:TPU:25 now
where the time goes in v15:
time: 41.2 us; the launch traced here: 40.9 us
  Pallas kernels  21.3 us (52%)
  starting transfers between devices  15 us (36%)
  waiting for transfers between devices  3.84 us (9%)
  between operations  0.69 us (2%)
    pallas_call x1, Pallas kernels, factor_planes(): pl.pallas_call(factor_kernel, out_shape=(strip, strip, strip), in_specs=[...  15.9 us
    all_to_all x1, starting transfers between devices, per_device(): lax.all_to_all(copies, ('sub', 'layer'), split_axis=0, concat_axis=0, til...  7.06 us
    pallas_call x3, Pallas kernels, local_call(): pl.pallas_call(body, out_shape=shapes, in_specs=[VMEM_BLOCK] * len(operan...  3.95 us
    ppermute x1, starting transfers between devices, per_device(): before_layer = lax.ppermute(layer_send, 'layer', up_layer)  3.12 us
    ppermute x1, starting transfers between devices, per_device(): after_sub = lax.ppermute(after_send, 'sub', down_sub)  2.27 us
    all_to_all x1, waiting for transfers between devices, per_device(): lax.all_to_all(copies, ('sub', 'layer'), split_axis=0, concat_axis=0, til...  1.7 us
    pallas_call x1, Pallas kernels, per_device(): pl.pallas_call(pick_kernel, out_shape=held, in_specs=[HBM_BLOCK] * len(ta...  1.44 us
    ppermute x1, waiting for transfers between devices, per_device(): after_layer = lax.ppermute(picked_layer, 'layer', down_layer)  1.39 us
  transfers between devices with their start and end apart: 5, of which 3 were waited for; matrix products, arithmetic and copies ran while one was open for 0% of the time, Pallas kernels for 7%

profile of v15, /device:TPU:25, one launch (start us, length us, event | category | flops | bytes accessed | tf_op | source)
XLA Modules:
  0.0 40.9 jit_solution(13393402138694482429)
XLA Ops:
  0.6 1.4 %pick_rows.1 = (f32[24,4096]{1,0:T(8,128)S(1)}, s32[4,128]{1,0:T(4,128)S(1)}, f32[2,128]{1,0:T(2,128)S(1)}, f32[32,128]{1,0:T(8,128)S(1)}, f32[96,128]{1,0:T(8,1...) custom-call(f32[24,4096]{1,0:T(8,128)} %bitcast.11, s32[4,128]{1,0:T(4,128)} %bitcast.14, f32[2,128]{1,0:T(2,128)} %bitcast.15, ...), custom_call_target="tpu_custom_call" | custom-call | tf_op jit(solution)/shard_map/pick_rows/pallas_call | solution.py:567
  2.1 3.1 %collective-permute-start = (f32[32,128]{1,0:T(8,128)S(1)}, f32[32,128]{1,0:T(8,128)S(1)}, u32[]{:S(2)}, u32[]{:S(2)}) collective-permute-start(f32[32,128]{1,0:T(8,128)S(1)} %get-tuple-element.28.layer_ref.up_layer_ref), channel_id=1, source_target_pairs={{0,1},{1,2},{2,3},{4,5},{5,6},{6,7},{8,9},{9,10},{10,11},{12,13},{... | collective-permute-start | bytes 49160 | tf_op jit(solution)/shard_map/ppermute | solution.py:576
  5.2 1.3 %collective-permute-start.1 = (f32[32,128]{1,0:T(8,128)S(1)}, f32[32,128]{1,0:T(8,128)S(1)}, u32[]{:S(2)}, u32[]{:S(2)}) collective-permute-start(f32[32,128]{1,0:T(8,128)S(1)} %get-tuple-element.29.sub_ref.up_sub_ref), channel_id=1, source_target_pairs={{0,4},{4,8},{8,12},{12,16},{16,20},{20,24},{24,28},{1,5},{5,9},{9,... | collective-permute-start | bytes 49160 | tf_op jit(solution)/shard_map/ppermute | solution.py:577
  6.5 0.0 collective-permute-done.theirs_ref.before_layer_ref
  6.5 1.5 %own_rows.1 = (f32[24,4096]{1,0:T(8,128)S(1)}, f32[24,24]{1,0:T(8,128)S(1)}, f32[24,24]{1,0:T(8,128)S(1)}, f32[24,128]{1,0:T(8,128)S(1)}, f32[24,128]{1,0:T(8,128)S(1)}) custom-call(f32[24,4096]{1,0:T(8,128)S(1)} %get-tuple-element.23.vectors_ref, s32[4,128]{1,0:T(4,128)S(1)} %get-tuple-element.24.lists_ref, f32[2,128]{1,0:T(2,128)S(1)} %get-tuple-element.25.face_ref, ...), custom_call_target="tpu_custom_call" | custom-call | flops 8388608 | bytes 8388608 | tf_op jit(solution)/shard_map/own_rows/pallas_call | solution.py:533
  8.0 0.7 %collective-permute-done.1.sub_ref.before_sub_ref = f32[32,128]{1,0:T(8,128)S(1)} collective-permute-done((f32[32,128]{1,0:T(8,128)S(1)}, f32[32,128]{1,0:T(8,128)S(1)}, u32[]{:S(2)}, u32[]{:S(2)}) %collective-permute-start.1) | collective-permute-done | bytes 16416 | tf_op jit(solution)/shard_map/ppermute | solution.py:577
  8.7 1.2 %coarse_tiles.1 = (f32[32,16,128]{2,1,0:T(8,128)}, f32[24,128]{1,0:T(8,128)S(1)}) custom-call(f32[24,24]{1,0:T(8,128)S(1)} %get-tuple-element.33.own_ref, f32[24,24]{1,0:T(8,128)S(1)} %get-tuple-element.34.side_ref, f32[24,128]{1,0:T(8,128)S(1)} %get-tuple-element.31.mine_sub_ref.down_sub_ref, f32[32,128]{1,0:T(8,128)S(1)} %collective-permute-done.1.sub_ref.before_sub_ref), custom_call_target="tpu_custom_call" | custom-call | tf_op jit(solution)/shard_map/coarse_tiles/pallas_call | solution.py:533
  9.9 7.1 %all-to-all-start = ((f32[32,16,128]{2,1,0:T(8,128)}), f32[32,16,128]{2,1,0:T(8,128)S(1)}, u32[]{:S(2)}, u32[]{:S(2)}) async-start(f32[32,16,128]{2,1,0:T(8,128)} %get-tuple-element.37), calls=%async_computation | async-start | bytes 524288 | tf_op jit(solution)/shard_map/all_to_all | solution.py:592
  17.0 1.3 %collective-permute-start.3 = (f32[24,128]{1,0:T(8,128)S(1)}, f32[24,128]{1,0:T(8,128)S(1)}, u32[]{:S(2)}, u32[]{:S(2)}) collective-permute-start(f32[24,128]{1,0:T(8,128)S(1)} %get-tuple-element.32.down_layer_ref), channel_id=1, source_target_pairs={{1,0},{2,1},{3,2},{5,4},{6,5},{7,6},{9,8},{10,9},{11,10},{13,12},{... | collective-permute-start | bytes 36872 | tf_op jit(solution)/shard_map/ppermute | solution.py:585
  18.3 2.3 %collective-permute-start.2 = (f32[24,128]{1,0:T(8,128)S(1)}, f32[24,128]{1,0:T(8,128)S(1)}, u32[]{:S(2)}, u32[]{:S(2)}) collective-permute-start(f32[24,128]{1,0:T(8,128)S(1)} %get-tuple-element.35), channel_id=1, source_target_pairs={{4,0},{8,4},{12,8},{16,12},{20,16},{24,20},{28,24},{5,1},{9,5},{13... | collective-permute-start | bytes 36872 | tf_op jit(solution)/shard_map/ppermute | solution.py:593
  20.5 1.4 %collective-permute-done.3.after_layer_ref = f32[24,128]{1,0:T(8,128)S(1)} collective-permute-done((f32[24,128]{1,0:T(8,128)S(1)}, f32[24,128]{1,0:T(8,128)S(1)}, u32[]{:S(2)}, u32[]{:S(2)}) %collective-permute-start.3) | collective-permute-done | bytes 12320 | tf_op jit(solution)/shard_map/ppermute | solution.py:585
  21.9 0.0 collective-permute-done.2.after_sub_ref
  21.9 1.3 %spread_rows.1 = (f32[24,4096]{1,0:T(8,128)}, f32[8,128]{1,0:T(8,128)S(1)}) custom-call(f32[24,4096]{1,0:T(8,128)S(1)} %get-tuple-element.30.base_ref, s32[4,128]{1,0:T(4,128)S(1)} %get-tuple-element.24.lists_ref, f32[2,128]{1,0:T(2,128)S(1)} %get-tuple-element.25.face_ref, f32[32,128]{1,0:T(8,128)S(1)} %get-tuple-element.29.sub_ref.up_sub_ref, ...), custom_call_target="tpu_custom_call" | custom-call | flops 8388608 | bytes 8388608 | tf_op jit(solution)/shard_map/spread_rows/pallas_call | solution.py:533
  23.2 1.7 %all-to-all-done = f32[32,16,128]{2,1,0:T(8,128)S(1)} async-done(((f32[32,16,128]{2,1,0:T(8,128)}), f32[32,16,128]{2,1,0:T(8,128)S(1)}, u32[]{:S(2)}, u32[]{:S(2)}) %all-to-all-start) | async-done | bytes 262176 | tf_op jit(solution)/shard_map/all_to_all | solution.py:592
  24.9 15.9 %factor_planes.1 = (f32[24,96]{1,0:T(8,128)}, f32[24,96]{1,0:T(8,128)}, f32[24,96]{1,0:T(8,128)}) custom-call(f32[8,4,16,128]{3,2,1,0:T(8,128)S(1)} %bitcast.10, f32[8,128]{1,0:T(8,128)S(1)} %get-tuple-element.38.after_ref), custom_call_target="tpu_custom_call" | custom-call | tf_op jit(solution)/shard_map/factor_planes/pallas_call | solution.py:355
Async XLA Ops:
  2.1 4.4 %collective-permute-start = (f32[32,128]{1,0:T(8,128)S(1)}, f32[32,128]{1,0:T(8,128)S(1)}, u32[]{:S(2)}, u32[]{:S(2)}) collective-permute-start(f32[32,128]{1,0:T(8,128)S(1)} %get-tuple-element.28.layer_ref.up_layer_ref), channel_id=1, source_target_pairs={{0,1},{1,2},{2,3},{4,5},{5,6},{6,7},{8,9},{9,10},{10,11},{12,13},{... | collective-permute-start | bytes 49160 | tf_op jit(solution)/shard_map/ppermute | solution.py:576
  5.2 3.5 %collective-permute-start.1 = (f32[32,128]{1,0:T(8,128)S(1)}, f32[32,128]{1,0:T(8,128)S(1)}, u32[]{:S(2)}, u32[]{:S(2)}) collective-permute-start(f32[32,128]{1,0:T(8,128)S(1)} %get-tuple-element.29.sub_ref.up_sub_ref), channel_id=1, source_target_pairs={{0,4},{4,8},{8,12},{12,16},{16,20},{20,24},{24,28},{1,5},{5,9},{9,... | collective-permute-start | bytes 49160 | tf_op jit(solution)/shard_map/ppermute | solution.py:577
  9.9 15.1 %all-to-all-start = ((f32[32,16,128]{2,1,0:T(8,128)}), f32[32,16,128]{2,1,0:T(8,128)S(1)}, u32[]{:S(2)}, u32[]{:S(2)}) async-start(f32[32,16,128]{2,1,0:T(8,128)} %get-tuple-element.37), calls=%async_computation | async-start | bytes 524288 | tf_op jit(solution)/shard_map/all_to_all | solution.py:592
  17.0 5.0 %collective-permute-start.3 = (f32[24,128]{1,0:T(8,128)S(1)}, f32[24,128]{1,0:T(8,128)S(1)}, u32[]{:S(2)}, u32[]{:S(2)}) collective-permute-start(f32[24,128]{1,0:T(8,128)S(1)} %get-tuple-element.32.down_layer_ref), channel_id=1, source_target_pairs={{1,0},{2,1},{3,2},{5,4},{6,5},{7,6},{9,8},{10,9},{11,10},{13,12},{... | collective-permute-start | bytes 36872 | tf_op jit(solution)/shard_map/ppermute | solution.py:585
  18.3 3.7 %collective-permute-start.2 = (f32[24,128]{1,0:T(8,128)S(1)}, f32[24,128]{1,0:T(8,128)S(1)}, u32[]{:S(2)}, u32[]{:S(2)}) collective-permute-start(f32[24,128]{1,0:T(8,128)S(1)} %get-tuple-element.35), channel_id=1, source_target_pairs={{4,0},{8,4},{12,8},{16,12},{20,16},{24,20},{28,24},{5,1},{9,5},{13... | collective-permute-start | bytes 36872 | tf_op jit(solution)/shard_map/ppermute | solution.py:593

commit v16 on v15

--- a/solution.py
+++ b/solution.py
@@ -12,7 +12,7 @@
 LANES = 128
 ROWS = 8
 UNROLLED_LAYERS = 4
-PLANES_AT_ONCE = 4
+PLANES_AT_ONCE = 1
 NARROW_DEPTH = LANES + LANES // 4
 
 

time: 41.2 us -> 39.4 us (0.956)
  Pallas kernels: 21.3 us -> 19.5 us
    pallas_call x1, Pallas kernels: 15.9 us -> 14.2 us  [factor_planes(): pl.pallas_call(factor_kernel, out_shape=(strip, strip, strip), in_specs=[...]
where the time goes in v16:
time: 39.4 us; the launch traced here: 39.1 us
  Pallas kernels  19.5 us (49%)
  starting transfers between devices  15 us (38%)
  waiting for transfers between devices  3.84 us (10%)
  between operations  0.69 us (2%)
    pallas_call x1, Pallas kernels, factor_planes(): pl.pallas_call(factor_kernel, out_shape=(strip, strip, strip), in_specs=[...  14.2 us
    all_to_all x1, starting transfers between devices, per_device(): lax.all_to_all(copies, ('sub', 'layer'), split_axis=0, concat_axis=0, til...  7.06 us
    pallas_call x3, Pallas kernels, local_call(): pl.pallas_call(body, out_shape=shapes, in_specs=[VMEM_BLOCK] * len(operan...  3.95 us
    ppermute x1, starting transfers between devices, per_device(): before_layer = lax.ppermute(layer_send, 'layer', up_layer)  3.12 us
    ppermute x1, starting transfers between devices, per_device(): after_sub = lax.ppermute(after_send, 'sub', down_sub)  2.27 us
    all_to_all x1, waiting for transfers between devices, per_device(): lax.all_to_all(copies, ('sub', 'layer'), split_axis=0, concat_axis=0, til...  1.7 us
    pallas_call x1, Pallas kernels, per_device(): pl.pallas_call(pick_kernel, out_shape=held, in_specs=[HBM_BLOCK] * len(ta...  1.44 us
    ppermute x1, waiting for transfers between devices, per_device(): after_layer = lax.ppermute(picked_layer, 'layer', down_layer)  1.39 us
  transfers between devices with their start and end apart: 5, of which 3 were waited for; matrix products, arithmetic and copies ran while one was open for 0% of the time, Pallas kernels for 7%

profile of v16, /device:TPU:25, one launch (start us, length us, event | category | flops | bytes accessed | tf_op | source)
XLA Modules:
  0.0 39.1 jit_solution(183323814051581902)
XLA Ops:
  0.6 1.4 %pick_rows.1 = (f32[24,4096]{1,0:T(8,128)S(1)}, s32[4,128]{1,0:T(4,128)S(1)}, f32[2,128]{1,0:T(2,128)S(1)}, f32[32,128]{1,0:T(8,128)S(1)}, f32[96,128]{1,0:T(8,1...) custom-call(f32[24,4096]{1,0:T(8,128)} %bitcast.11, s32[4,128]{1,0:T(4,128)} %bitcast.14, f32[2,128]{1,0:T(2,128)} %bitcast.15, ...), custom_call_target="tpu_custom_call" | custom-call | tf_op jit(solution)/shard_map/pick_rows/pallas_call | solution.py:567
  2.1 3.1 %collective-permute-start = (f32[32,128]{1,0:T(8,128)S(1)}, f32[32,128]{1,0:T(8,128)S(1)}, u32[]{:S(2)}, u32[]{:S(2)}) collective-permute-start(f32[32,128]{1,0:T(8,128)S(1)} %get-tuple-element.28.layer_ref.up_layer_ref), channel_id=1, source_target_pairs={{0,1},{1,2},{2,3},{4,5},{5,6},{6,7},{8,9},{9,10},{10,11},{12,13},{... | collective-permute-start | bytes 49160 | tf_op jit(solution)/shard_map/ppermute | solution.py:576
  5.2 1.3 %collective-permute-start.1 = (f32[32,128]{1,0:T(8,128)S(1)}, f32[32,128]{1,0:T(8,128)S(1)}, u32[]{:S(2)}, u32[]{:S(2)}) collective-permute-start(f32[32,128]{1,0:T(8,128)S(1)} %get-tuple-element.29.sub_ref.up_sub_ref), channel_id=1, source_target_pairs={{0,4},{4,8},{8,12},{12,16},{16,20},{20,24},{24,28},{1,5},{5,9},{9,... | collective-permute-start | bytes 49160 | tf_op jit(solution)/shard_map/ppermute | solution.py:577
  6.5 0.0 collective-permute-done.theirs_ref.before_layer_ref
  6.5 1.5 %own_rows.1 = (f32[24,4096]{1,0:T(8,128)S(1)}, f32[24,24]{1,0:T(8,128)S(1)}, f32[24,24]{1,0:T(8,128)S(1)}, f32[24,128]{1,0:T(8,128)S(1)}, f32[24,128]{1,0:T(8,128)S(1)}) custom-call(f32[24,4096]{1,0:T(8,128)S(1)} %get-tuple-element.23.vectors_ref, s32[4,128]{1,0:T(4,128)S(1)} %get-tuple-element.24.lists_ref, f32[2,128]{1,0:T(2,128)S(1)} %get-tuple-element.25.face_ref, ...), custom_call_target="tpu_custom_call" | custom-call | flops 8388608 | bytes 8388608 | tf_op jit(solution)/shard_map/own_rows/pallas_call | solution.py:533
  8.0 0.7 %collective-permute-done.1.sub_ref.before_sub_ref = f32[32,128]{1,0:T(8,128)S(1)} collective-permute-done((f32[32,128]{1,0:T(8,128)S(1)}, f32[32,128]{1,0:T(8,128)S(1)}, u32[]{:S(2)}, u32[]{:S(2)}) %collective-permute-start.1) | collective-permute-done | bytes 16416 | tf_op jit(solution)/shard_map/ppermute | solution.py:577
  8.7 1.2 %coarse_tiles.1 = (f32[32,16,128]{2,1,0:T(8,128)}, f32[24,128]{1,0:T(8,128)S(1)}) custom-call(f32[24,24]{1,0:T(8,128)S(1)} %get-tuple-element.33.own_ref, f32[24,24]{1,0:T(8,128)S(1)} %get-tuple-element.34.side_ref, f32[24,128]{1,0:T(8,128)S(1)} %get-tuple-element.31.mine_sub_ref.down_sub_ref, f32[32,128]{1,0:T(8,128)S(1)} %collective-permute-done.1.sub_ref.before_sub_ref), custom_call_target="tpu_custom_call" | custom-call | tf_op jit(solution)/shard_map/coarse_tiles/pallas_call | solution.py:533
  9.9 7.1 %all-to-all-start = ((f32[32,16,128]{2,1,0:T(8,128)}), f32[32,16,128]{2,1,0:T(8,128)S(1)}, u32[]{:S(2)}, u32[]{:S(2)}) async-start(f32[32,16,128]{2,1,0:T(8,128)} %get-tuple-element.37), calls=%async_computation | async-start | bytes 524288 | tf_op jit(solution)/shard_map/all_to_all | solution.py:592
  17.0 1.3 %collective-permute-start.3 = (f32[24,128]{1,0:T(8,128)S(1)}, f32[24,128]{1,0:T(8,128)S(1)}, u32[]{:S(2)}, u32[]{:S(2)}) collective-permute-start(f32[24,128]{1,0:T(8,128)S(1)} %get-tuple-element.32.down_layer_ref), channel_id=1, source_target_pairs={{1,0},{2,1},{3,2},{5,4},{6,5},{7,6},{9,8},{10,9},{11,10},{13,12},{... | collective-permute-start | bytes 36872 | tf_op jit(solution)/shard_map/ppermute | solution.py:585
  18.3 2.3 %collective-permute-start.2 = (f32[24,128]{1,0:T(8,128)S(1)}, f32[24,128]{1,0:T(8,128)S(1)}, u32[]{:S(2)}, u32[]{:S(2)}) collective-permute-start(f32[24,128]{1,0:T(8,128)S(1)} %get-tuple-element.35), channel_id=1, source_target_pairs={{4,0},{8,4},{12,8},{16,12},{20,16},{24,20},{28,24},{5,1},{9,5},{13... | collective-permute-start | bytes 36872 | tf_op jit(solution)/shard_map/ppermute | solution.py:593
  20.5 1.4 %collective-permute-done.3.after_layer_ref = f32[24,128]{1,0:T(8,128)S(1)} collective-permute-done((f32[24,128]{1,0:T(8,128)S(1)}, f32[24,128]{1,0:T(8,128)S(1)}, u32[]{:S(2)}, u32[]{:S(2)}) %collective-permute-start.3) | collective-permute-done | bytes 12320 | tf_op jit(solution)/shard_map/ppermute | solution.py:585
  21.9 0.0 collective-permute-done.2.after_sub_ref
  21.9 1.3 %spread_rows.1 = (f32[24,4096]{1,0:T(8,128)}, f32[8,128]{1,0:T(8,128)S(1)}) custom-call(f32[24,4096]{1,0:T(8,128)S(1)} %get-tuple-element.30.base_ref, s32[4,128]{1,0:T(4,128)S(1)} %get-tuple-element.24.lists_ref, f32[2,128]{1,0:T(2,128)S(1)} %get-tuple-element.25.face_ref, f32[32,128]{1,0:T(8,128)S(1)} %get-tuple-element.29.sub_ref.up_sub_ref, ...), custom_call_target="tpu_custom_call" | custom-call | flops 8388608 | bytes 8388608 | tf_op jit(solution)/shard_map/spread_rows/pallas_call | solution.py:533
  23.2 1.7 %all-to-all-done = f32[32,16,128]{2,1,0:T(8,128)S(1)} async-done(((f32[32,16,128]{2,1,0:T(8,128)}), f32[32,16,128]{2,1,0:T(8,128)S(1)}, u32[]{:S(2)}, u32[]{:S(2)}) %all-to-all-start) | async-done | bytes 262176 | tf_op jit(solution)/shard_map/all_to_all | solution.py:592
  24.9 14.2 %factor_planes.1 = (f32[24,96]{1,0:T(8,128)}, f32[24,96]{1,0:T(8,128)}, f32[24,96]{1,0:T(8,128)}) custom-call(f32[8,4,16,128]{3,2,1,0:T(8,128)S(1)} %bitcast.10, f32[8,128]{1,0:T(8,128)S(1)} %get-tuple-element.38.after_ref), custom_call_target="tpu_custom_call" | custom-call | tf_op jit(solution)/shard_map/factor_planes/pallas_call | solution.py:355
Async XLA Ops:
  2.1 4.4 %collective-permute-start = (f32[32,128]{1,0:T(8,128)S(1)}, f32[32,128]{1,0:T(8,128)S(1)}, u32[]{:S(2)}, u32[]{:S(2)}) collective-permute-start(f32[32,128]{1,0:T(8,128)S(1)} %get-tuple-element.28.layer_ref.up_layer_ref), channel_id=1, source_target_pairs={{0,1},{1,2},{2,3},{4,5},{5,6},{6,7},{8,9},{9,10},{10,11},{12,13},{... | collective-permute-start | bytes 49160 | tf_op jit(solution)/shard_map/ppermute | solution.py:576
  5.2 3.5 %collective-permute-start.1 = (f32[32,128]{1,0:T(8,128)S(1)}, f32[32,128]{1,0:T(8,128)S(1)}, u32[]{:S(2)}, u32[]{:S(2)}) collective-permute-start(f32[32,128]{1,0:T(8,128)S(1)} %get-tuple-element.29.sub_ref.up_sub_ref), channel_id=1, source_target_pairs={{0,4},{4,8},{8,12},{12,16},{16,20},{20,24},{24,28},{1,5},{5,9},{9,... | collective-permute-start | bytes 49160 | tf_op jit(solution)/shard_map/ppermute | solution.py:577
  9.9 15.1 %all-to-all-start = ((f32[32,16,128]{2,1,0:T(8,128)}), f32[32,16,128]{2,1,0:T(8,128)S(1)}, u32[]{:S(2)}, u32[]{:S(2)}) async-start(f32[32,16,128]{2,1,0:T(8,128)} %get-tuple-element.37), calls=%async_computation | async-start | bytes 524288 | tf_op jit(solution)/shard_map/all_to_all | solution.py:592
  17.0 5.0 %collective-permute-start.3 = (f32[24,128]{1,0:T(8,128)S(1)}, f32[24,128]{1,0:T(8,128)S(1)}, u32[]{:S(2)}, u32[]{:S(2)}) collective-permute-start(f32[24,128]{1,0:T(8,128)S(1)} %get-tuple-element.32.down_layer_ref), channel_id=1, source_target_pairs={{1,0},{2,1},{3,2},{5,4},{6,5},{7,6},{9,8},{10,9},{11,10},{13,12},{... | collective-permute-start | bytes 36872 | tf_op jit(solution)/shard_map/ppermute | solution.py:585
  18.3 3.7 %collective-permute-start.2 = (f32[24,128]{1,0:T(8,128)S(1)}, f32[24,128]{1,0:T(8,128)S(1)}, u32[]{:S(2)}, u32[]{:S(2)}) collective-permute-start(f32[24,128]{1,0:T(8,128)S(1)} %get-tuple-element.35), channel_id=1, source_target_pairs={{4,0},{8,4},{12,8},{16,12},{20,16},{24,20},{28,24},{5,1},{9,5},{13... | collective-permute-start | bytes 36872 | tf_op jit(solution)/shard_map/ppermute | solution.py:593

commit v17 on v16

--- a/solution.py
+++ b/solution.py
@@ -13,7 +13,6 @@
 ROWS = 8
 UNROLLED_LAYERS = 4
 PLANES_AT_ONCE = 1
-NARROW_DEPTH = LANES + LANES // 4
 
 
 def turned_dot(left, right):
@@ -40,25 +39,6 @@
     return lax.dot_general(
         left, right, (((1,), (0,)), ((), ())), preferred_element_type=jnp.float32
     )
-
-
-def narrow_columns(turned, modes):
-    height = turned.shape[0]
-    lane = lax.broadcasted_iota(jnp.int32, (height, LANES), 1)
-    wide = jnp.concatenate([turned, jnp.zeros((height, LANES - 3 * modes), jnp.float32)], axis=1)
-    again = pltpu.roll(wide, 3 * modes, 1)
-    left = jnp.where(lane < 3 * modes, wide, jnp.where(lane < 5 * modes, again, 0.0))
-    last = jnp.where(lane < modes, wide, 0.0)
-    return jnp.concatenate([left, last], axis=1)[:, 0:NARROW_DEPTH].astype(jnp.bfloat16)
-
-
-def narrow_rows(pieces):
-    first, second, third = pieces
-    modes, width = first.shape
-    gap = jnp.zeros((LANES - 5 * modes, width), jnp.float32)
-    tail = jnp.zeros((NARROW_DEPTH - LANES - modes, width), jnp.float32)
-    rows = jnp.concatenate([first] * 3 + [second] * 2 + [gap, third, tail], axis=0)
-    return rows.astype(jnp.bfloat16)
 
 
 def plain_dot(left, right):
@@ -180,12 +160,9 @@
         if static:
             below = (panel + 1) * modes
             end = min(below + modes, order) if banded else order
-            pieces = pieces_of(panel_rows)
-            right = narrow_rows(pieces)
-            stacked = jnp.concatenate(pieces, axis=0)
             if below < order:
-                columns = narrow_columns(stacked[:, 0:part].T[below:end], modes)
-                grid_ref[plane, below:end, 0:lanes_used] -= single_dot(columns, right)
+                columns = panel_rows[:, 0:part].T[below:end]
+                grid_ref[plane, below:end, 0:lanes_used] -= plain_dot(columns, panel_rows)
         else:
             lane = lax.broadcasted_iota(jnp.int32, (modes, part), 1)
             columns = jnp.where(lane >= first_row + modes, panel_rows[:, 0:part], 0.0)

time: 39.4 us -> 39.7 us (level)
  no operation moved by 1% of the time
where the time goes in v17:
time: 39.7 us; the launch traced here: 39.4 us
  Pallas kernels  19.8 us (50%)
  starting transfers between devices  15 us (38%)
  waiting for transfers between devices  3.84 us (10%)
  between operations  0.69 us (2%)
    pallas_call x1, Pallas kernels, factor_planes(): pl.pallas_call(factor_kernel, out_shape=(strip, strip, strip), in_specs=[...  14.5 us
    all_to_all x1, starting transfers between devices, per_device(): lax.all_to_all(copies, ('sub', 'layer'), split_axis=0, concat_axis=0, til...  7.06 us
    pallas_call x3, Pallas kernels, local_call(): pl.pallas_call(body, out_shape=shapes, in_specs=[VMEM_BLOCK] * len(operan...  3.95 us
    ppermute x1, starting transfers between devices, per_device(): before_layer = lax.ppermute(layer_send, 'layer', up_layer)  3.12 us
    ppermute x1, starting transfers between devices, per_device(): after_sub = lax.ppermute(after_send, 'sub', down_sub)  2.27 us
    all_to_all x1, waiting for transfers between devices, per_device(): lax.all_to_all(copies, ('sub', 'layer'), split_axis=0, concat_axis=0, til...  1.7 us
    pallas_call x1, Pallas kernels, per_device(): pl.pallas_call(pick_kernel, out_shape=held, in_specs=[HBM_BLOCK] * len(ta...  1.44 us
    ppermute x1, waiting for transfers between devices, per_device(): after_layer = lax.ppermute(picked_layer, 'layer', down_layer)  1.39 us
  transfers between devices with their start and end apart: 5, of which 3 were waited for; matrix products, arithmetic and copies ran while one was open for 0% of the time, Pallas kernels for 7%

profile of v17, /device:TPU:25, one launch (start us, length us, event | category | flops | bytes accessed | tf_op | source)
XLA Modules:
  0.0 39.4 jit_solution(10476456726992684346)
XLA Ops:
  0.6 1.4 %pick_rows.1 = (f32[24,4096]{1,0:T(8,128)S(1)}, s32[4,128]{1,0:T(4,128)S(1)}, f32[2,128]{1,0:T(2,128)S(1)}, f32[32,128]{1,0:T(8,128)S(1)}, f32[96,128]{1,0:T(8,1...) custom-call(f32[24,4096]{1,0:T(8,128)} %bitcast.11, s32[4,128]{1,0:T(4,128)} %bitcast.14, f32[2,128]{1,0:T(2,128)} %bitcast.15, ...), custom_call_target="tpu_custom_call" | custom-call | tf_op jit(solution)/shard_map/pick_rows/pallas_call | solution.py:544
  2.1 3.1 %collective-permute-start = (f32[32,128]{1,0:T(8,128)S(1)}, f32[32,128]{1,0:T(8,128)S(1)}, u32[]{:S(2)}, u32[]{:S(2)}) collective-permute-start(f32[32,128]{1,0:T(8,128)S(1)} %get-tuple-element.28.layer_ref.up_layer_ref), channel_id=1, source_target_pairs={{0,1},{1,2},{2,3},{4,5},{5,6},{6,7},{8,9},{9,10},{10,11},{12,13},{... | collective-permute-start | bytes 49160 | tf_op jit(solution)/shard_map/ppermute | solution.py:553
  5.2 1.3 %collective-permute-start.1 = (f32[32,128]{1,0:T(8,128)S(1)}, f32[32,128]{1,0:T(8,128)S(1)}, u32[]{:S(2)}, u32[]{:S(2)}) collective-permute-start(f32[32,128]{1,0:T(8,128)S(1)} %get-tuple-element.29.sub_ref.up_sub_ref), channel_id=1, source_target_pairs={{0,4},{4,8},{8,12},{12,16},{16,20},{20,24},{24,28},{1,5},{5,9},{9,... | collective-permute-start | bytes 49160 | tf_op jit(solution)/shard_map/ppermute | solution.py:554
  6.5 0.0 collective-permute-done.theirs_ref.before_layer_ref
  6.5 1.5 %own_rows.1 = (f32[24,4096]{1,0:T(8,128)S(1)}, f32[24,24]{1,0:T(8,128)S(1)}, f32[24,24]{1,0:T(8,128)S(1)}, f32[24,128]{1,0:T(8,128)S(1)}, f32[24,128]{1,0:T(8,128)S(1)}) custom-call(f32[24,4096]{1,0:T(8,128)S(1)} %get-tuple-element.23.vectors_ref, s32[4,128]{1,0:T(4,128)S(1)} %get-tuple-element.24.lists_ref, f32[2,128]{1,0:T(2,128)S(1)} %get-tuple-element.25.face_ref, ...), custom_call_target="tpu_custom_call" | custom-call | flops 8388608 | bytes 8388608 | tf_op jit(solution)/shard_map/own_rows/pallas_call | solution.py:510
  8.0 0.7 %collective-permute-done.1.sub_ref.before_sub_ref = f32[32,128]{1,0:T(8,128)S(1)} collective-permute-done((f32[32,128]{1,0:T(8,128)S(1)}, f32[32,128]{1,0:T(8,128)S(1)}, u32[]{:S(2)}, u32[]{:S(2)}) %collective-permute-start.1) | collective-permute-done | bytes 16416 | tf_op jit(solution)/shard_map/ppermute | solution.py:554
  8.7 1.2 %coarse_tiles.1 = (f32[32,16,128]{2,1,0:T(8,128)}, f32[24,128]{1,0:T(8,128)S(1)}) custom-call(f32[24,24]{1,0:T(8,128)S(1)} %get-tuple-element.33.own_ref, f32[24,24]{1,0:T(8,128)S(1)} %get-tuple-element.34.side_ref, f32[24,128]{1,0:T(8,128)S(1)} %get-tuple-element.31.mine_sub_ref.down_sub_ref, f32[32,128]{1,0:T(8,128)S(1)} %collective-permute-done.1.sub_ref.before_sub_ref), custom_call_target="tpu_custom_call" | custom-call | tf_op jit(solution)/shard_map/coarse_tiles/pallas_call | solution.py:510
  9.9 7.1 %all-to-all-start = ((f32[32,16,128]{2,1,0:T(8,128)}), f32[32,16,128]{2,1,0:T(8,128)S(1)}, u32[]{:S(2)}, u32[]{:S(2)}) async-start(f32[32,16,128]{2,1,0:T(8,128)} %get-tuple-element.37), calls=%async_computation | async-start | bytes 524288 | tf_op jit(solution)/shard_map/all_to_all | solution.py:569
  17.0 1.3 %collective-permute-start.3 = (f32[24,128]{1,0:T(8,128)S(1)}, f32[24,128]{1,0:T(8,128)S(1)}, u32[]{:S(2)}, u32[]{:S(2)}) collective-permute-start(f32[24,128]{1,0:T(8,128)S(1)} %get-tuple-element.32.down_layer_ref), channel_id=1, source_target_pairs={{1,0},{2,1},{3,2},{5,4},{6,5},{7,6},{9,8},{10,9},{11,10},{13,12},{... | collective-permute-start | bytes 36872 | tf_op jit(solution)/shard_map/ppermute | solution.py:562
  18.3 2.3 %collective-permute-start.2 = (f32[24,128]{1,0:T(8,128)S(1)}, f32[24,128]{1,0:T(8,128)S(1)}, u32[]{:S(2)}, u32[]{:S(2)}) collective-permute-start(f32[24,128]{1,0:T(8,128)S(1)} %get-tuple-element.35), channel_id=1, source_target_pairs={{4,0},{8,4},{12,8},{16,12},{20,16},{24,20},{28,24},{5,1},{9,5},{13... | collective-permute-start | bytes 36872 | tf_op jit(solution)/shard_map/ppermute | solution.py:570
  20.5 1.4 %collective-permute-done.3.after_layer_ref = f32[24,128]{1,0:T(8,128)S(1)} collective-permute-done((f32[24,128]{1,0:T(8,128)S(1)}, f32[24,128]{1,0:T(8,128)S(1)}, u32[]{:S(2)}, u32[]{:S(2)}) %collective-permute-start.3) | collective-permute-done | bytes 12320 | tf_op jit(solution)/shard_map/ppermute | solution.py:562
  21.9 0.0 collective-permute-done.2.after_sub_ref
  21.9 1.3 %spread_rows.1 = (f32[24,4096]{1,0:T(8,128)}, f32[8,128]{1,0:T(8,128)S(1)}) custom-call(f32[24,4096]{1,0:T(8,128)S(1)} %get-tuple-element.30.base_ref, s32[4,128]{1,0:T(4,128)S(1)} %get-tuple-element.24.lists_ref, f32[2,128]{1,0:T(2,128)S(1)} %get-tuple-element.25.face_ref, f32[32,128]{1,0:T(8,128)S(1)} %get-tuple-element.29.sub_ref.up_sub_ref, ...), custom_call_target="tpu_custom_call" | custom-call | flops 8388608 | bytes 8388608 | tf_op jit(solution)/shard_map/spread_rows/pallas_call | solution.py:510
  23.2 1.7 %all-to-all-done = f32[32,16,128]{2,1,0:T(8,128)S(1)} async-done(((f32[32,16,128]{2,1,0:T(8,128)}), f32[32,16,128]{2,1,0:T(8,128)S(1)}, u32[]{:S(2)}, u32[]{:S(2)}) %all-to-all-start) | async-done | bytes 262176 | tf_op jit(solution)/shard_map/all_to_all | solution.py:569
  24.9 14.5 %factor_planes.1 = (f32[24,96]{1,0:T(8,128)}, f32[24,96]{1,0:T(8,128)}, f32[24,96]{1,0:T(8,128)}) custom-call(f32[8,4,16,128]{3,2,1,0:T(8,128)S(1)} %bitcast.10, f32[8,128]{1,0:T(8,128)S(1)} %get-tuple-element.38.after_ref), custom_call_target="tpu_custom_call" | custom-call | tf_op jit(solution)/shard_map/factor_planes/pallas_call | solution.py:332
Async XLA Ops:
  2.1 4.4 %collective-permute-start = (f32[32,128]{1,0:T(8,128)S(1)}, f32[32,128]{1,0:T(8,128)S(1)}, u32[]{:S(2)}, u32[]{:S(2)}) collective-permute-start(f32[32,128]{1,0:T(8,128)S(1)} %get-tuple-element.28.layer_ref.up_layer_ref), channel_id=1, source_target_pairs={{0,1},{1,2},{2,3},{4,5},{5,6},{6,7},{8,9},{9,10},{10,11},{12,13},{... | collective-permute-start | bytes 49160 | tf_op jit(solution)/shard_map/ppermute | solution.py:553
  5.2 3.5 %collective-permute-start.1 = (f32[32,128]{1,0:T(8,128)S(1)}, f32[32,128]{1,0:T(8,128)S(1)}, u32[]{:S(2)}, u32[]{:S(2)}) collective-permute-start(f32[32,128]{1,0:T(8,128)S(1)} %get-tuple-element.29.sub_ref.up_sub_ref), channel_id=1, source_target_pairs={{0,4},{4,8},{8,12},{12,16},{16,20},{20,24},{24,28},{1,5},{5,9},{9,... | collective-permute-start | bytes 49160 | tf_op jit(solution)/shard_map/ppermute | solution.py:554
  9.9 15.1 %all-to-all-start = ((f32[32,16,128]{2,1,0:T(8,128)}), f32[32,16,128]{2,1,0:T(8,128)S(1)}, u32[]{:S(2)}, u32[]{:S(2)}) async-start(f32[32,16,128]{2,1,0:T(8,128)} %get-tuple-element.37), calls=%async_computation | async-start | bytes 524288 | tf_op jit(solution)/shard_map/all_to_all | solution.py:569
  17.0 5.0 %collective-permute-start.3 = (f32[24,128]{1,0:T(8,128)S(1)}, f32[24,128]{1,0:T(8,128)S(1)}, u32[]{:S(2)}, u32[]{:S(2)}) collective-permute-start(f32[24,128]{1,0:T(8,128)S(1)} %get-tuple-element.32.down_layer_ref), channel_id=1, source_target_pairs={{1,0},{2,1},{3,2},{5,4},{6,5},{7,6},{9,8},{10,9},{11,10},{13,12},{... | collective-permute-start | bytes 36872 | tf_op jit(solution)/shard_map/ppermute | solution.py:562
  18.3 3.7 %collective-permute-start.2 = (f32[24,128]{1,0:T(8,128)S(1)}, f32[24,128]{1,0:T(8,128)S(1)}, u32[]{:S(2)}, u32[]{:S(2)}) collective-permute-start(f32[24,128]{1,0:T(8,128)S(1)} %get-tuple-element.35), channel_id=1, source_target_pairs={{4,0},{8,4},{12,8},{16,12},{20,16},{24,20},{28,24},{5,1},{9,5},{13... | collective-permute-start | bytes 36872 | tf_op jit(solution)/shard_map/ppermute | solution.py:570

commit v18 on v16

--- a/solution.py
+++ b/solution.py
@@ -12,7 +12,7 @@
 LANES = 128
 ROWS = 8
 UNROLLED_LAYERS = 4
-PLANES_AT_ONCE = 1
+PLANES_AT_ONCE = 0
 NARROW_DEPTH = LANES + LANES // 4
 
 

time: 39.4 us -> 40.5 us (1.028)
  Pallas kernels: 19.5 us -> 20.6 us
    pallas_call x1, Pallas kernels: 14.2 us -> 15.2 us  [factor_planes(): pl.pallas_call(factor_kernel, out_shape=(strip, strip, strip), in_specs=[...]
where the time goes in v18:
time: 40.5 us; the launch traced here: 40.2 us
  Pallas kernels  20.6 us (51%)
  starting transfers between devices  15 us (37%)
  waiting for transfers between devices  3.84 us (9%)
  between operations  0.69 us (2%)
    pallas_call x1, Pallas kernels, factor_planes(): pl.pallas_call(factor_kernel, out_shape=(strip, strip, strip), in_specs=[...  15.2 us
    all_to_all x1, starting transfers between devices, per_device(): lax.all_to_all(copies, ('sub', 'layer'), split_axis=0, concat_axis=0, til...  7.06 us
    pallas_call x3, Pallas kernels, local_call(): pl.pallas_call(body, out_shape=shapes, in_specs=[VMEM_BLOCK] * len(operan...  3.95 us
    ppermute x1, starting transfers between devices, per_device(): before_layer = lax.ppermute(layer_send, 'layer', up_layer)  3.12 us
    ppermute x1, starting transfers between devices, per_device(): after_sub = lax.ppermute(after_send, 'sub', down_sub)  2.27 us
    all_to_all x1, waiting for transfers between devices, per_device(): lax.all_to_all(copies, ('sub', 'layer'), split_axis=0, concat_axis=0, til...  1.7 us
    pallas_call x1, Pallas kernels, per_device(): pl.pallas_call(pick_kernel, out_shape=held, in_specs=[HBM_BLOCK] * len(ta...  1.44 us
    ppermute x1, waiting for transfers between devices, per_device(): after_layer = lax.ppermute(picked_layer, 'layer', down_layer)  1.39 us
  transfers between devices with their start and end apart: 5, of which 3 were waited for; matrix products, arithmetic and copies ran while one was open for 0% of the time, Pallas kernels for 7%

profile of v18, /device:TPU:25, one launch (start us, length us, event | category | flops | bytes accessed | tf_op | source)
XLA Modules:
  0.0 40.2 jit_solution(4376591673743495393)
XLA Ops:
  0.6 1.4 %pick_rows.1 = (f32[24,4096]{1,0:T(8,128)S(1)}, s32[4,128]{1,0:T(4,128)S(1)}, f32[2,128]{1,0:T(2,128)S(1)}, f32[32,128]{1,0:T(8,128)S(1)}, f32[96,128]{1,0:T(8,1...) custom-call(f32[24,4096]{1,0:T(8,128)} %bitcast.11, s32[4,128]{1,0:T(4,128)} %bitcast.14, f32[2,128]{1,0:T(2,128)} %bitcast.15, ...), custom_call_target="tpu_custom_call" | custom-call | tf_op jit(solution)/shard_map/pick_rows/pallas_call | solution.py:567
  2.1 3.1 %collective-permute-start = (f32[32,128]{1,0:T(8,128)S(1)}, f32[32,128]{1,0:T(8,128)S(1)}, u32[]{:S(2)}, u32[]{:S(2)}) collective-permute-start(f32[32,128]{1,0:T(8,128)S(1)} %get-tuple-element.28.layer_ref.up_layer_ref), channel_id=1, source_target_pairs={{0,1},{1,2},{2,3},{4,5},{5,6},{6,7},{8,9},{9,10},{10,11},{12,13},{... | collective-permute-start | bytes 49160 | tf_op jit(solution)/shard_map/ppermute | solution.py:576
  5.2 1.3 %collective-permute-start.1 = (f32[32,128]{1,0:T(8,128)S(1)}, f32[32,128]{1,0:T(8,128)S(1)}, u32[]{:S(2)}, u32[]{:S(2)}) collective-permute-start(f32[32,128]{1,0:T(8,128)S(1)} %get-tuple-element.29.sub_ref.up_sub_ref), channel_id=1, source_target_pairs={{0,4},{4,8},{8,12},{12,16},{16,20},{20,24},{24,28},{1,5},{5,9},{9,... | collective-permute-start | bytes 49160 | tf_op jit(solution)/shard_map/ppermute | solution.py:577
  6.5 0.0 collective-permute-done.theirs_ref.before_layer_ref
  6.5 1.5 %own_rows.1 = (f32[24,4096]{1,0:T(8,128)S(1)}, f32[24,24]{1,0:T(8,128)S(1)}, f32[24,24]{1,0:T(8,128)S(1)}, f32[24,128]{1,0:T(8,128)S(1)}, f32[24,128]{1,0:T(8,128)S(1)}) custom-call(f32[24,4096]{1,0:T(8,128)S(1)} %get-tuple-element.23.vectors_ref, s32[4,128]{1,0:T(4,128)S(1)} %get-tuple-element.24.lists_ref, f32[2,128]{1,0:T(2,128)S(1)} %get-tuple-element.25.face_ref, ...), custom_call_target="tpu_custom_call" | custom-call | flops 8388608 | bytes 8388608 | tf_op jit(solution)/shard_map/own_rows/pallas_call | solution.py:533
  8.0 0.7 %collective-permute-done.1.sub_ref.before_sub_ref = f32[32,128]{1,0:T(8,128)S(1)} collective-permute-done((f32[32,128]{1,0:T(8,128)S(1)}, f32[32,128]{1,0:T(8,128)S(1)}, u32[]{:S(2)}, u32[]{:S(2)}) %collective-permute-start.1) | collective-permute-done | bytes 16416 | tf_op jit(solution)/shard_map/ppermute | solution.py:577
  8.7 1.2 %coarse_tiles.1 = (f32[32,16,128]{2,1,0:T(8,128)}, f32[24,128]{1,0:T(8,128)S(1)}) custom-call(f32[24,24]{1,0:T(8,128)S(1)} %get-tuple-element.33.own_ref, f32[24,24]{1,0:T(8,128)S(1)} %get-tuple-element.34.side_ref, f32[24,128]{1,0:T(8,128)S(1)} %get-tuple-element.31.mine_sub_ref.down_sub_ref, f32[32,128]{1,0:T(8,128)S(1)} %collective-permute-done.1.sub_ref.before_sub_ref), custom_call_target="tpu_custom_call" | custom-call | tf_op jit(solution)/shard_map/coarse_tiles/pallas_call | solution.py:533
  9.9 7.1 %all-to-all-start = ((f32[32,16,128]{2,1,0:T(8,128)}), f32[32,16,128]{2,1,0:T(8,128)S(1)}, u32[]{:S(2)}, u32[]{:S(2)}) async-start(f32[32,16,128]{2,1,0:T(8,128)} %get-tuple-element.37), calls=%async_computation | async-start | bytes 524288 | tf_op jit(solution)/shard_map/all_to_all | solution.py:592
  17.0 1.3 %collective-permute-start.3 = (f32[24,128]{1,0:T(8,128)S(1)}, f32[24,128]{1,0:T(8,128)S(1)}, u32[]{:S(2)}, u32[]{:S(2)}) collective-permute-start(f32[24,128]{1,0:T(8,128)S(1)} %get-tuple-element.32.down_layer_ref), channel_id=1, source_target_pairs={{1,0},{2,1},{3,2},{5,4},{6,5},{7,6},{9,8},{10,9},{11,10},{13,12},{... | collective-permute-start | bytes 36872 | tf_op jit(solution)/shard_map/ppermute | solution.py:585
  18.3 2.3 %collective-permute-start.2 = (f32[24,128]{1,0:T(8,128)S(1)}, f32[24,128]{1,0:T(8,128)S(1)}, u32[]{:S(2)}, u32[]{:S(2)}) collective-permute-start(f32[24,128]{1,0:T(8,128)S(1)} %get-tuple-element.35), channel_id=1, source_target_pairs={{4,0},{8,4},{12,8},{16,12},{20,16},{24,20},{28,24},{5,1},{9,5},{13... | collective-permute-start | bytes 36872 | tf_op jit(solution)/shard_map/ppermute | solution.py:593
  20.5 1.4 %collective-permute-done.3.after_layer_ref = f32[24,128]{1,0:T(8,128)S(1)} collective-permute-done((f32[24,128]{1,0:T(8,128)S(1)}, f32[24,128]{1,0:T(8,128)S(1)}, u32[]{:S(2)}, u32[]{:S(2)}) %collective-permute-start.3) | collective-permute-done | bytes 12320 | tf_op jit(solution)/shard_map/ppermute | solution.py:585
  21.9 0.0 collective-permute-done.2.after_sub_ref
  21.9 1.3 %spread_rows.1 = (f32[24,4096]{1,0:T(8,128)}, f32[8,128]{1,0:T(8,128)S(1)}) custom-call(f32[24,4096]{1,0:T(8,128)S(1)} %get-tuple-element.30.base_ref, s32[4,128]{1,0:T(4,128)S(1)} %get-tuple-element.24.lists_ref, f32[2,128]{1,0:T(2,128)S(1)} %get-tuple-element.25.face_ref, f32[32,128]{1,0:T(8,128)S(1)} %get-tuple-element.29.sub_ref.up_sub_ref, ...), custom_call_target="tpu_custom_call" | custom-call | flops 8388608 | bytes 8388608 | tf_op jit(solution)/shard_map/spread_rows/pallas_call | solution.py:533
  23.2 1.7 %all-to-all-done = f32[32,16,128]{2,1,0:T(8,128)S(1)} async-done(((f32[32,16,128]{2,1,0:T(8,128)}), f32[32,16,128]{2,1,0:T(8,128)S(1)}, u32[]{:S(2)}, u32[]{:S(2)}) %all-to-all-start) | async-done | bytes 262176 | tf_op jit(solution)/shard_map/all_to_all | solution.py:592
  24.9 15.2 %factor_planes.1 = (f32[24,96]{1,0:T(8,128)}, f32[24,96]{1,0:T(8,128)}, f32[24,96]{1,0:T(8,128)}) custom-call(f32[8,4,16,128]{3,2,1,0:T(8,128)S(1)} %bitcast.10, f32[8,128]{1,0:T(8,128)S(1)} %get-tuple-element.38.after_ref), custom_call_target="tpu_custom_call" | custom-call | tf_op jit(solution)/shard_map/factor_planes/pallas_call | solution.py:355
Async XLA Ops:
  2.1 4.4 %collective-permute-start = (f32[32,128]{1,0:T(8,128)S(1)}, f32[32,128]{1,0:T(8,128)S(1)}, u32[]{:S(2)}, u32[]{:S(2)}) collective-permute-start(f32[32,128]{1,0:T(8,128)S(1)} %get-tuple-element.28.layer_ref.up_layer_ref), channel_id=1, source_target_pairs={{0,1},{1,2},{2,3},{4,5},{5,6},{6,7},{8,9},{9,10},{10,11},{12,13},{... | collective-permute-start | bytes 49160 | tf_op jit(solution)/shard_map/ppermute | solution.py:576
  5.2 3.5 %collective-permute-start.1 = (f32[32,128]{1,0:T(8,128)S(1)}, f32[32,128]{1,0:T(8,128)S(1)}, u32[]{:S(2)}, u32[]{:S(2)}) collective-permute-start(f32[32,128]{1,0:T(8,128)S(1)} %get-tuple-element.29.sub_ref.up_sub_ref), channel_id=1, source_target_pairs={{0,4},{4,8},{8,12},{12,16},{16,20},{20,24},{24,28},{1,5},{5,9},{9,... | collective-permute-start | bytes 49160 | tf_op jit(solution)/shard_map/ppermute | solution.py:577
  9.9 15.1 %all-to-all-start = ((f32[32,16,128]{2,1,0:T(8,128)}), f32[32,16,128]{2,1,0:T(8,128)S(1)}, u32[]{:S(2)}, u32[]{:S(2)}) async-start(f32[32,16,128]{2,1,0:T(8,128)} %get-tuple-element.37), calls=%async_computation | async-start | bytes 524288 | tf_op jit(solution)/shard_map/all_to_all | solution.py:592
  17.0 5.0 %collective-permute-start.3 = (f32[24,128]{1,0:T(8,128)S(1)}, f32[24,128]{1,0:T(8,128)S(1)}, u32[]{:S(2)}, u32[]{:S(2)}) collective-permute-start(f32[24,128]{1,0:T(8,128)S(1)} %get-tuple-element.32.down_layer_ref), channel_id=1, source_target_pairs={{1,0},{2,1},{3,2},{5,4},{6,5},{7,6},{9,8},{10,9},{11,10},{13,12},{... | collective-permute-start | bytes 36872 | tf_op jit(solution)/shard_map/ppermute | solution.py:585
  18.3 3.7 %collective-permute-start.2 = (f32[24,128]{1,0:T(8,128)S(1)}, f32[24,128]{1,0:T(8,128)S(1)}, u32[]{:S(2)}, u32[]{:S(2)}) collective-permute-start(f32[24,128]{1,0:T(8,128)S(1)} %get-tuple-element.35), channel_id=1, source_target_pairs={{4,0},{8,4},{12,8},{16,12},{20,16},{24,20},{28,24},{5,1},{9,5},{13... | collective-permute-start | bytes 36872 | tf_op jit(solution)/shard_map/ppermute | solution.py:593
